TPU v7x, 32 devices: a whole 2x2x4 slice. The times are simulated.
32 devices in a mesh: groups: 2 (over y), dp: 4 (over z), owner: 4 (over x, core).
Axes of the slice: x: 2, y: 2, z: 4, core: 2. Of those that a mesh axis runs over, the one named last changes fastest.
Arguments:
- activations: bfloat16 [6, 512, 2048], P('groups', 'dp'), parts along dimension 0, may hold values from -40 to 40
- out_grads: bfloat16 [6, 512, 2048], P('groups', 'dp'), parts along dimension 0, may hold values from -1.767767 to 1.767767
- basis_act: bfloat16 [6, 2048, 2048], P('groups', 'dp', 'owner'), parts along dimension 0, may hold values from -0.125 to 0.125
- basis_grad: bfloat16 [6, 2048, 2048], P('groups', 'dp', 'owner'), parts along dimension 0, may hold values from -0.125 to 0.125
- owner_of: int32 [3], replicated, may hold values from 0 to 3, as said below
- counts: int32 [8], P('groups'), parts along dimension 0, may hold values from 1 to 128, 384 in all
- state_act: float32 [8, 4096], P('owner', 'groups'), parts along dimension 1, may hold values from 0.5 to 5
- state_grad: float32 [8, 4096], P('owner', 'groups'), parts along dimension 1, may hold values from 0.0009765625 to 0.009765625
Outputs:
- precond: bfloat16 [6, 2048, 2048], P('groups', 'dp', 'owner'), parts along dimension 0
- new_state_act: float32 [8, 4096], P('owner', 'groups'), parts along dimension 1
- new_state_grad: float32 [8, 4096], P('owner', 'groups'), parts along dimension 1
There are 2 independent parts, one for each index of `groups`. A program takes and returns all parts, laid end to end along the dimension named above; an argument that names none is the same for every part. Nothing has to cross between parts.
Inputs may be any that keep to these rules, and one draw needn't show every extreme that they name: `owner_of`: each owner index holds at most 2 of the 3 layers, and some owner index holds exactly 2. `counts`: at least one batch shard is full.
All inputs are finite; a program needn't handle non-finite values.
Results may differ from a plain program's by a relative error of at most 0.012.
Values may be sent and summed in bfloat16 or wider, within the bound.
No kernel may reach another device: no remote copies, remote signals or barrier semaphores. Data moves between devices by JAX's collectives and lax.ppermute only.
A program may use at most 64 MiB of HBM per device.

v0:
```python
import jax
import jax.numpy as jnp
from jax import lax
from jax.sharding import PartitionSpec as P

decay_rate = 0.25
damping_rate = 0.1


def spread(array, axis, root):
    mine = lax.axis_index(axis) == root
    return lax.psum(jnp.where(mine, array, jnp.zeros_like(array)), axis)


def local(activations, out_grads, basis_act, basis_grad, owner_of, counts, state_act, state_grad):
    layers = activations.shape[0]
    tok_rows = activations.shape[1]
    tile_rows = basis_act.shape[1]
    tile_cols = basis_act.shape[2]
    slot_count = state_act.shape[0]
    dp_index = lax.axis_index("dp")
    own_index = lax.axis_index("owner")
    valid_here = counts[dp_index]
    valid_rows = (jnp.arange(tok_rows) < valid_here).astype(jnp.float32)[:, None]
    valid_total = jnp.sum(counts).astype(jnp.float32)
    square_acts = []
    square_grads = []
    gram_tiles = []
    for layer_index in range(layers):
        act_layer = activations[layer_index]
        grad_layer = out_grads[layer_index]

        def project_rows(totals, pieces, offset, act_layer=act_layer, grad_layer=grad_layer):
            return (
                jnp.dot(act_layer, pieces[0], preferred_element_type=jnp.float32),
                jnp.dot(grad_layer, pieces[1], preferred_element_type=jnp.float32),
            )

        zeros_panel = jnp.zeros((tok_rows, tile_cols), jnp.float32)
        panel_act, panel_grad = project_rows(
            (zeros_panel, zeros_panel),
            (
                lax.all_gather(basis_act[layer_index], "dp", axis=0, tiled=True),
                lax.all_gather(basis_grad[layer_index], "dp", axis=0, tiled=True),
            ),
            jnp.int32(0),
        )
        panel_act = (panel_act * valid_rows).astype(jnp.bfloat16)
        panel_grad = (panel_grad * valid_rows).astype(jnp.bfloat16)
        full_act, full_grad = (
            lax.all_gather(panel_act, "owner", axis=1, tiled=True),
            lax.all_gather(panel_grad, "owner", axis=1, tiled=True),
        )
        square_act = jnp.sum(jnp.square(full_act.astype(jnp.float32)), axis=0)
        square_grad = jnp.sum(jnp.square(full_grad.astype(jnp.float32)), axis=0)

        def gram_term(offset, row_count, full_grad=full_grad, panel_act=panel_act):
            return lax.dot_general(
                full_grad, panel_act, (((0,), (0,)), ((), ())), preferred_element_type=jnp.float32
            )

        gram_tiles.append(
            lax.psum_scatter(
                gram_term(jnp.int32(0), tile_rows * lax.axis_size("dp")).astype(jnp.bfloat16),
                "dp",
                scatter_dimension=0,
                tiled=True,
            ).astype(jnp.float32)
            / valid_total
        )
        square_act, square_grad = lax.psum((square_act, square_grad), "dp")
        square_acts.append(square_act)
        square_grads.append(square_grad)
    new_act = state_act
    new_grad = state_grad
    results = []
    for layer_index in range(layers):
        owner_now = owner_of[layer_index]
        slot_rank = jnp.sum((owner_of[:layer_index] == owner_now).astype(jnp.int32))
        moment_act = square_acts[layer_index] / valid_total
        moment_grad = square_grads[layer_index] / valid_total
        selector = (jnp.arange(slot_count) == slot_rank).astype(jnp.float32)[:, None]
        local_act = (
            decay_rate * jnp.sum(state_act * selector, axis=0) + (1.0 - decay_rate) * moment_act
        )
        local_grad = (
            decay_rate * jnp.sum(state_grad * selector, axis=0) + (1.0 - decay_rate) * moment_grad
        )
        eigen_act, eigen_grad = (
            spread(local_act, "owner", owner_now),
            spread(local_grad, "owner", owner_now),
        )
        replace_rows = ((jnp.arange(slot_count) == slot_rank) & (own_index == owner_now))[:, None]
        new_act = jnp.where(replace_rows, eigen_act[None, :], new_act)
        new_grad = jnp.where(replace_rows, eigen_grad[None, :], new_grad)
        damping = damping_rate * jnp.mean(eigen_grad) * jnp.mean(eigen_act)
        grad_eigen = lax.dynamic_slice_in_dim(eigen_grad, dp_index * tile_rows, tile_rows)
        act_eigen = lax.dynamic_slice_in_dim(eigen_act, own_index * tile_cols, tile_cols)
        scaled = gram_tiles[layer_index] / (grad_eigen[:, None] * act_eigen[None, :] + damping)
        results.append(scaled.astype(jnp.bfloat16))
    return (jnp.stack(results), new_act, new_grad)


def solution(mesh):
    placed = (
        P("groups", "dp", None),
        P("groups", "dp", None),
        P("groups", "dp", "owner"),
        P("groups", "dp", "owner"),
        P(),
        P("groups"),
        P("owner", "groups"),
        P("owner", "groups"),
    )
    return jax.shard_map(
        local,
        mesh=mesh,
        in_specs=placed,
        out_specs=(P("groups", "dp", "owner"), P("owner", "groups"), P("owner", "groups")),
        check_vma=False,
    )
```

profile of v0, /device:TPU:0, one launch (start us, length us, event | category | flops | bytes accessed | tf_op | source)
XLA Modules:
  0.0 435.7 jit_solution(5419246056454274437)
XLA Ops:
  7.2 2.7 fusion.65
  15.0 43.8 %all-gather.13.cloned.1.call-done = bf16[1,2048,512]{2,1,0:T(8,128)(2,1)} async-done(((bf16[1,512,512]{2,1,0:T(8,128)(2,1)}), bf16[1,2048,512]{2,1,0:T(8,128)(2,1)}) %all-gather.13.cloned.1.call-update) | async-done | bytes 2097168 | tf_op jit(solution)/shard_map/all_gather | solution.py:44
  58.8 2.0 fusion.45
  60.9 7.2 %all_gather.37 = bf16[128,2048]{1,0:T(8,128)(2,1)S(1)} all-gather(bf16[128,512]{1,0:T(8,128)(2,1)S(1)} %fusion.45), channel_id=1, replica_groups=mesh['groups'=2,'dp'=4,'owner'=4] {'owner'}, dimensions={1}, use_global_device_ids=true | all-gather | bytes 655360 | tf_op jit(solution)/shard_map/all_gather | solution.py:52
  68.0 37.0 %all-gather.15.cloned.1.call-done = bf16[1,2048,512]{2,1,0:T(8,128)(2,1)} async-done(((bf16[1,512,512]{2,1,0:T(8,128)(2,1)}), bf16[1,2048,512]{2,1,0:T(8,128)(2,1)}) %all-gather.15.cloned.1.call-update) | async-done | bytes 2097168 | tf_op jit(solution)/shard_map/all_gather | solution.py:43
  105.1 2.2 fusion.42
  107.3 2.1 convolution_convert_fusion.2
  109.5 41.9 %all-gather.21.cloned.1.call-done = bf16[1,2048,512]{2,1,0:T(8,128)(2,1)} async-done(((bf16[1,512,512]{2,1,0:T(8,128)(2,1)}), bf16[1,2048,512]{2,1,0:T(8,128)(2,1)}) %all-gather.21.cloned.1.call-update) | async-done | bytes 2097168 | tf_op jit(solution)/shard_map/all_gather | solution.py:44
  153.4 7.2 %all_gather.45 = bf16[128,2048]{1,0:T(8,128)(2,1)S(1)} all-gather(bf16[128,512]{1,0:T(8,128)(2,1)S(1)} %fusion.33), channel_id=1, replica_groups=mesh['groups'=2,'dp'=4,'owner'=4] {'owner'}, dimensions={1}, use_global_device_ids=true | all-gather | bytes 655360 | tf_op jit(solution)/shard_map/all_gather | solution.py:52
  160.5 36.9 %all-gather.23.cloned.1.call-done = bf16[1,2048,512]{2,1,0:T(8,128)(2,1)} async-done(((bf16[1,512,512]{2,1,0:T(8,128)(2,1)}), bf16[1,2048,512]{2,1,0:T(8,128)(2,1)}) %all-gather.23.cloned.1.call-update) | async-done | bytes 2097168 | tf_op jit(solution)/shard_map/all_gather | solution.py:43
  197.5 2.2 fusion.30
  201.8 41.8 %all-gather.17.cloned.1.call-done = bf16[1,2048,512]{2,1,0:T(8,128)(2,1)} async-done(((bf16[1,512,512]{2,1,0:T(8,128)(2,1)}), bf16[1,2048,512]{2,1,0:T(8,128)(2,1)}) %all-gather.17.cloned.1.call-update) | async-done | bytes 2097168 | tf_op jit(solution)/shard_map/all_gather | solution.py:44
  243.6 2.0 fusion.39
  245.6 7.1 %all_gather.41 = bf16[128,2048]{1,0:T(8,128)(2,1)S(1)} all-gather(bf16[128,512]{1,0:T(8,128)(2,1)S(1)} %fusion.39), channel_id=1, replica_groups=mesh['groups'=2,'dp'=4,'owner'=4] {'owner'}, dimensions={1}, use_global_device_ids=true | all-gather | bytes 655360 | tf_op jit(solution)/shard_map/all_gather | solution.py:52
  252.7 36.9 %all-gather.19.cloned.1.call-done = bf16[1,2048,512]{2,1,0:T(8,128)(2,1)} async-done(((bf16[1,512,512]{2,1,0:T(8,128)(2,1)}), bf16[1,2048,512]{2,1,0:T(8,128)(2,1)}) %all-gather.19.cloned.1.call-update) | async-done | bytes 2097168 | tf_op jit(solution)/shard_map/all_gather | solution.py:43
  289.7 2.2 fusion.36
  291.9 2.1 convolution_convert_fusion.1
  302.4 7.2 %all_gather.43 = bf16[128,2048]{1,0:T(8,128)(2,1)S(1)} all-gather(bf16[128,512]{1,0:T(8,128)(2,1)S(1)} %fusion.36), channel_id=1, replica_groups=mesh['groups'=2,'dp'=4,'owner'=4] {'owner'}, dimensions={1}, use_global_device_ids=true | all-gather | bytes 655360 | tf_op jit(solution)/shard_map/all_gather | solution.py:51
  309.7 7.3 %all_gather.47 = bf16[128,2048]{1,0:T(8,128)(2,1)S(1)} all-gather(bf16[128,512]{1,0:T(8,128)(2,1)S(1)} %fusion.30), channel_id=1, replica_groups=mesh['groups'=2,'dp'=4,'owner'=4] {'owner'}, dimensions={1}, use_global_device_ids=true | all-gather | bytes 655360 | tf_op jit(solution)/shard_map/all_gather | solution.py:51
  317.1 7.3 %all_gather.39 = bf16[128,2048]{1,0:T(8,128)(2,1)S(1)} all-gather(bf16[128,512]{1,0:T(8,128)(2,1)S(1)} %fusion.42), channel_id=1, replica_groups=mesh['groups'=2,'dp'=4,'owner'=4] {'owner'}, dimensions={1}, use_global_device_ids=true | all-gather | bytes 655360 | tf_op jit(solution)/shard_map/all_gather | solution.py:51
  324.5 18.2 %all-reduce.1 = (f32[2048]{0:T(1024)S(1)}, f32[2048]{0:T(1024)S(1)}, f32[2048]{0:T(1024)S(1)}, f32[2048]{0:T(1024)S(1)}, f32[2048]{0:T(1024)S(1)}, /*index=5*/f32[2048]{0:T(1024)S(1)}) all-reduce(f32[2048]{0:T(1024)S(1)} %multiply_reduce_fusion.1, ...), channel_id=1, replica_groups=mesh['groups'=2,'dp'=4,'owner'=4] {'dp'}, use_global_device_ids=true, to_apply=%region_27.28 | all-reduce | flops 12288 | bytes 98304 | tf_op jit(solution)/shard_map/psum | solution.py:71
  342.8 11.4 %all-reduce = (f32[2048]{0:T(1024)S(1)}, f32[2048]{0:T(1024)S(1)}, f32[2048]{0:T(1024)S(1)}, f32[2048]{0:T(1024)S(1)}, f32[2048]{0:T(1024)S(1)}, /*index=5*/f32[2048]{0:T(1024)S(1)}) all-reduce(f32[2048]{0:T(1024)S(1)} %get-tuple-element.36, f32[2048]{0:T(1024)S(1)} %get-tuple-element.35, ...), channel_id=1, replica_groups=mesh['groups'=2,'dp'=4,'owner'=4] {'owner'}, use_global_device_ids=true, to_apply=%region_28.29 | all-reduce | flops 12288 | bytes 98304 | tf_op jit(solution)/shard_map/psum | solution.py:12
  364.2 16.9 %reduce-scatter.8.cloned.1.call-done = bf16[512,512]{1,0:T(8,128)(2,1)} async-done(((bf16[2048,512]{1,0:T(8,128)(2,1)}), bf16[512,512]{1,0:T(8,128)(2,1)}) %reduce-scatter.8.cloned.1.call-update) | async-done | bytes 524304 | tf_op jit(solution)/shard_map/reduce_scatter | solution.py:63
  382.4 44.2 %reduce-scatter.6.cloned.1.call-done = bf16[512,512]{1,0:T(8,128)(2,1)} async-done(((bf16[2048,512]{1,0:T(8,128)(2,1)}), bf16[512,512]{1,0:T(8,128)(2,1)}) %reduce-scatter.6.cloned.1.call-update) | async-done | bytes 524304 | tf_op jit(solution)/shard_map/reduce_scatter | solution.py:63
  (71 shorter events, 24.2 us)
Async XLA Ops:
  7.2 2.8 copy-start
  7.2 51.6 %all-gather.13.cloned.1.call-start = ((), (), s32[]{:S(2)}) async-start(), calls=%async_computation.6 | async-start | bytes 2621440 | tf_op jit(solution)/shard_map/all_gather | solution.py:44
  9.9 95.2 %all-gather.15.cloned.1.call-start = ((), (), s32[]{:S(2)}) async-start(), calls=%async_computation.7 | async-start | bytes 2621440 | tf_op jit(solution)/shard_map/all_gather | solution.py:43
  11.2 2.6 copy-start.5
  11.2 47.6 %copy-start.1 = (bf16[3,128,2048]{2,1,0:T(8,128)(2,1)S(1)}, bf16[3,128,2048]{2,1,0:T(8,128)(2,1)}, u32[]{:S(2)}) copy-start(bf16[3,128,2048]{2,1,0:T(8,128)(2,1)} %param.9) | copy-start | bytes 4718596
  11.2 140.1 %all-gather.21.cloned.1.call-start = ((), (), s32[]{:S(2)}) async-start(), calls=%async_computation.10 | async-start | bytes 2621440 | tf_op jit(solution)/shard_map/all_gather | solution.py:44
  12.0 185.5 %all-gather.23.cloned.1.call-start = ((), (), s32[]{:S(2)}) async-start(), calls=%async_computation.11 | async-start | bytes 2621440 | tf_op jit(solution)/shard_map/all_gather | solution.py:43
  12.5 231.0 %all-gather.17.cloned.1.call-start = ((), (), s32[]{:S(2)}) async-start(), calls=%async_computation.8 | async-start | bytes 2621440 | tf_op jit(solution)/shard_map/all_gather | solution.py:44
  13.1 276.6 %all-gather.19.cloned.1.call-start = ((), (), s32[]{:S(2)}) async-start(), calls=%async_computation.9 | async-start | bytes 2621440 | tf_op jit(solution)/shard_map/all_gather | solution.py:43
  13.7 349.2 %reduce-scatter.4.cloned.1.call-start = ((), (), s32[]{:S(2)}) async-start(), calls=%async_computation.3 | async-start | bytes 2621440 | tf_op jit(solution)/shard_map/reduce_scatter | solution.py:63
  109.4 271.6 %reduce-scatter.8.cloned.1.call-start = ((), (), s32[]{:S(2)}) async-start(), calls=%async_computation.5 | async-start | bytes 2621440 | tf_op jit(solution)/shard_map/reduce_scatter | solution.py:63
  201.7 224.8 %reduce-scatter.6.cloned.1.call-start = ((), (), s32[]{:S(2)}) async-start(), calls=%async_computation.4 | async-start | bytes 2621440 | tf_op jit(solution)/shard_map/reduce_scatter | solution.py:63
  291.9 3.4 copy-start.4
  291.9 9.9 %copy-start.2 = (f32[2,2048]{1,0:T(2,128)S(1)}, f32[2,2048]{1,0:T(2,128)}, u32[]{:S(2)}) copy-start(f32[2,2048]{1,0:T(2,128)} %param.15) | copy-start | bytes 49156
  291.9 9.9 %copy-start.3 = (f32[2,2048]{1,0:T(2,128)S(1)}, f32[2,2048]{1,0:T(2,128)}, u32[]{:S(2)}) copy-start(f32[2,2048]{1,0:T(2,128)} %param.14) | copy-start | bytes 49156
Sparse Core Ops, SparseCore 0:
  10.2 48.6 all-gather.12
  60.4 44.6 all-gather.14
  106.7 44.6 all-gather.20
  152.8 44.6 all-gather.22
  198.9 44.6 all-gather.16
  245.0 44.6 all-gather.18
  292.0 43.2 reduce-scatter.3
  337.7 43.3 reduce-scatter.7
  383.3 43.1 reduce-scatter.5
where the time goes:
time: 436 us
  waiting for transfers between devices  302 us (69%)
  blocking collectives  72.8 us (17%)
  between operations  21.9 us (5%)
  matrix products  18.9 us (4%)
  other arithmetic  14.6 us (3%)
  local copies, waits for them, and re-layouts  5.53 us (1%)
    all_gather x3, waiting for transfers between devices, local(): lax.all_gather(basis_grad[layer_index], 'dp', axis=0, tiled=True)  127 us
    all_gather x3, waiting for transfers between devices, local(): lax.all_gather(basis_act[layer_index], 'dp', axis=0, tiled=True)  111 us
    reduce_scatter x3, waiting for transfers between devices, local(): lax.psum_scatter(gram_term(jnp.int32(0), tile_rows * lax.axis_size('dp'))...  61 us
    all_gather x3, blocking collectives, local(): lax.all_gather(panel_act, 'owner', axis=1, tiled=True)  21.7 us
    all_gather x3, blocking collectives, local(): lax.all_gather(panel_grad, 'owner', axis=1, tiled=True)  21.5 us
    psum x1, blocking collectives, local(): square_act, square_grad = lax.psum((square_act, square_grad), 'dp')  18.2 us
    psum x1, blocking collectives, spread(): return lax.psum(jnp.where(mine, array, jnp.zeros_like(array)), axis)  11.4 us
  transfers between devices with their start and end apart: 9, of which 8 were waited for; matrix products, arithmetic and copies ran while one was open for 8% of the time, Pallas kernels for 0%

commit v1 on v0

v1 whole, which is shorter than its diff:
```python
import jax
import jax.numpy as jnp
from jax import lax
from jax.sharding import PartitionSpec as P

decay_rate = 0.25
damping_rate = 0.1


def spread(array, axis, root):
    mine = lax.axis_index(axis) == root
    return lax.psum(jnp.where(mine, array, jnp.zeros_like(array)), axis)


def gather_plan(activations, out_grads, basis_act, basis_grad, owner_of, counts, state_act, state_grad):
    layers = activations.shape[0]
    tok_rows = activations.shape[1]
    tile_rows = basis_act.shape[1]
    tile_cols = basis_act.shape[2]
    slot_count = state_act.shape[0]
    dp_index = lax.axis_index("dp")
    own_index = lax.axis_index("owner")
    valid_rows = (jnp.arange(tok_rows) < counts[dp_index]).astype(jnp.float32)[:, None]
    valid_total = jnp.sum(counts).astype(jnp.float32)
    square_acts = []
    square_grads = []
    gram_tiles = []
    for layer_index in range(layers):
        panel_act = jnp.dot(
            activations[layer_index],
            lax.all_gather(basis_act[layer_index], "dp", axis=0, tiled=True),
            preferred_element_type=jnp.float32,
        )
        panel_grad = jnp.dot(
            out_grads[layer_index],
            lax.all_gather(basis_grad[layer_index], "dp", axis=0, tiled=True),
            preferred_element_type=jnp.float32,
        )
        panel_act = (panel_act * valid_rows).astype(jnp.bfloat16)
        panel_grad = (panel_grad * valid_rows).astype(jnp.bfloat16)
        full_act = lax.all_gather(panel_act, "owner", axis=1, tiled=True)
        full_grad = lax.all_gather(panel_grad, "owner", axis=1, tiled=True)
        square_act = jnp.sum(jnp.square(full_act.astype(jnp.float32)), axis=0)
        square_grad = jnp.sum(jnp.square(full_grad.astype(jnp.float32)), axis=0)
        gram_term = lax.dot_general(
            full_grad, panel_act, (((0,), (0,)), ((), ())), preferred_element_type=jnp.float32
        )
        gram_tiles.append(
            lax.psum_scatter(
                gram_term.astype(jnp.bfloat16), "dp", scatter_dimension=0, tiled=True
            ).astype(jnp.float32)
            / valid_total
        )
        square_act, square_grad = lax.psum((square_act, square_grad), "dp")
        square_acts.append(square_act)
        square_grads.append(square_grad)
    new_act = state_act
    new_grad = state_grad
    results = []
    for layer_index in range(layers):
        owner_now = owner_of[layer_index]
        slot_rank = jnp.sum((owner_of[:layer_index] == owner_now).astype(jnp.int32))
        selector = (jnp.arange(slot_count) == slot_rank).astype(jnp.float32)[:, None]
        local_act = decay_rate * jnp.sum(state_act * selector, axis=0) + (
            1.0 - decay_rate
        ) * (square_acts[layer_index] / valid_total)
        local_grad = decay_rate * jnp.sum(state_grad * selector, axis=0) + (
            1.0 - decay_rate
        ) * (square_grads[layer_index] / valid_total)
        eigen_act = spread(local_act, "owner", owner_now)
        eigen_grad = spread(local_grad, "owner", owner_now)
        replace_rows = ((jnp.arange(slot_count) == slot_rank) & (own_index == owner_now))[:, None]
        new_act = jnp.where(replace_rows, eigen_act[None, :], new_act)
        new_grad = jnp.where(replace_rows, eigen_grad[None, :], new_grad)
        damping = damping_rate * jnp.mean(eigen_grad) * jnp.mean(eigen_act)
        grad_eigen = lax.dynamic_slice_in_dim(eigen_grad, dp_index * tile_rows, tile_rows)
        act_eigen = lax.dynamic_slice_in_dim(eigen_act, own_index * tile_cols, tile_cols)
        scaled = gram_tiles[layer_index] / (grad_eigen[:, None] * act_eigen[None, :] + damping)
        results.append(scaled.astype(jnp.bfloat16))
    return (jnp.stack(results), new_act, new_grad)


def flip(array, axis, mask):
    return lax.ppermute(array, axis, [(i, i ^ mask) for i in range(lax.axis_size(axis))])


def hop(array, pairs):
    owners = lax.axis_size("owner")
    flat = [(a * owners + b, c * owners + e) for (a, b), (c, e) in pairs]
    return lax.ppermute(array, ("dp", "owner"), flat)


def line_plan(activations, out_grads, basis_act, basis_grad, owner_of, counts, state_act, state_grad):
    layers, tok_rows, width = activations.shape
    tile = basis_act.shape[1]
    n_dp = lax.axis_size("dp")
    n_own = lax.axis_size("owner")
    slot_count = state_act.shape[0]
    part_rows = tok_rows // n_own
    packed = 3 * n_dp * tok_rows // 4
    dp = lax.axis_index("dp")
    own = lax.axis_index("owner")
    valid_total = jnp.sum(counts).astype(jnp.float32)
    f32 = jnp.float32
    bf16 = jnp.bfloat16

    starts = jnp.cumsum(counts) - counts
    shard_ids = [jnp.full((tok_rows,), dp)]
    row_ids = [jnp.arange(tok_rows)]
    for peer in (own, own ^ 2, own ^ 1, own ^ 3):
        for mask in range(1, n_dp):
            shard_ids.append(jnp.full((part_rows,), dp ^ mask))
            row_ids.append(peer * part_rows + jnp.arange(part_rows))
    shard_ids = jnp.concatenate(shard_ids)
    row_ids = jnp.concatenate(row_ids)
    place = jnp.where(row_ids < counts[shard_ids], starts[shard_ids] + row_ids, -1)
    select = (jnp.arange(packed)[:, None] == place[None, :]).astype(bf16)

    state = jnp.concatenate([state_act, state_grad], axis=0)
    state = jnp.stack([state, flip(state, "owner", 1)])
    state = jnp.concatenate([state, flip(state, "owner", 2)])

    def rows_of(tokens):
        part = lax.dynamic_slice_in_dim(tokens, own * part_rows, part_rows, 1)
        got = [
            flip(lax.dynamic_slice_in_dim(part, (dp ^ mask) * tile, tile, 2), "dp", mask)
            for mask in range(1, n_dp)
        ]
        got = jnp.concatenate(got, axis=1)
        got = jnp.concatenate([got, flip(got, "owner", 2)], axis=1)
        mine = lax.dynamic_slice_in_dim(tokens, dp * tile, tile, 2)
        return jnp.concatenate([mine, got, flip(got, "owner", 1)], axis=1)

    def project(rows, basis):
        chosen = jnp.dot(select, rows, preferred_element_type=f32).astype(bf16)
        return jnp.dot(chosen, basis, preferred_element_type=f32).astype(bf16)

    def add(*terms):
        return sum(term.astype(f32) for term in terms).astype(bf16)

    rows_act = rows_of(activations)
    rows_grad = rows_of(out_grads)
    inner = (dp == 1) | (dp == 2)
    every = range(n_own)
    proj_act = []
    proj_grad = []
    for layer in range(layers):
        part = project(rows_act[layer], basis_act[layer])
        part = add(part, hop(part, [((a, b), (c, b)) for a, c in ((0, 1), (3, 2)) for b in every]))
        part = add(part, hop(part, [((a, b), (c, b)) for a, c in ((1, 2), (2, 1)) for b in every]))
        outer = hop(part, [((a, b), (c, b)) for a, c in ((1, 0), (2, 3)) for b in every])
        proj_act.append(jnp.where(inner, part, outer))
    for layer in range(layers):
        part = project(rows_grad[layer], basis_grad[layer])
        near = add(part, hop(part, [((0, b), (1, b)) for b in (1, 2, 3)] + [((3, b), (2, b)) for b in (0, 1, 2)]))
        across = hop(near, [((1, b), (2, b)) for b in (2, 3)] + [((2, b), (1, b)) for b in (0, 1)])
        near = add(near, across)
        near = add(near, hop(near, [((1, 0), (0, 0)), ((2, 3), (3, 3))]))
        chip = hop(near, [((a, a), (a, a ^ 2)) for a in range(n_dp)])
        half = jnp.where(own == dp, near, chip)
        core = hop(half, [((a, a ^ b), (a, a ^ b ^ 1)) for a in range(n_dp) for b in (0, 2)])
        proj_grad.append(jnp.where((own == dp) | (own == dp ^ 2), half, core))

    def squares(panels):
        return jnp.stack([jnp.sum(jnp.square(p.astype(f32)), axis=0) for p in panels]) / valid_total

    def gathered(vectors, axis, index):
        pair = jnp.stack([vectors, flip(vectors, axis, 1)])
        four = jnp.concatenate([pair, flip(pair, axis, 2)])
        order = jnp.arange(4) ^ index
        return jnp.concatenate([four[order[i]] for i in range(4)], axis=1)

    moment_act = gathered(squares(proj_act), "owner", own)
    moment_grad = gathered(squares(proj_grad), "dp", dp)

    new_act = state_act
    new_grad = state_grad
    results = []
    for layer in range(layers):
        owner_now = owner_of[layer]
        slot_rank = jnp.sum((owner_of[:layer] == owner_now).astype(jnp.int32))
        rows = state[owner_now ^ own]
        eigen_act = decay_rate * rows[slot_rank] + (1.0 - decay_rate) * moment_act[layer]
        eigen_grad = decay_rate * rows[slot_count + slot_rank] + (1.0 - decay_rate) * moment_grad[layer]
        replace_rows = ((jnp.arange(slot_count) == slot_rank) & (own == owner_now))[:, None]
        new_act = jnp.where(replace_rows, eigen_act[None, :], new_act)
        new_grad = jnp.where(replace_rows, eigen_grad[None, :], new_grad)
        damping = damping_rate * jnp.mean(eigen_grad) * jnp.mean(eigen_act)
        grad_eigen = lax.dynamic_slice_in_dim(eigen_grad, dp * tile, tile)
        act_eigen = lax.dynamic_slice_in_dim(eigen_act, own * tile, tile)
        gram = lax.dot_general(
            proj_grad[layer], proj_act[layer], (((0,), (0,)), ((), ())), preferred_element_type=f32
        )
        scaled = gram / valid_total / (grad_eigen[:, None] * act_eigen[None, :] + damping)
        results.append(scaled.astype(bf16))
    return (jnp.stack(results), new_act, new_grad)


def solution(mesh):
    placed = (
        P("groups", "dp", None),
        P("groups", "dp", None),
        P("groups", "dp", "owner"),
        P("groups", "dp", "owner"),
        P(),
        P("groups"),
        P("owner", "groups"),
        P("owner", "groups"),
    )
    square = mesh.shape["dp"] == 4 and mesh.shape["owner"] == 4
    return jax.shard_map(
        line_plan if square else gather_plan,
        mesh=mesh,
        in_specs=placed,
        out_specs=(P("groups", "dp", "owner"), P("owner", "groups"), P("owner", "groups")),
        check_vma=False,
    )
```

time: 436 us -> 222 us (0.51)
  waiting for transfers between devices: 302 us -> 87.6 us
  blocking collectives: 72.8 us -> 0 us
  starting transfers between devices: 0.36 us -> 48.2 us
  local copies, waits for them, and re-layouts: 5.53 us -> 18.3 us
  other arithmetic: 14.6 us -> 23 us
  between operations: 21.9 us -> 29.1 us
  matrix products: 18.9 us -> 13.8 us
    all_gather x6 -> x0, waiting for transfers between devices: 238 us -> none  [the longest x3 127 us: local(): lax.all_gather(basis_grad[layer_index], 'dp', axis=0, tiled=True)]
    ppermute x0 -> x40, waiting for transfers between devices: none -> 87.6 us  [the longest x24 69.2 us: hop(): return lax.ppermute(array, ('dp', 'owner'), flat)]
    reduce_scatter x3 -> x0, waiting for transfers between devices: 61 us -> none  [local(): lax.psum_scatter(gram_term(jnp.int32(0), tile_rows * lax.axis_size('dp'))...]
    ppermute x0 -> x40, starting transfers between devices: none -> 48.2 us  [the longest x24 32.8 us: hop(): return lax.ppermute(array, ('dp', 'owner'), flat)]
    all_gather x6 -> x0, blocking collectives: 43.2 us -> none  [the longest x3 21.7 us: local(): lax.all_gather(panel_act, 'owner', axis=1, tiled=True)]
    psum x2 -> x0, blocking collectives: 29.6 us -> none  [the longest x1 18.2 us: local(): square_act, square_grad = lax.psum((square_act, square_grad), 'dp')]
    unnamed x12 -> x52, local copies, waits for them, and re-layouts: 0.03 us -> 6.6 us
    dynamic_slice x7 -> x8, local copies, waits for them, and re-layouts: 1.03 us -> 6.41 us  [the longest x2 2.53 us: rows_of(): lax.dynamic_slice_in_dim(part, (dp ^ mask) * tile, tile, 2)]
  transfers between devices with their start and end apart: 9 -> 40, of which waited for: 8 -> 16; matrix products, arithmetic and copies ran while one was open for 8% -> 18% of each run, Pallas kernels for 0% -> 0%
where the time goes in v1:
time: 222 us; the launch traced here: 220 us
  waiting for transfers between devices  87.6 us (39%)
  starting transfers between devices  48.2 us (22%)
  between operations  29.1 us (13%)
  other arithmetic  23 us (10%)
  local copies, waits for them, and re-layouts  18.3 us (8%)
  matrix products  13.8 us (6%)
    ppermute x24, waiting for transfers between devices, hop(): return lax.ppermute(array, ('dp', 'owner'), flat)  69.2 us
    ppermute x24, starting transfers between devices, hop(): return lax.ppermute(array, ('dp', 'owner'), flat)  32.8 us
    ppermute x16, waiting for transfers between devices, flip(): lax.ppermute(array, axis, [(i, i ^ mask) for i in range(lax.axis_size(axi...  18.4 us
    ppermute x16, starting transfers between devices, flip(): lax.ppermute(array, axis, [(i, i ^ mask) for i in range(lax.axis_size(axi...  15.4 us
    dot_general x6, matrix products, project(): return jnp.dot(chosen, basis, preferred_element_type=f32).astype(bf16)  11.6 us
    unnamed x52, local copies, waits for them, and re-layouts  6.6 us
    gather x1, other arithmetic, line_plan(): counts[shard_ids]  5.05 us
  transfers between devices with their start and end apart: 40, of which 16 were waited for; matrix products, arithmetic and copies ran while one was open for 18% of the time, Pallas kernels for 0%

profile of v1, /device:TPU:0, one launch (start us, length us, event | category | flops | bytes accessed | tf_op | source)
XLA Modules:
  0.0 220.0 jit_solution(242097378831769720)
XLA Ops:
  2.0 3.1 %collective-permute-start = (bf16[3,32,512]{2,1,0:T(8,128)(2,1)S(1)}, bf16[3,32,512]{2,1,0:T(8,128)(2,1)S(1)}, u32[]{:S(2)}, u32[]{:S(2)}) collective-permute-start(bf16[3,32,512]{2,1,0:T(8,128)(2,1)S(1)} %get-tuple-element.37), channel_id=1, source_target_pairs={{0,4},{4,0},{8,12},{12,8},{1,5},{5,1},{9,13},{13,9},{2,6},{6,2},{1... | collective-permute-start | bytes 294920 | tf_op jit(solution)/shard_map/ppermute | solution.py:84
  5.1 2.6 %collective-permute-start.1 = (bf16[3,32,512]{2,1,0:T(8,128)(2,1)S(1)}, bf16[3,32,512]{2,1,0:T(8,128)(2,1)S(1)}, u32[]{:S(2)}, u32[]{:S(2)}) collective-permute-start(bf16[3,32,512]{2,1,0:T(8,128)(2,1)S(1)} %get-tuple-element.38), channel_id=1, source_target_pairs={{0,8},{4,12},{8,0},{12,4},{1,9},{5,13},{9,1},{13,5},{2,10},{6,14},... | collective-permute-start | bytes 294920 | tf_op jit(solution)/shard_map/ppermute | solution.py:84
  21.7 5.1 %compare_select_fusion.1 = (s32[512,1]{0,1:T(1,128)S(1)}, s32[512,1]{0,1:T(1,128)S(1)}) fusion(s32[]{:T(128)} %bitcast, s32[]{:T(128)} %bitcast.1, s32[]{:T(128)} %bitcast.3, s32[]{:T(128)} %bitcast.2, s32[512,1]{0,1:T(1,128)S(1)} %concatenate.90, s32[]{:T(128)} %bitcast.10, s32[]{:T(128)} %bitcast.9, s32[]{:T(128)} %bitcast.8, s32[]{:T(128)} %bitcast.7), kind=kLoop, calls=%fused_computation.145 | loop fusion | flops 6144 | bytes 6176 | tf_op jit(solution)/shard_map/gather | solution.py:116
  53.2 3.5 %collective-permute-start.11 = (bf16[3,32,512]{2,1,0:T(8,128)(2,1)S(1)}, bf16[3,32,512]{2,1,0:T(8,128)(2,1)S(1)}, u32[]{:S(2)}, u32[]{:S(2)}) collective-permute-start(bf16[3,32,512]{2,1,0:T(8,128)(2,1)S(1)} %get-tuple-element.35), channel_id=1, source_target_pairs={{0,8},{4,12},{8,0},{12,4},{1,9},{5,13},{9,1},{13,5},{2,10},{6,14},... | collective-permute-start | bytes 294920 | tf_op jit(solution)/shard_map/ppermute | solution.py:84
  59.1 3.3 %collective-permute-done.11 = bf16[3,32,512]{2,1,0:T(8,128)(2,1)S(1)} collective-permute-done((bf16[3,32,512]{2,1,0:T(8,128)(2,1)S(1)}, bf16[3,32,512]{2,1,0:T(8,128)(2,1)S(1)}, u32[]{:S(2)}, u32[]{:S(2)}) %collective-permute-start.11) | collective-permute-done | bytes 98336 | tf_op jit(solution)/shard_map/ppermute | solution.py:84
  67.6 4.2 %collective-permute-done.13 = bf16[3,96,512]{2,1,0:T(8,128)(2,1)S(1)} collective-permute-done((bf16[3,96,512]{2,1,0:T(8,128)(2,1)S(1)}, bf16[3,96,512]{2,1,0:T(8,128)(2,1)S(1)}, u32[]{:S(2)}, u32[]{:S(2)}) %collective-permute-start.13) | collective-permute-done | bytes 294944 | tf_op jit(solution)/shard_map/ppermute | solution.py:84
  73.6 2.6 %convolution_convert_fusion.5 = bf16[384,512]{1,0:T(8,128)(2,1)} fusion(bf16[3,512,512]{2,1,0:T(8,128)(2,1)} %constant_dynamic-update-slice_fusion, bf16[3,512,512]{2,1,0:T(8,128)(2,1)} %param.11, s32[512]{0:T(512)S(1)} %add_select_fusion), kind=kOutput, calls=%fused_computation.12 | convolution fusion | flops 403243008 | bytes 1443840 | tf_op jit(solution)/shard_map/dot_general | solution.py:136
  77.6 1.8 convolution_convert_fusion.3
  80.8 1.8 convolution_convert_fusion.2
  84.2 1.8 convolution_convert_fusion.4
  86.0 4.2 %collective-permute-start.15 = (bf16[384,512]{1,0:T(8,128)(2,1)S(1)}, bf16[384,512]{1,0:T(8,128)(2,1)S(1)}, u32[]{:S(2)}, u32[]{:S(2)}) collective-permute-start(bf16[384,512]{1,0:T(8,128)(2,1)S(1)} %convolution_convert_fusion.4), channel_id=1, source_target_pairs={{0,4},{1,5},{2,6},{3,7},{12,8},{13,9},{14,10},{15,11},{16,20},{17,... | collective-permute-start | bytes 1179656 | tf_op jit(solution)/shard_map/ppermute | solution.py:90
  90.2 1.8 convolution_convert_fusion.1
  93.3 1.8 convolution_convert_fusion
  101.1 7.0 %collective-permute-done.32 = bf16[384,512]{1,0:T(8,128)(2,1)S(1)} collective-permute-done((bf16[384,512]{1,0:T(8,128)(2,1)S(1)}, bf16[384,512]{1,0:T(8,128)(2,1)S(1)}, u32[]{:S(2)}, u32[]{:S(2)}) %collective-permute-start.32) | collective-permute-done | bytes 393248 | tf_op jit(solution)/shard_map/ppermute | solution.py:90
  108.9 7.6 %collective-permute-done.35 = bf16[384,512]{1,0:T(8,128)(2,1)S(1)} collective-permute-done((bf16[384,512]{1,0:T(8,128)(2,1)S(1)}, bf16[384,512]{1,0:T(8,128)(2,1)S(1)}, u32[]{:S(2)}, u32[]{:S(2)}) %collective-permute-start.35) | collective-permute-done | bytes 393248 | tf_op jit(solution)/shard_map/ppermute | solution.py:90
  125.2 22.0 %collective-permute-done.7 = bf16[384,512]{1,0:T(8,128)(2,1)S(1)} collective-permute-done((bf16[384,512]{1,0:T(8,128)(2,1)S(1)}, bf16[384,512]{1,0:T(8,128)(2,1)S(1)}, u32[]{:S(2)}, u32[]{:S(2)}) %collective-permute-start.7) | collective-permute-done | bytes 393248 | tf_op jit(solution)/shard_map/ppermute | solution.py:90
  148.6 5.9 %collective-permute-done.22 = bf16[384,512]{1,0:T(8,128)(2,1)S(1)} collective-permute-done((bf16[384,512]{1,0:T(8,128)(2,1)S(1)}, bf16[384,512]{1,0:T(8,128)(2,1)S(1)}, u32[]{:S(2)}, u32[]{:S(2)}) %collective-permute-start.22) | collective-permute-done | bytes 393248 | tf_op jit(solution)/shard_map/ppermute | solution.py:90
  155.9 15.4 %collective-permute-done.17 = bf16[384,512]{1,0:T(8,128)(2,1)S(1)} collective-permute-done((bf16[384,512]{1,0:T(8,128)(2,1)S(1)}, bf16[384,512]{1,0:T(8,128)(2,1)S(1)}, u32[]{:S(2)}, u32[]{:S(2)}) %collective-permute-start.17) | collective-permute-done | bytes 393248 | tf_op jit(solution)/shard_map/ppermute | solution.py:90
  172.9 3.9 %collective-permute-done.34 = bf16[384,512]{1,0:T(8,128)(2,1)S(1)} collective-permute-done((bf16[384,512]{1,0:T(8,128)(2,1)S(1)}, bf16[384,512]{1,0:T(8,128)(2,1)S(1)}, u32[]{:S(2)}, u32[]{:S(2)}) %collective-permute-start.34) | collective-permute-done | bytes 393248 | tf_op jit(solution)/shard_map/ppermute | solution.py:90
  176.9 4.1 %collective-permute-done.37 = bf16[384,512]{1,0:T(8,128)(2,1)S(1)} collective-permute-done((bf16[384,512]{1,0:T(8,128)(2,1)S(1)}, bf16[384,512]{1,0:T(8,128)(2,1)S(1)}, u32[]{:S(2)}, u32[]{:S(2)}) %collective-permute-start.37) | collective-permute-done | bytes 393248 | tf_op jit(solution)/shard_map/ppermute | solution.py:90
  182.5 3.9 %collective-permute-start.28 = (bf16[384,512]{1,0:T(8,128)(2,1)S(1)}, bf16[384,512]{1,0:T(8,128)(2,1)S(1)}, u32[]{:S(2)}, u32[]{:S(2)}) collective-permute-start(bf16[384,512]{1,0:T(8,128)(2,1)S(1)} %add_convert_fusion.4), channel_id=1, source_target_pairs={{0,2},{5,7},{10,8},{15,13},{16,18},{21,23},{26,24},{31,29}} | collective-permute-start | bytes 1179656 | tf_op jit(solution)/shard_map/ppermute | solution.py:90
  189.2 2.5 %collective-permute-done.28 = bf16[384,512]{1,0:T(8,128)(2,1)S(1)} collective-permute-done((bf16[384,512]{1,0:T(8,128)(2,1)S(1)}, bf16[384,512]{1,0:T(8,128)(2,1)S(1)}, u32[]{:S(2)}, u32[]{:S(2)}) %collective-permute-start.28) | collective-permute-done | bytes 393248 | tf_op jit(solution)/shard_map/ppermute | solution.py:90
  195.2 3.6 %collective-permute-done.30 = f32[3,512]{1,0:T(4,128)S(1)} collective-permute-done((f32[3,512]{1,0:T(4,128)S(1)}, f32[3,512]{1,0:T(4,128)S(1)}, u32[]{:S(2)}, u32[]{:S(2)}) %collective-permute-start.30) | collective-permute-done | bytes 6176 | tf_op jit(solution)/shard_map/ppermute | solution.py:84
  200.4 3.1 %collective-permute-done.31 = f32[2,3,512]{2,1,0:T(4,128)S(1)} collective-permute-done((f32[2,3,512]{2,1,0:T(4,128)S(1)}, f32[2,3,512]{2,1,0:T(4,128)S(1)}, u32[]{:S(2)}, u32[]{:S(2)}) %collective-permute-start.31) | collective-permute-done | bytes 12320 | tf_op jit(solution)/shard_map/ppermute | solution.py:84
  (200 shorter events, 74.2 us)
Async XLA Ops:
  2.0 55.4 %collective-permute-start = (bf16[3,32,512]{2,1,0:T(8,128)(2,1)S(1)}, bf16[3,32,512]{2,1,0:T(8,128)(2,1)S(1)}, u32[]{:S(2)}, u32[]{:S(2)}) collective-permute-start(bf16[3,32,512]{2,1,0:T(8,128)(2,1)S(1)} %get-tuple-element.37), channel_id=1, source_target_pairs={{0,4},{4,0},{8,12},{12,8},{1,5},{5,1},{9,13},{13,9},{2,6},{6,2},{1... | collective-permute-start | bytes 294920 | tf_op jit(solution)/shard_map/ppermute | solution.py:84
  5.1 52.3 %collective-permute-start.1 = (bf16[3,32,512]{2,1,0:T(8,128)(2,1)S(1)}, bf16[3,32,512]{2,1,0:T(8,128)(2,1)S(1)}, u32[]{:S(2)}, u32[]{:S(2)}) collective-permute-start(bf16[3,32,512]{2,1,0:T(8,128)(2,1)S(1)} %get-tuple-element.38), channel_id=1, source_target_pairs={{0,8},{4,12},{8,0},{12,4},{1,9},{5,13},{9,1},{13,5},{2,10},{6,14},... | collective-permute-start | bytes 294920 | tf_op jit(solution)/shard_map/ppermute | solution.py:84
  7.7 49.7 %collective-permute-start.2 = (bf16[3,32,512]{2,1,0:T(8,128)(2,1)S(1)}, bf16[3,32,512]{2,1,0:T(8,128)(2,1)S(1)}, u32[]{:S(2)}, u32[]{:S(2)}) collective-permute-start(bf16[3,32,512]{2,1,0:T(8,128)(2,1)S(1)} %get-tuple-element.36), channel_id=1, source_target_pairs={{0,12},{4,8},{8,4},{12,0},{1,13},{5,9},{9,5},{13,1},{2,14},{6,10},... | collective-permute-start | bytes 294920 | tf_op jit(solution)/shard_map/ppermute | solution.py:84
  8.4 40.4 %collective-permute-start.18 = (f32[4,2048]{1,0:T(4,128)S(1)}, f32[4,2048]{1,0:T(4,128)S(1)}, u32[]{:S(2)}, u32[]{:S(2)}) collective-permute-start(f32[4,2048]{1,0:T(4,128)S(1)} %get-tuple-element.56), channel_id=1, source_target_pairs={{0,1},{1,0},{2,3},{3,2},{4,5},{5,4},{6,7},{7,6},{8,9},{9,8},{10,11... | collective-permute-start | bytes 98312 | tf_op jit(solution)/shard_map/ppermute | solution.py:84
  9.8 49.4 %collective-permute-start.10 = (bf16[3,32,512]{2,1,0:T(8,128)(2,1)S(1)}, bf16[3,32,512]{2,1,0:T(8,128)(2,1)S(1)}, u32[]{:S(2)}, u32[]{:S(2)}) collective-permute-start(bf16[3,32,512]{2,1,0:T(8,128)(2,1)S(1)} %get-tuple-element.34), channel_id=1, source_target_pairs={{0,4},{4,0},{8,12},{12,8},{1,5},{5,1},{9,13},{13,9},{2,6},{6,2},{1... | collective-permute-start | bytes 294920 | tf_op jit(solution)/shard_map/ppermute | solution.py:84
  71.8 11.5 %collective-permute-start.14 = (bf16[3,192,512]{2,1,0:T(8,128)(2,1)S(1)}, bf16[3,192,512]{2,1,0:T(8,128)(2,1)S(1)}, u32[]{:S(2)}, u32[]{:S(2)}) collective-permute-start(bf16[3,192,512]{2,1,0:T(8,128)(2,1)S(1)} %pad_maximum_fusion.2), channel_id=1, source_target_pairs={{0,1},{1,0},{2,3},{3,2},{4,5},{5,4},{6,7},{7,6},{8,9},{9,8},{10,11... | collective-permute-start | bytes 1769480 | tf_op jit(solution)/shard_map/ppermute | solution.py:84
  76.1 19.0 %collective-permute-start.5 = (bf16[384,512]{1,0:T(8,128)(2,1)}, bf16[384,512]{1,0:T(8,128)(2,1)}, u32[]{:S(2)}, u32[]{:S(2)}) collective-permute-start(bf16[384,512]{1,0:T(8,128)(2,1)} %convolution_convert_fusion.5), channel_id=1, source_target_pairs={{1,5},{2,6},{3,7},{12,8},{13,9},{14,10},{17,21},{18,22},{19,23},{2... | collective-permute-start | bytes 1179656 | tf_op jit(solution)/shard_map/ppermute | solution.py:90
  79.4 18.3 %collective-permute-start.20 = (bf16[384,512]{1,0:T(8,128)(2,1)S(1)}, bf16[384,512]{1,0:T(8,128)(2,1)}, u32[]{:S(2)}, u32[]{:S(2)}) collective-permute-start(bf16[384,512]{1,0:T(8,128)(2,1)S(1)} %convolution_convert_fusion.3), channel_id=1, source_target_pairs={{1,5},{2,6},{3,7},{12,8},{13,9},{14,10},{17,21},{18,22},{19,23},{2... | collective-permute-start | bytes 1179656 | tf_op jit(solution)/shard_map/ppermute | solution.py:90
  82.6 16.9 %collective-permute-start.25 = (bf16[384,512]{1,0:T(8,128)(2,1)S(1)}, bf16[384,512]{1,0:T(8,128)(2,1)S(1)}, u32[]{:S(2)}, u32[]{:S(2)}) collective-permute-start(bf16[384,512]{1,0:T(8,128)(2,1)S(1)} %convolution_convert_fusion.2), channel_id=1, source_target_pairs={{1,5},{2,6},{3,7},{12,8},{13,9},{14,10},{17,21},{18,22},{19,23},{2... | collective-permute-start | bytes 1179656 | tf_op jit(solution)/shard_map/ppermute | solution.py:90
  86.0 14.3 %collective-permute-start.15 = (bf16[384,512]{1,0:T(8,128)(2,1)S(1)}, bf16[384,512]{1,0:T(8,128)(2,1)S(1)}, u32[]{:S(2)}, u32[]{:S(2)}) collective-permute-start(bf16[384,512]{1,0:T(8,128)(2,1)S(1)} %convolution_convert_fusion.4), channel_id=1, source_target_pairs={{0,4},{1,5},{2,6},{3,7},{12,8},{13,9},{14,10},{15,11},{16,20},{17,... | collective-permute-start | bytes 1179656 | tf_op jit(solution)/shard_map/ppermute | solution.py:90
  92.0 16.1 %collective-permute-start.32 = (bf16[384,512]{1,0:T(8,128)(2,1)S(1)}, bf16[384,512]{1,0:T(8,128)(2,1)S(1)}, u32[]{:S(2)}, u32[]{:S(2)}) collective-permute-start(bf16[384,512]{1,0:T(8,128)(2,1)S(1)} %convolution_convert_fusion.1), channel_id=1, source_target_pairs={{0,4},{1,5},{2,6},{3,7},{12,8},{13,9},{14,10},{15,11},{16,20},{17,... | collective-permute-start | bytes 1179656 | tf_op jit(solution)/shard_map/ppermute | solution.py:90
  95.1 21.4 %collective-permute-start.35 = (bf16[384,512]{1,0:T(8,128)(2,1)S(1)}, bf16[384,512]{1,0:T(8,128)(2,1)S(1)}, u32[]{:S(2)}, u32[]{:S(2)}) collective-permute-start(bf16[384,512]{1,0:T(8,128)(2,1)S(1)} %convolution_convert_fusion), channel_id=1, source_target_pairs={{0,4},{1,5},{2,6},{3,7},{12,8},{13,9},{14,10},{15,11},{16,20},{17,... | collective-permute-start | bytes 1179656 | tf_op jit(solution)/shard_map/ppermute | solution.py:90
  97.7 19.7 %collective-permute-start.6 = (bf16[384,512]{1,0:T(8,128)(2,1)S(1)}, bf16[384,512]{1,0:T(8,128)(2,1)S(1)}, u32[]{:S(2)}, u32[]{:S(2)}) collective-permute-start(bf16[384,512]{1,0:T(8,128)(2,1)S(1)} %add_convert_fusion.14), channel_id=1, source_target_pairs={{6,10},{7,11},{8,4},{9,5},{22,26},{23,27},{24,20},{25,21}} | collective-permute-start | bytes 1179656 | tf_op jit(solution)/shard_map/ppermute | solution.py:90
  99.5 18.7 %collective-permute-start.21 = (bf16[384,512]{1,0:T(8,128)(2,1)S(1)}, bf16[384,512]{1,0:T(8,128)(2,1)S(1)}, u32[]{:S(2)}, u32[]{:S(2)}) collective-permute-start(bf16[384,512]{1,0:T(8,128)(2,1)S(1)} %add_convert_fusion.9), channel_id=1, source_target_pairs={{6,10},{7,11},{8,4},{9,5},{22,26},{23,27},{24,20},{25,21}} | collective-permute-start | bytes 1179656 | tf_op jit(solution)/shard_map/ppermute | solution.py:90
  100.3 19.3 %collective-permute-start.26 = (bf16[384,512]{1,0:T(8,128)(2,1)S(1)}, bf16[384,512]{1,0:T(8,128)(2,1)S(1)}, u32[]{:S(2)}, u32[]{:S(2)}) collective-permute-start(bf16[384,512]{1,0:T(8,128)(2,1)S(1)} %add_convert_fusion.6), channel_id=1, source_target_pairs={{6,10},{7,11},{8,4},{9,5},{22,26},{23,27},{24,20},{25,21}} | collective-permute-start | bytes 1179656 | tf_op jit(solution)/shard_map/ppermute | solution.py:90
  108.1 12.9 %collective-permute-start.16 = (bf16[384,512]{1,0:T(8,128)(2,1)S(1)}, bf16[384,512]{1,0:T(8,128)(2,1)S(1)}, u32[]{:S(2)}, u32[]{:S(2)}) collective-permute-start(bf16[384,512]{1,0:T(8,128)(2,1)S(1)} %add_convert_fusion.11), channel_id=1, source_target_pairs={{4,8},{5,9},{6,10},{7,11},{8,4},{9,5},{10,6},{11,7},{20,24},{21,25... | collective-permute-start | bytes 1179656 | tf_op jit(solution)/shard_map/ppermute | solution.py:90
  118.2 29.1 %collective-permute-start.7 = (bf16[384,512]{1,0:T(8,128)(2,1)S(1)}, bf16[384,512]{1,0:T(8,128)(2,1)S(1)}, u32[]{:S(2)}, u32[]{:S(2)}) collective-permute-start(bf16[384,512]{1,0:T(8,128)(2,1)S(1)} %add_convert_fusion.13), channel_id=1, source_target_pairs={{4,0},{11,15},{20,16},{27,31}} | collective-permute-start | bytes 1179656 | tf_op jit(solution)/shard_map/ppermute | solution.py:90
  119.6 35.0 %collective-permute-start.22 = (bf16[384,512]{1,0:T(8,128)(2,1)S(1)}, bf16[384,512]{1,0:T(8,128)(2,1)S(1)}, u32[]{:S(2)}, u32[]{:S(2)}) collective-permute-start(bf16[384,512]{1,0:T(8,128)(2,1)S(1)} %add_convert_fusion.8), channel_id=1, source_target_pairs={{4,0},{11,15},{20,16},{27,31}} | collective-permute-start | bytes 1179656 | tf_op jit(solution)/shard_map/ppermute | solution.py:90
  121.0 61.4 %collective-permute-start.27 = (bf16[384,512]{1,0:T(8,128)(2,1)S(1)}, bf16[384,512]{1,0:T(8,128)(2,1)S(1)}, u32[]{:S(2)}, u32[]{:S(2)}) collective-permute-start(bf16[384,512]{1,0:T(8,128)(2,1)S(1)} %add_convert_fusion.5), channel_id=1, source_target_pairs={{4,0},{11,15},{20,16},{27,31}} | collective-permute-start | bytes 1179656 | tf_op jit(solution)/shard_map/ppermute | solution.py:90
  122.4 49.0 %collective-permute-start.17 = (bf16[384,512]{1,0:T(8,128)(2,1)S(1)}, bf16[384,512]{1,0:T(8,128)(2,1)S(1)}, u32[]{:S(2)}, u32[]{:S(2)}) collective-permute-start(bf16[384,512]{1,0:T(8,128)(2,1)S(1)} %add_convert_fusion.10), channel_id=1, source_target_pairs={{4,0},{5,1},{6,2},{7,3},{8,12},{9,13},{10,14},{11,15},{20,16},{21,... | collective-permute-start | bytes 1179656 | tf_op jit(solution)/shard_map/ppermute | solution.py:90
  123.8 52.9 %collective-permute-start.34 = (bf16[384,512]{1,0:T(8,128)(2,1)S(1)}, bf16[384,512]{1,0:T(8,128)(2,1)S(1)}, u32[]{:S(2)}, u32[]{:S(2)}) collective-permute-start(bf16[384,512]{1,0:T(8,128)(2,1)S(1)} %add_convert_fusion.2), channel_id=1, source_target_pairs={{4,0},{5,1},{6,2},{7,3},{8,12},{9,13},{10,14},{11,15},{20,16},{21,... | collective-permute-start | bytes 1179656 | tf_op jit(solution)/shard_map/ppermute | solution.py:90
  147.2 33.7 %collective-permute-start.37 = (bf16[384,512]{1,0:T(8,128)(2,1)S(1)}, bf16[384,512]{1,0:T(8,128)(2,1)S(1)}, u32[]{:S(2)}, u32[]{:S(2)}) collective-permute-start(bf16[384,512]{1,0:T(8,128)(2,1)S(1)} %add_convert_fusion), channel_id=1, source_target_pairs={{4,0},{5,1},{6,2},{7,3},{8,12},{9,13},{10,14},{11,15},{20,16},{21,... | collective-permute-start | bytes 1179656 | tf_op jit(solution)/shard_map/ppermute | solution.py:90
  154.5 31.9 %collective-permute-start.8 = (bf16[384,512]{1,0:T(8,128)(2,1)S(1)}, bf16[384,512]{1,0:T(8,128)(2,1)S(1)}, u32[]{:S(2)}, u32[]{:S(2)}) collective-permute-start(bf16[384,512]{1,0:T(8,128)(2,1)S(1)} %add_convert_fusion.12), channel_id=1, source_target_pairs={{0,2},{5,7},{10,8},{15,13},{16,18},{21,23},{26,24},{31,29}} | collective-permute-start | bytes 1179656 | tf_op jit(solution)/shard_map/ppermute | solution.py:90
  171.4 16.5 %collective-permute-start.23 = (bf16[384,512]{1,0:T(8,128)(2,1)S(1)}, bf16[384,512]{1,0:T(8,128)(2,1)S(1)}, u32[]{:S(2)}, u32[]{:S(2)}) collective-permute-start(bf16[384,512]{1,0:T(8,128)(2,1)S(1)} %add_convert_fusion.7), channel_id=1, source_target_pairs={{0,2},{5,7},{10,8},{15,13},{16,18},{21,23},{26,24},{31,29}} | collective-permute-start | bytes 1179656 | tf_op jit(solution)/shard_map/ppermute | solution.py:90
  (37 other events, 147.6 us)

commit v2 on v1

v2 whole, which is shorter than its diff:
```python
import jax
import jax.numpy as jnp
from jax import lax
from jax.experimental import pallas as pl
from jax.experimental.pallas import tpu as pltpu
from jax.sharding import PartitionSpec as P

decay_rate = 0.25
damping_rate = 0.1


def spread(array, axis, root):
    mine = lax.axis_index(axis) == root
    return lax.psum(jnp.where(mine, array, jnp.zeros_like(array)), axis)


def gather_plan(activations, out_grads, basis_act, basis_grad, owner_of, counts, state_act, state_grad):
    layers = activations.shape[0]
    tok_rows = activations.shape[1]
    tile_rows = basis_act.shape[1]
    tile_cols = basis_act.shape[2]
    slot_count = state_act.shape[0]
    dp_index = lax.axis_index("dp")
    own_index = lax.axis_index("owner")
    valid_rows = (jnp.arange(tok_rows) < counts[dp_index]).astype(jnp.float32)[:, None]
    valid_total = jnp.sum(counts).astype(jnp.float32)
    square_acts = []
    square_grads = []
    gram_tiles = []
    for layer_index in range(layers):
        panel_act = jnp.dot(
            activations[layer_index],
            lax.all_gather(basis_act[layer_index], "dp", axis=0, tiled=True),
            preferred_element_type=jnp.float32,
        )
        panel_grad = jnp.dot(
            out_grads[layer_index],
            lax.all_gather(basis_grad[layer_index], "dp", axis=0, tiled=True),
            preferred_element_type=jnp.float32,
        )
        panel_act = (panel_act * valid_rows).astype(jnp.bfloat16)
        panel_grad = (panel_grad * valid_rows).astype(jnp.bfloat16)
        full_act = lax.all_gather(panel_act, "owner", axis=1, tiled=True)
        full_grad = lax.all_gather(panel_grad, "owner", axis=1, tiled=True)
        square_act = jnp.sum(jnp.square(full_act.astype(jnp.float32)), axis=0)
        square_grad = jnp.sum(jnp.square(full_grad.astype(jnp.float32)), axis=0)
        gram_term = lax.dot_general(
            full_grad, panel_act, (((0,), (0,)), ((), ())), preferred_element_type=jnp.float32
        )
        gram_tiles.append(
            lax.psum_scatter(
                gram_term.astype(jnp.bfloat16), "dp", scatter_dimension=0, tiled=True
            ).astype(jnp.float32)
            / valid_total
        )
        square_act, square_grad = lax.psum((square_act, square_grad), "dp")
        square_acts.append(square_act)
        square_grads.append(square_grad)
    new_act = state_act
    new_grad = state_grad
    results = []
    for layer_index in range(layers):
        owner_now = owner_of[layer_index]
        slot_rank = jnp.sum((owner_of[:layer_index] == owner_now).astype(jnp.int32))
        selector = (jnp.arange(slot_count) == slot_rank).astype(jnp.float32)[:, None]
        local_act = decay_rate * jnp.sum(state_act * selector, axis=0) + (
            1.0 - decay_rate
        ) * (square_acts[layer_index] / valid_total)
        local_grad = decay_rate * jnp.sum(state_grad * selector, axis=0) + (
            1.0 - decay_rate
        ) * (square_grads[layer_index] / valid_total)
        eigen_act = spread(local_act, "owner", owner_now)
        eigen_grad = spread(local_grad, "owner", owner_now)
        replace_rows = ((jnp.arange(slot_count) == slot_rank) & (own_index == owner_now))[:, None]
        new_act = jnp.where(replace_rows, eigen_act[None, :], new_act)
        new_grad = jnp.where(replace_rows, eigen_grad[None, :], new_grad)
        damping = damping_rate * jnp.mean(eigen_grad) * jnp.mean(eigen_act)
        grad_eigen = lax.dynamic_slice_in_dim(eigen_grad, dp_index * tile_rows, tile_rows)
        act_eigen = lax.dynamic_slice_in_dim(eigen_act, own_index * tile_cols, tile_cols)
        scaled = gram_tiles[layer_index] / (grad_eigen[:, None] * act_eigen[None, :] + damping)
        results.append(scaled.astype(jnp.bfloat16))
    return (jnp.stack(results), new_act, new_grad)


def flip(array, axis, mask):
    return lax.ppermute(array, axis, [(i, i ^ mask) for i in range(lax.axis_size(axis))])


def hop(array, pairs):
    owners = lax.axis_size("owner")
    flat = [(a * owners + b, c * owners + e) for (a, b), (c, e) in pairs]
    return lax.ppermute(array, ("dp", "owner"), flat)


def whole(*arrays):
    return [pl.BlockSpec(a.shape, lambda i, *s, n=a.ndim: (0,) * n) for a in arrays]


def project_rows(place, counts, tokens, pieces, basis):
    layers, tok_rows, _ = tokens.shape
    tile, cols = basis.shape[1:]
    n_dp = len(pieces) + 1
    n_own = len(pieces[0])
    part_rows = tok_rows // n_own
    packed = 3 * n_dp * tok_rows // 4
    flat = [p for group in pieces for p in group]

    def kernel(place_ref, counts_ref, tokens_ref, basis_ref, *refs):
        piece_refs, out_refs = refs[: len(flat)], refs[len(flat) :]
        dp, own = place_ref[0], place_ref[1]
        row = lax.broadcasted_iota(jnp.int32, (packed, tok_rows), 0)
        col = lax.broadcasted_iota(jnp.int32, (packed, tok_rows), 1)
        turn = (col // part_rows) % n_own
        shared = (own ^ (((turn & 1) << 1) | (turn >> 1))) * part_rows + col % part_rows
        picks = []
        for mask in range(n_dp):
            shard = dp ^ mask
            start = jnp.int32(0)
            for other in range(n_dp):
                start += jnp.where(other < shard, counts_ref[other], 0)
            index = col if mask == 0 else shared
            picks.append(((row == start + index) & (index < counts_ref[shard])).astype(jnp.bfloat16))
        select = jnp.concatenate(picks, axis=1)
        for layer in range(layers):
            rows = jnp.concatenate([tokens_ref[layer]] + [p[layer] for p in piece_refs], axis=0)
            chosen = jnp.dot(select, rows, preferred_element_type=jnp.float32).astype(jnp.bfloat16)
            out_refs[layer][...] = jnp.dot(
                chosen, basis_ref[layer], preferred_element_type=jnp.float32
            ).astype(jnp.bfloat16)

    return pl.pallas_call(
        kernel,
        out_shape=[jax.ShapeDtypeStruct((packed, cols), jnp.bfloat16)] * layers,
        grid_spec=pltpu.PrefetchScalarGridSpec(
            num_scalar_prefetch=2,
            grid=(1,),
            in_specs=[pl.BlockSpec((layers, tok_rows, tile), lambda i, place, n: (0, 0, place[0]))]
            + whole(basis, *flat),
            out_specs=[pl.BlockSpec((packed, cols), lambda i, *s: (0, 0))] * layers,
        ),
        compiler_params=pltpu.CompilerParams(vmem_limit_bytes=32 * 1024 * 1024),
        cost_estimate=pl.CostEstimate(
            flops=layers * 2 * packed * tile * (n_dp * tok_rows + cols),
            bytes_accessed=2 * layers * tile * (n_dp * tok_rows + 2 * cols),
            transcendentals=0,
        ),
    )(place, counts, tokens, basis, *flat)


def settle(flags, near, far):
    def kernel(flags_ref, near_ref, *refs):
        far_refs, panel_ref, square_ref = refs[:-2], refs[-2], refs[-1]
        value = near_ref[...]
        for index, far_ref in enumerate(far_refs):
            value = jnp.where(flags_ref[0] == index + 1, far_ref[...], value)
        panel_ref[...] = value
        wide = value.astype(jnp.float32)
        square_ref[...] = jnp.sum(wide * wide, axis=0, keepdims=True)

    return pl.pallas_call(
        kernel,
        out_shape=[
            jax.ShapeDtypeStruct(near.shape, near.dtype),
            jax.ShapeDtypeStruct((1, near.shape[1]), jnp.float32),
        ],
        grid_spec=pltpu.PrefetchScalarGridSpec(
            num_scalar_prefetch=1,
            grid=(1,),
            in_specs=whole(near, *far),
            out_specs=[
                pl.BlockSpec(near.shape, lambda i, *s: (0, 0)),
                pl.BlockSpec((1, near.shape[1]), lambda i, *s: (0, 0)),
            ],
        ),
        compiler_params=pltpu.CompilerParams(vmem_limit_bytes=16 * 1024 * 1024),
        cost_estimate=pl.CostEstimate(
            flops=3 * near.size, bytes_accessed=4 * near.size, transcendentals=0
        ),
    )(flags, near, *far)


def finish(place, counts, owner_of, states, acts, grads, square_acts, square_grads):
    layers = len(acts)
    n_own, n_dp = len(square_acts), len(square_grads)
    tile = acts[0].shape[1]
    slot_count = states[0].shape[0] // 2
    width = states[0].shape[1]
    operands = [*states, *acts, *grads, *square_acts, *square_grads]

    def kernel(place_ref, counts_ref, owner_ref, *refs):
        refs = list(refs)
        take = lambda n: [refs.pop(0) for _ in range(n)]
        state_refs, act_refs, grad_refs = take(n_own), take(layers), take(layers)
        square_act_refs, square_grad_refs = take(n_own), take(n_dp)
        out_ref, new_act_ref, new_grad_ref, act_full, grad_full = refs
        dp, own = place_ref[0], place_ref[1]
        total = counts_ref[0]
        for index in range(1, counts_ref.shape[0]):
            total += counts_ref[index]
        total = total.astype(jnp.float32)
        for mask in range(n_own):
            at = pl.ds(pl.multiple_of((own ^ mask) * tile, tile), tile)
            act_full[:, at] = square_act_refs[mask][...] / total
        for mask in range(n_dp):
            at = pl.ds(pl.multiple_of((dp ^ mask) * tile, tile), tile)
            grad_full[:, at] = square_grad_refs[mask][...] / total
        new_act_ref[...] = state_refs[0][:slot_count]
        new_grad_ref[...] = state_refs[0][slot_count:]
        for layer in range(layers):
            owner_now = owner_ref[layer]
            rank = jnp.int32(0)
            for earlier in range(layer):
                rank += jnp.where(owner_ref[earlier] == owner_now, 1, 0)
            old_act = jnp.zeros((1, width), jnp.float32)
            old_grad = jnp.zeros((1, width), jnp.float32)
            for mask in range(n_own):
                for slot in range(slot_count):
                    here = (owner_now == own ^ mask) & (rank == slot)
                    old_act = jnp.where(here, state_refs[mask][slot : slot + 1], old_act)
                    old_grad = jnp.where(
                        here, state_refs[mask][slot_count + slot : slot_count + slot + 1], old_grad
                    )
            act_full[layer : layer + 1] = eigen_act = (
                decay_rate * old_act + (1.0 - decay_rate) * act_full[layer : layer + 1]
            )
            grad_full[layer : layer + 1] = eigen_grad = (
                decay_rate * old_grad + (1.0 - decay_rate) * grad_full[layer : layer + 1]
            )
            for slot in range(slot_count):

                @pl.when((owner_now == own) & (rank == slot))
                def _(slot=slot, eigen_act=eigen_act, eigen_grad=eigen_grad):
                    new_act_ref[slot : slot + 1] = eigen_act
                    new_grad_ref[slot : slot + 1] = eigen_grad

            damping = damping_rate * (jnp.sum(eigen_grad) / width) * (jnp.sum(eigen_act) / width)
            rows = grad_full[layer : layer + 1, pl.ds(pl.multiple_of(dp * tile, tile), tile)]
            cols = act_full[layer : layer + 1, pl.ds(pl.multiple_of(own * tile, tile), tile)]
            rows = jnp.transpose(jnp.broadcast_to(rows, (128, tile)))
            rows = jnp.concatenate([rows] * (tile // 128), axis=1)
            gram = lax.dot_general(
                grad_refs[layer][...],
                act_refs[layer][...],
                (((0,), (0,)), ((), ())),
                preferred_element_type=jnp.float32,
            )
            out_ref[layer] = (gram / total / (rows * cols + damping)).astype(jnp.bfloat16)

    out_shape = [
        jax.ShapeDtypeStruct((layers, tile, tile), jnp.bfloat16),
        jax.ShapeDtypeStruct((slot_count, width), jnp.float32),
        jax.ShapeDtypeStruct((slot_count, width), jnp.float32),
    ]
    return pl.pallas_call(
        kernel,
        out_shape=out_shape,
        grid_spec=pltpu.PrefetchScalarGridSpec(
            num_scalar_prefetch=3,
            grid=(1,),
            in_specs=whole(*operands),
            out_specs=whole(*out_shape),
            scratch_shapes=[pltpu.VMEM((layers, width), jnp.float32)] * 2,
        ),
        compiler_params=pltpu.CompilerParams(vmem_limit_bytes=32 * 1024 * 1024),
    )(place, counts, owner_of, *operands)


def line_plan(activations, out_grads, basis_act, basis_grad, owner_of, counts, state_act, state_grad):
    layers, tok_rows, width = activations.shape
    tile = basis_act.shape[1]
    n_dp = lax.axis_size("dp")
    n_own = lax.axis_size("owner")
    part_rows = tok_rows // n_own
    dp = lax.axis_index("dp")
    own = lax.axis_index("owner")
    place = jnp.stack([dp, own]).astype(jnp.int32)
    f32 = jnp.float32

    def pieces_of(tokens):
        part = lax.dynamic_slice_in_dim(tokens, own * part_rows, part_rows, 1)
        groups = []
        for mask in range(1, n_dp):
            got = flip(lax.dynamic_slice_in_dim(part, (dp ^ mask) * tile, tile, 2), "dp", mask)
            chip = flip(got, "owner", 2)
            groups.append([got, chip, flip(got, "owner", 1), flip(chip, "owner", 1)])
        return groups

    def add(*terms):
        return sum(term.astype(f32) for term in terms).astype(jnp.bfloat16)

    pieces_act = pieces_of(activations)
    pieces_grad = pieces_of(out_grads)

    states = [jnp.concatenate([state_act, state_grad], axis=0)]
    states += [flip(states[0], "owner", mask) for mask in range(1, n_own)]

    parts_act = project_rows(place, counts, activations, pieces_act, basis_act)
    parts_grad = project_rows(place, counts, out_grads, pieces_grad, basis_grad)
    outer = (dp == 0) | (dp == n_dp - 1)
    take_outer = jnp.where(outer, 1, 0).astype(jnp.int32)[None]
    home = jnp.where(own == dp, 0, jnp.where(own == dp ^ 2, 1, 2)).astype(jnp.int32)[None]
    every = range(n_own)
    acts, grads, square_acts, square_grads = [], [], [], []
    for layer in range(layers):
        part = parts_act[layer]
        part = add(part, hop(part, [((a, b), (c, b)) for a, c in ((0, 1), (3, 2)) for b in every]))
        part = add(part, hop(part, [((a, b), (c, b)) for a, c in ((1, 2), (2, 1)) for b in every]))
        back = hop(part, [((a, b), (c, b)) for a, c in ((1, 0), (2, 3)) for b in every])
        panel, square = settle(take_outer, part, [back])
        acts.append(panel)
        square_acts.append(square)
        part = parts_grad[layer]
        part = add(part, hop(part, [((0, b), (1, b)) for b in (1, 2, 3)] + [((3, b), (2, b)) for b in (0, 1, 2)]))
        part = add(part, hop(part, [((1, b), (2, b)) for b in (2, 3)] + [((2, b), (1, b)) for b in (0, 1)]))
        part = add(part, hop(part, [((1, 0), (0, 0)), ((2, 3), (3, 3))]))
        chip = hop(part, [((a, a), (a, a ^ 2)) for a in range(n_dp)])
        half = jnp.where(own == dp, part, chip)
        core = hop(half, [((a, a ^ b), (a, a ^ b ^ 1)) for a in range(n_dp) for b in (0, 2)])
        panel, square = settle(home, part, [chip, core])
        grads.append(panel)
        square_grads.append(square)
    square_act = jnp.concatenate(square_acts, axis=0)
    square_grad = jnp.concatenate(square_grads, axis=0)
    square_acts = [square_act] + [flip(square_act, "owner", mask) for mask in range(1, n_own)]
    square_grads = [square_grad] + [flip(square_grad, "dp", mask) for mask in range(1, n_dp)]
    return tuple(finish(place, counts, owner_of, states, acts, grads, square_acts, square_grads))


def solution(mesh):
    placed = (
        P("groups", "dp", None),
        P("groups", "dp", None),
        P("groups", "dp", "owner"),
        P("groups", "dp", "owner"),
        P(),
        P("groups"),
        P("owner", "groups"),
        P("owner", "groups"),
    )
    square = mesh.shape["dp"] == 4 and mesh.shape["owner"] == 4
    return jax.shard_map(
        line_plan if square else gather_plan,
        mesh=mesh,
        in_specs=placed,
        out_specs=(P("groups", "dp", "owner"), P("owner", "groups"), P("owner", "groups")),
        check_vma=False,
    )
```

time: 222 us -> 168 us (0.76)
  between operations: 29.1 us -> 1.25 us
  waiting for transfers between devices: 87.6 us -> 69.5 us
  starting transfers between devices: 48.2 us -> 64.8 us
  other arithmetic: 23 us -> 6.78 us
  Pallas kernels: 0 us -> 13.9 us
  matrix products: 13.8 us -> 0 us
  local copies, waits for them, and re-layouts: 18.3 us -> 10.7 us
    ppermute x16 -> x33, starting transfers between devices: 15.4 us -> 35.6 us  [flip(): lax.ppermute(array, axis, [(i, i ^ mask) for i in range(lax.axis_size(axi...]
    ppermute x24, waiting for transfers between devices: 69.2 us -> 50.6 us  [hop(): return lax.ppermute(array, ('dp', 'owner'), flat)]
    pallas_call x0 -> x9, Pallas kernels: none -> 13.9 us  [the longest x6 5.58 us: settle(): pl.pallas_call(kernel, out_shape=[jax.ShapeDtypeStruct(near.shape, near.d...]
    dot_general x9 -> x0, matrix products: 13.8 us -> none  [the longest x6 11.6 us: project(): return jnp.dot(chosen, basis, preferred_element_type=f32).astype(bf16)]
    reduce_sum x11 -> x0, other arithmetic: 5.53 us -> none  [the longest x3 2.63 us: line_plan(): damping = damping_rate * jnp.mean(eigen_grad) * jnp.mean(eigen_act)]
    gather x1 -> x0, other arithmetic: 5.05 us -> none  [line_plan(): counts[shard_ids]]
    dynamic_slice x8 -> x2, local copies, waits for them, and re-layouts: 6.41 us -> 2.5 us  [pieces_of(): lax.dynamic_slice_in_dim(part, (dp ^ mask) * tile, tile, 2)]
    ppermute x24, starting transfers between devices: 32.8 us -> 29.3 us  [hop(): return lax.ppermute(array, ('dp', 'owner'), flat)]
  transfers between devices with their start and end apart: 40 -> 57, of which waited for: 16 -> 17; matrix products, arithmetic and copies ran while one was open for 18% -> 5% of each run, Pallas kernels for 0% -> 6%
where the time goes in v2:
time: 168 us; the launch traced here: 167 us
  waiting for transfers between devices  69.5 us (41%)
  starting transfers between devices  64.8 us (39%)
  Pallas kernels  13.9 us (8%)
  local copies, waits for them, and re-layouts  10.7 us (6%)
  other arithmetic  6.78 us (4%)
    ppermute x24, waiting for transfers between devices, hop(): return lax.ppermute(array, ('dp', 'owner'), flat)  50.6 us
    ppermute x33, starting transfers between devices, flip(): lax.ppermute(array, axis, [(i, i ^ mask) for i in range(lax.axis_size(axi...  35.6 us
    ppermute x24, starting transfers between devices, hop(): return lax.ppermute(array, ('dp', 'owner'), flat)  29.3 us
    ppermute x33, waiting for transfers between devices, flip(): lax.ppermute(array, axis, [(i, i ^ mask) for i in range(lax.axis_size(axi...  18.9 us
    unnamed x22, local copies, waits for them, and re-layouts  8.15 us
    pallas_call x6, Pallas kernels, settle(): pl.pallas_call(kernel, out_shape=[jax.ShapeDtypeStruct(near.shape, near.d...  5.58 us
    pallas_call x2, Pallas kernels, project_rows(): pl.pallas_call(kernel, out_shape=[jax.ShapeDtypeStruct((packed, cols), jn...  5.12 us
    convert_element_type x15, other arithmetic, add(): return sum((term.astype(f32) for term in terms)).astype(jnp.bfloat16)  3.53 us
  transfers between devices with their start and end apart: 57, of which 17 were waited for; matrix products, arithmetic and copies ran while one was open for 5% of the time, Pallas kernels for 6%

profile of v2, /device:TPU:0, one launch (start us, length us, event | category | flops | bytes accessed | tf_op | source)
XLA Modules:
  0.0 166.9 jit_solution(15730441969218732643)
XLA Ops:
  1.9 7.1 %collective-permute-start.32 = (bf16[3,32,512]{2,1,0:T(8,128)(2,1)S(1)}, bf16[3,32,512]{2,1,0:T(8,128)(2,1)S(1)}, u32[]{:S(2)}, u32[]{:S(2)}) collective-permute-start(bf16[3,32,512]{2,1,0:T(8,128)(2,1)S(1)} %get-tuple-element.39), channel_id=1, source_target_pairs={{0,12},{4,8},{8,4},{12,0},{1,13},{5,9},{9,5},{13,1},{2,14},{6,10},... | collective-permute-start | bytes 294920 | tf_op jit(solution)/shard_map/ppermute | solution.py:86
  9.1 2.8 %collective-permute-start.28 = (bf16[3,32,512]{2,1,0:T(8,128)(2,1)S(1)}, bf16[3,32,512]{2,1,0:T(8,128)(2,1)S(1)}, u32[]{:S(2)}, u32[]{:S(2)}) collective-permute-start(bf16[3,32,512]{2,1,0:T(8,128)(2,1)S(1)} %get-tuple-element.40), channel_id=1, source_target_pairs={{0,8},{4,12},{8,0},{12,4},{1,9},{5,13},{9,1},{13,5},{2,10},{6,14},... | collective-permute-start | bytes 294920 | tf_op jit(solution)/shard_map/ppermute | solution.py:86
  18.0 5.9 %collective-permute-done.28.refs_4_ = bf16[3,32,512]{2,1,0:T(8,128)(2,1)S(1)} collective-permute-done((bf16[3,32,512]{2,1,0:T(8,128)(2,1)S(1)}, bf16[3,32,512]{2,1,0:T(8,128)(2,1)S(1)}, u32[]{:S(2)}, u32[]{:S(2)}) %collective-permute-start.28) | collective-permute-done | bytes 98336 | tf_op jit(solution)/shard_map/ppermute | solution.py:86
  26.5 2.4 %collective-permute-done.29.refs_5_ = bf16[3,32,512]{2,1,0:T(8,128)(2,1)S(1)} collective-permute-done((bf16[3,32,512]{2,1,0:T(8,128)(2,1)S(1)}, bf16[3,32,512]{2,1,0:T(8,128)(2,1)S(1)}, u32[]{:S(2)}, u32[]{:S(2)}) %collective-permute-start.29) | collective-permute-done | bytes 98336 | tf_op jit(solution)/shard_map/ppermute | solution.py:86
  30.1 2.1 %collective-permute-start.3 = (bf16[3,32,512]{2,1,0:T(8,128)(2,1)S(1)}, bf16[3,32,512]{2,1,0:T(8,128)(2,1)S(1)}, u32[]{:S(2)}, u32[]{:S(2)}) collective-permute-start(bf16[3,32,512]{2,1,0:T(8,128)(2,1)S(1)} %get-tuple-element.44), channel_id=1, source_target_pairs={{0,4},{4,0},{8,12},{12,8},{1,5},{5,1},{9,13},{13,9},{2,6},{6,2},{1... | collective-permute-start | bytes 294920 | tf_op jit(solution)/shard_map/ppermute | solution.py:86
  35.7 2.1 %shard_map.107 = (bf16[384,512]{1,0:T(8,128)(2,1)S(1)}, bf16[384,512]{1,0:T(8,128)(2,1)S(1)}, bf16[384,512]{1,0:T(8,128)(2,1)S(1)}) custom-call(s32[2]{0:T(128)S(1)} %pad_add_fusion.place_ref, s32[4]{0:T(128)S(1)} %copy-done.4, bf16[3,128,2048]{2,1,0:T(8,128)(2,1)S(1)} %copy-done.2, bf16[3,512,512]{2,1,0:T(8,128)(2,1)S(1)} %copy-done.7, ...), custom_call_target="tpu_custom_call" | custom-call | flops 1207959552 | bytes 4718592 | tf_op jit(solution)/shard_map/pallas_call | solution.py:131
  39.2 3.2 %collective-permute-start.12 = (bf16[3,32,512]{2,1,0:T(8,128)(2,1)S(1)}, bf16[3,32,512]{2,1,0:T(8,128)(2,1)S(1)}, u32[]{:S(2)}, u32[]{:S(2)}) collective-permute-start(bf16[3,32,512]{2,1,0:T(8,128)(2,1)S(1)} %collective-permute-done.11.refs_8_), channel_id=1, source_target_pairs={{0,2},{1,3},{2,0},{3,1},{4,6},{5,7},{6,4},{7,5},{8,10},{9,11},{10,... | collective-permute-start | bytes 294920 | tf_op jit(solution)/shard_map/ppermute | solution.py:86
  42.5 2.0 %collective-permute-start.4 = (bf16[3,32,512]{2,1,0:T(8,128)(2,1)S(1)}, bf16[3,32,512]{2,1,0:T(8,128)(2,1)S(1)}, u32[]{:S(2)}, u32[]{:S(2)}) collective-permute-start(bf16[3,32,512]{2,1,0:T(8,128)(2,1)S(1)} %collective-permute-done.3.refs_0_), channel_id=1, source_target_pairs={{0,2},{1,3},{2,0},{3,1},{4,6},{5,7},{6,4},{7,5},{8,10},{9,11},{10,... | collective-permute-start | bytes 294920 | tf_op jit(solution)/shard_map/ppermute | solution.py:86
  46.1 2.0 %collective-permute-done.8.refs_5_ = bf16[3,32,512]{2,1,0:T(8,128)(2,1)S(1)} collective-permute-done((bf16[3,32,512]{2,1,0:T(8,128)(2,1)S(1)}, bf16[3,32,512]{2,1,0:T(8,128)(2,1)S(1)}, u32[]{:S(2)}, u32[]{:S(2)}) %collective-permute-start.8) | collective-permute-done | bytes 98336 | tf_op jit(solution)/shard_map/ppermute | solution.py:86
  54.8 3.1 %shard_map.103 = (bf16[384,512]{1,0:T(8,128)(2,1)S(1)}, bf16[384,512]{1,0:T(8,128)(2,1)S(1)}, bf16[384,512]{1,0:T(8,128)(2,1)S(1)}) custom-call(s32[2]{0:T(128)S(1)} %pad_add_fusion.place_ref, s32[4]{0:T(128)S(1)} %copy-done.5, bf16[3,128,2048]{2,1,0:T(8,128)(2,1)S(1)} %copy-done.3, bf16[3,512,512]{2,1,0:T(8,128)(2,1)S(1)} %copy-done.8, ...), custom_call_target="tpu_custom_call" | custom-call | flops 1207959552 | bytes 4718592 | tf_op jit(solution)/shard_map/pallas_call | solution.py:131
  65.6 3.2 %collective-permute-done.15 = bf16[384,512]{1,0:T(8,128)(2,1)S(1)} collective-permute-done((bf16[384,512]{1,0:T(8,128)(2,1)S(1)}, bf16[384,512]{1,0:T(8,128)(2,1)S(1)}, u32[]{:S(2)}, u32[]{:S(2)}) %collective-permute-start.15) | collective-permute-done | bytes 393248 | tf_op jit(solution)/shard_map/ppermute | solution.py:92
  69.5 7.6 %collective-permute-done.18 = bf16[384,512]{1,0:T(8,128)(2,1)S(1)} collective-permute-done((bf16[384,512]{1,0:T(8,128)(2,1)S(1)}, bf16[384,512]{1,0:T(8,128)(2,1)S(1)}, u32[]{:S(2)}, u32[]{:S(2)}) %collective-permute-start.18) | collective-permute-done | bytes 393248 | tf_op jit(solution)/shard_map/ppermute | solution.py:92
  77.9 7.6 %collective-permute-done.21 = bf16[384,512]{1,0:T(8,128)(2,1)S(1)} collective-permute-done((bf16[384,512]{1,0:T(8,128)(2,1)S(1)}, bf16[384,512]{1,0:T(8,128)(2,1)S(1)}, u32[]{:S(2)}, u32[]{:S(2)}) %collective-permute-start.21) | collective-permute-done | bytes 393248 | tf_op jit(solution)/shard_map/ppermute | solution.py:92
  94.3 15.3 %collective-permute-done.38 = bf16[384,512]{1,0:T(8,128)(2,1)S(1)} collective-permute-done((bf16[384,512]{1,0:T(8,128)(2,1)S(1)}, bf16[384,512]{1,0:T(8,128)(2,1)S(1)}, u32[]{:S(2)}, u32[]{:S(2)}) %collective-permute-start.38) | collective-permute-done | bytes 393248 | tf_op jit(solution)/shard_map/ppermute | solution.py:92
  110.9 5.5 %collective-permute-done.43 = bf16[384,512]{1,0:T(8,128)(2,1)S(1)} collective-permute-done((bf16[384,512]{1,0:T(8,128)(2,1)S(1)}, bf16[384,512]{1,0:T(8,128)(2,1)S(1)}, u32[]{:S(2)}, u32[]{:S(2)}) %collective-permute-start.43) | collective-permute-done | bytes 393248 | tf_op jit(solution)/shard_map/ppermute | solution.py:92
  117.8 7.0 %collective-permute-done.48 = bf16[384,512]{1,0:T(8,128)(2,1)S(1)} collective-permute-done((bf16[384,512]{1,0:T(8,128)(2,1)S(1)}, bf16[384,512]{1,0:T(8,128)(2,1)S(1)}, u32[]{:S(2)}, u32[]{:S(2)}) %collective-permute-start.48) | collective-permute-done | bytes 393248 | tf_op jit(solution)/shard_map/ppermute | solution.py:92
  128.4 3.0 %collective-permute-done.44.refs_0_ = bf16[384,512]{1,0:T(8,128)(2,1)S(1)} collective-permute-done((bf16[384,512]{1,0:T(8,128)(2,1)S(1)}, bf16[384,512]{1,0:T(8,128)(2,1)S(1)}, u32[]{:S(2)}, u32[]{:S(2)}) %collective-permute-start.44) | collective-permute-done | bytes 393248 | tf_op jit(solution)/shard_map/ppermute | solution.py:92
  131.4 2.0 %collective-permute-start.40 = (bf16[384,512]{1,0:T(8,128)(2,1)}, bf16[384,512]{1,0:T(8,128)(2,1)}, u32[]{:S(2)}, u32[]{:S(2)}) collective-permute-start(bf16[384,512]{1,0:T(8,128)(2,1)} %broadcast_select_fusion.2), channel_id=1, source_target_pairs={{0,1},{2,3},{5,4},{7,6},{10,11},{8,9},{15,14},{13,12},{16,17},{18,... | collective-permute-start | bytes 1179656 | tf_op jit(solution)/shard_map/ppermute | solution.py:92
  135.6 2.0 %collective-permute-start.45 = (bf16[384,512]{1,0:T(8,128)(2,1)}, bf16[384,512]{1,0:T(8,128)(2,1)}, u32[]{:S(2)}, u32[]{:S(2)}) collective-permute-start(bf16[384,512]{1,0:T(8,128)(2,1)} %broadcast_select_fusion.1), channel_id=1, source_target_pairs={{0,1},{2,3},{5,4},{7,6},{10,11},{8,9},{15,14},{13,12},{16,17},{18,... | collective-permute-start | bytes 1179656 | tf_op jit(solution)/shard_map/ppermute | solution.py:92
  139.2 2.0 %collective-permute-start.50 = (bf16[384,512]{1,0:T(8,128)(2,1)}, bf16[384,512]{1,0:T(8,128)(2,1)}, u32[]{:S(2)}, u32[]{:S(2)}) collective-permute-start(bf16[384,512]{1,0:T(8,128)(2,1)} %broadcast_select_fusion), channel_id=1, source_target_pairs={{0,1},{2,3},{5,4},{7,6},{10,11},{8,9},{15,14},{13,12},{16,17},{18,... | collective-permute-start | bytes 1179656 | tf_op jit(solution)/shard_map/ppermute | solution.py:92
  144.2 2.5 %collective-permute-start.1 = (f32[4,2048]{1,0:T(4,128)S(1)}, f32[4,2048]{1,0:T(4,128)S(1)}, u32[]{:S(2)}, u32[]{:S(2)}) collective-permute-start(f32[4,2048]{1,0:T(4,128)S(1)} %pad_maximum_fusion.refs_0_), channel_id=1, source_target_pairs={{0,2},{1,3},{2,0},{3,1},{4,6},{5,7},{6,4},{7,5},{8,10},{9,11},{10,... | collective-permute-start | bytes 98312 | tf_op jit(solution)/shard_map/ppermute | solution.py:86
  153.8 6.2 %collective-permute-start.55 = (f32[3,512]{1,0:T(4,128)S(1)}, f32[3,512]{1,0:T(4,128)S(1)}, u32[]{:S(2)}, u32[]{:S(2)}) collective-permute-start(f32[3,512]{1,0:T(4,128)S(1)} %pad_maximum_fusion.2.refs_14_), channel_id=1, source_target_pairs={{0,8},{4,12},{8,0},{12,4},{1,9},{5,13},{9,1},{13,5},{2,10},{6,14},... | collective-permute-start | bytes 18440 | tf_op jit(solution)/shard_map/ppermute | solution.py:86
  161.7 2.0 %collective-permute-done.54.refs_15_ = f32[3,512]{1,0:T(4,128)S(1)} collective-permute-done((f32[3,512]{1,0:T(4,128)S(1)}, f32[3,512]{1,0:T(4,128)S(1)}, u32[]{:S(2)}, u32[]{:S(2)}) %collective-permute-start.54) | collective-permute-done | bytes 6176 | tf_op jit(solution)/shard_map/ppermute | solution.py:86
  163.7 3.2 %shard_map.111 = (bf16[3,512,512]{2,1,0:T(8,128)(2,1)}, f32[2,2048]{1,0:T(2,128)}, f32[2,2048]{1,0:T(2,128)}) custom-call(s32[2]{0:T(128)S(1)} %pad_add_fusion.place_ref, s32[4]{0:T(128)S(1)} %copy-done.5, s32[3]{0:T(128)S(1)} %copy-done.6, f32[4,2048]{1,0:T(4,128)S(1)} %pad_maximum_fusion.refs_0_, f32[4,2048]{1,0:T(4,128)S(1)} %collective-permute-done.refs_1_, ...), custom_call_target="tpu_custom_call" | custom-call | tf_op jit(solution)/shard_map/pallas_call | solution.py:254
  (145 shorter events, 63.7 us)
Async XLA Ops:
  1.9 14.6 %collective-permute-start.32 = (bf16[3,32,512]{2,1,0:T(8,128)(2,1)S(1)}, bf16[3,32,512]{2,1,0:T(8,128)(2,1)S(1)}, u32[]{:S(2)}, u32[]{:S(2)}) collective-permute-start(bf16[3,32,512]{2,1,0:T(8,128)(2,1)S(1)} %get-tuple-element.39), channel_id=1, source_target_pairs={{0,12},{4,8},{8,4},{12,0},{1,13},{5,9},{9,5},{13,1},{2,14},{6,10},... | collective-permute-start | bytes 294920 | tf_op jit(solution)/shard_map/ppermute | solution.py:86
  9.1 14.8 %collective-permute-start.28 = (bf16[3,32,512]{2,1,0:T(8,128)(2,1)S(1)}, bf16[3,32,512]{2,1,0:T(8,128)(2,1)S(1)}, u32[]{:S(2)}, u32[]{:S(2)}) collective-permute-start(bf16[3,32,512]{2,1,0:T(8,128)(2,1)S(1)} %get-tuple-element.40), channel_id=1, source_target_pairs={{0,8},{4,12},{8,0},{12,4},{1,9},{5,13},{9,1},{13,5},{2,10},{6,14},... | collective-permute-start | bytes 294920 | tf_op jit(solution)/shard_map/ppermute | solution.py:86
  11.9 13.5 %collective-permute-start.24 = (bf16[3,32,512]{2,1,0:T(8,128)(2,1)S(1)}, bf16[3,32,512]{2,1,0:T(8,128)(2,1)S(1)}, u32[]{:S(2)}, u32[]{:S(2)}) collective-permute-start(bf16[3,32,512]{2,1,0:T(8,128)(2,1)S(1)} %get-tuple-element.41), channel_id=1, source_target_pairs={{0,4},{4,0},{8,12},{12,8},{1,5},{5,1},{9,13},{13,9},{2,6},{6,2},{1... | collective-permute-start | bytes 294920 | tf_op jit(solution)/shard_map/ppermute | solution.py:86
  14.6 11.3 %collective-permute-start.11 = (bf16[3,32,512]{2,1,0:T(8,128)(2,1)S(1)}, bf16[3,32,512]{2,1,0:T(8,128)(2,1)S(1)}, u32[]{:S(2)}, u32[]{:S(2)}) collective-permute-start(bf16[3,32,512]{2,1,0:T(8,128)(2,1)S(1)} %get-tuple-element.42), channel_id=1, source_target_pairs={{0,12},{4,8},{8,4},{12,0},{1,13},{5,9},{9,5},{13,1},{2,14},{6,10},... | collective-permute-start | bytes 294920 | tf_op jit(solution)/shard_map/ppermute | solution.py:86
  30.1 12.3 %collective-permute-start.7 = (bf16[3,32,512]{2,1,0:T(8,128)(2,1)S(1)}, bf16[3,32,512]{2,1,0:T(8,128)(2,1)S(1)}, u32[]{:S(2)}, u32[]{:S(2)}) collective-permute-start(bf16[3,32,512]{2,1,0:T(8,128)(2,1)S(1)} %get-tuple-element.43), channel_id=1, source_target_pairs={{0,8},{4,12},{8,0},{12,4},{1,9},{5,13},{9,1},{13,5},{2,10},{6,14},... | collective-permute-start | bytes 294920 | tf_op jit(solution)/shard_map/ppermute | solution.py:86
  30.1 12.3 %collective-permute-start.3 = (bf16[3,32,512]{2,1,0:T(8,128)(2,1)S(1)}, bf16[3,32,512]{2,1,0:T(8,128)(2,1)S(1)}, u32[]{:S(2)}, u32[]{:S(2)}) collective-permute-start(bf16[3,32,512]{2,1,0:T(8,128)(2,1)S(1)} %get-tuple-element.44), channel_id=1, source_target_pairs={{0,4},{4,0},{8,12},{12,8},{1,5},{5,1},{9,13},{13,9},{2,6},{6,2},{1... | collective-permute-start | bytes 294920 | tf_op jit(solution)/shard_map/ppermute | solution.py:86
  37.8 22.7 %collective-permute-start.36 = (bf16[384,512]{1,0:T(8,128)(2,1)S(1)}, bf16[384,512]{1,0:T(8,128)(2,1)}, u32[]{:S(2)}, u32[]{:S(2)}) collective-permute-start(bf16[384,512]{1,0:T(8,128)(2,1)S(1)} %get-tuple-element.27), channel_id=1, source_target_pairs={{1,5},{2,6},{3,7},{12,8},{13,9},{14,10},{17,21},{18,22},{19,23},{2... | collective-permute-start | bytes 1179656 | tf_op jit(solution)/shard_map/ppermute | solution.py:92
  50.4 12.6 %collective-permute-start.41 = (bf16[384,512]{1,0:T(8,128)(2,1)S(1)}, bf16[384,512]{1,0:T(8,128)(2,1)}, u32[]{:S(2)}, u32[]{:S(2)}) collective-permute-start(bf16[384,512]{1,0:T(8,128)(2,1)S(1)} %get-tuple-element.29), channel_id=1, source_target_pairs={{1,5},{2,6},{3,7},{12,8},{13,9},{14,10},{17,21},{18,22},{19,23},{2... | collective-permute-start | bytes 1179656 | tf_op jit(solution)/shard_map/ppermute | solution.py:92
  51.8 13.0 %collective-permute-start.46 = (bf16[384,512]{1,0:T(8,128)(2,1)S(1)}, bf16[384,512]{1,0:T(8,128)(2,1)S(1)}, u32[]{:S(2)}, u32[]{:S(2)}) collective-permute-start(bf16[384,512]{1,0:T(8,128)(2,1)S(1)} %get-tuple-element.31), channel_id=1, source_target_pairs={{1,5},{2,6},{3,7},{12,8},{13,9},{14,10},{17,21},{18,22},{19,23},{2... | collective-permute-start | bytes 1179656 | tf_op jit(solution)/shard_map/ppermute | solution.py:92
  59.2 18.0 %collective-permute-start.18 = (bf16[384,512]{1,0:T(8,128)(2,1)S(1)}, bf16[384,512]{1,0:T(8,128)(2,1)S(1)}, u32[]{:S(2)}, u32[]{:S(2)}) collective-permute-start(bf16[384,512]{1,0:T(8,128)(2,1)S(1)} %get-tuple-element.23), channel_id=1, source_target_pairs={{0,4},{1,5},{2,6},{3,7},{12,8},{13,9},{14,10},{15,11},{16,20},{17,... | collective-permute-start | bytes 1179656 | tf_op jit(solution)/shard_map/ppermute | solution.py:92
  60.5 25.1 %collective-permute-start.21 = (bf16[384,512]{1,0:T(8,128)(2,1)S(1)}, bf16[384,512]{1,0:T(8,128)(2,1)S(1)}, u32[]{:S(2)}, u32[]{:S(2)}) collective-permute-start(bf16[384,512]{1,0:T(8,128)(2,1)S(1)} %get-tuple-element.25), channel_id=1, source_target_pairs={{0,4},{1,5},{2,6},{3,7},{12,8},{13,9},{14,10},{15,11},{16,20},{17,... | collective-permute-start | bytes 1179656 | tf_op jit(solution)/shard_map/ppermute | solution.py:92
  63.0 23.4 %collective-permute-start.37 = (bf16[384,512]{1,0:T(8,128)(2,1)S(1)}, bf16[384,512]{1,0:T(8,128)(2,1)S(1)}, u32[]{:S(2)}, u32[]{:S(2)}) collective-permute-start(bf16[384,512]{1,0:T(8,128)(2,1)S(1)} %add_convert_fusion.8), channel_id=1, source_target_pairs={{6,10},{7,11},{8,4},{9,5},{22,26},{23,27},{24,20},{25,21}} | collective-permute-start | bytes 1179656 | tf_op jit(solution)/shard_map/ppermute | solution.py:92
  64.8 22.4 %collective-permute-start.42 = (bf16[384,512]{1,0:T(8,128)(2,1)S(1)}, bf16[384,512]{1,0:T(8,128)(2,1)S(1)}, u32[]{:S(2)}, u32[]{:S(2)}) collective-permute-start(bf16[384,512]{1,0:T(8,128)(2,1)S(1)} %add_convert_fusion.5), channel_id=1, source_target_pairs={{6,10},{7,11},{8,4},{9,5},{22,26},{23,27},{24,20},{25,21}} | collective-permute-start | bytes 1179656 | tf_op jit(solution)/shard_map/ppermute | solution.py:92
  68.7 19.9 %collective-permute-start.47 = (bf16[384,512]{1,0:T(8,128)(2,1)S(1)}, bf16[384,512]{1,0:T(8,128)(2,1)S(1)}, u32[]{:S(2)}, u32[]{:S(2)}) collective-permute-start(bf16[384,512]{1,0:T(8,128)(2,1)S(1)} %add_convert_fusion.2), channel_id=1, source_target_pairs={{6,10},{7,11},{8,4},{9,5},{22,26},{23,27},{24,20},{25,21}} | collective-permute-start | bytes 1179656 | tf_op jit(solution)/shard_map/ppermute | solution.py:92
  77.1 12.9 %collective-permute-start.16 = (bf16[384,512]{1,0:T(8,128)(2,1)S(1)}, bf16[384,512]{1,0:T(8,128)(2,1)S(1)}, u32[]{:S(2)}, u32[]{:S(2)}) collective-permute-start(bf16[384,512]{1,0:T(8,128)(2,1)S(1)} %add_convert_fusion.14), channel_id=1, source_target_pairs={{4,8},{5,9},{6,10},{7,11},{8,4},{9,5},{10,6},{11,7},{20,24},{21,25... | collective-permute-start | bytes 1179656 | tf_op jit(solution)/shard_map/ppermute | solution.py:92
  87.2 22.4 %collective-permute-start.38 = (bf16[384,512]{1,0:T(8,128)(2,1)S(1)}, bf16[384,512]{1,0:T(8,128)(2,1)S(1)}, u32[]{:S(2)}, u32[]{:S(2)}) collective-permute-start(bf16[384,512]{1,0:T(8,128)(2,1)S(1)} %add_convert_fusion.7), channel_id=1, source_target_pairs={{4,0},{11,15},{20,16},{27,31}} | collective-permute-start | bytes 1179656 | tf_op jit(solution)/shard_map/ppermute | solution.py:92
  88.6 27.8 %collective-permute-start.43 = (bf16[384,512]{1,0:T(8,128)(2,1)S(1)}, bf16[384,512]{1,0:T(8,128)(2,1)S(1)}, u32[]{:S(2)}, u32[]{:S(2)}) collective-permute-start(bf16[384,512]{1,0:T(8,128)(2,1)S(1)} %add_convert_fusion.4), channel_id=1, source_target_pairs={{4,0},{11,15},{20,16},{27,31}} | collective-permute-start | bytes 1179656 | tf_op jit(solution)/shard_map/ppermute | solution.py:92
  90.0 34.8 %collective-permute-start.48 = (bf16[384,512]{1,0:T(8,128)(2,1)S(1)}, bf16[384,512]{1,0:T(8,128)(2,1)S(1)}, u32[]{:S(2)}, u32[]{:S(2)}) collective-permute-start(bf16[384,512]{1,0:T(8,128)(2,1)S(1)} %add_convert_fusion.1), channel_id=1, source_target_pairs={{4,0},{11,15},{20,16},{27,31}} | collective-permute-start | bytes 1179656 | tf_op jit(solution)/shard_map/ppermute | solution.py:92
  91.4 47.0 %collective-permute-start.17 = (bf16[384,512]{1,0:T(8,128)(2,1)S(1)}, bf16[384,512]{1,0:T(8,128)(2,1)S(1)}, u32[]{:S(2)}, u32[]{:S(2)}) collective-permute-start(bf16[384,512]{1,0:T(8,128)(2,1)S(1)} %add_convert_fusion.13.near_ref), channel_id=1, source_target_pairs={{4,0},{5,1},{6,2},{7,3},{8,12},{9,13},{10,14},{11,15},{20,16},{21,... | collective-permute-start | bytes 1179656 | tf_op jit(solution)/shard_map/ppermute | solution.py:92
  92.8 50.2 %collective-permute-start.20 = (bf16[384,512]{1,0:T(8,128)(2,1)S(1)}, bf16[384,512]{1,0:T(8,128)(2,1)}, u32[]{:S(2)}, u32[]{:S(2)}) collective-permute-start(bf16[384,512]{1,0:T(8,128)(2,1)S(1)} %add_convert_fusion.11.near_ref), channel_id=1, source_target_pairs={{4,0},{5,1},{6,2},{7,3},{8,12},{9,13},{10,14},{11,15},{20,16},{21,... | collective-permute-start | bytes 1179656 | tf_op jit(solution)/shard_map/ppermute | solution.py:92
  109.6 34.6 %collective-permute-start.23 = (bf16[384,512]{1,0:T(8,128)(2,1)S(1)}, bf16[384,512]{1,0:T(8,128)(2,1)}, u32[]{:S(2)}, u32[]{:S(2)}) collective-permute-start(bf16[384,512]{1,0:T(8,128)(2,1)S(1)} %add_convert_fusion.9.near_ref), channel_id=1, source_target_pairs={{4,0},{5,1},{6,2},{7,3},{8,12},{9,13},{10,14},{11,15},{20,16},{21,... | collective-permute-start | bytes 1179656 | tf_op jit(solution)/shard_map/ppermute | solution.py:92
  131.4 16.4 %collective-permute-start.40 = (bf16[384,512]{1,0:T(8,128)(2,1)}, bf16[384,512]{1,0:T(8,128)(2,1)}, u32[]{:S(2)}, u32[]{:S(2)}) collective-permute-start(bf16[384,512]{1,0:T(8,128)(2,1)} %broadcast_select_fusion.2), channel_id=1, source_target_pairs={{0,1},{2,3},{5,4},{7,6},{10,11},{8,9},{15,14},{13,12},{16,17},{18,... | collective-permute-start | bytes 1179656 | tf_op jit(solution)/shard_map/ppermute | solution.py:92
  135.6 13.6 %collective-permute-start.45 = (bf16[384,512]{1,0:T(8,128)(2,1)}, bf16[384,512]{1,0:T(8,128)(2,1)}, u32[]{:S(2)}, u32[]{:S(2)}) collective-permute-start(bf16[384,512]{1,0:T(8,128)(2,1)} %broadcast_select_fusion.1), channel_id=1, source_target_pairs={{0,1},{2,3},{5,4},{7,6},{10,11},{8,9},{15,14},{13,12},{16,17},{18,... | collective-permute-start | bytes 1179656 | tf_op jit(solution)/shard_map/ppermute | solution.py:92
  139.2 12.6 %collective-permute-start.50 = (bf16[384,512]{1,0:T(8,128)(2,1)}, bf16[384,512]{1,0:T(8,128)(2,1)}, u32[]{:S(2)}, u32[]{:S(2)}) collective-permute-start(bf16[384,512]{1,0:T(8,128)(2,1)} %broadcast_select_fusion), channel_id=1, source_target_pairs={{0,1},{2,3},{5,4},{7,6},{10,11},{8,9},{15,14},{13,12},{16,17},{18,... | collective-permute-start | bytes 1179656 | tf_op jit(solution)/shard_map/ppermute | solution.py:92
  (44 other events, 282.0 us)

commit v3 on v2

--- a/solution.py
+++ b/solution.py
@@ -96,19 +96,22 @@
     return [pl.BlockSpec(a.shape, lambda i, *s, n=a.ndim: (0,) * n) for a in arrays]
 
 
-def project_rows(place, counts, tokens, pieces, basis):
+def project_rows(place, counts, tokens, pieces, basis, groups):
     layers, tok_rows, _ = tokens.shape
     tile, cols = basis.shape[1:]
     n_dp = len(pieces) + 1
     n_own = len(pieces[0])
     part_rows = tok_rows // n_own
     packed = 3 * n_dp * tok_rows // 4
+    half = packed // 2
     flat = [p for group in pieces for p in group]
+    shapes = [(len(group), half, cols) for group in groups for _ in range(2)]
 
     def kernel(place_ref, counts_ref, tokens_ref, basis_ref, *refs):
         piece_refs, out_refs = refs[: len(flat)], refs[len(flat) :]
         dp, own = place_ref[0], place_ref[1]
         row = lax.broadcasted_iota(jnp.int32, (packed, tok_rows), 0)
+        row = jnp.where(dp % 2 == 0, row, jnp.where(row < half, row + half, row - half))
         col = lax.broadcasted_iota(jnp.int32, (packed, tok_rows), 1)
         turn = (col // part_rows) % n_own
         shared = (own ^ (((turn & 1) << 1) | (turn >> 1))) * part_rows + col % part_rows
@@ -121,22 +124,25 @@
             index = col if mask == 0 else shared
             picks.append(((row == start + index) & (index < counts_ref[shard])).astype(jnp.bfloat16))
         select = jnp.concatenate(picks, axis=1)
-        for layer in range(layers):
-            rows = jnp.concatenate([tokens_ref[layer]] + [p[layer] for p in piece_refs], axis=0)
-            chosen = jnp.dot(select, rows, preferred_element_type=jnp.float32).astype(jnp.bfloat16)
-            out_refs[layer][...] = jnp.dot(
-                chosen, basis_ref[layer], preferred_element_type=jnp.float32
-            ).astype(jnp.bfloat16)
+        for number, group in enumerate(groups):
+            for at, layer in enumerate(group):
+                rows = jnp.concatenate([tokens_ref[layer]] + [p[layer] for p in piece_refs], axis=0)
+                chosen = jnp.dot(select, rows, preferred_element_type=jnp.float32).astype(jnp.bfloat16)
+                result = jnp.dot(
+                    chosen, basis_ref[layer], preferred_element_type=jnp.float32
+                ).astype(jnp.bfloat16)
+                out_refs[2 * number][at] = result[:half]
+                out_refs[2 * number + 1][at] = result[half:]
 
     return pl.pallas_call(
         kernel,
-        out_shape=[jax.ShapeDtypeStruct((packed, cols), jnp.bfloat16)] * layers,
+        out_shape=[jax.ShapeDtypeStruct(shape, jnp.bfloat16) for shape in shapes],
         grid_spec=pltpu.PrefetchScalarGridSpec(
             num_scalar_prefetch=2,
             grid=(1,),
             in_specs=[pl.BlockSpec((layers, tok_rows, tile), lambda i, place, n: (0, 0, place[0]))]
             + whole(basis, *flat),
-            out_specs=[pl.BlockSpec((packed, cols), lambda i, *s: (0, 0))] * layers,
+            out_specs=[pl.BlockSpec(shape, lambda i, *s: (0, 0, 0)) for shape in shapes],
         ),
         compiler_params=pltpu.CompilerParams(vmem_limit_bytes=32 * 1024 * 1024),
         cost_estimate=pl.CostEstimate(
@@ -147,51 +153,77 @@
     )(place, counts, tokens, basis, *flat)
 
 
-def settle(flags, near, far):
-    def kernel(flags_ref, near_ref, *refs):
-        far_refs, panel_ref, square_ref = refs[:-2], refs[-2], refs[-1]
-        value = near_ref[...]
-        for index, far_ref in enumerate(far_refs):
-            value = jnp.where(flags_ref[0] == index + 1, far_ref[...], value)
-        panel_ref[...] = value
-        wide = value.astype(jnp.float32)
-        square_ref[...] = jnp.sum(wide * wide, axis=0, keepdims=True)
+def column_squares(ref, other_ref, layer):
+    near = ref[layer].astype(jnp.float32)
+    far = other_ref[layer].astype(jnp.float32)
+    return jnp.sum(near * near, axis=0, keepdims=True) + jnp.sum(far * far, axis=0, keepdims=True)
+
+
+def settle_acts(state_act, state_grad, panels):
+    slot_count, width = state_act.shape
+    cols = panels[0].shape[2]
+    layers = sum(panel.shape[0] for panel in panels[::2])
+
+    def kernel(state_act_ref, state_grad_ref, *refs):
+        packet_ref = refs[-1]
+        packet_ref[...] = jnp.zeros_like(packet_ref)
+        packet_ref[:slot_count] = state_act_ref[...]
+        packet_ref[slot_count : 2 * slot_count] = state_grad_ref[...]
+        layer = 2 * slot_count
+        for near_ref, far_ref in zip(refs[:-1:2], refs[1:-1:2], strict=True):
+            for at in range(near_ref.shape[0]):
+                packet_ref[layer : layer + 1, :cols] = column_squares(near_ref, far_ref, at)
+                layer += 1
 
     return pl.pallas_call(
         kernel,
-        out_shape=[
-            jax.ShapeDtypeStruct(near.shape, near.dtype),
-            jax.ShapeDtypeStruct((1, near.shape[1]), jnp.float32),
-        ],
+        out_shape=jax.ShapeDtypeStruct((2 * slot_count + layers, width), jnp.float32),
+        compiler_params=pltpu.CompilerParams(vmem_limit_bytes=32 * 1024 * 1024),
+    )(state_act, state_grad, *panels)
+
+
+def settle_grads(place, home, arrivals):
+    layers, half, cols = arrivals[0][0].shape
+    flat = [array for pair in arrivals for array in pair]
+
+    def kernel(home_ref, *refs):
+        in_refs, (near_ref, far_ref, square_ref) = refs[:-3], refs[-3:]
+        for index in range(len(arrivals)):
+
+            @pl.when(home_ref[0] == index)
+            def _(index=index):
+                near_ref[...] = in_refs[2 * index][...]
+                far_ref[...] = in_refs[2 * index + 1][...]
+
+        for layer in range(layers):
+            square_ref[layer : layer + 1] = column_squares(near_ref, far_ref, layer)
+
+    out_shape = [jax.ShapeDtypeStruct((layers, half, cols), jnp.bfloat16)] * 2 + [
+        jax.ShapeDtypeStruct((layers, cols), jnp.float32)
+    ]
+    return pl.pallas_call(
+        kernel,
+        out_shape=out_shape,
         grid_spec=pltpu.PrefetchScalarGridSpec(
-            num_scalar_prefetch=1,
-            grid=(1,),
-            in_specs=whole(near, *far),
-            out_specs=[
-                pl.BlockSpec(near.shape, lambda i, *s: (0, 0)),
-                pl.BlockSpec((1, near.shape[1]), lambda i, *s: (0, 0)),
-            ],
+            num_scalar_prefetch=1, grid=(1,), in_specs=whole(*flat), out_specs=whole(*out_shape)
         ),
-        compiler_params=pltpu.CompilerParams(vmem_limit_bytes=16 * 1024 * 1024),
-        cost_estimate=pl.CostEstimate(
-            flops=3 * near.size, bytes_accessed=4 * near.size, transcendentals=0
-        ),
-    )(flags, near, *far)
-
-
-def finish(place, counts, owner_of, states, acts, grads, square_acts, square_grads):
-    layers = len(acts)
-    n_own, n_dp = len(square_acts), len(square_grads)
-    tile = acts[0].shape[1]
-    slot_count = states[0].shape[0] // 2
-    width = states[0].shape[1]
-    operands = [*states, *acts, *grads, *square_acts, *square_grads]
+        compiler_params=pltpu.CompilerParams(vmem_limit_bytes=32 * 1024 * 1024),
+    )(home, *flat)
+
+
+def finish(place, counts, owner_of, packets, squares, acts, grads, slot_count):
+    layers = owner_of.shape[0]
+    n_own, n_dp = len(packets), len(squares)
+    tile = acts[0].shape[2]
+    width = packets[0].shape[1]
+    where_act = [(2 * number, at) for number, a in enumerate(acts[::2]) for at in range(a.shape[0])]
+    operands = [*packets, *squares, *acts, *grads]
 
     def kernel(place_ref, counts_ref, owner_ref, *refs):
-        refs = list(refs)
-        take = lambda n: [refs.pop(0) for _ in range(n)]
-        state_refs, act_refs, grad_refs = take(n_own), take(layers), take(layers)
-        square_act_refs, square_grad_refs = take(n_own), take(n_dp)
+        packet_refs, refs = refs[:n_own], refs[n_own:]
+        square_refs, refs = refs[:n_dp], refs[n_dp:]
+        act_refs, refs = refs[: len(acts)], refs[len(acts) :]
+        grad_refs, refs = refs[:2], refs[2:]
         out_ref, new_act_ref, new_grad_ref, act_full, grad_full = refs
         dp, own = place_ref[0], place_ref[1]
         total = counts_ref[0]
@@ -200,12 +232,12 @@
         total = total.astype(jnp.float32)
         for mask in range(n_own):
             at = pl.ds(pl.multiple_of((own ^ mask) * tile, tile), tile)
-            act_full[:, at] = square_act_refs[mask][...] / total
+            act_full[:, at] = packet_refs[mask][2 * slot_count :, :tile] / total
         for mask in range(n_dp):
             at = pl.ds(pl.multiple_of((dp ^ mask) * tile, tile), tile)
-            grad_full[:, at] = square_grad_refs[mask][...] / total
-        new_act_ref[...] = state_refs[0][:slot_count]
-        new_grad_ref[...] = state_refs[0][slot_count:]
+            grad_full[:, at] = square_refs[mask][...] / total
+        new_act_ref[...] = packet_refs[0][:slot_count]
+        new_grad_ref[...] = packet_refs[0][slot_count : 2 * slot_count]
         for layer in range(layers):
             owner_now = owner_ref[layer]
             rank = jnp.int32(0)
@@ -216,16 +248,13 @@
             for mask in range(n_own):
                 for slot in range(slot_count):
                     here = (owner_now == own ^ mask) & (rank == slot)
-                    old_act = jnp.where(here, state_refs[mask][slot : slot + 1], old_act)
-                    old_grad = jnp.where(
-                        here, state_refs[mask][slot_count + slot : slot_count + slot + 1], old_grad
-                    )
-            act_full[layer : layer + 1] = eigen_act = (
-                decay_rate * old_act + (1.0 - decay_rate) * act_full[layer : layer + 1]
-            )
-            grad_full[layer : layer + 1] = eigen_grad = (
-                decay_rate * old_grad + (1.0 - decay_rate) * grad_full[layer : layer + 1]
-            )
+                    down = slot_count + slot
+                    old_act = jnp.where(here, packet_refs[mask][slot : slot + 1], old_act)
+                    old_grad = jnp.where(here, packet_refs[mask][down : down + 1], old_grad)
+            eigen_act = decay_rate * old_act + (1.0 - decay_rate) * act_full[layer : layer + 1]
+            eigen_grad = decay_rate * old_grad + (1.0 - decay_rate) * grad_full[layer : layer + 1]
+            act_full[layer : layer + 1] = eigen_act
+            grad_full[layer : layer + 1] = eigen_grad
             for slot in range(slot_count):
 
                 @pl.when((owner_now == own) & (rank == slot))
@@ -238,11 +267,15 @@
             cols = act_full[layer : layer + 1, pl.ds(pl.multiple_of(own * tile, tile), tile)]
             rows = jnp.transpose(jnp.broadcast_to(rows, (128, tile)))
             rows = jnp.concatenate([rows] * (tile // 128), axis=1)
-            gram = lax.dot_general(
-                grad_refs[layer][...],
-                act_refs[layer][...],
-                (((0,), (0,)), ((), ())),
-                preferred_element_type=jnp.float32,
+            number, at = where_act[layer]
+            gram = sum(
+                lax.dot_general(
+                    grad_refs[side][layer],
+                    act_refs[number + side][at],
+                    (((0,), (0,)), ((), ())),
+                    preferred_element_type=jnp.float32,
+                )
+                for side in range(2)
             )
             out_ref[layer] = (gram / total / (rows * cols + damping)).astype(jnp.bfloat16)
 
@@ -274,7 +307,6 @@
     dp = lax.axis_index("dp")
     own = lax.axis_index("owner")
     place = jnp.stack([dp, own]).astype(jnp.int32)
-    f32 = jnp.float32
 
     def pieces_of(tokens):
         part = lax.dynamic_slice_in_dim(tokens, own * part_rows, part_rows, 1)
@@ -285,45 +317,42 @@
             groups.append([got, chip, flip(got, "owner", 1), flip(chip, "owner", 1)])
         return groups
 
-    def add(*terms):
-        return sum(term.astype(f32) for term in terms).astype(jnp.bfloat16)
+    def add(first, second):
+        return (first.astype(jnp.float32) + second.astype(jnp.float32)).astype(jnp.bfloat16)
+
+    swapped = lax.ppermute(basis_grad, "owner", [(o, -o % n_own) for o in range(n_own)])
+    held = [-o % n_own for o in range(n_own)]
 
     pieces_act = pieces_of(activations)
     pieces_grad = pieces_of(out_grads)
-
-    states = [jnp.concatenate([state_act, state_grad], axis=0)]
-    states += [flip(states[0], "owner", mask) for mask in range(1, n_own)]
-
-    parts_act = project_rows(place, counts, activations, pieces_act, basis_act)
-    parts_grad = project_rows(place, counts, out_grads, pieces_grad, basis_grad)
-    outer = (dp == 0) | (dp == n_dp - 1)
-    take_outer = jnp.where(outer, 1, 0).astype(jnp.int32)[None]
-    home = jnp.where(own == dp, 0, jnp.where(own == dp ^ 2, 1, 2)).astype(jnp.int32)[None]
-    every = range(n_own)
-    acts, grads, square_acts, square_grads = [], [], [], []
-    for layer in range(layers):
-        part = parts_act[layer]
-        part = add(part, hop(part, [((a, b), (c, b)) for a, c in ((0, 1), (3, 2)) for b in every]))
-        part = add(part, hop(part, [((a, b), (c, b)) for a, c in ((1, 2), (2, 1)) for b in every]))
-        back = hop(part, [((a, b), (c, b)) for a, c in ((1, 0), (2, 3)) for b in every])
-        panel, square = settle(take_outer, part, [back])
-        acts.append(panel)
-        square_acts.append(square)
-        part = parts_grad[layer]
-        part = add(part, hop(part, [((0, b), (1, b)) for b in (1, 2, 3)] + [((3, b), (2, b)) for b in (0, 1, 2)]))
-        part = add(part, hop(part, [((1, b), (2, b)) for b in (2, 3)] + [((2, b), (1, b)) for b in (0, 1)]))
-        part = add(part, hop(part, [((1, 0), (0, 0)), ((2, 3), (3, 3))]))
-        chip = hop(part, [((a, a), (a, a ^ 2)) for a in range(n_dp)])
-        half = jnp.where(own == dp, part, chip)
-        core = hop(half, [((a, a ^ b), (a, a ^ b ^ 1)) for a in range(n_dp) for b in (0, 2)])
-        panel, square = settle(home, part, [chip, core])
-        grads.append(panel)
-        square_grads.append(square)
-    square_act = jnp.concatenate(square_acts, axis=0)
-    square_grad = jnp.concatenate(square_grads, axis=0)
-    square_acts = [square_act] + [flip(square_act, "owner", mask) for mask in range(1, n_own)]
-    square_grads = [square_grad] + [flip(square_grad, "dp", mask) for mask in range(1, n_dp)]
-    return tuple(finish(place, counts, owner_of, states, acts, grads, square_acts, square_grads))
+    early = [[*range(layers - 1)], [layers - 1]]
+    parts_act = project_rows(place, counts, activations, pieces_act, basis_act, early)
+    keep, send = project_rows(place, counts, out_grads, pieces_grad, swapped, [[*range(layers)]])
+
+    def total_of(keep, send):
+        part = add(keep, flip(send, "dp", 1))
+        part = add(part, flip(part, "dp", 2))
+        return [part, flip(part, "dp", 1)]
+
+    first = total_of(*parts_act[:2])
+
+    part = add(keep, flip(send, "dp", 1))
+    pairs = [((a, o), (a ^ 2, o)) for a in range(n_dp) for o in range(n_own) if (a ^ held[o]) & 2]
+    near = add(part, hop(part, pairs))
+    far = hop(near, [((held[o] ^ 1, o), (held[o], o)) for o in range(n_own)])
+    arrivals = [(near, far)]
+    arrivals.append([hop(a, [((held[o], o), (held[o], o ^ 2)) for o in range(n_own)]) for a in (near, far)])
+    source = -dp % n_own
+    pairs = [((held[o], o ^ b), (held[o], o ^ b ^ 1)) for o in range(n_own) for b in (0, 2)]
+    arrivals.append([hop(jnp.where(own == source, a, b), pairs) for a, b in zip(*arrivals, strict=True)])
+    home = jnp.where(own == source, 0, jnp.where(own == source ^ 2, 1, 2)).astype(jnp.int32)[None]
+    *grads, squares = settle_grads(place, home, arrivals)
+    squares = [squares] + [flip(squares, "dp", mask) for mask in range(1, n_dp)]
+
+    acts = first + total_of(*parts_act[2:])
+    packet = settle_acts(state_act, state_grad, acts)
+    packets = [packet] + [flip(packet, "owner", mask) for mask in range(1, n_own)]
+    return tuple(finish(place, counts, owner_of, packets, squares, acts, grads, state_act.shape[0]))
 
 
 def solution(mesh):

time: 168 us -> 162 us (0.964)
  waiting for transfers between devices: 69.5 us -> 87.2 us
  starting transfers between devices: 64.8 us -> 55 us
  local copies, waits for them, and re-layouts: 10.7 us -> 3.55 us
  Pallas kernels: 13.9 us -> 10.5 us
  other arithmetic: 6.78 us -> 4.35 us
    ppermute x33 -> x37, waiting for transfers between devices: 18.9 us -> 79.9 us  [flip(): lax.ppermute(array, axis, [(i, i ^ mask) for i in range(lax.axis_size(axi...]
    ppermute x24 -> x6, waiting for transfers between devices: 50.6 us -> 7.21 us  [hop(): return lax.ppermute(array, ('dp', 'owner'), flat)]
    ppermute x24 -> x6, starting transfers between devices: 29.3 us -> 10.5 us  [hop(): return lax.ppermute(array, ('dp', 'owner'), flat)]
    ppermute x33 -> x37, starting transfers between devices: 35.6 us -> 42.5 us  [flip(): lax.ppermute(array, axis, [(i, i ^ mask) for i in range(lax.axis_size(axi...]
    unnamed x22 -> x16, local copies, waits for them, and re-layouts: 8.15 us -> 2.09 us
    pallas_call x8 -> x4, Pallas kernels: 10.7 us -> 6.29 us  [the longest x2 4.14 us: project_rows(): pl.pallas_call(kernel, out_shape=[jax.ShapeDtypeStruct(shape, jnp.bfloat1...]
    ppermute x0 -> x1, starting transfers between devices: none -> 2.07 us  [line_plan(): lax.ppermute(basis_grad, 'owner', [(o, -o % n_own) for o in range(n_own)])]
    convert_element_type x15 -> x6, other arithmetic: 3.53 us -> 2.52 us  [add(): (first.astype(jnp.float32) + second.astype(jnp.float32)).astype(jnp.bfloa...]
  transfers between devices with their start and end apart: 57 -> 44, of which waited for: 17 -> 20; matrix products, arithmetic and copies ran while one was open for 5% -> 4% of each run, Pallas kernels for 6% -> 3%
where the time goes in v3:
time: 162 us; the launch traced here: 161 us
  waiting for transfers between devices  87.2 us (54%)
  starting transfers between devices  55 us (34%)
  Pallas kernels  10.5 us (6%)
  other arithmetic  4.35 us (3%)
  local copies, waits for them, and re-layouts  3.55 us (2%)
    ppermute x37, waiting for transfers between devices, flip(): lax.ppermute(array, axis, [(i, i ^ mask) for i in range(lax.axis_size(axi...  79.9 us
    ppermute x37, starting transfers between devices, flip(): lax.ppermute(array, axis, [(i, i ^ mask) for i in range(lax.axis_size(axi...  42.5 us
    ppermute x6, starting transfers between devices, hop(): return lax.ppermute(array, ('dp', 'owner'), flat)  10.5 us
    ppermute x6, waiting for transfers between devices, hop(): return lax.ppermute(array, ('dp', 'owner'), flat)  7.21 us
    pallas_call x1, Pallas kernels, finish(): pl.pallas_call(kernel, out_shape=out_shape, grid_spec=pltpu.PrefetchScala...  4.19 us
    pallas_call x2, Pallas kernels, project_rows(): pl.pallas_call(kernel, out_shape=[jax.ShapeDtypeStruct(shape, jnp.bfloat1...  4.14 us
  transfers between devices with their start and end apart: 44, of which 20 were waited for; matrix products, arithmetic and copies ran while one was open for 4% of the time, Pallas kernels for 3%

profile of v3, /device:TPU:0, one launch (start us, length us, event | category | flops | bytes accessed | tf_op | source)
XLA Modules:
  0.0 161.4 jit_solution(18147460830363329011)
XLA Ops:
  0.6 2.1 %collective-permute-start.21 = (bf16[3,512,512]{2,1,0:T(8,128)(2,1)}, bf16[3,512,512]{2,1,0:T(8,128)(2,1)S(1)}, u32[]{:S(2)}, u32[]{:S(2)}) collective-permute-start(bf16[3,512,512]{2,1,0:T(8,128)(2,1)} %param.11), channel_id=1, source_target_pairs={{0,0},{1,3},{2,2},{3,1},{4,4},{5,7},{6,6},{7,5},{8,8},{9,11},{10,1... | collective-permute-start | bytes 4718600 | tf_op jit(solution)/shard_map/ppermute | solution.py:323
  3.9 3.1 %collective-permute-start.22 = (bf16[3,32,512]{2,1,0:T(8,128)(2,1)S(1)}, bf16[3,32,512]{2,1,0:T(8,128)(2,1)S(1)}, u32[]{:S(2)}, u32[]{:S(2)}) collective-permute-start(bf16[3,32,512]{2,1,0:T(8,128)(2,1)S(1)} %get-tuple-element.23), channel_id=1, source_target_pairs={{0,4},{4,0},{8,12},{12,8},{1,5},{5,1},{9,13},{13,9},{2,6},{6,2},{1... | collective-permute-start | bytes 294920 | tf_op jit(solution)/shard_map/ppermute | solution.py:86
  7.0 2.6 %collective-permute-start.26 = (bf16[3,32,512]{2,1,0:T(8,128)(2,1)S(1)}, bf16[3,32,512]{2,1,0:T(8,128)(2,1)S(1)}, u32[]{:S(2)}, u32[]{:S(2)}) collective-permute-start(bf16[3,32,512]{2,1,0:T(8,128)(2,1)S(1)} %get-tuple-element.22), channel_id=1, source_target_pairs={{0,8},{4,12},{8,0},{12,4},{1,9},{5,13},{9,1},{13,5},{2,10},{6,14},... | collective-permute-start | bytes 294920 | tf_op jit(solution)/shard_map/ppermute | solution.py:86
  11.6 6.2 %collective-permute-done.26.refs_4_ = bf16[3,32,512]{2,1,0:T(8,128)(2,1)S(1)} collective-permute-done((bf16[3,32,512]{2,1,0:T(8,128)(2,1)S(1)}, bf16[3,32,512]{2,1,0:T(8,128)(2,1)S(1)}, u32[]{:S(2)}, u32[]{:S(2)}) %collective-permute-start.26) | collective-permute-done | bytes 98336 | tf_op jit(solution)/shard_map/ppermute | solution.py:86
  19.8 7.4 %collective-permute-start.28 = (bf16[3,32,512]{2,1,0:T(8,128)(2,1)S(1)}, bf16[3,32,512]{2,1,0:T(8,128)(2,1)S(1)}, u32[]{:S(2)}, u32[]{:S(2)}) collective-permute-start(bf16[3,32,512]{2,1,0:T(8,128)(2,1)S(1)} %collective-permute-done.26.refs_4_), channel_id=1, source_target_pairs={{0,1},{1,0},{2,3},{3,2},{4,5},{5,4},{6,7},{7,6},{8,9},{9,8},{10,11... | collective-permute-start | bytes 294920 | tf_op jit(solution)/shard_map/ppermute | solution.py:86
  32.9 2.1 %shard_map.105 = (bf16[3,192,512]{2,1,0:T(8,128)(2,1)S(1)}, bf16[3,192,512]{2,1,0:T(8,128)(2,1)S(1)}) custom-call(s32[2]{0:T(128)S(1)} %pad_add_fusion.place_ref, s32[4]{0:T(128)S(1)} %copy-done.4, bf16[3,128,2048]{2,1,0:T(8,128)(2,1)S(1)} %copy-done, bf16[3,512,512]{2,1,0:T(8,128)(2,1)S(1)} %collective-permute-done.21.basis_ref, ...), custom_call_target="tpu_custom_call" | custom-call | flops 1207959552 | bytes 4718592 | tf_op jit(solution)/shard_map/pallas_call | solution.py:137
  36.9 13.8 %collective-permute-done.34 = bf16[3,192,512]{2,1,0:T(8,128)(2,1)S(1)} collective-permute-done((bf16[3,192,512]{2,1,0:T(8,128)(2,1)S(1)}, bf16[3,192,512]{2,1,0:T(8,128)(2,1)S(1)}, u32[]{:S(2)}, u32[]{:S(2)}) %collective-permute-start.34) | collective-permute-done | bytes 589856 | tf_op jit(solution)/shard_map/ppermute | solution.py:86
  52.6 4.8 %collective-permute-start.8 = (bf16[3,32,512]{2,1,0:T(8,128)(2,1)S(1)}, bf16[3,32,512]{2,1,0:T(8,128)(2,1)S(1)}, u32[]{:S(2)}, u32[]{:S(2)}) collective-permute-start(bf16[3,32,512]{2,1,0:T(8,128)(2,1)S(1)} %get-tuple-element.24), channel_id=1, source_target_pairs={{0,12},{4,8},{8,4},{12,0},{1,13},{5,9},{9,5},{13,1},{2,14},{6,10},... | collective-permute-start | bytes 294920 | tf_op jit(solution)/shard_map/ppermute | solution.py:86
  58.0 11.1 %collective-permute-done.8.refs_8_ = bf16[3,32,512]{2,1,0:T(8,128)(2,1)S(1)} collective-permute-done((bf16[3,32,512]{2,1,0:T(8,128)(2,1)S(1)}, bf16[3,32,512]{2,1,0:T(8,128)(2,1)S(1)}, u32[]{:S(2)}, u32[]{:S(2)}) %collective-permute-start.8) | collective-permute-done | bytes 98336 | tf_op jit(solution)/shard_map/ppermute | solution.py:86
  69.1 7.2 %collective-permute-done.35 = bf16[3,192,512]{2,1,0:T(8,128)(2,1)S(1)} collective-permute-done((bf16[3,192,512]{2,1,0:T(8,128)(2,1)S(1)}, bf16[3,192,512]{2,1,0:T(8,128)(2,1)S(1)}, u32[]{:S(2)}, u32[]{:S(2)}) %collective-permute-start.35) | collective-permute-done | bytes 589856 | tf_op jit(solution)/shard_map/ppermute | solution.py:92
  80.4 3.1 %collective-permute-done.1.refs_1_ = bf16[3,32,512]{2,1,0:T(8,128)(2,1)S(1)} collective-permute-done((bf16[3,32,512]{2,1,0:T(8,128)(2,1)S(1)}, bf16[3,32,512]{2,1,0:T(8,128)(2,1)S(1)}, u32[]{:S(2)}, u32[]{:S(2)}) %collective-permute-start.1) | collective-permute-done | bytes 98336 | tf_op jit(solution)/shard_map/ppermute | solution.py:86
  87.5 2.1 %shard_map.103 = (bf16[2,192,512]{2,1,0:T(8,128)(2,1)S(1)}, bf16[2,192,512]{2,1,0:T(8,128)(2,1)S(1)}, bf16[1,192,512]{2,1,0:T(8,128)(2,1)S(1)}, bf16[1,192,512]{2,1,0:T(8,128)(2,1)S(1)}) custom-call(s32[2]{0:T(128)S(1)} %pad_add_fusion.place_ref, s32[4]{0:T(128)S(1)} %copy-done.4, bf16[3,128,2048]{2,1,0:T(8,128)(2,1)S(1)} %copy-done.1, ...), custom_call_target="tpu_custom_call" | custom-call | flops 1207959552 | bytes 4718592 | tf_op jit(solution)/shard_map/pallas_call | solution.py:137
  91.6 2.1 %collective-permute-start.37 = (bf16[3,192,512]{2,1,0:T(8,128)(2,1)S(1)}, bf16[3,192,512]{2,1,0:T(8,128)(2,1)S(1)}, u32[]{:S(2)}, u32[]{:S(2)}) collective-permute-start(bf16[3,192,512]{2,1,0:T(8,128)(2,1)S(1)} %add_convert_fusion.refs_0_), channel_id=1, source_target_pairs={{0,2},{13,15},{10,8},{7,5},{16,18},{29,31},{26,24},{23,21}} | collective-permute-start | bytes 1769480 | tf_op jit(solution)/shard_map/ppermute | solution.py:92
  95.1 2.4 %collective-permute-done.15 = bf16[1,192,512]{2,1,0:T(8,128)(2,1)} collective-permute-done((bf16[1,192,512]{2,1,0:T(8,128)(2,1)S(1)}, bf16[1,192,512]{2,1,0:T(8,128)(2,1)}, u32[]{:S(2)}, u32[]{:S(2)}) %collective-permute-start.15) | collective-permute-done | bytes 196640 | tf_op jit(solution)/shard_map/ppermute | solution.py:86
  98.4 2.1 %collective-permute-start.16 = (bf16[1,192,512]{2,1,0:T(8,128)(2,1)S(1)}, bf16[1,192,512]{2,1,0:T(8,128)(2,1)S(1)}, u32[]{:S(2)}, u32[]{:S(2)}) collective-permute-start(bf16[1,192,512]{2,1,0:T(8,128)(2,1)S(1)} %add_convert_fusion.5), channel_id=1, source_target_pairs={{0,8},{4,12},{8,0},{12,4},{1,9},{5,13},{9,1},{13,5},{2,10},{6,14},... | collective-permute-start | bytes 589832 | tf_op jit(solution)/shard_map/ppermute | solution.py:86
  100.5 8.8 %collective-permute-done.12 = bf16[2,192,512]{2,1,0:T(8,128)(2,1)} collective-permute-done((bf16[2,192,512]{2,1,0:T(8,128)(2,1)S(1)}, bf16[2,192,512]{2,1,0:T(8,128)(2,1)}, u32[]{:S(2)}, u32[]{:S(2)}) %collective-permute-start.12) | collective-permute-done | bytes 393248 | tf_op jit(solution)/shard_map/ppermute | solution.py:86
  112.0 2.3 %collective-permute-start.39 = (bf16[3,192,512]{2,1,0:T(8,128)(2,1)}, bf16[3,192,512]{2,1,0:T(8,128)(2,1)}, u32[]{:S(2)}, u32[]{:S(2)}) collective-permute-start(bf16[3,192,512]{2,1,0:T(8,128)(2,1)} %broadcast_select_fusion.1), channel_id=1, source_target_pairs={{0,1},{2,3},{13,12},{15,14},{10,11},{8,9},{7,6},{5,4},{16,17},{18,... | collective-permute-start | bytes 1769480 | tf_op jit(solution)/shard_map/ppermute | solution.py:92
  115.2 2.1 %collective-permute-start.40 = (bf16[3,192,512]{2,1,0:T(8,128)(2,1)}, bf16[3,192,512]{2,1,0:T(8,128)(2,1)}, u32[]{:S(2)}, u32[]{:S(2)}) collective-permute-start(bf16[3,192,512]{2,1,0:T(8,128)(2,1)} %broadcast_select_fusion), channel_id=1, source_target_pairs={{0,1},{2,3},{13,12},{15,14},{10,11},{8,9},{7,6},{5,4},{16,17},{18,... | collective-permute-start | bytes 1769480 | tf_op jit(solution)/shard_map/ppermute | solution.py:92
  117.3 12.8 %collective-permute-done.13 = bf16[2,192,512]{2,1,0:T(8,128)(2,1)S(1)} collective-permute-done((bf16[2,192,512]{2,1,0:T(8,128)(2,1)S(1)}, bf16[2,192,512]{2,1,0:T(8,128)(2,1)S(1)}, u32[]{:S(2)}, u32[]{:S(2)}) %collective-permute-start.13) | collective-permute-done | bytes 393248 | tf_op jit(solution)/shard_map/ppermute | solution.py:86
  130.4 2.1 %collective-permute-start.17 = (bf16[1,192,512]{2,1,0:T(8,128)(2,1)S(1)}, bf16[1,192,512]{2,1,0:T(8,128)(2,1)S(1)}, u32[]{:S(2)}, u32[]{:S(2)}) collective-permute-start(bf16[1,192,512]{2,1,0:T(8,128)(2,1)S(1)} %add_convert_fusion.4.refs_2_.refs_10_), channel_id=1, source_target_pairs={{0,4},{4,0},{8,12},{12,8},{1,5},{5,1},{9,13},{13,9},{2,6},{6,2},{1... | collective-permute-start | bytes 589832 | tf_op jit(solution)/shard_map/ppermute | solution.py:86
  132.5 13.0 %collective-permute-done.17.refs_3_.refs_11_ = bf16[1,192,512]{2,1,0:T(8,128)(2,1)S(1)} collective-permute-done((bf16[1,192,512]{2,1,0:T(8,128)(2,1)S(1)}, bf16[1,192,512]{2,1,0:T(8,128)(2,1)S(1)}, u32[]{:S(2)}, u32[]{:S(2)}) %collective-permute-start.17) | collective-permute-done | bytes 196640 | tf_op jit(solution)/shard_map/ppermute | solution.py:86
  151.8 2.2 %collective-permute-start.43 = (f32[3,512]{1,0:T(4,128)S(1)}, f32[3,512]{1,0:T(4,128)S(1)}, u32[]{:S(2)}, u32[]{:S(2)}) collective-permute-start(f32[3,512]{1,0:T(4,128)S(1)} %get-tuple-element.18.refs_4_), channel_id=1, source_target_pairs={{0,12},{4,8},{8,4},{12,0},{1,13},{5,9},{9,5},{13,1},{2,14},{6,10},... | collective-permute-start | bytes 18440 | tf_op jit(solution)/shard_map/ppermute | solution.py:86
  154.4 2.8 %collective-permute-done.43.refs_7_ = f32[3,512]{1,0:T(4,128)S(1)} collective-permute-done((f32[3,512]{1,0:T(4,128)S(1)}, f32[3,512]{1,0:T(4,128)S(1)}, u32[]{:S(2)}, u32[]{:S(2)}) %collective-permute-start.43) | collective-permute-done | bytes 6176 | tf_op jit(solution)/shard_map/ppermute | solution.py:86
  157.3 4.2 %shard_map.107 = (bf16[3,512,512]{2,1,0:T(8,128)(2,1)}, f32[2,2048]{1,0:T(2,128)}, f32[2,2048]{1,0:T(2,128)}) custom-call(s32[2]{0:T(128)S(1)} %pad_add_fusion.place_ref, s32[4]{0:T(128)S(1)} %copy-done.5, s32[3]{0:T(128)S(1)} %copy-done.6, f32[7,2048]{1,0:T(8,128)} %shard_map.104.refs_0_, f32[7,2048]{1,0:T(8,128)} %collective-permute-done.18.refs_1_, ...), custom_call_target="tpu_custom_call" | custom-call | tf_op jit(solution)/shard_map/pallas_call | solution.py:287
  (96 shorter events, 38.1 us)
Async XLA Ops:
  0.6 30.2 %collective-permute-start.21 = (bf16[3,512,512]{2,1,0:T(8,128)(2,1)}, bf16[3,512,512]{2,1,0:T(8,128)(2,1)S(1)}, u32[]{:S(2)}, u32[]{:S(2)}) collective-permute-start(bf16[3,512,512]{2,1,0:T(8,128)(2,1)} %param.11), channel_id=1, source_target_pairs={{0,0},{1,3},{2,2},{3,1},{4,4},{5,7},{6,6},{7,5},{8,8},{9,11},{10,1... | collective-permute-start | bytes 4718600 | tf_op jit(solution)/shard_map/ppermute | solution.py:323
  7.0 10.8 %collective-permute-start.26 = (bf16[3,32,512]{2,1,0:T(8,128)(2,1)S(1)}, bf16[3,32,512]{2,1,0:T(8,128)(2,1)S(1)}, u32[]{:S(2)}, u32[]{:S(2)}) collective-permute-start(bf16[3,32,512]{2,1,0:T(8,128)(2,1)S(1)} %get-tuple-element.22), channel_id=1, source_target_pairs={{0,8},{4,12},{8,0},{12,4},{1,9},{5,13},{9,1},{13,5},{2,10},{6,14},... | collective-permute-start | bytes 294920 | tf_op jit(solution)/shard_map/ppermute | solution.py:86
  9.6 9.5 %collective-permute-start.30 = (bf16[3,32,512]{2,1,0:T(8,128)(2,1)S(1)}, bf16[3,32,512]{2,1,0:T(8,128)(2,1)S(1)}, u32[]{:S(2)}, u32[]{:S(2)}) collective-permute-start(bf16[3,32,512]{2,1,0:T(8,128)(2,1)S(1)} %get-tuple-element.21), channel_id=1, source_target_pairs={{0,12},{4,8},{8,4},{12,0},{1,13},{5,9},{9,5},{13,1},{2,14},{6,10},... | collective-permute-start | bytes 294920 | tf_op jit(solution)/shard_map/ppermute | solution.py:86
  10.3 9.5 %collective-permute-start.23 = (bf16[3,32,512]{2,1,0:T(8,128)(2,1)S(1)}, bf16[3,32,512]{2,1,0:T(8,128)(2,1)S(1)}, u32[]{:S(2)}, u32[]{:S(2)}) collective-permute-start(bf16[3,32,512]{2,1,0:T(8,128)(2,1)S(1)} %collective-permute-done.22.refs_0_), channel_id=1, source_target_pairs={{0,2},{1,3},{2,0},{3,1},{4,6},{5,7},{6,4},{7,5},{8,10},{9,11},{10,... | collective-permute-start | bytes 294920 | tf_op jit(solution)/shard_map/ppermute | solution.py:86
  17.8 9.4 %collective-permute-start.27 = (bf16[3,32,512]{2,1,0:T(8,128)(2,1)S(1)}, bf16[3,32,512]{2,1,0:T(8,128)(2,1)S(1)}, u32[]{:S(2)}, u32[]{:S(2)}) collective-permute-start(bf16[3,32,512]{2,1,0:T(8,128)(2,1)S(1)} %collective-permute-done.26.refs_4_), channel_id=1, source_target_pairs={{0,2},{1,3},{2,0},{3,1},{4,6},{5,7},{6,4},{7,5},{8,10},{9,11},{10,... | collective-permute-start | bytes 294920 | tf_op jit(solution)/shard_map/ppermute | solution.py:86
  19.1 9.2 %collective-permute-start.31 = (bf16[3,32,512]{2,1,0:T(8,128)(2,1)S(1)}, bf16[3,32,512]{2,1,0:T(8,128)(2,1)S(1)}, u32[]{:S(2)}, u32[]{:S(2)}) collective-permute-start(bf16[3,32,512]{2,1,0:T(8,128)(2,1)S(1)} %collective-permute-done.30.refs_8_), channel_id=1, source_target_pairs={{0,2},{1,3},{2,0},{3,1},{4,6},{5,7},{6,4},{7,5},{8,10},{9,11},{10,... | collective-permute-start | bytes 294920 | tf_op jit(solution)/shard_map/ppermute | solution.py:86
  19.8 9.5 %collective-permute-start.24 = (bf16[3,32,512]{2,1,0:T(8,128)(2,1)S(1)}, bf16[3,32,512]{2,1,0:T(8,128)(2,1)S(1)}, u32[]{:S(2)}, u32[]{:S(2)}) collective-permute-start(bf16[3,32,512]{2,1,0:T(8,128)(2,1)S(1)} %collective-permute-done.22.refs_0_), channel_id=1, source_target_pairs={{0,1},{1,0},{2,3},{3,2},{4,5},{5,4},{6,7},{7,6},{8,9},{9,8},{10,11... | collective-permute-start | bytes 294920 | tf_op jit(solution)/shard_map/ppermute | solution.py:86
  19.8 9.5 %collective-permute-start.28 = (bf16[3,32,512]{2,1,0:T(8,128)(2,1)S(1)}, bf16[3,32,512]{2,1,0:T(8,128)(2,1)S(1)}, u32[]{:S(2)}, u32[]{:S(2)}) collective-permute-start(bf16[3,32,512]{2,1,0:T(8,128)(2,1)S(1)} %collective-permute-done.26.refs_4_), channel_id=1, source_target_pairs={{0,1},{1,0},{2,3},{3,2},{4,5},{5,4},{6,7},{7,6},{8,9},{9,8},{10,11... | collective-permute-start | bytes 294920 | tf_op jit(solution)/shard_map/ppermute | solution.py:86
  35.0 15.7 %collective-permute-start.34 = (bf16[3,192,512]{2,1,0:T(8,128)(2,1)S(1)}, bf16[3,192,512]{2,1,0:T(8,128)(2,1)S(1)}, u32[]{:S(2)}, u32[]{:S(2)}) collective-permute-start(bf16[3,192,512]{2,1,0:T(8,128)(2,1)S(1)} %get-tuple-element.17), channel_id=1, source_target_pairs={{0,4},{4,0},{8,12},{12,8},{1,5},{5,1},{9,13},{13,9},{2,6},{6,2},{1... | collective-permute-start | bytes 1769480 | tf_op jit(solution)/shard_map/ppermute | solution.py:86
  50.9 25.4 %collective-permute-start.35 = (bf16[3,192,512]{2,1,0:T(8,128)(2,1)S(1)}, bf16[3,192,512]{2,1,0:T(8,128)(2,1)S(1)}, u32[]{:S(2)}, u32[]{:S(2)}) collective-permute-start(bf16[3,192,512]{2,1,0:T(8,128)(2,1)S(1)} %add_convert_fusion.1), channel_id=1, source_target_pairs={{1,9},{2,10},{5,13},{6,14},{8,0},{11,3},{12,4},{15,7},{17,25},{18,... | collective-permute-start | bytes 1769480 | tf_op jit(solution)/shard_map/ppermute | solution.py:92
  52.6 16.6 %collective-permute-start.8 = (bf16[3,32,512]{2,1,0:T(8,128)(2,1)S(1)}, bf16[3,32,512]{2,1,0:T(8,128)(2,1)S(1)}, u32[]{:S(2)}, u32[]{:S(2)}) collective-permute-start(bf16[3,32,512]{2,1,0:T(8,128)(2,1)S(1)} %get-tuple-element.24), channel_id=1, source_target_pairs={{0,12},{4,8},{8,4},{12,0},{1,13},{5,9},{9,5},{13,1},{2,14},{6,10},... | collective-permute-start | bytes 294920 | tf_op jit(solution)/shard_map/ppermute | solution.py:86
  57.4 20.4 %collective-permute-start = (bf16[3,32,512]{2,1,0:T(8,128)(2,1)S(1)}, bf16[3,32,512]{2,1,0:T(8,128)(2,1)S(1)}, u32[]{:S(2)}, u32[]{:S(2)}) collective-permute-start(bf16[3,32,512]{2,1,0:T(8,128)(2,1)S(1)} %get-tuple-element.26), channel_id=1, source_target_pairs={{0,4},{4,0},{8,12},{12,8},{1,5},{5,1},{9,13},{13,9},{2,6},{6,2},{1... | collective-permute-start | bytes 294920 | tf_op jit(solution)/shard_map/ppermute | solution.py:86
  57.4 21.1 %collective-permute-start.4 = (bf16[3,32,512]{2,1,0:T(8,128)(2,1)S(1)}, bf16[3,32,512]{2,1,0:T(8,128)(2,1)S(1)}, u32[]{:S(2)}, u32[]{:S(2)}) collective-permute-start(bf16[3,32,512]{2,1,0:T(8,128)(2,1)S(1)} %get-tuple-element.25), channel_id=1, source_target_pairs={{0,8},{4,12},{8,0},{12,4},{1,9},{5,13},{9,1},{13,5},{2,10},{6,14},... | collective-permute-start | bytes 294920 | tf_op jit(solution)/shard_map/ppermute | solution.py:86
  69.1 11.2 %collective-permute-start.9 = (bf16[3,32,512]{2,1,0:T(8,128)(2,1)S(1)}, bf16[3,32,512]{2,1,0:T(8,128)(2,1)S(1)}, u32[]{:S(2)}, u32[]{:S(2)}) collective-permute-start(bf16[3,32,512]{2,1,0:T(8,128)(2,1)S(1)} %collective-permute-done.8.refs_8_), channel_id=1, source_target_pairs={{0,2},{1,3},{2,0},{3,1},{4,6},{5,7},{6,4},{7,5},{8,10},{9,11},{10,... | collective-permute-start | bytes 294920 | tf_op jit(solution)/shard_map/ppermute | solution.py:86
  76.5 17.3 %collective-permute-start.36 = (bf16[3,192,512]{2,1,0:T(8,128)(2,1)S(1)}, bf16[3,192,512]{2,1,0:T(8,128)(2,1)S(1)}, u32[]{:S(2)}, u32[]{:S(2)}) collective-permute-start(bf16[3,192,512]{2,1,0:T(8,128)(2,1)S(1)} %add_convert_fusion.refs_0_), channel_id=1, source_target_pairs={{4,0},{9,13},{14,10},{3,7},{20,16},{25,29},{30,26},{19,23}} | collective-permute-start | bytes 1769480 | tf_op jit(solution)/shard_map/ppermute | solution.py:92
  90.5 18.8 %collective-permute-start.12 = (bf16[2,192,512]{2,1,0:T(8,128)(2,1)S(1)}, bf16[2,192,512]{2,1,0:T(8,128)(2,1)}, u32[]{:S(2)}, u32[]{:S(2)}) collective-permute-start(bf16[2,192,512]{2,1,0:T(8,128)(2,1)S(1)} %get-tuple-element.13), channel_id=1, source_target_pairs={{0,4},{4,0},{8,12},{12,8},{1,5},{5,1},{9,13},{13,9},{2,6},{6,2},{1... | collective-permute-start | bytes 1179656 | tf_op jit(solution)/shard_map/ppermute | solution.py:86
  91.6 19.5 %collective-permute-start.37 = (bf16[3,192,512]{2,1,0:T(8,128)(2,1)S(1)}, bf16[3,192,512]{2,1,0:T(8,128)(2,1)S(1)}, u32[]{:S(2)}, u32[]{:S(2)}) collective-permute-start(bf16[3,192,512]{2,1,0:T(8,128)(2,1)S(1)} %add_convert_fusion.refs_0_), channel_id=1, source_target_pairs={{0,2},{13,15},{10,8},{7,5},{16,18},{29,31},{26,24},{23,21}} | collective-permute-start | bytes 1769480 | tf_op jit(solution)/shard_map/ppermute | solution.py:92
  93.8 20.5 %collective-permute-start.38 = (bf16[3,192,512]{2,1,0:T(8,128)(2,1)S(1)}, bf16[3,192,512]{2,1,0:T(8,128)(2,1)S(1)}, u32[]{:S(2)}, u32[]{:S(2)}) collective-permute-start(bf16[3,192,512]{2,1,0:T(8,128)(2,1)S(1)} %collective-permute-done.36.refs_1_), channel_id=1, source_target_pairs={{0,2},{13,15},{10,8},{7,5},{16,18},{29,31},{26,24},{23,21}} | collective-permute-start | bytes 1769480 | tf_op jit(solution)/shard_map/ppermute | solution.py:92
  98.4 31.9 %collective-permute-start.16 = (bf16[1,192,512]{2,1,0:T(8,128)(2,1)S(1)}, bf16[1,192,512]{2,1,0:T(8,128)(2,1)S(1)}, u32[]{:S(2)}, u32[]{:S(2)}) collective-permute-start(bf16[1,192,512]{2,1,0:T(8,128)(2,1)S(1)} %add_convert_fusion.5), channel_id=1, source_target_pairs={{0,8},{4,12},{8,0},{12,4},{1,9},{5,13},{9,1},{13,5},{2,10},{6,14},... | collective-permute-start | bytes 589832 | tf_op jit(solution)/shard_map/ppermute | solution.py:86
  110.4 19.7 %collective-permute-start.13 = (bf16[2,192,512]{2,1,0:T(8,128)(2,1)S(1)}, bf16[2,192,512]{2,1,0:T(8,128)(2,1)S(1)}, u32[]{:S(2)}, u32[]{:S(2)}) collective-permute-start(bf16[2,192,512]{2,1,0:T(8,128)(2,1)S(1)} %add_convert_fusion.3), channel_id=1, source_target_pairs={{0,8},{4,12},{8,0},{12,4},{1,9},{5,13},{9,1},{13,5},{2,10},{6,14},... | collective-permute-start | bytes 1179656 | tf_op jit(solution)/shard_map/ppermute | solution.py:86
  112.0 36.1 %collective-permute-start.39 = (bf16[3,192,512]{2,1,0:T(8,128)(2,1)}, bf16[3,192,512]{2,1,0:T(8,128)(2,1)}, u32[]{:S(2)}, u32[]{:S(2)}) collective-permute-start(bf16[3,192,512]{2,1,0:T(8,128)(2,1)} %broadcast_select_fusion.1), channel_id=1, source_target_pairs={{0,1},{2,3},{13,12},{15,14},{10,11},{8,9},{7,6},{5,4},{16,17},{18,... | collective-permute-start | bytes 1769480 | tf_op jit(solution)/shard_map/ppermute | solution.py:92
  115.2 32.9 %collective-permute-start.40 = (bf16[3,192,512]{2,1,0:T(8,128)(2,1)}, bf16[3,192,512]{2,1,0:T(8,128)(2,1)}, u32[]{:S(2)}, u32[]{:S(2)}) collective-permute-start(bf16[3,192,512]{2,1,0:T(8,128)(2,1)} %broadcast_select_fusion), channel_id=1, source_target_pairs={{0,1},{2,3},{13,12},{15,14},{10,11},{8,9},{7,6},{5,4},{16,17},{18,... | collective-permute-start | bytes 1769480 | tf_op jit(solution)/shard_map/ppermute | solution.py:92
  130.2 15.3 %collective-permute-start.14 = (bf16[2,192,512]{2,1,0:T(8,128)(2,1)S(1)}, bf16[2,192,512]{2,1,0:T(8,128)(2,1)S(1)}, u32[]{:S(2)}, u32[]{:S(2)}) collective-permute-start(bf16[2,192,512]{2,1,0:T(8,128)(2,1)S(1)} %add_convert_fusion.2.refs_0_.refs_8_), channel_id=1, source_target_pairs={{0,4},{4,0},{8,12},{12,8},{1,5},{5,1},{9,13},{13,9},{2,6},{6,2},{1... | collective-permute-start | bytes 1179656 | tf_op jit(solution)/shard_map/ppermute | solution.py:86
  130.4 15.1 %collective-permute-start.17 = (bf16[1,192,512]{2,1,0:T(8,128)(2,1)S(1)}, bf16[1,192,512]{2,1,0:T(8,128)(2,1)S(1)}, u32[]{:S(2)}, u32[]{:S(2)}) collective-permute-start(bf16[1,192,512]{2,1,0:T(8,128)(2,1)S(1)} %add_convert_fusion.4.refs_2_.refs_10_), channel_id=1, source_target_pairs={{0,4},{4,0},{8,12},{12,8},{1,5},{5,1},{9,13},{13,9},{2,6},{6,2},{1... | collective-permute-start | bytes 589832 | tf_op jit(solution)/shard_map/ppermute | solution.py:86
  (28 other events, 229.7 us)

commit v4 on v3

--- a/solution.py
+++ b/solution.py
@@ -7,6 +7,9 @@
 
 decay_rate = 0.25
 damping_rate = 0.1
+vmem_spec = pl.BlockSpec(memory_space=pltpu.VMEM)
+scalar_spec = pl.BlockSpec(memory_space=pltpu.SMEM)
+light = pl.CostEstimate(flops=0, bytes_accessed=0, transcendentals=0)
 
 
 def spread(array, axis, root):
@@ -92,11 +95,7 @@
     return lax.ppermute(array, ("dp", "owner"), flat)
 
 
-def whole(*arrays):
-    return [pl.BlockSpec(a.shape, lambda i, *s, n=a.ndim: (0,) * n) for a in arrays]
-
-
-def project_rows(place, counts, tokens, pieces, basis, groups):
+def project_rows(scalars, tokens, pieces, basis):
     layers, tok_rows, _ = tokens.shape
     tile, cols = basis.shape[1:]
     n_dp = len(pieces) + 1
@@ -105,11 +104,25 @@
     packed = 3 * n_dp * tok_rows // 4
     half = packed // 2
     flat = [p for group in pieces for p in group]
-    shapes = [(len(group), half, cols) for group in groups for _ in range(2)]
-
-    def kernel(place_ref, counts_ref, tokens_ref, basis_ref, *refs):
-        piece_refs, out_refs = refs[: len(flat)], refs[len(flat) :]
-        dp, own = place_ref[0], place_ref[1]
+    shapes = [(layers, half, cols)] * 2
+
+    def kernel(scalar_ref, tokens_hbm, basis_hbm, *refs):
+        piece_refs, refs = refs[: len(flat)], refs[len(flat) :]
+        out_refs, (tokens_ref, basis_ref, sems) = refs[: len(shapes)], refs[len(shapes) :]
+        dp, own = scalar_ref[0], scalar_ref[1]
+        at = pl.ds(pl.multiple_of(dp * tile, tile), tile)
+        copies = []
+        for layer in range(layers):
+            copies.append(
+                [
+                    pltpu.make_async_copy(
+                        tokens_hbm.at[layer, :, at], tokens_ref.at[layer], sems.at[2 * layer]
+                    ),
+                    pltpu.make_async_copy(basis_hbm.at[layer], basis_ref.at[layer], sems.at[2 * layer + 1]),
+                ]
+            )
+            for copy in copies[-1]:
+                copy.start()
         row = lax.broadcasted_iota(jnp.int32, (packed, tok_rows), 0)
         row = jnp.where(dp % 2 == 0, row, jnp.where(row < half, row + half, row - half))
         col = lax.broadcasted_iota(jnp.int32, (packed, tok_rows), 1)
@@ -120,37 +133,104 @@
             shard = dp ^ mask
             start = jnp.int32(0)
             for other in range(n_dp):
-                start += jnp.where(other < shard, counts_ref[other], 0)
+                start += jnp.where(other < shard, scalar_ref[2 + other], 0)
             index = col if mask == 0 else shared
-            picks.append(((row == start + index) & (index < counts_ref[shard])).astype(jnp.bfloat16))
+            chosen = (row == start + index) & (index < scalar_ref[2 + shard])
+            picks.append(chosen.astype(jnp.bfloat16))
         select = jnp.concatenate(picks, axis=1)
-        for number, group in enumerate(groups):
-            for at, layer in enumerate(group):
-                rows = jnp.concatenate([tokens_ref[layer]] + [p[layer] for p in piece_refs], axis=0)
-                chosen = jnp.dot(select, rows, preferred_element_type=jnp.float32).astype(jnp.bfloat16)
-                result = jnp.dot(
-                    chosen, basis_ref[layer], preferred_element_type=jnp.float32
-                ).astype(jnp.bfloat16)
-                out_refs[2 * number][at] = result[:half]
-                out_refs[2 * number + 1][at] = result[half:]
+        for layer in range(layers):
+            copies[layer][0].wait()
+            rows = jnp.concatenate([tokens_ref[layer]] + [p[layer] for p in piece_refs], axis=0)
+            chosen = jnp.dot(select, rows, preferred_element_type=jnp.float32).astype(jnp.bfloat16)
+            copies[layer][1].wait()
+            result = jnp.dot(chosen, basis_ref[layer], preferred_element_type=jnp.float32).astype(
+                jnp.bfloat16
+            )
+            out_refs[0][layer] = result[:half]
+            out_refs[1][layer] = result[half:]
 
     return pl.pallas_call(
         kernel,
         out_shape=[jax.ShapeDtypeStruct(shape, jnp.bfloat16) for shape in shapes],
-        grid_spec=pltpu.PrefetchScalarGridSpec(
-            num_scalar_prefetch=2,
-            grid=(1,),
-            in_specs=[pl.BlockSpec((layers, tok_rows, tile), lambda i, place, n: (0, 0, place[0]))]
-            + whole(basis, *flat),
-            out_specs=[pl.BlockSpec(shape, lambda i, *s: (0, 0, 0)) for shape in shapes],
-        ),
-        compiler_params=pltpu.CompilerParams(vmem_limit_bytes=32 * 1024 * 1024),
-        cost_estimate=pl.CostEstimate(
-            flops=layers * 2 * packed * tile * (n_dp * tok_rows + cols),
-            bytes_accessed=2 * layers * tile * (n_dp * tok_rows + 2 * cols),
-            transcendentals=0,
-        ),
-    )(place, counts, tokens, basis, *flat)
+        in_specs=[scalar_spec] + [pl.BlockSpec(memory_space=pltpu.HBM)] * 2 + [vmem_spec] * len(flat),
+        out_specs=[vmem_spec] * len(shapes),
+        scratch_shapes=[
+            pltpu.VMEM((layers, tok_rows, tile), jnp.bfloat16),
+            pltpu.VMEM((layers, tile, cols), jnp.bfloat16),
+            pltpu.SemaphoreType.DMA((2 * layers,)),
+        ],
+        compiler_params=pltpu.CompilerParams(vmem_limit_bytes=16 * 1024 * 1024),
+        cost_estimate=light,
+    )(scalars, *[pltpu.with_memory_space_constraint(array, pltpu.HBM) for array in (tokens, basis)], *flat)
+
+
+def add(first, second):
+    def kernel(first_ref, second_ref, out_ref):
+        total = first_ref[...].astype(jnp.float32) + second_ref[...].astype(jnp.float32)
+        out_ref[...] = total.astype(out_ref.dtype)
+
+    return pl.pallas_call(
+        kernel,
+        out_shape=jax.ShapeDtypeStruct(first.shape, first.dtype),
+        in_specs=[vmem_spec] * 2,
+        out_specs=vmem_spec,
+        compiler_params=pltpu.CompilerParams(vmem_limit_bytes=8 * 1024 * 1024),
+        cost_estimate=light,
+    )(first, second)
+
+
+def cut_rows(arrays, tile, n_own, n_dp):
+    layers, tok_rows, _ = arrays[0].shape
+    part_rows = tok_rows // n_own
+    peers = n_dp - 1
+
+    def kernel(*refs):
+        in_refs, out_refs, sems = refs[: len(arrays)], refs[len(arrays) : -1], refs[-1]
+        dp, own = lax.axis_index("dp"), lax.axis_index("owner")
+        rows = pl.ds(pl.multiple_of(own * part_rows, part_rows), part_rows)
+        copies = []
+        for number, out_ref in enumerate(out_refs):
+            block = dp ^ (number % peers + 1)
+            cols = pl.ds(pl.multiple_of(block * tile, tile), tile)
+            copies.append(
+                pltpu.make_async_copy(in_refs[number // peers].at[:, rows, cols], out_ref, sems.at[number])
+            )
+            copies[-1].start()
+        for copy in copies:
+            copy.wait()
+
+    count = len(arrays) * peers
+    return pl.pallas_call(
+        kernel,
+        out_shape=[jax.ShapeDtypeStruct((layers, part_rows, tile), arrays[0].dtype)] * count,
+        in_specs=[pl.BlockSpec(memory_space=pltpu.HBM)] * len(arrays),
+        out_specs=[vmem_spec] * count,
+        scratch_shapes=[pltpu.SemaphoreType.DMA((count,))],
+        compiler_params=pltpu.CompilerParams(vmem_limit_bytes=8 * 1024 * 1024),
+        cost_estimate=light,
+    )(*[pltpu.with_memory_space_constraint(array, pltpu.HBM) for array in arrays])
+
+
+def pick(home, choices):
+    flat = [array for arrays in choices for array in arrays]
+    count = len(choices[0])
+
+    def kernel(home_ref, *refs):
+        for number, out_ref in enumerate(refs[len(flat) :]):
+            for index in range(count):
+
+                @pl.when(home_ref[0] == index)
+                def _(number=number, index=index, out_ref=out_ref):
+                    out_ref[...] = refs[number * count + index][...]
+
+    return pl.pallas_call(
+        kernel,
+        out_shape=[jax.ShapeDtypeStruct(arrays[0].shape, arrays[0].dtype) for arrays in choices],
+        in_specs=[scalar_spec] + [vmem_spec] * len(flat),
+        out_specs=[vmem_spec] * len(choices),
+        compiler_params=pltpu.CompilerParams(vmem_limit_bytes=8 * 1024 * 1024),
+        cost_estimate=light,
+    )(home, *flat)
 
 
 def column_squares(ref, other_ref, layer):
@@ -162,27 +242,28 @@
 def settle_acts(state_act, state_grad, panels):
     slot_count, width = state_act.shape
     cols = panels[0].shape[2]
-    layers = sum(panel.shape[0] for panel in panels[::2])
+    layers = panels[0].shape[0]
 
     def kernel(state_act_ref, state_grad_ref, *refs):
         packet_ref = refs[-1]
         packet_ref[...] = jnp.zeros_like(packet_ref)
         packet_ref[:slot_count] = state_act_ref[...]
         packet_ref[slot_count : 2 * slot_count] = state_grad_ref[...]
-        layer = 2 * slot_count
-        for near_ref, far_ref in zip(refs[:-1:2], refs[1:-1:2], strict=True):
-            for at in range(near_ref.shape[0]):
-                packet_ref[layer : layer + 1, :cols] = column_squares(near_ref, far_ref, at)
-                layer += 1
+        for layer in range(layers):
+            row = 2 * slot_count + layer
+            packet_ref[row : row + 1, :cols] = column_squares(refs[0], refs[1], layer)
 
     return pl.pallas_call(
         kernel,
         out_shape=jax.ShapeDtypeStruct((2 * slot_count + layers, width), jnp.float32),
-        compiler_params=pltpu.CompilerParams(vmem_limit_bytes=32 * 1024 * 1024),
+        in_specs=[vmem_spec] * (2 + len(panels)),
+        out_specs=vmem_spec,
+        compiler_params=pltpu.CompilerParams(vmem_limit_bytes=8 * 1024 * 1024),
+        cost_estimate=light,
     )(state_act, state_grad, *panels)
 
 
-def settle_grads(place, home, arrivals):
+def settle_grads(home, arrivals):
     layers, half, cols = arrivals[0][0].shape
     flat = [array for pair in arrivals for array in pair]
 
@@ -204,32 +285,31 @@
     return pl.pallas_call(
         kernel,
         out_shape=out_shape,
-        grid_spec=pltpu.PrefetchScalarGridSpec(
-            num_scalar_prefetch=1, grid=(1,), in_specs=whole(*flat), out_specs=whole(*out_shape)
-        ),
-        compiler_params=pltpu.CompilerParams(vmem_limit_bytes=32 * 1024 * 1024),
+        in_specs=[scalar_spec] + [vmem_spec] * len(flat),
+        out_specs=[vmem_spec] * len(out_shape),
+        compiler_params=pltpu.CompilerParams(vmem_limit_bytes=8 * 1024 * 1024),
+        cost_estimate=light,
     )(home, *flat)
 
 
-def finish(place, counts, owner_of, packets, squares, acts, grads, slot_count):
-    layers = owner_of.shape[0]
+def finish(scalars, packets, squares, acts, grads, slot_count):
     n_own, n_dp = len(packets), len(squares)
-    tile = acts[0].shape[2]
+    layers, _, tile = acts[0].shape
     width = packets[0].shape[1]
-    where_act = [(2 * number, at) for number, a in enumerate(acts[::2]) for at in range(a.shape[0])]
     operands = [*packets, *squares, *acts, *grads]
 
-    def kernel(place_ref, counts_ref, owner_ref, *refs):
+    def kernel(scalar_ref, *refs):
         packet_refs, refs = refs[:n_own], refs[n_own:]
         square_refs, refs = refs[:n_dp], refs[n_dp:]
         act_refs, refs = refs[: len(acts)], refs[len(acts) :]
         grad_refs, refs = refs[:2], refs[2:]
         out_ref, new_act_ref, new_grad_ref, act_full, grad_full = refs
-        dp, own = place_ref[0], place_ref[1]
-        total = counts_ref[0]
-        for index in range(1, counts_ref.shape[0]):
-            total += counts_ref[index]
+        dp, own = scalar_ref[0], scalar_ref[1]
+        total = scalar_ref[2]
+        for index in range(1, n_dp):
+            total += scalar_ref[2 + index]
         total = total.astype(jnp.float32)
+        owners = [scalar_ref[2 + n_dp + layer] for layer in range(layers)]
         for mask in range(n_own):
             at = pl.ds(pl.multiple_of((own ^ mask) * tile, tile), tile)
             act_full[:, at] = packet_refs[mask][2 * slot_count :, :tile] / total
@@ -239,10 +319,10 @@
         new_act_ref[...] = packet_refs[0][:slot_count]
         new_grad_ref[...] = packet_refs[0][slot_count : 2 * slot_count]
         for layer in range(layers):
-            owner_now = owner_ref[layer]
+            owner_now = owners[layer]
             rank = jnp.int32(0)
             for earlier in range(layer):
-                rank += jnp.where(owner_ref[earlier] == owner_now, 1, 0)
+                rank += jnp.where(owners[earlier] == owner_now, 1, 0)
             old_act = jnp.zeros((1, width), jnp.float32)
             old_grad = jnp.zeros((1, width), jnp.float32)
             for mask in range(n_own):
@@ -267,11 +347,10 @@
             cols = act_full[layer : layer + 1, pl.ds(pl.multiple_of(own * tile, tile), tile)]
             rows = jnp.transpose(jnp.broadcast_to(rows, (128, tile)))
             rows = jnp.concatenate([rows] * (tile // 128), axis=1)
-            number, at = where_act[layer]
             gram = sum(
                 lax.dot_general(
                     grad_refs[side][layer],
-                    act_refs[number + side][at],
+                    act_refs[side][layer],
                     (((0,), (0,)), ((), ())),
                     preferred_element_type=jnp.float32,
                 )
@@ -287,15 +366,12 @@
     return pl.pallas_call(
         kernel,
         out_shape=out_shape,
-        grid_spec=pltpu.PrefetchScalarGridSpec(
-            num_scalar_prefetch=3,
-            grid=(1,),
-            in_specs=whole(*operands),
-            out_specs=whole(*out_shape),
-            scratch_shapes=[pltpu.VMEM((layers, width), jnp.float32)] * 2,
-        ),
-        compiler_params=pltpu.CompilerParams(vmem_limit_bytes=32 * 1024 * 1024),
-    )(place, counts, owner_of, *operands)
+        in_specs=[scalar_spec] + [vmem_spec] * len(operands),
+        out_specs=[vmem_spec] * len(out_shape),
+        scratch_shapes=[pltpu.VMEM((layers, width), jnp.float32)] * 2,
+        compiler_params=pltpu.CompilerParams(vmem_limit_bytes=16 * 1024 * 1024),
+        cost_estimate=light,
+    )(scalars, *operands)
 
 
 def line_plan(activations, out_grads, basis_act, basis_grad, owner_of, counts, state_act, state_grad):
@@ -303,56 +379,76 @@
     tile = basis_act.shape[1]
     n_dp = lax.axis_size("dp")
     n_own = lax.axis_size("owner")
-    part_rows = tok_rows // n_own
     dp = lax.axis_index("dp")
     own = lax.axis_index("owner")
-    place = jnp.stack([dp, own]).astype(jnp.int32)
-
-    def pieces_of(tokens):
-        part = lax.dynamic_slice_in_dim(tokens, own * part_rows, part_rows, 1)
-        groups = []
-        for mask in range(1, n_dp):
-            got = flip(lax.dynamic_slice_in_dim(part, (dp ^ mask) * tile, tile, 2), "dp", mask)
-            chip = flip(got, "owner", 2)
-            groups.append([got, chip, flip(got, "owner", 1), flip(chip, "owner", 1)])
-        return groups
-
-    def add(first, second):
-        return (first.astype(jnp.float32) + second.astype(jnp.float32)).astype(jnp.bfloat16)
-
-    swapped = lax.ppermute(basis_grad, "owner", [(o, -o % n_own) for o in range(n_own)])
-    held = [-o % n_own for o in range(n_own)]
-
-    pieces_act = pieces_of(activations)
-    pieces_grad = pieces_of(out_grads)
-    early = [[*range(layers - 1)], [layers - 1]]
-    parts_act = project_rows(place, counts, activations, pieces_act, basis_act, early)
-    keep, send = project_rows(place, counts, out_grads, pieces_grad, swapped, [[*range(layers)]])
-
-    def total_of(keep, send):
-        part = add(keep, flip(send, "dp", 1))
-        part = add(part, flip(part, "dp", 2))
-        return [part, flip(part, "dp", 1)]
-
-    first = total_of(*parts_act[:2])
-
-    part = add(keep, flip(send, "dp", 1))
-    pairs = [((a, o), (a ^ 2, o)) for a in range(n_dp) for o in range(n_own) if (a ^ held[o]) & 2]
-    near = add(part, hop(part, pairs))
-    far = hop(near, [((held[o] ^ 1, o), (held[o], o)) for o in range(n_own)])
-    arrivals = [(near, far)]
-    arrivals.append([hop(a, [((held[o], o), (held[o], o ^ 2)) for o in range(n_own)]) for a in (near, far)])
-    source = -dp % n_own
-    pairs = [((held[o], o ^ b), (held[o], o ^ b ^ 1)) for o in range(n_own) for b in (0, 2)]
-    arrivals.append([hop(jnp.where(own == source, a, b), pairs) for a, b in zip(*arrivals, strict=True)])
-    home = jnp.where(own == source, 0, jnp.where(own == source ^ 2, 1, 2)).astype(jnp.int32)[None]
-    *grads, squares = settle_grads(place, home, arrivals)
+    scalars = jnp.concatenate([jnp.stack([dp, own]), counts, owner_of]).astype(jnp.int32)
+
+    def after(array, *others):
+        return lax.optimization_barrier((array, *others))[0]
+
+    def step(arrays, *others):
+        return lax.optimization_barrier((*arrays, *others))[: len(arrays)]
+
+    def sent(cuts):
+        return [flip(cut, "dp", mask) for mask, cut in enumerate(cuts, 1)]
+
+    def pieces_of(gots, chips):
+        return [
+            [got, chip, flip(got, "owner", 1), flip(chip, "owner", 1)]
+            for got, chip in zip(gots, chips, strict=True)
+        ]
+
+    cuts = cut_rows((out_grads, activations), tile, n_own, n_dp)
+    got_grad = sent(cuts[: n_dp - 1])
+    chips_grad = [flip(got, "owner", 2) for got in got_grad]
+    got_act = sent(after(cut, *got_grad) for cut in cuts[n_dp - 1 :])
+    pieces_grad = pieces_of(got_grad, chips_grad)
+    pieces_grad[0][0] = after(pieces_grad[0][0], *got_act)
+    keep, send = project_rows(scalars, out_grads, pieces_grad, basis_grad)
+
+    owners = range(n_own)
+    to_home = [((o ^ 1, o), (o, o)) for o in owners]
+    swaps = [((a, o), (a ^ 1, o)) for a in range(n_dp) for o in owners if (a ^ o) & 2]
+    near = hop(send, to_home + swaps)
+    far = hop(keep, to_home)
+    chips_act = [flip(after(got, keep), "owner", 2) for got in got_act]
+    keep, send, near, far, *chips_act = step([keep, send, near, far, *chips_act])
+    part = add(keep, near)
+    rest = add(send, far)
+    pieces_act = pieces_of(got_act, chips_act)
+    pieces_act[0][0] = after(pieces_act[0][0], part, rest)
+    keep_act, send_act = project_rows(scalars, activations, pieces_act, basis_act)
+    near = hop(part, [((o ^ 2, o), (o, o)) for o in owners])
+    far = hop(part, [((o ^ 3, o), (o, o)) for o in owners])
+    near_act = flip(send_act, "dp", 1)
+
+    part, rest, near, far, keep_act, near_act = step([part, rest, near, far, keep_act, near_act])
+    part_act = add(keep_act, near_act)
+    cross_act = flip(part_act, "dp", 2)
+    part = add(part, near)
+    rest = add(rest, far)
+    to_chip = [((o, o), (o, o ^ 2)) for o in owners]
+    part_chip = hop(part, to_chip)
+    rest_chip = hop(rest, to_chip)
+
+    part_act, cross_act, part, rest, part_chip, rest_chip = step(
+        [part_act, cross_act, part, rest, part_chip, rest_chip]
+    )
+    full_act = add(part_act, cross_act)
+    back_act = flip(full_act, "dp", 1)
+    to_core = [((o, o ^ b), (o, o ^ b ^ 1)) for o in owners for b in (0, 2)]
+    home = jnp.where(own == dp, 0, jnp.where(own == dp ^ 2, 1, 2)).astype(jnp.int32)[None]
+    part_half, rest_half = pick(home, [(part, part_chip), (rest, rest_chip)])
+    part_core = hop(part_half, to_core)
+    rest_core = hop(rest_half, to_core)
+    *grads, squares = settle_grads(home // 2, [(part_half, rest_half), (part_core, rest_core)])
     squares = [squares] + [flip(squares, "dp", mask) for mask in range(1, n_dp)]
 
-    acts = first + total_of(*parts_act[2:])
+    full_act, back_act, *squares = step([full_act, back_act, *squares])
+    acts = [full_act, back_act]
     packet = settle_acts(state_act, state_grad, acts)
     packets = [packet] + [flip(packet, "owner", mask) for mask in range(1, n_own)]
-    return tuple(finish(place, counts, owner_of, packets, squares, acts, grads, state_act.shape[0]))
+    return tuple(finish(scalars, packets, squares, acts, grads, state_act.shape[0]))
 
 
 def solution(mesh):

time: 162 us -> 142 us (0.88)
  starting transfers between devices: 55 us -> 38.7 us
  other arithmetic: 4.35 us -> 0.08 us
  local copies, waits for them, and re-layouts: 3.55 us -> 0.02 us
  Pallas kernels: 10.5 us -> 13.1 us
  waiting for transfers between devices: 87.2 us -> 89 us
    ppermute x6 -> x8, waiting for transfers between devices: 7.21 us -> 41.9 us  [hop(): return lax.ppermute(array, ('dp', 'owner'), flat)]
    ppermute x37 -> x33, waiting for transfers between devices: 79.9 us -> 47 us  [flip(): lax.ppermute(array, axis, [(i, i ^ mask) for i in range(lax.axis_size(axi...]
    ppermute x37 -> x33, starting transfers between devices: 42.5 us -> 27.9 us  [flip(): lax.ppermute(array, axis, [(i, i ^ mask) for i in range(lax.axis_size(axi...]
    pallas_call x2, Pallas kernels: 4.14 us -> 7.47 us  [project_rows(): pl.pallas_call(kernel, out_shape=[jax.ShapeDtypeStruct(shape, jnp.bfloat1...]
    convert_element_type x6 -> x0, other arithmetic: 2.52 us -> none  [add(): (first.astype(jnp.float32) + second.astype(jnp.float32)).astype(jnp.bfloa...]
    unnamed x16 -> x8, local copies, waits for them, and re-layouts: 2.09 us -> 0.02 us
    ppermute x1 -> x0, starting transfers between devices: 2.07 us -> none  [line_plan(): lax.ppermute(basis_grad, 'owner', [(o, -o % n_own) for o in range(n_own)])]
    select_n x2 -> x0, other arithmetic: 1.76 us -> none  [line_plan(): jnp.where(own == source, a, b)]
  transfers between devices with their start and end apart: 44 -> 41, of which waited for: 20 -> 22; matrix products, arithmetic and copies ran while one was open for 4% -> 0% of each run, Pallas kernels for 3% -> 3%
where the time goes in v4:
time: 142 us
  waiting for transfers between devices  89 us (63%)
  starting transfers between devices  38.7 us (27%)
  Pallas kernels  13.1 us (9%)
    ppermute x33, waiting for transfers between devices, flip(): lax.ppermute(array, axis, [(i, i ^ mask) for i in range(lax.axis_size(axi...  47 us
    ppermute x8, waiting for transfers between devices, hop(): return lax.ppermute(array, ('dp', 'owner'), flat)  41.9 us
    ppermute x33, starting transfers between devices, flip(): lax.ppermute(array, axis, [(i, i ^ mask) for i in range(lax.axis_size(axi...  27.9 us
    ppermute x8, starting transfers between devices, hop(): return lax.ppermute(array, ('dp', 'owner'), flat)  10.8 us
    pallas_call x2, Pallas kernels, project_rows(): pl.pallas_call(kernel, out_shape=[jax.ShapeDtypeStruct(shape, jnp.bfloat1...  7.47 us
    pallas_call x1, Pallas kernels, finish(): pl.pallas_call(kernel, out_shape=out_shape, in_specs=[scalar_spec] + [vme...  3.23 us
  transfers between devices with their start and end apart: 41, of which 22 were waited for; matrix products, arithmetic and copies ran while one was open for 0% of the time, Pallas kernels for 3%

profile of v4, /device:TPU:0, one launch (start us, length us, event | category | flops | bytes accessed | tf_op | source)
XLA Modules:
  0.0 141.8 jit_solution(1962763484904929393)
XLA Ops:
  1.9 3.1 %collective-permute-start = (bf16[3,32,512]{2,1,0:T(8,128)(2,1)S(1)}, bf16[3,32,512]{2,1,0:T(8,128)(2,1)S(1)}, u32[]{:S(2)}, u32[]{:S(2)}) collective-permute-start(bf16[3,32,512]{2,1,0:T(8,128)(2,1)S(1)} %get-tuple-element.51), channel_id=1, source_target_pairs={{0,4},{4,0},{8,12},{12,8},{1,5},{5,1},{9,13},{13,9},{2,6},{6,2},{1... | collective-permute-start | bytes 294920 | tf_op jit(solution)/shard_map/ppermute | solution.py:89
  5.0 2.6 %collective-permute-start.1 = (bf16[3,32,512]{2,1,0:T(8,128)(2,1)S(1)}, bf16[3,32,512]{2,1,0:T(8,128)(2,1)S(1)}, u32[]{:S(2)}, u32[]{:S(2)}) collective-permute-start(bf16[3,32,512]{2,1,0:T(8,128)(2,1)S(1)} %get-tuple-element.53), channel_id=1, source_target_pairs={{0,8},{4,12},{8,0},{12,4},{1,9},{5,13},{9,1},{13,5},{2,10},{6,14},... | collective-permute-start | bytes 294920 | tf_op jit(solution)/shard_map/ppermute | solution.py:89
  7.8 1.7 %collective-permute-start.6 = (bf16[3,32,512]{2,1,0:T(8,128)(2,1)S(1)}, bf16[3,32,512]{2,1,0:T(8,128)(2,1)S(1)}, u32[]{:S(2)}, u32[]{:S(2)}) collective-permute-start(bf16[3,32,512]{2,1,0:T(8,128)(2,1)S(1)} %collective-permute-done.refs_0_), channel_id=1, source_target_pairs={{0,2},{1,3},{2,0},{3,1},{4,6},{5,7},{6,4},{7,5},{8,10},{9,11},{10,... | collective-permute-start | bytes 294920 | tf_op jit(solution)/shard_map/ppermute | solution.py:89
  9.5 5.9 %collective-permute-done.1.refs_4_ = bf16[3,32,512]{2,1,0:T(8,128)(2,1)S(1)} collective-permute-done((bf16[3,32,512]{2,1,0:T(8,128)(2,1)S(1)}, bf16[3,32,512]{2,1,0:T(8,128)(2,1)S(1)}, u32[]{:S(2)}, u32[]{:S(2)}) %collective-permute-start.1) | collective-permute-done | bytes 98336 | tf_op jit(solution)/shard_map/ppermute | solution.py:89
  15.4 1.5 %collective-permute-start.9 = (bf16[3,32,512]{2,1,0:T(8,128)(2,1)S(1)}, bf16[3,32,512]{2,1,0:T(8,128)(2,1)S(1)}, u32[]{:S(2)}, u32[]{:S(2)}) collective-permute-start(bf16[3,32,512]{2,1,0:T(8,128)(2,1)S(1)} %collective-permute-done.1.refs_4_), channel_id=1, source_target_pairs={{0,2},{1,3},{2,0},{3,1},{4,6},{5,7},{6,4},{7,5},{8,10},{9,11},{10,... | collective-permute-start | bytes 294920 | tf_op jit(solution)/shard_map/ppermute | solution.py:89
  16.9 1.6 %collective-permute-start.3 = (bf16[3,32,512]{2,1,0:T(8,128)(2,1)S(1)}, bf16[3,32,512]{2,1,0:T(8,128)(2,1)S(1)}, u32[]{:S(2)}, u32[]{:S(2)}) collective-permute-start(bf16[3,32,512]{2,1,0:T(8,128)(2,1)S(1)} %get-tuple-element.55), channel_id=1, source_target_pairs={{0,4},{4,0},{8,12},{12,8},{1,5},{5,1},{9,13},{13,9},{2,6},{6,2},{1... | collective-permute-start | bytes 294920 | tf_op jit(solution)/shard_map/ppermute | solution.py:89
  18.5 1.4 %collective-permute-start.4 = (bf16[3,32,512]{2,1,0:T(8,128)(2,1)S(1)}, bf16[3,32,512]{2,1,0:T(8,128)(2,1)S(1)}, u32[]{:S(2)}, u32[]{:S(2)}) collective-permute-start(bf16[3,32,512]{2,1,0:T(8,128)(2,1)S(1)} %get-tuple-element.57), channel_id=1, source_target_pairs={{0,8},{4,12},{8,0},{12,4},{1,9},{5,13},{9,1},{13,5},{2,10},{6,14},... | collective-permute-start | bytes 294920 | tf_op jit(solution)/shard_map/ppermute | solution.py:89
  22.3 5.2 %collective-permute-done.4.refs_4_ = bf16[3,32,512]{2,1,0:T(8,128)(2,1)S(1)} collective-permute-done((bf16[3,32,512]{2,1,0:T(8,128)(2,1)S(1)}, bf16[3,32,512]{2,1,0:T(8,128)(2,1)S(1)}, u32[]{:S(2)}, u32[]{:S(2)}) %collective-permute-start.4) | collective-permute-done | bytes 98336 | tf_op jit(solution)/shard_map/ppermute | solution.py:89
  29.3 3.7 %shard_map.104 = (bf16[3,192,512]{2,1,0:T(8,128)(2,1)S(1)}, bf16[3,192,512]{2,1,0:T(8,128)(2,1)S(1)}) custom-call(s32[9]{0:T(128)S(1)} %pad_add_fusion.scalar_ref, bf16[3,128,2048]{2,1,0:T(8,128)(2,1)} %tokens_hbm.2, bf16[3,512,512]{2,1,0:T(8,128)(2,1)} %basis_hbm.2, bf16[3,32,512]{2,1,0:T(8,128)(2,1)S(1)} %collective-permute-done.refs_0_, ...), custom_call_target="tpu_custom_call" | custom-call | tf_op jit(solution)/shard_map/pallas_call | solution.py:152
  35.6 1.9 %collective-permute-start.17 = (bf16[3,32,512]{2,1,0:T(8,128)(2,1)S(1)}, bf16[3,32,512]{2,1,0:T(8,128)(2,1)S(1)}, u32[]{:S(2)}, u32[]{:S(2)}) collective-permute-start(bf16[3,32,512]{2,1,0:T(8,128)(2,1)S(1)} %collective-permute-done.3.refs_0_), channel_id=1, source_target_pairs={{0,2},{1,3},{2,0},{3,1},{4,6},{5,7},{6,4},{7,5},{8,10},{9,11},{10,... | collective-permute-start | bytes 294920 | tf_op jit(solution)/shard_map/ppermute | solution.py:89
  37.7 1.8 %collective-permute-start.19 = (bf16[3,32,512]{2,1,0:T(8,128)(2,1)S(1)}, bf16[3,32,512]{2,1,0:T(8,128)(2,1)S(1)}, u32[]{:S(2)}, u32[]{:S(2)}) collective-permute-start(bf16[3,32,512]{2,1,0:T(8,128)(2,1)S(1)} %collective-permute-done.5.refs_8_), channel_id=1, source_target_pairs={{0,2},{1,3},{2,0},{3,1},{4,6},{5,7},{6,4},{7,5},{8,10},{9,11},{10,... | collective-permute-start | bytes 294920 | tf_op jit(solution)/shard_map/ppermute | solution.py:89
  45.7 5.4 %collective-permute-done.16.second_ref = bf16[3,192,512]{2,1,0:T(8,128)(2,1)S(1)} collective-permute-done((bf16[3,192,512]{2,1,0:T(8,128)(2,1)S(1)}, bf16[3,192,512]{2,1,0:T(8,128)(2,1)S(1)}, u32[]{:S(2)}, u32[]{:S(2)}) %collective-permute-start.16) | collective-permute-done | bytes 589856 | tf_op jit(solution)/shard_map/ppermute | solution.py:95
  54.6 3.7 %shard_map.107 = (bf16[3,192,512]{2,1,0:T(8,128)(2,1)S(1)}, bf16[3,192,512]{2,1,0:T(8,128)(2,1)S(1)}) custom-call(s32[9]{0:T(128)S(1)} %pad_add_fusion.scalar_ref, bf16[3,128,2048]{2,1,0:T(8,128)(2,1)} %tokens_hbm.3, bf16[3,512,512]{2,1,0:T(8,128)(2,1)} %basis_hbm.3, bf16[3,32,512]{2,1,0:T(8,128)(2,1)S(1)} %collective-permute-done.3.refs_0_, ...), custom_call_target="tpu_custom_call" | custom-call | tf_op jit(solution)/shard_map/pallas_call | solution.py:152
  58.4 13.4 %collective-permute-done.21.second_ref = bf16[3,192,512]{2,1,0:T(8,128)(2,1)S(1)} collective-permute-done((bf16[3,192,512]{2,1,0:T(8,128)(2,1)S(1)}, bf16[3,192,512]{2,1,0:T(8,128)(2,1)S(1)}, u32[]{:S(2)}, u32[]{:S(2)}) %collective-permute-start.21) | collective-permute-done | bytes 589856 | tf_op jit(solution)/shard_map/ppermute | solution.py:95
  71.8 9.8 %collective-permute-done.20.second_ref = bf16[3,192,512]{2,1,0:T(8,128)(2,1)S(1)} collective-permute-done((bf16[3,192,512]{2,1,0:T(8,128)(2,1)S(1)}, bf16[3,192,512]{2,1,0:T(8,128)(2,1)S(1)}, u32[]{:S(2)}, u32[]{:S(2)}) %collective-permute-start.20) | collective-permute-done | bytes 589856 | tf_op jit(solution)/shard_map/ppermute | solution.py:95
  81.7 3.4 %collective-permute-done.28.second_ref = bf16[3,192,512]{2,1,0:T(8,128)(2,1)S(1)} collective-permute-done((bf16[3,192,512]{2,1,0:T(8,128)(2,1)S(1)}, bf16[3,192,512]{2,1,0:T(8,128)(2,1)S(1)}, u32[]{:S(2)}, u32[]{:S(2)}) %collective-permute-start.28) | collective-permute-done | bytes 589856 | tf_op jit(solution)/shard_map/ppermute | solution.py:89
  88.3 5.6 %collective-permute-done.31.refs_3_ = bf16[3,192,512]{2,1,0:T(8,128)(2,1)S(1)} collective-permute-done((bf16[3,192,512]{2,1,0:T(8,128)(2,1)S(1)}, bf16[3,192,512]{2,1,0:T(8,128)(2,1)S(1)}, u32[]{:S(2)}, u32[]{:S(2)}) %collective-permute-start.31) | collective-permute-done | bytes 589856 | tf_op jit(solution)/shard_map/ppermute | solution.py:95
  93.9 6.3 %collective-permute-done.30.refs_1_ = bf16[3,192,512]{2,1,0:T(8,128)(2,1)S(1)} collective-permute-done((bf16[3,192,512]{2,1,0:T(8,128)(2,1)S(1)}, bf16[3,192,512]{2,1,0:T(8,128)(2,1)S(1)}, u32[]{:S(2)}, u32[]{:S(2)}) %collective-permute-start.30) | collective-permute-done | bytes 589856 | tf_op jit(solution)/shard_map/ppermute | solution.py:95
  100.2 14.8 %collective-permute-done.29.second_ref = bf16[3,192,512]{2,1,0:T(8,128)(2,1)S(1)} collective-permute-done((bf16[3,192,512]{2,1,0:T(8,128)(2,1)S(1)}, bf16[3,192,512]{2,1,0:T(8,128)(2,1)S(1)}, u32[]{:S(2)}, u32[]{:S(2)}) %collective-permute-start.29) | collective-permute-done | bytes 589856 | tf_op jit(solution)/shard_map/ppermute | solution.py:89
  115.1 1.6 %collective-permute-start.33 = (bf16[3,192,512]{2,1,0:T(8,128)(2,1)S(1)}, bf16[3,192,512]{2,1,0:T(8,128)(2,1)S(1)}, u32[]{:S(2)}, u32[]{:S(2)}) collective-permute-start(bf16[3,192,512]{2,1,0:T(8,128)(2,1)S(1)} %get-tuple-element.88.refs_0_), channel_id=1, source_target_pairs={{0,1},{2,3},{5,4},{7,6},{10,11},{8,9},{15,14},{13,12},{16,17},{18,... | collective-permute-start | bytes 1769480 | tf_op jit(solution)/shard_map/ppermute | solution.py:95
  122.0 2.3 %collective-permute-start.35 = (f32[3,512]{1,0:T(4,128)S(1)}, f32[3,512]{1,0:T(4,128)S(1)}, u32[]{:S(2)}, u32[]{:S(2)}) collective-permute-start(f32[3,512]{1,0:T(4,128)S(1)} %get-tuple-element.93.refs_4_), channel_id=1, source_target_pairs={{0,4},{4,0},{8,12},{12,8},{1,5},{5,1},{9,13},{13,9},{2,6},{6,2},{1... | collective-permute-start | bytes 18440 | tf_op jit(solution)/shard_map/ppermute | solution.py:89
  124.2 8.9 %collective-permute-done.32.refs_1_.refs_9_ = bf16[3,192,512]{2,1,0:T(8,128)(2,1)S(1)} collective-permute-done((bf16[3,192,512]{2,1,0:T(8,128)(2,1)S(1)}, bf16[3,192,512]{2,1,0:T(8,128)(2,1)S(1)}, u32[]{:S(2)}, u32[]{:S(2)}) %collective-permute-start.32) | collective-permute-done | bytes 589856 | tf_op jit(solution)/shard_map/ppermute | solution.py:89
  135.4 2.3 %collective-permute-done.40.refs_3_ = f32[7,2048]{1,0:T(8,128)S(1)} collective-permute-done((f32[7,2048]{1,0:T(8,128)S(1)}, f32[7,2048]{1,0:T(8,128)S(1)}, u32[]{:S(2)}, u32[]{:S(2)}) %collective-permute-start.40) | collective-permute-done | bytes 57376 | tf_op jit(solution)/shard_map/ppermute | solution.py:89
  138.5 3.2 %shard_map.115 = (bf16[3,512,512]{2,1,0:T(8,128)(2,1)}, f32[2,2048]{1,0:T(2,128)}, f32[2,2048]{1,0:T(2,128)}) custom-call(s32[9]{0:T(128)S(1)} %pad_add_fusion.scalar_ref, f32[7,2048]{1,0:T(8,128)S(1)} %shard_map.114.refs_0_, f32[7,2048]{1,0:T(8,128)S(1)} %collective-permute-done.38.refs_1_, f32[7,2048]{1,0:T(8,128)S(1)} %collective-permute-done.39.refs_2_, ...), custom_call_target="tpu_custom_call" | custom-call | tf_op jit(solution)/shard_map/pallas_call | solution.py:366
  (80 shorter events, 29.6 us)
Async XLA Ops:
  5.0 10.4 %collective-permute-start.1 = (bf16[3,32,512]{2,1,0:T(8,128)(2,1)S(1)}, bf16[3,32,512]{2,1,0:T(8,128)(2,1)S(1)}, u32[]{:S(2)}, u32[]{:S(2)}) collective-permute-start(bf16[3,32,512]{2,1,0:T(8,128)(2,1)S(1)} %get-tuple-element.53), channel_id=1, source_target_pairs={{0,8},{4,12},{8,0},{12,4},{1,9},{5,13},{9,1},{13,5},{2,10},{6,14},... | collective-permute-start | bytes 294920 | tf_op jit(solution)/shard_map/ppermute | solution.py:89
  7.5 7.8 %collective-permute-start.2 = (bf16[3,32,512]{2,1,0:T(8,128)(2,1)S(1)}, bf16[3,32,512]{2,1,0:T(8,128)(2,1)S(1)}, u32[]{:S(2)}, u32[]{:S(2)}) collective-permute-start(bf16[3,32,512]{2,1,0:T(8,128)(2,1)S(1)} %get-tuple-element.54), channel_id=1, source_target_pairs={{0,12},{4,8},{8,4},{12,0},{1,13},{5,9},{9,5},{13,1},{2,14},{6,10},... | collective-permute-start | bytes 294920 | tf_op jit(solution)/shard_map/ppermute | solution.py:89
  7.7 12.2 %collective-permute-start.7 = (bf16[3,32,512]{2,1,0:T(8,128)(2,1)S(1)}, bf16[3,32,512]{2,1,0:T(8,128)(2,1)S(1)}, u32[]{:S(2)}, u32[]{:S(2)}) collective-permute-start(bf16[3,32,512]{2,1,0:T(8,128)(2,1)S(1)} %collective-permute-done.refs_0_), channel_id=1, source_target_pairs={{0,1},{1,0},{2,3},{3,2},{4,5},{5,4},{6,7},{7,6},{8,9},{9,8},{10,11... | collective-permute-start | bytes 294920 | tf_op jit(solution)/shard_map/ppermute | solution.py:89
  7.8 13.5 %collective-permute-start.6 = (bf16[3,32,512]{2,1,0:T(8,128)(2,1)S(1)}, bf16[3,32,512]{2,1,0:T(8,128)(2,1)S(1)}, u32[]{:S(2)}, u32[]{:S(2)}) collective-permute-start(bf16[3,32,512]{2,1,0:T(8,128)(2,1)S(1)} %collective-permute-done.refs_0_), channel_id=1, source_target_pairs={{0,2},{1,3},{2,0},{3,1},{4,6},{5,7},{6,4},{7,5},{8,10},{9,11},{10,... | collective-permute-start | bytes 294920 | tf_op jit(solution)/shard_map/ppermute | solution.py:89
  15.4 6.4 %collective-permute-start.9 = (bf16[3,32,512]{2,1,0:T(8,128)(2,1)S(1)}, bf16[3,32,512]{2,1,0:T(8,128)(2,1)S(1)}, u32[]{:S(2)}, u32[]{:S(2)}) collective-permute-start(bf16[3,32,512]{2,1,0:T(8,128)(2,1)S(1)} %collective-permute-done.1.refs_4_), channel_id=1, source_target_pairs={{0,2},{1,3},{2,0},{3,1},{4,6},{5,7},{6,4},{7,5},{8,10},{9,11},{10,... | collective-permute-start | bytes 294920 | tf_op jit(solution)/shard_map/ppermute | solution.py:89
  18.5 9.0 %collective-permute-start.4 = (bf16[3,32,512]{2,1,0:T(8,128)(2,1)S(1)}, bf16[3,32,512]{2,1,0:T(8,128)(2,1)S(1)}, u32[]{:S(2)}, u32[]{:S(2)}) collective-permute-start(bf16[3,32,512]{2,1,0:T(8,128)(2,1)S(1)} %get-tuple-element.57), channel_id=1, source_target_pairs={{0,8},{4,12},{8,0},{12,4},{1,9},{5,13},{9,1},{13,5},{2,10},{6,14},... | collective-permute-start | bytes 294920 | tf_op jit(solution)/shard_map/ppermute | solution.py:89
  19.9 7.6 %collective-permute-start.5 = (bf16[3,32,512]{2,1,0:T(8,128)(2,1)S(1)}, bf16[3,32,512]{2,1,0:T(8,128)(2,1)S(1)}, u32[]{:S(2)}, u32[]{:S(2)}) collective-permute-start(bf16[3,32,512]{2,1,0:T(8,128)(2,1)S(1)} %get-tuple-element.59), channel_id=1, source_target_pairs={{0,12},{4,8},{8,4},{12,0},{1,13},{5,9},{9,5},{13,1},{2,14},{6,10},... | collective-permute-start | bytes 294920 | tf_op jit(solution)/shard_map/ppermute | solution.py:89
  21.3 6.7 %collective-permute-start.12 = (bf16[3,32,512]{2,1,0:T(8,128)(2,1)S(1)}, bf16[3,32,512]{2,1,0:T(8,128)(2,1)S(1)}, u32[]{:S(2)}, u32[]{:S(2)}) collective-permute-start(bf16[3,32,512]{2,1,0:T(8,128)(2,1)S(1)} %collective-permute-done.2.refs_8_), channel_id=1, source_target_pairs={{0,2},{1,3},{2,0},{3,1},{4,6},{5,7},{6,4},{7,5},{8,10},{9,11},{10,... | collective-permute-start | bytes 294920 | tf_op jit(solution)/shard_map/ppermute | solution.py:89
  33.0 12.7 %collective-permute-start.15 = (bf16[3,192,512]{2,1,0:T(8,128)(2,1)S(1)}, bf16[3,192,512]{2,1,0:T(8,128)(2,1)S(1)}, u32[]{:S(2)}, u32[]{:S(2)}) collective-permute-start(bf16[3,192,512]{2,1,0:T(8,128)(2,1)S(1)} %get-tuple-element.68.first_ref), channel_id=1, source_target_pairs={{4,0},{1,5},{14,10},{11,15},{2,6},{3,7},{6,2},{7,3},{8,12},{9,13},... | collective-permute-start | bytes 1769480 | tf_op jit(solution)/shard_map/ppermute | solution.py:95
  34.4 16.8 %collective-permute-start.16 = (bf16[3,192,512]{2,1,0:T(8,128)(2,1)S(1)}, bf16[3,192,512]{2,1,0:T(8,128)(2,1)S(1)}, u32[]{:S(2)}, u32[]{:S(2)}) collective-permute-start(bf16[3,192,512]{2,1,0:T(8,128)(2,1)S(1)} %get-tuple-element.66.first_ref), channel_id=1, source_target_pairs={{4,0},{1,5},{14,10},{11,15},{20,16},{17,21},{30,26},{27,31}} | collective-permute-start | bytes 1769480 | tf_op jit(solution)/shard_map/ppermute | solution.py:95
  37.7 7.5 %collective-permute-start.19 = (bf16[3,32,512]{2,1,0:T(8,128)(2,1)S(1)}, bf16[3,32,512]{2,1,0:T(8,128)(2,1)S(1)}, u32[]{:S(2)}, u32[]{:S(2)}) collective-permute-start(bf16[3,32,512]{2,1,0:T(8,128)(2,1)S(1)} %collective-permute-done.5.refs_8_), channel_id=1, source_target_pairs={{0,2},{1,3},{2,0},{3,1},{4,6},{5,7},{6,4},{7,5},{8,10},{9,11},{10,... | collective-permute-start | bytes 294920 | tf_op jit(solution)/shard_map/ppermute | solution.py:89
  40.7 11.0 %collective-permute-start.22 = (bf16[3,32,512]{2,1,0:T(8,128)(2,1)S(1)}, bf16[3,32,512]{2,1,0:T(8,128)(2,1)S(1)}, u32[]{:S(2)}, u32[]{:S(2)}) collective-permute-start(bf16[3,32,512]{2,1,0:T(8,128)(2,1)S(1)} %collective-permute-done.3.refs_0_), channel_id=1, source_target_pairs={{0,1},{1,0},{2,3},{3,2},{4,5},{5,4},{6,7},{7,6},{8,9},{9,8},{10,11... | collective-permute-start | bytes 294920 | tf_op jit(solution)/shard_map/ppermute | solution.py:89
  43.2 8.8 %collective-permute-start.24 = (bf16[3,32,512]{2,1,0:T(8,128)(2,1)S(1)}, bf16[3,32,512]{2,1,0:T(8,128)(2,1)S(1)}, u32[]{:S(2)}, u32[]{:S(2)}) collective-permute-start(bf16[3,32,512]{2,1,0:T(8,128)(2,1)S(1)} %collective-permute-done.4.refs_4_), channel_id=1, source_target_pairs={{0,1},{1,0},{2,3},{3,2},{4,5},{5,4},{6,7},{7,6},{8,9},{9,8},{10,11... | collective-permute-start | bytes 294920 | tf_op jit(solution)/shard_map/ppermute | solution.py:89
  45.3 8.0 %collective-permute-start.26 = (bf16[3,32,512]{2,1,0:T(8,128)(2,1)S(1)}, bf16[3,32,512]{2,1,0:T(8,128)(2,1)S(1)}, u32[]{:S(2)}, u32[]{:S(2)}) collective-permute-start(bf16[3,32,512]{2,1,0:T(8,128)(2,1)S(1)} %collective-permute-done.5.refs_8_), channel_id=1, source_target_pairs={{0,1},{1,0},{2,3},{3,2},{4,5},{5,4},{6,7},{7,6},{8,9},{9,8},{10,11... | collective-permute-start | bytes 294920 | tf_op jit(solution)/shard_map/ppermute | solution.py:89
  52.0 19.9 %collective-permute-start.21 = (bf16[3,192,512]{2,1,0:T(8,128)(2,1)S(1)}, bf16[3,192,512]{2,1,0:T(8,128)(2,1)S(1)}, u32[]{:S(2)}, u32[]{:S(2)}) collective-permute-start(bf16[3,192,512]{2,1,0:T(8,128)(2,1)S(1)} %shard_map.105.first_ref), channel_id=1, source_target_pairs={{12,0},{9,5},{6,10},{3,15},{28,16},{25,21},{22,26},{19,31}} | collective-permute-start | bytes 1769480 | tf_op jit(solution)/shard_map/ppermute | solution.py:95
  53.3 28.4 %collective-permute-start.20 = (bf16[3,192,512]{2,1,0:T(8,128)(2,1)S(1)}, bf16[3,192,512]{2,1,0:T(8,128)(2,1)S(1)}, u32[]{:S(2)}, u32[]{:S(2)}) collective-permute-start(bf16[3,192,512]{2,1,0:T(8,128)(2,1)S(1)} %shard_map.105.first_ref), channel_id=1, source_target_pairs={{8,0},{13,5},{2,10},{7,15},{24,16},{29,21},{18,26},{23,31}} | collective-permute-start | bytes 1769480 | tf_op jit(solution)/shard_map/ppermute | solution.py:95
  58.4 26.7 %collective-permute-start.28 = (bf16[3,192,512]{2,1,0:T(8,128)(2,1)S(1)}, bf16[3,192,512]{2,1,0:T(8,128)(2,1)S(1)}, u32[]{:S(2)}, u32[]{:S(2)}) collective-permute-start(bf16[3,192,512]{2,1,0:T(8,128)(2,1)S(1)} %get-tuple-element.75), channel_id=1, source_target_pairs={{0,4},{4,0},{8,12},{12,8},{1,5},{5,1},{9,13},{13,9},{2,6},{6,2},{1... | collective-permute-start | bytes 1769480 | tf_op jit(solution)/shard_map/ppermute | solution.py:89
  85.2 8.7 %collective-permute-start.31 = (bf16[3,192,512]{2,1,0:T(8,128)(2,1)S(1)}, bf16[3,192,512]{2,1,0:T(8,128)(2,1)S(1)}, u32[]{:S(2)}, u32[]{:S(2)}) collective-permute-start(bf16[3,192,512]{2,1,0:T(8,128)(2,1)S(1)} %shard_map.110.refs_2_), channel_id=1, source_target_pairs={{0,2},{5,7},{10,8},{15,13},{16,18},{21,23},{26,24},{31,29}} | collective-permute-start | bytes 1769480 | tf_op jit(solution)/shard_map/ppermute | solution.py:95
  86.7 13.5 %collective-permute-start.30 = (bf16[3,192,512]{2,1,0:T(8,128)(2,1)S(1)}, bf16[3,192,512]{2,1,0:T(8,128)(2,1)S(1)}, u32[]{:S(2)}, u32[]{:S(2)}) collective-permute-start(bf16[3,192,512]{2,1,0:T(8,128)(2,1)S(1)} %shard_map.109.refs_0_), channel_id=1, source_target_pairs={{0,2},{5,7},{10,8},{15,13},{16,18},{21,23},{26,24},{31,29}} | collective-permute-start | bytes 1769480 | tf_op jit(solution)/shard_map/ppermute | solution.py:95
  88.2 26.8 %collective-permute-start.29 = (bf16[3,192,512]{2,1,0:T(8,128)(2,1)S(1)}, bf16[3,192,512]{2,1,0:T(8,128)(2,1)S(1)}, u32[]{:S(2)}, u32[]{:S(2)}) collective-permute-start(bf16[3,192,512]{2,1,0:T(8,128)(2,1)S(1)} %shard_map.108.first_ref), channel_id=1, source_target_pairs={{0,8},{4,12},{8,0},{12,4},{1,9},{5,13},{9,1},{13,5},{2,10},{6,14},... | collective-permute-start | bytes 1769480 | tf_op jit(solution)/shard_map/ppermute | solution.py:89
  118.2 15.0 %collective-permute-start.32 = (bf16[3,192,512]{2,1,0:T(8,128)(2,1)S(1)}, bf16[3,192,512]{2,1,0:T(8,128)(2,1)S(1)}, u32[]{:S(2)}, u32[]{:S(2)}) collective-permute-start(bf16[3,192,512]{2,1,0:T(8,128)(2,1)S(1)} %shard_map.111.refs_0_.refs_8_), channel_id=1, source_target_pairs={{0,4},{4,0},{8,12},{12,8},{1,5},{5,1},{9,13},{13,9},{2,6},{6,2},{1... | collective-permute-start | bytes 1769480 | tf_op jit(solution)/shard_map/ppermute | solution.py:89
  119.8 13.6 %collective-permute-start.37 = (f32[3,512]{1,0:T(4,128)S(1)}, f32[3,512]{1,0:T(4,128)S(1)}, u32[]{:S(2)}, u32[]{:S(2)}) collective-permute-start(f32[3,512]{1,0:T(4,128)S(1)} %get-tuple-element.93.refs_4_), channel_id=1, source_target_pairs={{0,12},{4,8},{8,4},{12,0},{1,13},{5,9},{9,5},{13,1},{2,14},{6,10},... | collective-permute-start | bytes 18440 | tf_op jit(solution)/shard_map/ppermute | solution.py:89
  120.9 12.4 %collective-permute-start.36 = (f32[3,512]{1,0:T(4,128)S(1)}, f32[3,512]{1,0:T(4,128)S(1)}, u32[]{:S(2)}, u32[]{:S(2)}) collective-permute-start(f32[3,512]{1,0:T(4,128)S(1)} %get-tuple-element.93.refs_4_), channel_id=1, source_target_pairs={{0,8},{4,12},{8,0},{12,4},{1,9},{5,13},{9,1},{13,5},{2,10},{6,14},... | collective-permute-start | bytes 18440 | tf_op jit(solution)/shard_map/ppermute | solution.py:89
  122.0 11.4 %collective-permute-start.35 = (f32[3,512]{1,0:T(4,128)S(1)}, f32[3,512]{1,0:T(4,128)S(1)}, u32[]{:S(2)}, u32[]{:S(2)}) collective-permute-start(f32[3,512]{1,0:T(4,128)S(1)} %get-tuple-element.93.refs_4_), channel_id=1, source_target_pairs={{0,4},{4,0},{8,12},{12,8},{1,5},{5,1},{9,13},{13,9},{2,6},{6,2},{1... | collective-permute-start | bytes 18440 | tf_op jit(solution)/shard_map/ppermute | solution.py:89
  (21 other events, 152.7 us)

commit v5 on v4

--- a/solution.py
+++ b/solution.py
@@ -95,19 +95,16 @@
     return lax.ppermute(array, ("dp", "owner"), flat)
 
 
-def project_rows(scalars, tokens, pieces, basis):
+def project_rows(scalars, tokens, pieces, basis, n_own, n_dp):
     layers, tok_rows, _ = tokens.shape
     tile, cols = basis.shape[1:]
-    n_dp = len(pieces) + 1
-    n_own = len(pieces[0])
     part_rows = tok_rows // n_own
     packed = 3 * n_dp * tok_rows // 4
     half = packed // 2
-    flat = [p for group in pieces for p in group]
     shapes = [(layers, half, cols)] * 2
 
     def kernel(scalar_ref, tokens_hbm, basis_hbm, *refs):
-        piece_refs, refs = refs[: len(flat)], refs[len(flat) :]
+        piece_refs, refs = refs[: len(pieces)], refs[len(pieces) :]
         out_refs, (tokens_ref, basis_ref, sems) = refs[: len(shapes)], refs[len(shapes) :]
         dp, own = scalar_ref[0], scalar_ref[1]
         at = pl.ds(pl.multiple_of(dp * tile, tile), tile)
@@ -123,21 +120,24 @@
             )
             for copy in copies[-1]:
                 copy.start()
-        row = lax.broadcasted_iota(jnp.int32, (packed, tok_rows), 0)
-        row = jnp.where(dp % 2 == 0, row, jnp.where(row < half, row + half, row - half))
-        col = lax.broadcasted_iota(jnp.int32, (packed, tok_rows), 1)
-        turn = (col // part_rows) % n_own
-        shared = (own ^ (((turn & 1) << 1) | (turn >> 1))) * part_rows + col % part_rows
-        picks = []
-        for mask in range(n_dp):
-            shard = dp ^ mask
+        col = lax.broadcasted_iota(jnp.int32, (1, n_dp * tok_rows), 1)
+        turn = (col - tok_rows) // part_rows
+        peer = turn // (n_dp - 1)
+        peer = own ^ (((peer & 1) << 1) | (peer >> 1))
+        mine = col < tok_rows
+        mask = jnp.where(mine, 0, turn % (n_dp - 1) + 1)
+        index = jnp.where(mine, col, peer * part_rows + col % part_rows)
+        place = jnp.full_like(col, -1)
+        for number in range(n_dp):
+            shard = dp ^ number
             start = jnp.int32(0)
             for other in range(n_dp):
                 start += jnp.where(other < shard, scalar_ref[2 + other], 0)
-            index = col if mask == 0 else shared
-            chosen = (row == start + index) & (index < scalar_ref[2 + shard])
-            picks.append(chosen.astype(jnp.bfloat16))
-        select = jnp.concatenate(picks, axis=1)
+            here = (mask == number) & (index < scalar_ref[2 + shard])
+            place = jnp.where(here, start + index, place)
+        row = lax.broadcasted_iota(jnp.int32, (packed, n_dp * tok_rows), 0)
+        row = row + jnp.where(dp % 2 == 0, 0, jnp.where(row < half, half, -half))
+        select = (row == place).astype(jnp.bfloat16)
         for layer in range(layers):
             copies[layer][0].wait()
             rows = jnp.concatenate([tokens_ref[layer]] + [p[layer] for p in piece_refs], axis=0)
@@ -152,7 +152,7 @@
     return pl.pallas_call(
         kernel,
         out_shape=[jax.ShapeDtypeStruct(shape, jnp.bfloat16) for shape in shapes],
-        in_specs=[scalar_spec] + [pl.BlockSpec(memory_space=pltpu.HBM)] * 2 + [vmem_spec] * len(flat),
+        in_specs=[scalar_spec] + [pl.BlockSpec(memory_space=pltpu.HBM)] * 2 + [vmem_spec] * len(pieces),
         out_specs=[vmem_spec] * len(shapes),
         scratch_shapes=[
             pltpu.VMEM((layers, tok_rows, tile), jnp.bfloat16),
@@ -161,22 +161,43 @@
         ],
         compiler_params=pltpu.CompilerParams(vmem_limit_bytes=16 * 1024 * 1024),
         cost_estimate=light,
-    )(scalars, *[pltpu.with_memory_space_constraint(array, pltpu.HBM) for array in (tokens, basis)], *flat)
-
-
-def add(first, second):
-    def kernel(first_ref, second_ref, out_ref):
-        total = first_ref[...].astype(jnp.float32) + second_ref[...].astype(jnp.float32)
-        out_ref[...] = total.astype(out_ref.dtype)
-
-    return pl.pallas_call(
-        kernel,
-        out_shape=jax.ShapeDtypeStruct(first.shape, first.dtype),
-        in_specs=[vmem_spec] * 2,
-        out_specs=vmem_spec,
-        compiler_params=pltpu.CompilerParams(vmem_limit_bytes=8 * 1024 * 1024),
-        cost_estimate=light,
-    )(first, second)
+    )(scalars, *[pltpu.with_memory_space_constraint(array, pltpu.HBM) for array in (tokens, basis)], *pieces)
+
+
+def add(*pairs):
+    layers = pairs[0][0].shape[0]
+
+    def kernel(*refs):
+        for number in range(len(pairs)):
+            total = refs[2 * number][...].astype(jnp.float32) + refs[2 * number + 1][...].astype(jnp.float32)
+            refs[-1][number * layers : (number + 1) * layers] = total.astype(refs[-1].dtype)
+
+    first = pairs[0][0]
+    return pl.pallas_call(
+        kernel,
+        out_shape=jax.ShapeDtypeStruct((layers * len(pairs), *first.shape[1:]), first.dtype),
+        in_specs=[vmem_spec] * (2 * len(pairs)),
+        out_specs=vmem_spec,
+        compiler_params=pltpu.CompilerParams(vmem_limit_bytes=8 * 1024 * 1024),
+        cost_estimate=light,
+    )(*[array for pair in pairs for array in pair])
+
+
+def join(arrays):
+    layers, rows, cols = arrays[0].shape
+
+    def kernel(*refs):
+        for number, ref in enumerate(refs[:-1]):
+            refs[-1][:, number * rows : (number + 1) * rows] = ref[...]
+
+    return pl.pallas_call(
+        kernel,
+        out_shape=jax.ShapeDtypeStruct((layers, len(arrays) * rows, cols), arrays[0].dtype),
+        in_specs=[vmem_spec] * len(arrays),
+        out_specs=vmem_spec,
+        compiler_params=pltpu.CompilerParams(vmem_limit_bytes=8 * 1024 * 1024),
+        cost_estimate=light,
+    )(*arrays)
 
 
 def cut_rows(arrays, tile, n_own, n_dp):
@@ -212,97 +233,115 @@
 
 
 def pick(home, choices):
-    flat = [array for arrays in choices for array in arrays]
-    count = len(choices[0])
-
     def kernel(home_ref, *refs):
-        for number, out_ref in enumerate(refs[len(flat) :]):
-            for index in range(count):
-
-                @pl.when(home_ref[0] == index)
-                def _(number=number, index=index, out_ref=out_ref):
-                    out_ref[...] = refs[number * count + index][...]
-
-    return pl.pallas_call(
-        kernel,
-        out_shape=[jax.ShapeDtypeStruct(arrays[0].shape, arrays[0].dtype) for arrays in choices],
-        in_specs=[scalar_spec] + [vmem_spec] * len(flat),
-        out_specs=[vmem_spec] * len(choices),
-        compiler_params=pltpu.CompilerParams(vmem_limit_bytes=8 * 1024 * 1024),
-        cost_estimate=light,
-    )(home, *flat)
-
-
-def column_squares(ref, other_ref, layer):
-    near = ref[layer].astype(jnp.float32)
-    far = other_ref[layer].astype(jnp.float32)
-    return jnp.sum(near * near, axis=0, keepdims=True) + jnp.sum(far * far, axis=0, keepdims=True)
-
-
-def settle_acts(state_act, state_grad, panels):
-    slot_count, width = state_act.shape
-    cols = panels[0].shape[2]
-    layers = panels[0].shape[0]
-
-    def kernel(state_act_ref, state_grad_ref, *refs):
-        packet_ref = refs[-1]
-        packet_ref[...] = jnp.zeros_like(packet_ref)
-        packet_ref[:slot_count] = state_act_ref[...]
-        packet_ref[slot_count : 2 * slot_count] = state_grad_ref[...]
-        for layer in range(layers):
-            row = 2 * slot_count + layer
-            packet_ref[row : row + 1, :cols] = column_squares(refs[0], refs[1], layer)
-
-    return pl.pallas_call(
-        kernel,
-        out_shape=jax.ShapeDtypeStruct((2 * slot_count + layers, width), jnp.float32),
-        in_specs=[vmem_spec] * (2 + len(panels)),
-        out_specs=vmem_spec,
-        compiler_params=pltpu.CompilerParams(vmem_limit_bytes=8 * 1024 * 1024),
-        cost_estimate=light,
-    )(state_act, state_grad, *panels)
-
-
-def settle_grads(home, arrivals):
-    layers, half, cols = arrivals[0][0].shape
-    flat = [array for pair in arrivals for array in pair]
-
-    def kernel(home_ref, *refs):
-        in_refs, (near_ref, far_ref, square_ref) = refs[:-3], refs[-3:]
-        for index in range(len(arrivals)):
+        for index in range(len(choices)):
 
             @pl.when(home_ref[0] == index)
             def _(index=index):
-                near_ref[...] = in_refs[2 * index][...]
-                far_ref[...] = in_refs[2 * index + 1][...]
-
-        for layer in range(layers):
-            square_ref[layer : layer + 1] = column_squares(near_ref, far_ref, layer)
-
-    out_shape = [jax.ShapeDtypeStruct((layers, half, cols), jnp.bfloat16)] * 2 + [
-        jax.ShapeDtypeStruct((layers, cols), jnp.float32)
-    ]
-    return pl.pallas_call(
-        kernel,
-        out_shape=out_shape,
-        in_specs=[scalar_spec] + [vmem_spec] * len(flat),
-        out_specs=[vmem_spec] * len(out_shape),
-        compiler_params=pltpu.CompilerParams(vmem_limit_bytes=8 * 1024 * 1024),
-        cost_estimate=light,
-    )(home, *flat)
-
-
-def finish(scalars, packets, squares, acts, grads, slot_count):
-    n_own, n_dp = len(packets), len(squares)
-    layers, _, tile = acts[0].shape
+                refs[-1][...] = refs[index][...]
+
+    return pl.pallas_call(
+        kernel,
+        out_shape=jax.ShapeDtypeStruct(choices[0].shape, choices[0].dtype),
+        in_specs=[scalar_spec] + [vmem_spec] * len(choices),
+        out_specs=vmem_spec,
+        compiler_params=pltpu.CompilerParams(vmem_limit_bytes=8 * 1024 * 1024),
+        cost_estimate=light,
+    )(home, *choices)
+
+
+def squares_of(panel, layers):
+    parts, _, cols = panel.shape
+
+    def kernel(panel_ref, out_ref):
+        for layer in range(layers):
+            total = jnp.zeros((1, cols), jnp.float32)
+            for part in range(layer, parts, layers):
+                wide = panel_ref[part].astype(jnp.float32)
+                total += jnp.sum(wide * wide, axis=0, keepdims=True)
+            out_ref[layer : layer + 1] = total
+
+    return pl.pallas_call(
+        kernel,
+        out_shape=jax.ShapeDtypeStruct((layers, cols), jnp.float32),
+        in_specs=[vmem_spec],
+        out_specs=vmem_spec,
+        compiler_params=pltpu.CompilerParams(vmem_limit_bytes=8 * 1024 * 1024),
+        cost_estimate=light,
+    )(panel)
+
+
+def packet_of(home, state_act, state_grad, act_halves, grads):
+    slot_count, width = state_act.shape
+    layers, cols = grads[0].shape
+    arrays = [state_act, state_grad, *act_halves, *grads]
+
+    def kernel(home_ref, *refs):
+        packet_ref, refs = refs[-1], refs[:-1]
+        packet_ref[:slot_count] = refs[0][...]
+        packet_ref[slot_count : 2 * slot_count] = refs[1][...]
+        packet_ref[2 * slot_count :] = jnp.zeros_like(packet_ref[2 * slot_count :])
+        packet_ref[2 * slot_count : 2 * slot_count + layers, :cols] = refs[2][...] + refs[3][...]
+        total = jnp.where(home_ref[0] == 0, refs[4][...], 0.0)
+        for ref in refs[5:]:
+            total += ref[...]
+        packet_ref[2 * slot_count + layers :, :cols] = total
+
+    return pl.pallas_call(
+        kernel,
+        out_shape=jax.ShapeDtypeStruct((2 * (slot_count + layers), width), jnp.float32),
+        in_specs=[scalar_spec] + [vmem_spec] * len(arrays),
+        out_specs=vmem_spec,
+        compiler_params=pltpu.CompilerParams(vmem_limit_bytes=8 * 1024 * 1024),
+        cost_estimate=light,
+    )(home, *arrays)
+
+
+def gram_of(grads, act):
+    layers, _, cols = act.shape
+
+    def kernel(grad_ref, act_ref, out_ref):
+        for layer in range(layers):
+            out_ref[layer] = product_of(grad_ref[layer], act_ref[layer])
+
+    return pl.pallas_call(
+        kernel,
+        out_shape=jax.ShapeDtypeStruct((layers, grads.shape[2], cols), jnp.float32),
+        in_specs=[vmem_spec] * 2,
+        out_specs=vmem_spec,
+        compiler_params=pltpu.CompilerParams(vmem_limit_bytes=16 * 1024 * 1024),
+        cost_estimate=light,
+    )(grads, act)
+
+
+def product_of(grad, act):
+    return lax.dot_general(grad, act, (((0,), (0,)), ((), ())), preferred_element_type=jnp.float32)
+
+
+def finish(grads, act, grams, factors):
+    layers, tile, cols = grams.shape
+
+    def kernel(grad_ref, act_ref, gram_ref, factor_ref, out_ref):
+        for layer in range(layers):
+            gram = gram_ref[layer] + product_of(grad_ref[layers + layer], act_ref[layer])
+            out_ref[layer] = (gram * factor_ref[layer]).astype(jnp.bfloat16)
+
+    return pl.pallas_call(
+        kernel,
+        out_shape=jax.ShapeDtypeStruct((layers, tile, cols), jnp.bfloat16),
+        in_specs=[vmem_spec] * 4,
+        out_specs=vmem_spec,
+        compiler_params=pltpu.CompilerParams(vmem_limit_bytes=24 * 1024 * 1024),
+        cost_estimate=light,
+    )(grads, act, grams, factors)
+
+
+def eigenvalues(scalars, packets, layers, slot_count, n_dp, tile):
+    n_own = len(packets)
     width = packets[0].shape[1]
-    operands = [*packets, *squares, *acts, *grads]
 
     def kernel(scalar_ref, *refs):
         packet_refs, refs = refs[:n_own], refs[n_own:]
-        square_refs, refs = refs[:n_dp], refs[n_dp:]
-        act_refs, refs = refs[: len(acts)], refs[len(acts) :]
-        grad_refs, refs = refs[:2], refs[2:]
         out_ref, new_act_ref, new_grad_ref, act_full, grad_full = refs
         dp, own = scalar_ref[0], scalar_ref[1]
         total = scalar_ref[2]
@@ -312,10 +351,9 @@
         owners = [scalar_ref[2 + n_dp + layer] for layer in range(layers)]
         for mask in range(n_own):
             at = pl.ds(pl.multiple_of((own ^ mask) * tile, tile), tile)
-            act_full[:, at] = packet_refs[mask][2 * slot_count :, :tile] / total
-        for mask in range(n_dp):
-            at = pl.ds(pl.multiple_of((dp ^ mask) * tile, tile), tile)
-            grad_full[:, at] = square_refs[mask][...] / total
+            lower = 2 * slot_count + layers
+            act_full[:, at] = packet_refs[mask][2 * slot_count : lower, :tile] / total
+            grad_full[:, at] = packet_refs[mask][lower:, :tile] / total
         new_act_ref[...] = packet_refs[0][:slot_count]
         new_grad_ref[...] = packet_refs[0][slot_count : 2 * slot_count]
         for layer in range(layers):
@@ -347,31 +385,22 @@
             cols = act_full[layer : layer + 1, pl.ds(pl.multiple_of(own * tile, tile), tile)]
             rows = jnp.transpose(jnp.broadcast_to(rows, (128, tile)))
             rows = jnp.concatenate([rows] * (tile // 128), axis=1)
-            gram = sum(
-                lax.dot_general(
-                    grad_refs[side][layer],
-                    act_refs[side][layer],
-                    (((0,), (0,)), ((), ())),
-                    preferred_element_type=jnp.float32,
-                )
-                for side in range(2)
-            )
-            out_ref[layer] = (gram / total / (rows * cols + damping)).astype(jnp.bfloat16)
+            out_ref[layer] = 1.0 / (total * (rows * cols + damping))
 
     out_shape = [
-        jax.ShapeDtypeStruct((layers, tile, tile), jnp.bfloat16),
+        jax.ShapeDtypeStruct((layers, tile, tile), jnp.float32),
         jax.ShapeDtypeStruct((slot_count, width), jnp.float32),
         jax.ShapeDtypeStruct((slot_count, width), jnp.float32),
     ]
     return pl.pallas_call(
         kernel,
         out_shape=out_shape,
-        in_specs=[scalar_spec] + [vmem_spec] * len(operands),
+        in_specs=[scalar_spec] + [vmem_spec] * n_own,
         out_specs=[vmem_spec] * len(out_shape),
         scratch_shapes=[pltpu.VMEM((layers, width), jnp.float32)] * 2,
         compiler_params=pltpu.CompilerParams(vmem_limit_bytes=16 * 1024 * 1024),
         cost_estimate=light,
-    )(scalars, *operands)
+    )(scalars, *packets)
 
 
 def line_plan(activations, out_grads, basis_act, basis_grad, owner_of, counts, state_act, state_grad):
@@ -389,66 +418,55 @@
     def step(arrays, *others):
         return lax.optimization_barrier((*arrays, *others))[: len(arrays)]
 
-    def sent(cuts):
-        return [flip(cut, "dp", mask) for mask, cut in enumerate(cuts, 1)]
-
-    def pieces_of(gots, chips):
-        return [
-            [got, chip, flip(got, "owner", 1), flip(chip, "owner", 1)]
-            for got, chip in zip(gots, chips, strict=True)
-        ]
-
     cuts = cut_rows((out_grads, activations), tile, n_own, n_dp)
-    got_grad = sent(cuts[: n_dp - 1])
-    chips_grad = [flip(got, "owner", 2) for got in got_grad]
-    got_act = sent(after(cut, *got_grad) for cut in cuts[n_dp - 1 :])
-    pieces_grad = pieces_of(got_grad, chips_grad)
-    pieces_grad[0][0] = after(pieces_grad[0][0], *got_act)
-    keep, send = project_rows(scalars, out_grads, pieces_grad, basis_grad)
+    cuts = [flip(cut, "dp", number % (n_dp - 1) + 1) for number, cut in enumerate(cuts)]
+    got_grad, got_act = cuts[: n_dp - 1], cuts[n_dp - 1 :]
+    pieces = got_grad[:-1] + [after(got_grad[-1], got_act[0])]
+    pieces += [flip(piece, "owner", 2) for piece in pieces]
+    pieces += [flip(piece, "owner", 1) for piece in pieces]
+    keep, send = project_rows(scalars, out_grads, pieces, basis_grad, n_own, n_dp)
 
     owners = range(n_own)
     to_home = [((o ^ 1, o), (o, o)) for o in owners]
     swaps = [((a, o), (a ^ 1, o)) for a in range(n_dp) for o in owners if (a ^ o) & 2]
-    near = hop(send, to_home + swaps)
-    far = hop(keep, to_home)
-    chips_act = [flip(after(got, keep), "owner", 2) for got in got_act]
-    keep, send, near, far, *chips_act = step([keep, send, near, far, *chips_act])
-    part = add(keep, near)
-    rest = add(send, far)
-    pieces_act = pieces_of(got_act, chips_act)
-    pieces_act[0][0] = after(pieces_act[0][0], part, rest)
-    keep_act, send_act = project_rows(scalars, activations, pieces_act, basis_act)
+    near = hop(after(send, *got_act), to_home + swaps)
+    far = hop(after(keep, *got_act), to_home)
+    pieces = [join(got_act)]
+    pieces += [flip(pieces[0], "owner", 2)]
+    pieces += [flip(piece, "owner", 1) for piece in pieces]
+    keep_act, send_act = project_rows(scalars, activations, pieces, basis_act, n_own, n_dp)
+
+    keep, send, near, far, keep_act, send_act = step([keep, send, near, far, keep_act, send_act])
+    part = add((keep, near))
+    rest = add((send, far))
     near = hop(part, [((o ^ 2, o), (o, o)) for o in owners])
     far = hop(part, [((o ^ 3, o), (o, o)) for o in owners])
     near_act = flip(send_act, "dp", 1)
 
     part, rest, near, far, keep_act, near_act = step([part, rest, near, far, keep_act, near_act])
-    part_act = add(keep_act, near_act)
+    part_act = add((keep_act, near_act))
     cross_act = flip(part_act, "dp", 2)
-    part = add(part, near)
-    rest = add(rest, far)
-    to_chip = [((o, o), (o, o ^ 2)) for o in owners]
-    part_chip = hop(part, to_chip)
-    rest_chip = hop(rest, to_chip)
-
-    part_act, cross_act, part, rest, part_chip, rest_chip = step(
-        [part_act, cross_act, part, rest, part_chip, rest_chip]
-    )
-    full_act = add(part_act, cross_act)
-    back_act = flip(full_act, "dp", 1)
-    to_core = [((o, o ^ b), (o, o ^ b ^ 1)) for o in owners for b in (0, 2)]
+    full = add((after(part, part_act), near), (rest, far))
+    chip = hop(full, [((o, o), (o, o ^ 2)) for o in owners])
+    squares = [squares_of(full, layers)]
+    squares += [hop(squares[0], [((o, o), (o ^ mask, o)) for o in owners]) for mask in range(1, n_dp)]
+
+    part_act, cross_act, full, chip, *squares = step([part_act, cross_act, full, chip, *squares])
+    full_act = add((part_act, cross_act))
+    halves = [squares_of(full_act, layers)]
+    halves += [flip(halves[0], "dp", 1)]
     home = jnp.where(own == dp, 0, jnp.where(own == dp ^ 2, 1, 2)).astype(jnp.int32)[None]
-    part_half, rest_half = pick(home, [(part, part_chip), (rest, rest_chip)])
-    part_core = hop(part_half, to_core)
-    rest_core = hop(rest_half, to_core)
-    *grads, squares = settle_grads(home // 2, [(part_half, rest_half), (part_core, rest_core)])
-    squares = [squares] + [flip(squares, "dp", mask) for mask in range(1, n_dp)]
-
-    full_act, back_act, *squares = step([full_act, back_act, *squares])
-    acts = [full_act, back_act]
-    packet = settle_acts(state_act, state_grad, acts)
+    packet = packet_of(home, state_act, state_grad, halves, squares)
+    back_act = flip(after(full_act, packet), "dp", 1)
+    full = pick(home, [after(full, packet), chip])
+    core = hop(full, [((o, o ^ b), (o, o ^ b ^ 1)) for o in owners for b in (0, 2)])
     packets = [packet] + [flip(packet, "owner", mask) for mask in range(1, n_own)]
-    return tuple(finish(scalars, packets, squares, acts, grads, state_act.shape[0]))
+    factors, new_act, new_grad = eigenvalues(scalars, packets, layers, state_act.shape[0], n_dp, tile)
+    grads = pick(home // 2, [full, core])
+    grams = gram_of(grads, full_act)
+
+    grads, grams, factors, back_act = step([grads, grams, factors, back_act])
+    return finish(grads, back_act, grams, factors), new_act, new_grad
 
 
 def solution(mesh):

time: 142 us -> 130 us (0.915)
  waiting for transfers between devices: 89 us -> 74.5 us
  starting transfers between devices: 38.7 us -> 40.3 us
    ppermute x33 -> x25, waiting for transfers between devices: 47 us -> 36.4 us  [flip(): lax.ppermute(array, axis, [(i, i ^ mask) for i in range(lax.axis_size(axi...]
    ppermute x8 -> x9, starting transfers between devices: 10.8 us -> 15.2 us  [hop(): return lax.ppermute(array, ('dp', 'owner'), flat)]
    ppermute x8 -> x9, waiting for transfers between devices: 41.9 us -> 38.1 us  [hop(): return lax.ppermute(array, ('dp', 'owner'), flat)]
    ppermute x33 -> x25, starting transfers between devices: 27.9 us -> 25.1 us  [flip(): lax.ppermute(array, axis, [(i, i ^ mask) for i in range(lax.axis_size(axi...]
    pallas_call x10 -> x14, Pallas kernels: 4.4 us -> 5.48 us  [the longest x1 1.94 us: eigenvalues(): pl.pallas_call(kernel, out_shape=out_shape, in_specs=[scalar_spec] + [vme...]
  transfers between devices with their start and end apart: 41 -> 34, of which waited for: 22 -> 19; matrix products, arithmetic and copies ran while one was open for 0% -> 0% of each run, Pallas kernels for 3% -> 8%
where the time goes in v5:
time: 130 us
  waiting for transfers between devices  74.5 us (57%)
  starting transfers between devices  40.3 us (31%)
  Pallas kernels  14.1 us (11%)
    ppermute x9, waiting for transfers between devices, hop(): return lax.ppermute(array, ('dp', 'owner'), flat)  38.1 us
    ppermute x25, waiting for transfers between devices, flip(): lax.ppermute(array, axis, [(i, i ^ mask) for i in range(lax.axis_size(axi...  36.4 us
    ppermute x25, starting transfers between devices, flip(): lax.ppermute(array, axis, [(i, i ^ mask) for i in range(lax.axis_size(axi...  25.1 us
    ppermute x9, starting transfers between devices, hop(): return lax.ppermute(array, ('dp', 'owner'), flat)  15.2 us
    pallas_call x2, Pallas kernels, project_rows(): pl.pallas_call(kernel, out_shape=[jax.ShapeDtypeStruct(shape, jnp.bfloat1...  7.46 us
  transfers between devices with their start and end apart: 34, of which 19 were waited for; matrix products, arithmetic and copies ran while one was open for 0% of the time, Pallas kernels for 8%

profile of v5, /device:TPU:0, one launch (start us, length us, event | category | flops | bytes accessed | tf_op | source)
XLA Modules:
  0.0 129.9 jit_solution(1265139756446808503)
XLA Ops:
  1.9 5.1 %collective-permute-start.2 = (bf16[3,32,512]{2,1,0:T(8,128)(2,1)S(1)}, bf16[3,32,512]{2,1,0:T(8,128)(2,1)S(1)}, u32[]{:S(2)}, u32[]{:S(2)}) collective-permute-start(bf16[3,32,512]{2,1,0:T(8,128)(2,1)S(1)} %get-tuple-element.48), channel_id=1, source_target_pairs={{0,12},{4,8},{8,4},{12,0},{1,13},{5,9},{9,5},{13,1},{2,14},{6,10},... | collective-permute-start | bytes 294920 | tf_op jit(solution)/shard_map/ppermute | solution.py:89
  7.0 2.0 %collective-permute-start = (bf16[3,32,512]{2,1,0:T(8,128)(2,1)S(1)}, bf16[3,32,512]{2,1,0:T(8,128)(2,1)S(1)}, u32[]{:S(2)}, u32[]{:S(2)}) collective-permute-start(bf16[3,32,512]{2,1,0:T(8,128)(2,1)S(1)} %get-tuple-element.46), channel_id=1, source_target_pairs={{0,4},{4,0},{8,12},{12,8},{1,5},{5,1},{9,13},{13,9},{2,6},{6,2},{1... | collective-permute-start | bytes 294920 | tf_op jit(solution)/shard_map/ppermute | solution.py:89
  9.0 2.9 %collective-permute-start.13 = (bf16[3,32,512]{2,1,0:T(8,128)(2,1)S(1)}, bf16[3,32,512]{2,1,0:T(8,128)(2,1)S(1)}, u32[]{:S(2)}, u32[]{:S(2)}) collective-permute-start(bf16[3,32,512]{2,1,0:T(8,128)(2,1)S(1)} %get-tuple-element.53), channel_id=1, source_target_pairs={{0,8},{4,12},{8,0},{12,4},{1,9},{5,13},{9,1},{13,5},{2,10},{6,14},... | collective-permute-start | bytes 294920 | tf_op jit(solution)/shard_map/ppermute | solution.py:89
  11.9 2.6 %collective-permute-start.14 = (bf16[3,32,512]{2,1,0:T(8,128)(2,1)S(1)}, bf16[3,32,512]{2,1,0:T(8,128)(2,1)S(1)}, u32[]{:S(2)}, u32[]{:S(2)}) collective-permute-start(bf16[3,32,512]{2,1,0:T(8,128)(2,1)S(1)} %get-tuple-element.54), channel_id=1, source_target_pairs={{0,12},{4,8},{8,4},{12,0},{1,13},{5,9},{9,5},{13,1},{2,14},{6,10},... | collective-permute-start | bytes 294920 | tf_op jit(solution)/shard_map/ppermute | solution.py:89
  16.6 1.6 %collective-permute-start.4 = (bf16[3,32,512]{2,1,0:T(8,128)(2,1)S(1)}, bf16[3,32,512]{2,1,0:T(8,128)(2,1)S(1)}, u32[]{:S(2)}, u32[]{:S(2)}) collective-permute-start(bf16[3,32,512]{2,1,0:T(8,128)(2,1)S(1)} %collective-permute-done.refs_0_), channel_id=1, source_target_pairs={{0,2},{1,3},{2,0},{3,1},{4,6},{5,7},{6,4},{7,5},{8,10},{9,11},{10,... | collective-permute-start | bytes 294920 | tf_op jit(solution)/shard_map/ppermute | solution.py:89
  18.2 3.6 %collective-permute-done.1.refs_1_ = bf16[3,32,512]{2,1,0:T(8,128)(2,1)S(1)} collective-permute-done((bf16[3,32,512]{2,1,0:T(8,128)(2,1)S(1)}, bf16[3,32,512]{2,1,0:T(8,128)(2,1)S(1)}, u32[]{:S(2)}, u32[]{:S(2)}) %collective-permute-start.1) | collective-permute-done | bytes 98336 | tf_op jit(solution)/shard_map/ppermute | solution.py:89
  29.5 3.7 %shard_map.104 = (bf16[3,192,512]{2,1,0:T(8,128)(2,1)S(1)}, bf16[3,192,512]{2,1,0:T(8,128)(2,1)S(1)}) custom-call(s32[9]{0:T(128)S(1)} %pad_add_fusion.scalar_ref, bf16[3,128,2048]{2,1,0:T(8,128)(2,1)} %tokens_hbm.2, bf16[3,512,512]{2,1,0:T(8,128)(2,1)} %basis_hbm.2, bf16[3,32,512]{2,1,0:T(8,128)(2,1)S(1)} %collective-permute-done.refs_0_, ...), custom_call_target="tpu_custom_call" | custom-call | tf_op jit(solution)/shard_map/pallas_call | solution.py:152
  37.5 1.6 %collective-permute-done.19.refs_3_ = bf16[3,96,512]{2,1,0:T(8,128)(2,1)S(1)} collective-permute-done((bf16[3,96,512]{2,1,0:T(8,128)(2,1)S(1)}, bf16[3,96,512]{2,1,0:T(8,128)(2,1)S(1)}, u32[]{:S(2)}, u32[]{:S(2)}) %collective-permute-start.19) | collective-permute-done | bytes 294944 | tf_op jit(solution)/shard_map/ppermute | solution.py:89
  39.0 3.7 %shard_map.106 = (bf16[3,192,512]{2,1,0:T(8,128)(2,1)S(1)}, bf16[3,192,512]{2,1,0:T(8,128)(2,1)S(1)}) custom-call(s32[9]{0:T(128)S(1)} %pad_add_fusion.scalar_ref, bf16[3,128,2048]{2,1,0:T(8,128)(2,1)} %tokens_hbm.3, bf16[3,512,512]{2,1,0:T(8,128)(2,1)} %basis_hbm.3, bf16[3,96,512]{2,1,0:T(8,128)(2,1)S(1)} %shard_map.105.refs_0_, ...), custom_call_target="tpu_custom_call" | custom-call | tf_op jit(solution)/shard_map/pallas_call | solution.py:152
  42.8 2.2 %collective-permute-done.15.refs_1_ = bf16[3,192,512]{2,1,0:T(8,128)(2,1)S(1)} collective-permute-done((bf16[3,192,512]{2,1,0:T(8,128)(2,1)S(1)}, bf16[3,192,512]{2,1,0:T(8,128)(2,1)S(1)}, u32[]{:S(2)}, u32[]{:S(2)}) %collective-permute-start.15) | collective-permute-done | bytes 589856 | tf_op jit(solution)/shard_map/ppermute | solution.py:95
  45.0 6.3 %collective-permute-done.16.refs_1_ = bf16[3,192,512]{2,1,0:T(8,128)(2,1)S(1)} collective-permute-done((bf16[3,192,512]{2,1,0:T(8,128)(2,1)S(1)}, bf16[3,192,512]{2,1,0:T(8,128)(2,1)S(1)}, u32[]{:S(2)}, u32[]{:S(2)}) %collective-permute-start.16) | collective-permute-done | bytes 589856 | tf_op jit(solution)/shard_map/ppermute | solution.py:95
  54.3 17.1 %collective-permute-done.21.refs_3_ = bf16[3,192,512]{2,1,0:T(8,128)(2,1)S(1)} collective-permute-done((bf16[3,192,512]{2,1,0:T(8,128)(2,1)S(1)}, bf16[3,192,512]{2,1,0:T(8,128)(2,1)S(1)}, u32[]{:S(2)}, u32[]{:S(2)}) %collective-permute-start.21) | collective-permute-done | bytes 589856 | tf_op jit(solution)/shard_map/ppermute | solution.py:95
  71.4 8.0 %collective-permute-done.20.refs_1_ = bf16[3,192,512]{2,1,0:T(8,128)(2,1)S(1)} collective-permute-done((bf16[3,192,512]{2,1,0:T(8,128)(2,1)S(1)}, bf16[3,192,512]{2,1,0:T(8,128)(2,1)S(1)}, u32[]{:S(2)}, u32[]{:S(2)}) %collective-permute-start.20) | collective-permute-done | bytes 589856 | tf_op jit(solution)/shard_map/ppermute | solution.py:95
  79.8 3.0 %collective-permute-start.24 = (bf16[6,192,512]{2,1,0:T(8,128)(2,1)S(1)}, bf16[6,192,512]{2,1,0:T(8,128)(2,1)S(1)}, u32[]{:S(2)}, u32[]{:S(2)}) collective-permute-start(bf16[6,192,512]{2,1,0:T(8,128)(2,1)S(1)} %shard_map.110.panel_ref.refs_0_), channel_id=1, source_target_pairs={{0,2},{5,7},{10,8},{15,13},{16,18},{21,23},{26,24},{31,29}} | collective-permute-start | bytes 3538952 | tf_op jit(solution)/shard_map/ppermute | solution.py:95
  85.4 3.1 %collective-permute-start.26 = (f32[3,512]{1,0:T(4,128)S(1)}, f32[3,512]{1,0:T(4,128)S(1)}, u32[]{:S(2)}, u32[]{:S(2)}) collective-permute-start(f32[3,512]{1,0:T(4,128)S(1)} %shard_map.111.refs_4_), channel_id=1, source_target_pairs={{0,8},{5,13},{10,2},{15,7},{16,24},{21,29},{26,18},{31,23}} | collective-permute-start | bytes 18440 | tf_op jit(solution)/shard_map/ppermute | solution.py:95
  89.8 4.2 %collective-permute-done.27.refs_7_ = f32[3,512]{1,0:T(4,128)S(1)} collective-permute-done((f32[3,512]{1,0:T(4,128)S(1)}, f32[3,512]{1,0:T(4,128)S(1)}, u32[]{:S(2)}, u32[]{:S(2)}) %collective-permute-start.27) | collective-permute-done | bytes 6176 | tf_op jit(solution)/shard_map/ppermute | solution.py:95
  94.2 13.1 %collective-permute-done.23.refs_1_ = bf16[3,192,512]{2,1,0:T(8,128)(2,1)S(1)} collective-permute-done((bf16[3,192,512]{2,1,0:T(8,128)(2,1)S(1)}, bf16[3,192,512]{2,1,0:T(8,128)(2,1)S(1)}, u32[]{:S(2)}, u32[]{:S(2)}) %collective-permute-start.23) | collective-permute-done | bytes 589856 | tf_op jit(solution)/shard_map/ppermute | solution.py:89
  108.4 2.8 %collective-permute-done.28.refs_3_ = f32[3,512]{1,0:T(4,128)S(1)} collective-permute-done((f32[3,512]{1,0:T(4,128)S(1)}, f32[3,512]{1,0:T(4,128)S(1)}, u32[]{:S(2)}, u32[]{:S(2)}) %collective-permute-start.28) | collective-permute-done | bytes 6176 | tf_op jit(solution)/shard_map/ppermute | solution.py:89
  113.5 2.5 %collective-permute-start.32 = (f32[10,2048]{1,0:T(8,128)S(1)}, f32[10,2048]{1,0:T(8,128)S(1)}, u32[]{:S(2)}, u32[]{:S(2)}) collective-permute-start(f32[10,2048]{1,0:T(8,128)S(1)} %shard_map.114.refs_0_), channel_id=1, source_target_pairs={{0,3},{1,2},{2,1},{3,0},{4,7},{5,6},{6,5},{7,4},{8,11},{9,10},{10,... | collective-permute-start | bytes 245768 | tf_op jit(solution)/shard_map/ppermute | solution.py:89
  116.1 3.7 %collective-permute-done.32.refs_3_ = f32[10,2048]{1,0:T(8,128)S(1)} collective-permute-done((f32[10,2048]{1,0:T(8,128)S(1)}, f32[10,2048]{1,0:T(8,128)S(1)}, u32[]{:S(2)}, u32[]{:S(2)}) %collective-permute-start.32) | collective-permute-done | bytes 81952 | tf_op jit(solution)/shard_map/ppermute | solution.py:89
  119.9 3.0 %collective-permute-done.31.refs_2_ = f32[10,2048]{1,0:T(8,128)S(1)} collective-permute-done((f32[10,2048]{1,0:T(8,128)S(1)}, f32[10,2048]{1,0:T(8,128)S(1)}, u32[]{:S(2)}, u32[]{:S(2)}) %collective-permute-start.31) | collective-permute-done | bytes 81952 | tf_op jit(solution)/shard_map/ppermute | solution.py:89
  122.8 1.9 %shard_map.118 = (f32[3,512,512]{2,1,0:T(8,128)S(1)}, f32[2,2048]{1,0:T(2,128)}, f32[2,2048]{1,0:T(2,128)}) custom-call(s32[9]{0:T(128)S(1)} %pad_add_fusion.scalar_ref, f32[10,2048]{1,0:T(8,128)S(1)} %shard_map.114.refs_0_, f32[10,2048]{1,0:T(8,128)S(1)} %collective-permute-done.30.refs_1_, f32[10,2048]{1,0:T(8,128)S(1)} %collective-permute-done.31.refs_2_, ...), custom_call_target="tpu_custom_call" | custom-call | tf_op jit(solution)/shard_map/pallas_call | solution.py:395
  125.5 2.7 %collective-permute-done.33.act_ref = bf16[3,192,512]{2,1,0:T(8,128)(2,1)S(1)} collective-permute-done((bf16[3,192,512]{2,1,0:T(8,128)(2,1)S(1)}, bf16[3,192,512]{2,1,0:T(8,128)(2,1)S(1)}, u32[]{:S(2)}, u32[]{:S(2)}) %collective-permute-start.33) | collective-permute-done | bytes 589856 | tf_op jit(solution)/shard_map/ppermute | solution.py:89
  128.2 1.8 %shard_map.119 = bf16[3,512,512]{2,1,0:T(8,128)(2,1)} custom-call(bf16[6,192,512]{2,1,0:T(8,128)(2,1)S(1)} %shard_map.116.grad_ref, bf16[3,192,512]{2,1,0:T(8,128)(2,1)S(1)} %collective-permute-done.33.act_ref, f32[3,512,512]{2,1,0:T(8,128)S(1)} %shard_map.117.gram_ref, f32[3,512,512]{2,1,0:T(8,128)S(1)} %get-tuple-element.86.factor_ref), custom_call_target="tpu_custom_call" | custom-call | tf_op jit(solution)/shard_map/pallas_call | solution.py:329
  (70 shorter events, 26.7 us)
Async XLA Ops:
  1.9 10.1 %collective-permute-start.2 = (bf16[3,32,512]{2,1,0:T(8,128)(2,1)S(1)}, bf16[3,32,512]{2,1,0:T(8,128)(2,1)S(1)}, u32[]{:S(2)}, u32[]{:S(2)}) collective-permute-start(bf16[3,32,512]{2,1,0:T(8,128)(2,1)S(1)} %get-tuple-element.48), channel_id=1, source_target_pairs={{0,12},{4,8},{8,4},{12,0},{1,13},{5,9},{9,5},{13,1},{2,14},{6,10},... | collective-permute-start | bytes 294920 | tf_op jit(solution)/shard_map/ppermute | solution.py:89
  7.0 8.2 %collective-permute-start.3 = (bf16[3,32,512]{2,1,0:T(8,128)(2,1)S(1)}, bf16[3,32,512]{2,1,0:T(8,128)(2,1)S(1)}, u32[]{:S(2)}, u32[]{:S(2)}) collective-permute-start(bf16[3,32,512]{2,1,0:T(8,128)(2,1)S(1)} %get-tuple-element.49), channel_id=1, source_target_pairs={{0,4},{4,0},{8,12},{12,8},{1,5},{5,1},{9,13},{13,9},{2,6},{6,2},{1... | collective-permute-start | bytes 294920 | tf_op jit(solution)/shard_map/ppermute | solution.py:89
  7.0 9.6 %collective-permute-start = (bf16[3,32,512]{2,1,0:T(8,128)(2,1)S(1)}, bf16[3,32,512]{2,1,0:T(8,128)(2,1)S(1)}, u32[]{:S(2)}, u32[]{:S(2)}) collective-permute-start(bf16[3,32,512]{2,1,0:T(8,128)(2,1)S(1)} %get-tuple-element.46), channel_id=1, source_target_pairs={{0,4},{4,0},{8,12},{12,8},{1,5},{5,1},{9,13},{13,9},{2,6},{6,2},{1... | collective-permute-start | bytes 294920 | tf_op jit(solution)/shard_map/ppermute | solution.py:89
  9.0 12.8 %collective-permute-start.1 = (bf16[3,32,512]{2,1,0:T(8,128)(2,1)S(1)}, bf16[3,32,512]{2,1,0:T(8,128)(2,1)S(1)}, u32[]{:S(2)}, u32[]{:S(2)}) collective-permute-start(bf16[3,32,512]{2,1,0:T(8,128)(2,1)S(1)} %get-tuple-element.47), channel_id=1, source_target_pairs={{0,8},{4,12},{8,0},{12,4},{1,9},{5,13},{9,1},{13,5},{2,10},{6,14},... | collective-permute-start | bytes 294920 | tf_op jit(solution)/shard_map/ppermute | solution.py:89
  9.0 14.2 %collective-permute-start.13 = (bf16[3,32,512]{2,1,0:T(8,128)(2,1)S(1)}, bf16[3,32,512]{2,1,0:T(8,128)(2,1)S(1)}, u32[]{:S(2)}, u32[]{:S(2)}) collective-permute-start(bf16[3,32,512]{2,1,0:T(8,128)(2,1)S(1)} %get-tuple-element.53), channel_id=1, source_target_pairs={{0,8},{4,12},{8,0},{12,4},{1,9},{5,13},{9,1},{13,5},{2,10},{6,14},... | collective-permute-start | bytes 294920 | tf_op jit(solution)/shard_map/ppermute | solution.py:89
  11.9 12.7 %collective-permute-start.14 = (bf16[3,32,512]{2,1,0:T(8,128)(2,1)S(1)}, bf16[3,32,512]{2,1,0:T(8,128)(2,1)S(1)}, u32[]{:S(2)}, u32[]{:S(2)}) collective-permute-start(bf16[3,32,512]{2,1,0:T(8,128)(2,1)S(1)} %get-tuple-element.54), channel_id=1, source_target_pairs={{0,12},{4,8},{8,4},{12,0},{1,13},{5,9},{9,5},{13,1},{2,14},{6,10},... | collective-permute-start | bytes 294920 | tf_op jit(solution)/shard_map/ppermute | solution.py:89
  16.6 8.1 %collective-permute-start.7 = (bf16[3,32,512]{2,1,0:T(8,128)(2,1)S(1)}, bf16[3,32,512]{2,1,0:T(8,128)(2,1)S(1)}, u32[]{:S(2)}, u32[]{:S(2)}) collective-permute-start(bf16[3,32,512]{2,1,0:T(8,128)(2,1)S(1)} %collective-permute-done.refs_0_), channel_id=1, source_target_pairs={{0,1},{1,0},{2,3},{3,2},{4,5},{5,4},{6,7},{7,6},{8,9},{9,8},{10,11... | collective-permute-start | bytes 294920 | tf_op jit(solution)/shard_map/ppermute | solution.py:89
  16.6 8.6 %collective-permute-start.4 = (bf16[3,32,512]{2,1,0:T(8,128)(2,1)S(1)}, bf16[3,32,512]{2,1,0:T(8,128)(2,1)S(1)}, u32[]{:S(2)}, u32[]{:S(2)}) collective-permute-start(bf16[3,32,512]{2,1,0:T(8,128)(2,1)S(1)} %collective-permute-done.refs_0_), channel_id=1, source_target_pairs={{0,2},{1,3},{2,0},{3,1},{4,6},{5,7},{6,4},{7,5},{8,10},{9,11},{10,... | collective-permute-start | bytes 294920 | tf_op jit(solution)/shard_map/ppermute | solution.py:89
  28.0 9.5 %collective-permute-start.17 = (bf16[3,96,512]{2,1,0:T(8,128)(2,1)S(1)}, bf16[3,96,512]{2,1,0:T(8,128)(2,1)S(1)}, u32[]{:S(2)}, u32[]{:S(2)}) collective-permute-start(bf16[3,96,512]{2,1,0:T(8,128)(2,1)S(1)} %shard_map.105.refs_0_), channel_id=1, source_target_pairs={{0,2},{1,3},{2,0},{3,1},{4,6},{5,7},{6,4},{7,5},{8,10},{9,11},{10,... | collective-permute-start | bytes 884744 | tf_op jit(solution)/shard_map/ppermute | solution.py:89
  33.2 11.8 %collective-permute-start.15 = (bf16[3,192,512]{2,1,0:T(8,128)(2,1)S(1)}, bf16[3,192,512]{2,1,0:T(8,128)(2,1)S(1)}, u32[]{:S(2)}, u32[]{:S(2)}) collective-permute-start(bf16[3,192,512]{2,1,0:T(8,128)(2,1)S(1)} %get-tuple-element.61.refs_0_), channel_id=1, source_target_pairs={{4,0},{1,5},{14,10},{11,15},{2,6},{3,7},{6,2},{7,3},{8,12},{9,13},... | collective-permute-start | bytes 1769480 | tf_op jit(solution)/shard_map/ppermute | solution.py:95
  34.5 16.8 %collective-permute-start.16 = (bf16[3,192,512]{2,1,0:T(8,128)(2,1)S(1)}, bf16[3,192,512]{2,1,0:T(8,128)(2,1)S(1)}, u32[]{:S(2)}, u32[]{:S(2)}) collective-permute-start(bf16[3,192,512]{2,1,0:T(8,128)(2,1)S(1)} %get-tuple-element.59.refs_0_), channel_id=1, source_target_pairs={{4,0},{1,5},{14,10},{11,15},{20,16},{17,21},{30,26},{27,31}} | collective-permute-start | bytes 1769480 | tf_op jit(solution)/shard_map/ppermute | solution.py:95
  51.4 20.0 %collective-permute-start.21 = (bf16[3,192,512]{2,1,0:T(8,128)(2,1)S(1)}, bf16[3,192,512]{2,1,0:T(8,128)(2,1)S(1)}, u32[]{:S(2)}, u32[]{:S(2)}) collective-permute-start(bf16[3,192,512]{2,1,0:T(8,128)(2,1)S(1)} %shard_map.107.refs_0_), channel_id=1, source_target_pairs={{12,0},{9,5},{6,10},{3,15},{28,16},{25,21},{22,26},{19,31}} | collective-permute-start | bytes 1769480 | tf_op jit(solution)/shard_map/ppermute | solution.py:95
  52.7 26.6 %collective-permute-start.20 = (bf16[3,192,512]{2,1,0:T(8,128)(2,1)S(1)}, bf16[3,192,512]{2,1,0:T(8,128)(2,1)S(1)}, u32[]{:S(2)}, u32[]{:S(2)}) collective-permute-start(bf16[3,192,512]{2,1,0:T(8,128)(2,1)S(1)} %shard_map.107.refs_0_), channel_id=1, source_target_pairs={{8,0},{13,5},{2,10},{7,15},{24,16},{29,21},{18,26},{23,31}} | collective-permute-start | bytes 1769480 | tf_op jit(solution)/shard_map/ppermute | solution.py:95
  54.0 25.3 %collective-permute-start.22 = (bf16[3,192,512]{2,1,0:T(8,128)(2,1)S(1)}, bf16[3,192,512]{2,1,0:T(8,128)(2,1)S(1)}, u32[]{:S(2)}, u32[]{:S(2)}) collective-permute-start(bf16[3,192,512]{2,1,0:T(8,128)(2,1)S(1)} %get-tuple-element.64), channel_id=1, source_target_pairs={{0,4},{4,0},{8,12},{12,8},{1,5},{5,1},{9,13},{13,9},{2,6},{6,2},{1... | collective-permute-start | bytes 1769480 | tf_op jit(solution)/shard_map/ppermute | solution.py:89
  79.8 27.4 %collective-permute-start.24 = (bf16[6,192,512]{2,1,0:T(8,128)(2,1)S(1)}, bf16[6,192,512]{2,1,0:T(8,128)(2,1)S(1)}, u32[]{:S(2)}, u32[]{:S(2)}) collective-permute-start(bf16[6,192,512]{2,1,0:T(8,128)(2,1)S(1)} %shard_map.110.panel_ref.refs_0_), channel_id=1, source_target_pairs={{0,2},{5,7},{10,8},{15,13},{16,18},{21,23},{26,24},{31,29}} | collective-permute-start | bytes 3538952 | tf_op jit(solution)/shard_map/ppermute | solution.py:95
  82.8 24.4 %collective-permute-start.23 = (bf16[3,192,512]{2,1,0:T(8,128)(2,1)S(1)}, bf16[3,192,512]{2,1,0:T(8,128)(2,1)S(1)}, u32[]{:S(2)}, u32[]{:S(2)}) collective-permute-start(bf16[3,192,512]{2,1,0:T(8,128)(2,1)S(1)} %shard_map.109.refs_0_), channel_id=1, source_target_pairs={{0,8},{4,12},{8,0},{12,4},{1,9},{5,13},{9,1},{13,5},{2,10},{6,14},... | collective-permute-start | bytes 1769480 | tf_op jit(solution)/shard_map/ppermute | solution.py:89
  84.1 9.9 %collective-permute-start.27 = (f32[3,512]{1,0:T(4,128)S(1)}, f32[3,512]{1,0:T(4,128)S(1)}, u32[]{:S(2)}, u32[]{:S(2)}) collective-permute-start(f32[3,512]{1,0:T(4,128)S(1)} %shard_map.111.refs_4_), channel_id=1, source_target_pairs={{0,12},{5,9},{10,6},{15,3},{16,28},{21,25},{26,22},{31,19}} | collective-permute-start | bytes 18440 | tf_op jit(solution)/shard_map/ppermute | solution.py:95
  85.4 8.7 %collective-permute-start.26 = (f32[3,512]{1,0:T(4,128)S(1)}, f32[3,512]{1,0:T(4,128)S(1)}, u32[]{:S(2)}, u32[]{:S(2)}) collective-permute-start(f32[3,512]{1,0:T(4,128)S(1)} %shard_map.111.refs_4_), channel_id=1, source_target_pairs={{0,8},{5,13},{10,2},{15,7},{16,24},{21,29},{26,18},{31,23}} | collective-permute-start | bytes 18440 | tf_op jit(solution)/shard_map/ppermute | solution.py:95
  88.5 5.7 %collective-permute-start.25 = (f32[3,512]{1,0:T(4,128)S(1)}, f32[3,512]{1,0:T(4,128)S(1)}, u32[]{:S(2)}, u32[]{:S(2)}) collective-permute-start(f32[3,512]{1,0:T(4,128)S(1)} %shard_map.111.refs_4_), channel_id=1, source_target_pairs={{0,4},{5,1},{10,14},{15,11},{16,20},{21,17},{26,30},{31,27}} | collective-permute-start | bytes 18440 | tf_op jit(solution)/shard_map/ppermute | solution.py:95
  111.3 13.5 %collective-permute-start.29 = (bf16[6,192,512]{2,1,0:T(8,128)(2,1)S(1)}, bf16[6,192,512]{2,1,0:T(8,128)(2,1)S(1)}, u32[]{:S(2)}, u32[]{:S(2)}) collective-permute-start(bf16[6,192,512]{2,1,0:T(8,128)(2,1)S(1)} %shard_map.115.refs_0_), channel_id=1, source_target_pairs={{0,1},{2,3},{5,4},{7,6},{10,11},{8,9},{15,14},{13,12},{16,17},{18,... | collective-permute-start | bytes 3538952 | tf_op jit(solution)/shard_map/ppermute | solution.py:95
  112.7 15.5 %collective-permute-start.33 = (bf16[3,192,512]{2,1,0:T(8,128)(2,1)S(1)}, bf16[3,192,512]{2,1,0:T(8,128)(2,1)S(1)}, u32[]{:S(2)}, u32[]{:S(2)}) collective-permute-start(bf16[3,192,512]{2,1,0:T(8,128)(2,1)S(1)} %shard_map.112.panel_ref.act_ref), channel_id=1, source_target_pairs={{0,4},{4,0},{8,12},{12,8},{1,5},{5,1},{9,13},{13,9},{2,6},{6,2},{1... | collective-permute-start | bytes 1769480 | tf_op jit(solution)/shard_map/ppermute | solution.py:89
  113.5 6.4 %collective-permute-start.32 = (f32[10,2048]{1,0:T(8,128)S(1)}, f32[10,2048]{1,0:T(8,128)S(1)}, u32[]{:S(2)}, u32[]{:S(2)}) collective-permute-start(f32[10,2048]{1,0:T(8,128)S(1)} %shard_map.114.refs_0_), channel_id=1, source_target_pairs={{0,3},{1,2},{2,1},{3,0},{4,7},{5,6},{6,5},{7,4},{8,11},{9,10},{10,... | collective-permute-start | bytes 245768 | tf_op jit(solution)/shard_map/ppermute | solution.py:89
  116.0 6.9 %collective-permute-start.31 = (f32[10,2048]{1,0:T(8,128)S(1)}, f32[10,2048]{1,0:T(8,128)S(1)}, u32[]{:S(2)}, u32[]{:S(2)}) collective-permute-start(f32[10,2048]{1,0:T(8,128)S(1)} %shard_map.114.refs_0_), channel_id=1, source_target_pairs={{0,2},{1,3},{2,0},{3,1},{4,6},{5,7},{6,4},{7,5},{8,10},{9,11},{10,... | collective-permute-start | bytes 245768 | tf_op jit(solution)/shard_map/ppermute | solution.py:89
  116.0 6.8 %collective-permute-start.30 = (f32[10,2048]{1,0:T(8,128)S(1)}, f32[10,2048]{1,0:T(8,128)S(1)}, u32[]{:S(2)}, u32[]{:S(2)}) collective-permute-start(f32[10,2048]{1,0:T(8,128)S(1)} %shard_map.114.refs_0_), channel_id=1, source_target_pairs={{0,1},{1,0},{2,3},{3,2},{4,5},{5,4},{6,7},{7,6},{8,9},{9,8},{10,11... | collective-permute-start | bytes 245768 | tf_op jit(solution)/shard_map/ppermute | solution.py:89
  (14 other events, 150.4 us)

commit v6 on v5

--- a/solution.py
+++ b/solution.py
@@ -183,6 +183,26 @@
     )(*[array for pair in pairs for array in pair])
 
 
+def add_by_layer(*pairs):
+    layers, height, cols = pairs[0][0].shape
+
+    def kernel(*refs):
+        in_refs, out_refs = refs[: 2 * len(pairs)], refs[2 * len(pairs) :]
+        for layer in range(layers):
+            for number in range(len(pairs)):
+                near, far = [ref[layer].astype(jnp.float32) for ref in in_refs[2 * number : 2 * number + 2]]
+                out_refs[layer][number] = (near + far).astype(out_refs[layer].dtype)
+
+    return pl.pallas_call(
+        kernel,
+        out_shape=[jax.ShapeDtypeStruct((len(pairs), height, cols), pairs[0][0].dtype)] * layers,
+        in_specs=[vmem_spec] * (2 * len(pairs)),
+        out_specs=[vmem_spec] * layers,
+        compiler_params=pltpu.CompilerParams(vmem_limit_bytes=8 * 1024 * 1024),
+        cost_estimate=light,
+    )(*[array for pair in pairs for array in pair])
+
+
 def join(arrays):
     layers, rows, cols = arrays[0].shape
 
@@ -233,63 +253,62 @@
 
 
 def pick(home, choices):
+    flat = [array for arrays in choices for array in arrays]
+    count = len(choices[0])
+
     def kernel(home_ref, *refs):
-        for index in range(len(choices)):
+        for index in range(count):
 
             @pl.when(home_ref[0] == index)
             def _(index=index):
-                refs[-1][...] = refs[index][...]
-
-    return pl.pallas_call(
-        kernel,
-        out_shape=jax.ShapeDtypeStruct(choices[0].shape, choices[0].dtype),
-        in_specs=[scalar_spec] + [vmem_spec] * len(choices),
+                for number, out_ref in enumerate(refs[len(flat) :]):
+                    out_ref[...] = refs[number * count + index][...]
+
+    return pl.pallas_call(
+        kernel,
+        out_shape=[jax.ShapeDtypeStruct(arrays[0].shape, arrays[0].dtype) for arrays in choices],
+        in_specs=[scalar_spec] + [vmem_spec] * len(flat),
+        out_specs=[vmem_spec] * len(choices),
+        compiler_params=pltpu.CompilerParams(vmem_limit_bytes=12 * 1024 * 1024),
+        cost_estimate=light,
+    )(home, *flat)
+
+
+def squares_of(panels, by_layer):
+    layers = len(panels) if by_layer else panels[0].shape[0]
+    cols = panels[0].shape[2]
+
+    def kernel(*refs):
+        for layer in range(layers):
+            parts = [refs[layer][at] for at in range(panels[0].shape[0])] if by_layer else [refs[0][layer]]
+            wide = [part.astype(jnp.float32) for part in parts]
+            total = sum(part * part for part in wide)
+            refs[-1][layer : layer + 1] = jnp.sum(total, axis=0, keepdims=True)
+
+    return pl.pallas_call(
+        kernel,
+        out_shape=jax.ShapeDtypeStruct((layers, cols), jnp.float32),
+        in_specs=[vmem_spec] * len(panels),
         out_specs=vmem_spec,
         compiler_params=pltpu.CompilerParams(vmem_limit_bytes=8 * 1024 * 1024),
         cost_estimate=light,
-    )(home, *choices)
-
-
-def squares_of(panel, layers):
-    parts, _, cols = panel.shape
-
-    def kernel(panel_ref, out_ref):
-        for layer in range(layers):
-            total = jnp.zeros((1, cols), jnp.float32)
-            for part in range(layer, parts, layers):
-                wide = panel_ref[part].astype(jnp.float32)
-                total += jnp.sum(wide * wide, axis=0, keepdims=True)
-            out_ref[layer : layer + 1] = total
-
-    return pl.pallas_call(
-        kernel,
-        out_shape=jax.ShapeDtypeStruct((layers, cols), jnp.float32),
-        in_specs=[vmem_spec],
-        out_specs=vmem_spec,
-        compiler_params=pltpu.CompilerParams(vmem_limit_bytes=8 * 1024 * 1024),
-        cost_estimate=light,
-    )(panel)
-
-
-def packet_of(home, state_act, state_grad, act_halves, grads):
-    slot_count, width = state_act.shape
+    )(*panels)
+
+
+def packet_of(home, act_halves, grads):
     layers, cols = grads[0].shape
-    arrays = [state_act, state_grad, *act_halves, *grads]
+    arrays = [*act_halves, *grads]
 
     def kernel(home_ref, *refs):
-        packet_ref, refs = refs[-1], refs[:-1]
-        packet_ref[:slot_count] = refs[0][...]
-        packet_ref[slot_count : 2 * slot_count] = refs[1][...]
-        packet_ref[2 * slot_count :] = jnp.zeros_like(packet_ref[2 * slot_count :])
-        packet_ref[2 * slot_count : 2 * slot_count + layers, :cols] = refs[2][...] + refs[3][...]
-        total = jnp.where(home_ref[0] == 0, refs[4][...], 0.0)
-        for ref in refs[5:]:
+        refs[-1][:layers] = refs[0][...] + refs[1][...]
+        total = jnp.where(home_ref[0] == 0, refs[2][...], 0.0)
+        for ref in refs[3:-1]:
             total += ref[...]
-        packet_ref[2 * slot_count + layers :, :cols] = total
-
-    return pl.pallas_call(
-        kernel,
-        out_shape=jax.ShapeDtypeStruct((2 * (slot_count + layers), width), jnp.float32),
+        refs[-1][layers:] = total
+
+    return pl.pallas_call(
+        kernel,
+        out_shape=jax.ShapeDtypeStruct((2 * layers, cols), jnp.float32),
         in_specs=[scalar_spec] + [vmem_spec] * len(arrays),
         out_specs=vmem_spec,
         compiler_params=pltpu.CompilerParams(vmem_limit_bytes=8 * 1024 * 1024),
@@ -300,18 +319,18 @@
 def gram_of(grads, act):
     layers, _, cols = act.shape
 
-    def kernel(grad_ref, act_ref, out_ref):
-        for layer in range(layers):
-            out_ref[layer] = product_of(grad_ref[layer], act_ref[layer])
-
-    return pl.pallas_call(
-        kernel,
-        out_shape=jax.ShapeDtypeStruct((layers, grads.shape[2], cols), jnp.float32),
-        in_specs=[vmem_spec] * 2,
+    def kernel(*refs):
+        for layer in range(layers):
+            refs[-1][layer] = product_of(refs[layer][0], refs[-2][layer])
+
+    return pl.pallas_call(
+        kernel,
+        out_shape=jax.ShapeDtypeStruct((layers, grads[0].shape[2], cols), jnp.float32),
+        in_specs=[vmem_spec] * (layers + 1),
         out_specs=vmem_spec,
         compiler_params=pltpu.CompilerParams(vmem_limit_bytes=16 * 1024 * 1024),
         cost_estimate=light,
-    )(grads, act)
+    )(*grads, act)
 
 
 def product_of(grad, act):
@@ -321,27 +340,29 @@
 def finish(grads, act, grams, factors):
     layers, tile, cols = grams.shape
 
-    def kernel(grad_ref, act_ref, gram_ref, factor_ref, out_ref):
-        for layer in range(layers):
-            gram = gram_ref[layer] + product_of(grad_ref[layers + layer], act_ref[layer])
+    def kernel(*refs):
+        grad_refs, (act_ref, gram_ref, factor_ref, out_ref) = refs[:layers], refs[layers:]
+        for layer in range(layers):
+            gram = gram_ref[layer] + product_of(grad_refs[layer][1], act_ref[layer])
             out_ref[layer] = (gram * factor_ref[layer]).astype(jnp.bfloat16)
 
     return pl.pallas_call(
         kernel,
         out_shape=jax.ShapeDtypeStruct((layers, tile, cols), jnp.bfloat16),
-        in_specs=[vmem_spec] * 4,
+        in_specs=[vmem_spec] * (layers + 3),
         out_specs=vmem_spec,
         compiler_params=pltpu.CompilerParams(vmem_limit_bytes=24 * 1024 * 1024),
         cost_estimate=light,
-    )(grads, act, grams, factors)
-
-
-def eigenvalues(scalars, packets, layers, slot_count, n_dp, tile):
+    )(*grads, act, grams, factors)
+
+
+def eigenvalues(scalars, states, packets, n_dp):
     n_own = len(packets)
-    width = packets[0].shape[1]
+    layers, tile = packets[0].shape[0] // 2, packets[0].shape[1]
+    slot_count, width = states[0].shape[0] // 2, states[0].shape[1]
 
     def kernel(scalar_ref, *refs):
-        packet_refs, refs = refs[:n_own], refs[n_own:]
+        state_refs, packet_refs, refs = refs[:n_own], refs[n_own : 2 * n_own], refs[2 * n_own :]
         out_ref, new_act_ref, new_grad_ref, act_full, grad_full = refs
         dp, own = scalar_ref[0], scalar_ref[1]
         total = scalar_ref[2]
@@ -351,11 +372,10 @@
         owners = [scalar_ref[2 + n_dp + layer] for layer in range(layers)]
         for mask in range(n_own):
             at = pl.ds(pl.multiple_of((own ^ mask) * tile, tile), tile)
-            lower = 2 * slot_count + layers
-            act_full[:, at] = packet_refs[mask][2 * slot_count : lower, :tile] / total
-            grad_full[:, at] = packet_refs[mask][lower:, :tile] / total
-        new_act_ref[...] = packet_refs[0][:slot_count]
-        new_grad_ref[...] = packet_refs[0][slot_count : 2 * slot_count]
+            act_full[:, at] = packet_refs[mask][:layers] / total
+            grad_full[:, at] = packet_refs[mask][layers:] / total
+        new_act_ref[...] = state_refs[0][:slot_count]
+        new_grad_ref[...] = state_refs[0][slot_count:]
         for layer in range(layers):
             owner_now = owners[layer]
             rank = jnp.int32(0)
@@ -367,8 +387,8 @@
                 for slot in range(slot_count):
                     here = (owner_now == own ^ mask) & (rank == slot)
                     down = slot_count + slot
-                    old_act = jnp.where(here, packet_refs[mask][slot : slot + 1], old_act)
-                    old_grad = jnp.where(here, packet_refs[mask][down : down + 1], old_grad)
+                    old_act = jnp.where(here, state_refs[mask][slot : slot + 1], old_act)
+                    old_grad = jnp.where(here, state_refs[mask][down : down + 1], old_grad)
             eigen_act = decay_rate * old_act + (1.0 - decay_rate) * act_full[layer : layer + 1]
             eigen_grad = decay_rate * old_grad + (1.0 - decay_rate) * grad_full[layer : layer + 1]
             act_full[layer : layer + 1] = eigen_act
@@ -395,12 +415,12 @@
     return pl.pallas_call(
         kernel,
         out_shape=out_shape,
-        in_specs=[scalar_spec] + [vmem_spec] * n_own,
+        in_specs=[scalar_spec] + [vmem_spec] * (2 * n_own),
         out_specs=[vmem_spec] * len(out_shape),
         scratch_shapes=[pltpu.VMEM((layers, width), jnp.float32)] * 2,
         compiler_params=pltpu.CompilerParams(vmem_limit_bytes=16 * 1024 * 1024),
         cost_estimate=light,
-    )(scalars, *packets)
+    )(scalars, *states, *packets)
 
 
 def line_plan(activations, out_grads, basis_act, basis_grad, owner_of, counts, state_act, state_grad):
@@ -436,7 +456,10 @@
     pieces += [flip(piece, "owner", 1) for piece in pieces]
     keep_act, send_act = project_rows(scalars, activations, pieces, basis_act, n_own, n_dp)
 
-    keep, send, near, far, keep_act, send_act = step([keep, send, near, far, keep_act, send_act])
+    state = after(jnp.concatenate([state_act, state_grad], axis=0), keep)
+    states = [state] + [flip(state, "owner", mask) for mask in range(1, n_own)]
+
+    keep, send, near, far, keep_act, send_act, *states = step([keep, send, near, far, keep_act, send_act, *states])
     part = add((keep, near))
     rest = add((send, far))
     near = hop(part, [((o ^ 2, o), (o, o)) for o in owners])
@@ -446,26 +469,27 @@
     part, rest, near, far, keep_act, near_act = step([part, rest, near, far, keep_act, near_act])
     part_act = add((keep_act, near_act))
     cross_act = flip(part_act, "dp", 2)
-    full = add((after(part, part_act), near), (rest, far))
-    chip = hop(full, [((o, o), (o, o ^ 2)) for o in owners])
-    squares = [squares_of(full, layers)]
+    full = add_by_layer((part, near), (rest, far))
+    chip = [hop(array, [((o, o), (o, o ^ 2)) for o in owners]) for array in full]
+    squares = [squares_of(full, True)]
     squares += [hop(squares[0], [((o, o), (o ^ mask, o)) for o in owners]) for mask in range(1, n_dp)]
 
-    part_act, cross_act, full, chip, *squares = step([part_act, cross_act, full, chip, *squares])
+    done = step([part_act, cross_act, *full, *chip, *squares])
+    (part_act, cross_act), full, chip, squares = done[:2], done[2:][:layers], done[2 + layers :][:layers], done[2 + 2 * layers :]
     full_act = add((part_act, cross_act))
-    halves = [squares_of(full_act, layers)]
+    halves = [squares_of([full_act], False)]
     halves += [flip(halves[0], "dp", 1)]
     home = jnp.where(own == dp, 0, jnp.where(own == dp ^ 2, 1, 2)).astype(jnp.int32)[None]
-    packet = packet_of(home, state_act, state_grad, halves, squares)
+    packet = packet_of(home, halves, squares)
     back_act = flip(after(full_act, packet), "dp", 1)
-    full = pick(home, [after(full, packet), chip])
-    core = hop(full, [((o, o ^ b), (o, o ^ b ^ 1)) for o in owners for b in (0, 2)])
     packets = [packet] + [flip(packet, "owner", mask) for mask in range(1, n_own)]
-    factors, new_act, new_grad = eigenvalues(scalars, packets, layers, state_act.shape[0], n_dp, tile)
-    grads = pick(home // 2, [full, core])
+    full = pick(after(home, *packets), [*zip(full, chip, strict=True)])
+    core = [hop(array, [((o, o ^ b), (o, o ^ b ^ 1)) for o in owners for b in (0, 2)]) for array in full]
+    factors, new_act, new_grad = eigenvalues(scalars, states, packets, n_dp)
+    grads = pick(home // 2, [*zip(full, core, strict=True)])
     grams = gram_of(grads, full_act)
 
-    grads, grams, factors, back_act = step([grads, grams, factors, back_act])
+    grams, factors, back_act, *grads = step([grams, factors, back_act, *grads])
     return finish(grads, back_act, grams, factors), new_act, new_grad
 
 

time: 130 us -> 130 us (level)
  waiting for transfers between devices: 74.5 us -> 63.1 us
  starting transfers between devices: 40.3 us -> 50.6 us
    ppermute x25 -> x28, waiting for transfers between devices: 36.4 us -> 22.8 us  [flip(): lax.ppermute(array, axis, [(i, i ^ mask) for i in range(lax.axis_size(axi...]
    ppermute x9 -> x13, starting transfers between devices: 15.2 us -> 21.4 us  [hop(): return lax.ppermute(array, ('dp', 'owner'), flat)]
    ppermute x25 -> x28, starting transfers between devices: 25.1 us -> 29.2 us  [flip(): lax.ppermute(array, axis, [(i, i ^ mask) for i in range(lax.axis_size(axi...]
    ppermute x9 -> x13, waiting for transfers between devices: 38.1 us -> 40.3 us  [hop(): return lax.ppermute(array, ('dp', 'owner'), flat)]
  transfers between devices with their start and end apart: 34 -> 41, of which waited for: 19 -> 19; matrix products, arithmetic and copies ran while one was open for 0% -> 0% of each run, Pallas kernels for 8% -> 8%
where the time goes in v6:
time: 130 us; the launch traced here: 129 us
  waiting for transfers between devices  63.1 us (49%)
  starting transfers between devices  50.6 us (39%)
  Pallas kernels  14.4 us (11%)
    ppermute x13, waiting for transfers between devices, hop(): return lax.ppermute(array, ('dp', 'owner'), flat)  40.3 us
    ppermute x28, starting transfers between devices, flip(): lax.ppermute(array, axis, [(i, i ^ mask) for i in range(lax.axis_size(axi...  29.2 us
    ppermute x28, waiting for transfers between devices, flip(): lax.ppermute(array, axis, [(i, i ^ mask) for i in range(lax.axis_size(axi...  22.8 us
    ppermute x13, starting transfers between devices, hop(): return lax.ppermute(array, ('dp', 'owner'), flat)  21.4 us
    pallas_call x2, Pallas kernels, project_rows(): pl.pallas_call(kernel, out_shape=[jax.ShapeDtypeStruct(shape, jnp.bfloat1...  7.46 us
  transfers between devices with their start and end apart: 41, of which 19 were waited for; matrix products, arithmetic and copies ran while one was open for 0% of the time, Pallas kernels for 8%

profile of v6, /device:TPU:0, one launch (start us, length us, event | category | flops | bytes accessed | tf_op | source)
XLA Modules:
  0.0 129.1 jit_solution(13118451737295057939)
XLA Ops:
  1.9 5.1 %collective-permute-start.2 = (bf16[3,32,512]{2,1,0:T(8,128)(2,1)S(1)}, bf16[3,32,512]{2,1,0:T(8,128)(2,1)S(1)}, u32[]{:S(2)}, u32[]{:S(2)}) collective-permute-start(bf16[3,32,512]{2,1,0:T(8,128)(2,1)S(1)} %get-tuple-element.67), channel_id=1, source_target_pairs={{0,12},{4,8},{8,4},{12,0},{1,13},{5,9},{9,5},{13,1},{2,14},{6,10},... | collective-permute-start | bytes 294920 | tf_op jit(solution)/shard_map/ppermute | solution.py:89
  7.0 2.0 %collective-permute-start = (bf16[3,32,512]{2,1,0:T(8,128)(2,1)S(1)}, bf16[3,32,512]{2,1,0:T(8,128)(2,1)S(1)}, u32[]{:S(2)}, u32[]{:S(2)}) collective-permute-start(bf16[3,32,512]{2,1,0:T(8,128)(2,1)S(1)} %get-tuple-element.65), channel_id=1, source_target_pairs={{0,4},{4,0},{8,12},{12,8},{1,5},{5,1},{9,13},{13,9},{2,6},{6,2},{1... | collective-permute-start | bytes 294920 | tf_op jit(solution)/shard_map/ppermute | solution.py:89
  9.0 2.9 %collective-permute-start.13 = (bf16[3,32,512]{2,1,0:T(8,128)(2,1)S(1)}, bf16[3,32,512]{2,1,0:T(8,128)(2,1)S(1)}, u32[]{:S(2)}, u32[]{:S(2)}) collective-permute-start(bf16[3,32,512]{2,1,0:T(8,128)(2,1)S(1)} %get-tuple-element.72), channel_id=1, source_target_pairs={{0,8},{4,12},{8,0},{12,4},{1,9},{5,13},{9,1},{13,5},{2,10},{6,14},... | collective-permute-start | bytes 294920 | tf_op jit(solution)/shard_map/ppermute | solution.py:89
  11.9 2.6 %collective-permute-start.14 = (bf16[3,32,512]{2,1,0:T(8,128)(2,1)S(1)}, bf16[3,32,512]{2,1,0:T(8,128)(2,1)S(1)}, u32[]{:S(2)}, u32[]{:S(2)}) collective-permute-start(bf16[3,32,512]{2,1,0:T(8,128)(2,1)S(1)} %get-tuple-element.73), channel_id=1, source_target_pairs={{0,12},{4,8},{8,4},{12,0},{1,13},{5,9},{9,5},{13,1},{2,14},{6,10},... | collective-permute-start | bytes 294920 | tf_op jit(solution)/shard_map/ppermute | solution.py:89
  16.6 1.6 %collective-permute-start.4 = (bf16[3,32,512]{2,1,0:T(8,128)(2,1)S(1)}, bf16[3,32,512]{2,1,0:T(8,128)(2,1)S(1)}, u32[]{:S(2)}, u32[]{:S(2)}) collective-permute-start(bf16[3,32,512]{2,1,0:T(8,128)(2,1)S(1)} %collective-permute-done.refs_0_), channel_id=1, source_target_pairs={{0,2},{1,3},{2,0},{3,1},{4,6},{5,7},{6,4},{7,5},{8,10},{9,11},{10,... | collective-permute-start | bytes 294920 | tf_op jit(solution)/shard_map/ppermute | solution.py:89
  18.2 3.6 %collective-permute-done.1.refs_1_ = bf16[3,32,512]{2,1,0:T(8,128)(2,1)S(1)} collective-permute-done((bf16[3,32,512]{2,1,0:T(8,128)(2,1)S(1)}, bf16[3,32,512]{2,1,0:T(8,128)(2,1)S(1)}, u32[]{:S(2)}, u32[]{:S(2)}) %collective-permute-start.1) | collective-permute-done | bytes 98336 | tf_op jit(solution)/shard_map/ppermute | solution.py:89
  28.2 1.9 %collective-permute-done.6.refs_5_ = bf16[3,32,512]{2,1,0:T(8,128)(2,1)S(1)} collective-permute-done((bf16[3,32,512]{2,1,0:T(8,128)(2,1)S(1)}, bf16[3,32,512]{2,1,0:T(8,128)(2,1)S(1)}, u32[]{:S(2)}, u32[]{:S(2)}) %collective-permute-start.6) | collective-permute-done | bytes 98336 | tf_op jit(solution)/shard_map/ppermute | solution.py:89
  31.4 3.7 %shard_map.104 = (bf16[3,192,512]{2,1,0:T(8,128)(2,1)S(1)}, bf16[3,192,512]{2,1,0:T(8,128)(2,1)S(1)}) custom-call(s32[9]{0:T(128)S(1)} %pad_add_fusion.scalar_ref, bf16[3,128,2048]{2,1,0:T(8,128)(2,1)} %tokens_hbm.2, bf16[3,512,512]{2,1,0:T(8,128)(2,1)} %basis_hbm.2, bf16[3,32,512]{2,1,0:T(8,128)(2,1)S(1)} %collective-permute-done.refs_0_, ...), custom_call_target="tpu_custom_call" | custom-call | tf_op jit(solution)/shard_map/pallas_call | solution.py:152
  41.0 3.7 %shard_map.106 = (bf16[3,192,512]{2,1,0:T(8,128)(2,1)S(1)}, bf16[3,192,512]{2,1,0:T(8,128)(2,1)S(1)}) custom-call(s32[9]{0:T(128)S(1)} %pad_add_fusion.scalar_ref, bf16[3,128,2048]{2,1,0:T(8,128)(2,1)} %tokens_hbm.3, bf16[3,512,512]{2,1,0:T(8,128)(2,1)} %basis_hbm.3, bf16[3,96,512]{2,1,0:T(8,128)(2,1)S(1)} %shard_map.105.refs_0_, ...), custom_call_target="tpu_custom_call" | custom-call | tf_op jit(solution)/shard_map/pallas_call | solution.py:152
  44.8 2.1 %collective-permute-done.15.refs_1_ = bf16[3,192,512]{2,1,0:T(8,128)(2,1)S(1)} collective-permute-done((bf16[3,192,512]{2,1,0:T(8,128)(2,1)S(1)}, bf16[3,192,512]{2,1,0:T(8,128)(2,1)S(1)}, u32[]{:S(2)}, u32[]{:S(2)}) %collective-permute-start.15) | collective-permute-done | bytes 589856 | tf_op jit(solution)/shard_map/ppermute | solution.py:95
  46.9 6.3 %collective-permute-done.16.refs_1_ = bf16[3,192,512]{2,1,0:T(8,128)(2,1)S(1)} collective-permute-done((bf16[3,192,512]{2,1,0:T(8,128)(2,1)S(1)}, bf16[3,192,512]{2,1,0:T(8,128)(2,1)S(1)}, u32[]{:S(2)}, u32[]{:S(2)}) %collective-permute-start.16) | collective-permute-done | bytes 589856 | tf_op jit(solution)/shard_map/ppermute | solution.py:95
  56.2 17.1 %collective-permute-done.24.refs_3_ = bf16[3,192,512]{2,1,0:T(8,128)(2,1)S(1)} collective-permute-done((bf16[3,192,512]{2,1,0:T(8,128)(2,1)S(1)}, bf16[3,192,512]{2,1,0:T(8,128)(2,1)S(1)}, u32[]{:S(2)}, u32[]{:S(2)}) %collective-permute-start.24) | collective-permute-done | bytes 589856 | tf_op jit(solution)/shard_map/ppermute | solution.py:95
  73.3 7.9 %collective-permute-done.23.refs_1_ = bf16[3,192,512]{2,1,0:T(8,128)(2,1)S(1)} collective-permute-done((bf16[3,192,512]{2,1,0:T(8,128)(2,1)S(1)}, bf16[3,192,512]{2,1,0:T(8,128)(2,1)S(1)}, u32[]{:S(2)}, u32[]{:S(2)}) %collective-permute-start.23) | collective-permute-done | bytes 589856 | tf_op jit(solution)/shard_map/ppermute | solution.py:95
  81.4 3.9 %collective-permute-start.26 = (bf16[3,192,512]{2,1,0:T(8,128)(2,1)S(1)}, bf16[3,192,512]{2,1,0:T(8,128)(2,1)S(1)}, u32[]{:S(2)}, u32[]{:S(2)}) collective-permute-start(bf16[3,192,512]{2,1,0:T(8,128)(2,1)S(1)} %shard_map.109.refs_0_), channel_id=1, source_target_pairs={{0,8},{4,12},{8,0},{12,4},{1,9},{5,13},{9,1},{13,5},{2,10},{6,14},... | collective-permute-start | bytes 1769480 | tf_op jit(solution)/shard_map/ppermute | solution.py:89
  85.6 4.2 %collective-permute-start.27 = (bf16[2,192,512]{2,1,0:T(8,128)(2,1)S(1)}, bf16[2,192,512]{2,1,0:T(8,128)(2,1)S(1)}, u32[]{:S(2)}, u32[]{:S(2)}) collective-permute-start(bf16[2,192,512]{2,1,0:T(8,128)(2,1)S(1)} %get-tuple-element.101.refs_0_), channel_id=1, source_target_pairs={{0,2},{5,7},{10,8},{15,13},{16,18},{21,23},{26,24},{31,29}} | collective-permute-start | bytes 1179656 | tf_op jit(solution)/shard_map/ppermute | solution.py:95
  100.6 2.8 %collective-permute-done.29.refs_5_ = bf16[2,192,512]{2,1,0:T(8,128)(2,1)S(1)} collective-permute-done((bf16[2,192,512]{2,1,0:T(8,128)(2,1)S(1)}, bf16[2,192,512]{2,1,0:T(8,128)(2,1)S(1)}, u32[]{:S(2)}, u32[]{:S(2)}) %collective-permute-start.29) | collective-permute-done | bytes 393248 | tf_op jit(solution)/shard_map/ppermute | solution.py:95
  103.4 4.5 %collective-permute-done.26.refs_1_ = bf16[3,192,512]{2,1,0:T(8,128)(2,1)S(1)} collective-permute-done((bf16[3,192,512]{2,1,0:T(8,128)(2,1)S(1)}, bf16[3,192,512]{2,1,0:T(8,128)(2,1)S(1)}, u32[]{:S(2)}, u32[]{:S(2)}) %collective-permute-start.26) | collective-permute-done | bytes 589856 | tf_op jit(solution)/shard_map/ppermute | solution.py:89
  108.2 3.6 %collective-permute-done.33.refs_1_ = f32[3,512]{1,0:T(4,128)S(1)} collective-permute-done((f32[3,512]{1,0:T(4,128)S(1)}, f32[3,512]{1,0:T(4,128)S(1)}, u32[]{:S(2)}, u32[]{:S(2)}) %collective-permute-start.33) | collective-permute-done | bytes 6176 | tf_op jit(solution)/shard_map/ppermute | solution.py:89
  112.0 3.6 %collective-permute-start.35 = (f32[6,512]{1,0:T(8,128)S(1)}, f32[6,512]{1,0:T(8,128)S(1)}, u32[]{:S(2)}, u32[]{:S(2)}) collective-permute-start(f32[6,512]{1,0:T(8,128)S(1)} %shard_map.114.refs_4_), channel_id=1, source_target_pairs={{0,2},{1,3},{2,0},{3,1},{4,6},{5,7},{6,4},{7,5},{8,10},{9,11},{10,... | collective-permute-start | bytes 36872 | tf_op jit(solution)/shard_map/ppermute | solution.py:89
  115.6 1.8 %collective-permute-done.35.refs_6_ = f32[6,512]{1,0:T(8,128)S(1)} collective-permute-done((f32[6,512]{1,0:T(8,128)S(1)}, f32[6,512]{1,0:T(8,128)S(1)}, u32[]{:S(2)}, u32[]{:S(2)}) %collective-permute-start.35) | collective-permute-done | bytes 12320 | tf_op jit(solution)/shard_map/ppermute | solution.py:89
  117.5 2.9 %collective-permute-start.37 = (bf16[2,192,512]{2,1,0:T(8,128)(2,1)S(1)}, bf16[2,192,512]{2,1,0:T(8,128)(2,1)S(1)}, u32[]{:S(2)}, u32[]{:S(2)}) collective-permute-start(bf16[2,192,512]{2,1,0:T(8,128)(2,1)S(1)} %get-tuple-element.107.refs_0_), channel_id=1, source_target_pairs={{0,1},{2,3},{5,4},{7,6},{10,11},{8,9},{15,14},{13,12},{16,17},{18,... | collective-permute-start | bytes 1179656 | tf_op jit(solution)/shard_map/ppermute | solution.py:95
  123.1 1.9 %shard_map.118 = (f32[3,512,512]{2,1,0:T(8,128)S(1)}, f32[2,2048]{1,0:T(2,128)}, f32[2,2048]{1,0:T(2,128)}) custom-call(s32[9]{0:T(128)S(1)} %pad_add_fusion.scalar_ref, f32[4,2048]{1,0:T(4,128)S(1)} %pad_maximum_fusion.refs_0_, f32[4,2048]{1,0:T(4,128)S(1)} %collective-permute-done.20.refs_1_, f32[4,2048]{1,0:T(4,128)S(1)} %collective-permute-done.21.refs_2_, ...), custom_call_target="tpu_custom_call" | custom-call | tf_op jit(solution)/shard_map/pallas_call | solution.py:415
  125.8 1.6 %collective-permute-done.40.refs_3_ = bf16[3,192,512]{2,1,0:T(8,128)(2,1)S(1)} collective-permute-done((bf16[3,192,512]{2,1,0:T(8,128)(2,1)S(1)}, bf16[3,192,512]{2,1,0:T(8,128)(2,1)S(1)}, u32[]{:S(2)}, u32[]{:S(2)}) %collective-permute-start.40) | collective-permute-done | bytes 589856 | tf_op jit(solution)/shard_map/ppermute | solution.py:89
  127.4 1.8 %shard_map.119 = bf16[3,512,512]{2,1,0:T(8,128)(2,1)} custom-call(bf16[2,192,512]{2,1,0:T(8,128)(2,1)S(1)} %get-tuple-element.119.refs_0_, bf16[2,192,512]{2,1,0:T(8,128)(2,1)S(1)} %get-tuple-element.120.refs_1_, bf16[2,192,512]{2,1,0:T(8,128)(2,1)S(1)} %get-tuple-element.121.refs_2_, bf16[3,192,512]{2,1,0:T(8,128)(2,1)S(1)} %collective-permute-done.40.refs_3_, ...), custom_call_target="tpu_custom_call" | custom-call | tf_op jit(solution)/shard_map/pallas_call | solution.py:349
  (85 shorter events, 34.8 us)
Async XLA Ops:
  1.9 10.1 %collective-permute-start.2 = (bf16[3,32,512]{2,1,0:T(8,128)(2,1)S(1)}, bf16[3,32,512]{2,1,0:T(8,128)(2,1)S(1)}, u32[]{:S(2)}, u32[]{:S(2)}) collective-permute-start(bf16[3,32,512]{2,1,0:T(8,128)(2,1)S(1)} %get-tuple-element.67), channel_id=1, source_target_pairs={{0,12},{4,8},{8,4},{12,0},{1,13},{5,9},{9,5},{13,1},{2,14},{6,10},... | collective-permute-start | bytes 294920 | tf_op jit(solution)/shard_map/ppermute | solution.py:89
  7.0 8.2 %collective-permute-start.3 = (bf16[3,32,512]{2,1,0:T(8,128)(2,1)S(1)}, bf16[3,32,512]{2,1,0:T(8,128)(2,1)S(1)}, u32[]{:S(2)}, u32[]{:S(2)}) collective-permute-start(bf16[3,32,512]{2,1,0:T(8,128)(2,1)S(1)} %get-tuple-element.68), channel_id=1, source_target_pairs={{0,4},{4,0},{8,12},{12,8},{1,5},{5,1},{9,13},{13,9},{2,6},{6,2},{1... | collective-permute-start | bytes 294920 | tf_op jit(solution)/shard_map/ppermute | solution.py:89
  7.0 9.6 %collective-permute-start = (bf16[3,32,512]{2,1,0:T(8,128)(2,1)S(1)}, bf16[3,32,512]{2,1,0:T(8,128)(2,1)S(1)}, u32[]{:S(2)}, u32[]{:S(2)}) collective-permute-start(bf16[3,32,512]{2,1,0:T(8,128)(2,1)S(1)} %get-tuple-element.65), channel_id=1, source_target_pairs={{0,4},{4,0},{8,12},{12,8},{1,5},{5,1},{9,13},{13,9},{2,6},{6,2},{1... | collective-permute-start | bytes 294920 | tf_op jit(solution)/shard_map/ppermute | solution.py:89
  9.0 12.8 %collective-permute-start.1 = (bf16[3,32,512]{2,1,0:T(8,128)(2,1)S(1)}, bf16[3,32,512]{2,1,0:T(8,128)(2,1)S(1)}, u32[]{:S(2)}, u32[]{:S(2)}) collective-permute-start(bf16[3,32,512]{2,1,0:T(8,128)(2,1)S(1)} %get-tuple-element.66), channel_id=1, source_target_pairs={{0,8},{4,12},{8,0},{12,4},{1,9},{5,13},{9,1},{13,5},{2,10},{6,14},... | collective-permute-start | bytes 294920 | tf_op jit(solution)/shard_map/ppermute | solution.py:89
  9.0 14.1 %collective-permute-start.13 = (bf16[3,32,512]{2,1,0:T(8,128)(2,1)S(1)}, bf16[3,32,512]{2,1,0:T(8,128)(2,1)S(1)}, u32[]{:S(2)}, u32[]{:S(2)}) collective-permute-start(bf16[3,32,512]{2,1,0:T(8,128)(2,1)S(1)} %get-tuple-element.72), channel_id=1, source_target_pairs={{0,8},{4,12},{8,0},{12,4},{1,9},{5,13},{9,1},{13,5},{2,10},{6,14},... | collective-permute-start | bytes 294920 | tf_op jit(solution)/shard_map/ppermute | solution.py:89
  11.9 12.7 %collective-permute-start.14 = (bf16[3,32,512]{2,1,0:T(8,128)(2,1)S(1)}, bf16[3,32,512]{2,1,0:T(8,128)(2,1)S(1)}, u32[]{:S(2)}, u32[]{:S(2)}) collective-permute-start(bf16[3,32,512]{2,1,0:T(8,128)(2,1)S(1)} %get-tuple-element.73), channel_id=1, source_target_pairs={{0,12},{4,8},{8,4},{12,0},{1,13},{5,9},{9,5},{13,1},{2,14},{6,10},... | collective-permute-start | bytes 294920 | tf_op jit(solution)/shard_map/ppermute | solution.py:89
  16.6 8.6 %collective-permute-start.7 = (bf16[3,32,512]{2,1,0:T(8,128)(2,1)S(1)}, bf16[3,32,512]{2,1,0:T(8,128)(2,1)S(1)}, u32[]{:S(2)}, u32[]{:S(2)}) collective-permute-start(bf16[3,32,512]{2,1,0:T(8,128)(2,1)S(1)} %collective-permute-done.refs_0_), channel_id=1, source_target_pairs={{0,1},{1,0},{2,3},{3,2},{4,5},{5,4},{6,7},{7,6},{8,9},{9,8},{10,11... | collective-permute-start | bytes 294920 | tf_op jit(solution)/shard_map/ppermute | solution.py:89
  16.6 8.7 %collective-permute-start.4 = (bf16[3,32,512]{2,1,0:T(8,128)(2,1)S(1)}, bf16[3,32,512]{2,1,0:T(8,128)(2,1)S(1)}, u32[]{:S(2)}, u32[]{:S(2)}) collective-permute-start(bf16[3,32,512]{2,1,0:T(8,128)(2,1)S(1)} %collective-permute-done.refs_0_), channel_id=1, source_target_pairs={{0,2},{1,3},{2,0},{3,1},{4,6},{5,7},{6,4},{7,5},{8,10},{9,11},{10,... | collective-permute-start | bytes 294920 | tf_op jit(solution)/shard_map/ppermute | solution.py:89
  24.6 5.5 %collective-permute-start.6 = (bf16[3,32,512]{2,1,0:T(8,128)(2,1)S(1)}, bf16[3,32,512]{2,1,0:T(8,128)(2,1)S(1)}, u32[]{:S(2)}, u32[]{:S(2)}) collective-permute-start(bf16[3,32,512]{2,1,0:T(8,128)(2,1)S(1)} %collective-permute-done.2.refs_2_), channel_id=1, source_target_pairs={{0,2},{1,3},{2,0},{3,1},{4,6},{5,7},{6,4},{7,5},{8,10},{9,11},{10,... | collective-permute-start | bytes 294920 | tf_op jit(solution)/shard_map/ppermute | solution.py:89
  25.3 12.7 %collective-permute-start.17 = (bf16[3,96,512]{2,1,0:T(8,128)(2,1)S(1)}, bf16[3,96,512]{2,1,0:T(8,128)(2,1)S(1)}, u32[]{:S(2)}, u32[]{:S(2)}) collective-permute-start(bf16[3,96,512]{2,1,0:T(8,128)(2,1)S(1)} %shard_map.105.refs_0_), channel_id=1, source_target_pairs={{0,2},{1,3},{2,0},{3,1},{4,6},{5,7},{6,4},{7,5},{8,10},{9,11},{10,... | collective-permute-start | bytes 884744 | tf_op jit(solution)/shard_map/ppermute | solution.py:89
  35.1 11.8 %collective-permute-start.15 = (bf16[3,192,512]{2,1,0:T(8,128)(2,1)S(1)}, bf16[3,192,512]{2,1,0:T(8,128)(2,1)S(1)}, u32[]{:S(2)}, u32[]{:S(2)}) collective-permute-start(bf16[3,192,512]{2,1,0:T(8,128)(2,1)S(1)} %get-tuple-element.81.refs_0_), channel_id=1, source_target_pairs={{4,0},{1,5},{14,10},{11,15},{2,6},{3,7},{6,2},{7,3},{8,12},{9,13},... | collective-permute-start | bytes 1769480 | tf_op jit(solution)/shard_map/ppermute | solution.py:95
  36.4 16.8 %collective-permute-start.16 = (bf16[3,192,512]{2,1,0:T(8,128)(2,1)S(1)}, bf16[3,192,512]{2,1,0:T(8,128)(2,1)S(1)}, u32[]{:S(2)}, u32[]{:S(2)}) collective-permute-start(bf16[3,192,512]{2,1,0:T(8,128)(2,1)S(1)} %get-tuple-element.79.refs_0_), channel_id=1, source_target_pairs={{4,0},{1,5},{14,10},{11,15},{20,16},{17,21},{30,26},{27,31}} | collective-permute-start | bytes 1769480 | tf_op jit(solution)/shard_map/ppermute | solution.py:95
  38.3 6.4 %collective-permute-start.22 = (f32[4,2048]{1,0:T(4,128)S(1)}, f32[4,2048]{1,0:T(4,128)S(1)}, u32[]{:S(2)}, u32[]{:S(2)}) collective-permute-start(f32[4,2048]{1,0:T(4,128)S(1)} %pad_maximum_fusion.refs_0_), channel_id=1, source_target_pairs={{0,3},{1,2},{2,1},{3,0},{4,7},{5,6},{6,5},{7,4},{8,11},{9,10},{10,... | collective-permute-start | bytes 98312 | tf_op jit(solution)/shard_map/ppermute | solution.py:89
  39.7 5.0 %collective-permute-start.21 = (f32[4,2048]{1,0:T(4,128)S(1)}, f32[4,2048]{1,0:T(4,128)S(1)}, u32[]{:S(2)}, u32[]{:S(2)}) collective-permute-start(f32[4,2048]{1,0:T(4,128)S(1)} %pad_maximum_fusion.refs_0_), channel_id=1, source_target_pairs={{0,2},{1,3},{2,0},{3,1},{4,6},{5,7},{6,4},{7,5},{8,10},{9,11},{10,... | collective-permute-start | bytes 98312 | tf_op jit(solution)/shard_map/ppermute | solution.py:89
  53.4 20.0 %collective-permute-start.24 = (bf16[3,192,512]{2,1,0:T(8,128)(2,1)S(1)}, bf16[3,192,512]{2,1,0:T(8,128)(2,1)S(1)}, u32[]{:S(2)}, u32[]{:S(2)}) collective-permute-start(bf16[3,192,512]{2,1,0:T(8,128)(2,1)S(1)} %shard_map.107.refs_0_), channel_id=1, source_target_pairs={{12,0},{9,5},{6,10},{3,15},{28,16},{25,21},{22,26},{19,31}} | collective-permute-start | bytes 1769480 | tf_op jit(solution)/shard_map/ppermute | solution.py:95
  54.7 26.6 %collective-permute-start.23 = (bf16[3,192,512]{2,1,0:T(8,128)(2,1)S(1)}, bf16[3,192,512]{2,1,0:T(8,128)(2,1)S(1)}, u32[]{:S(2)}, u32[]{:S(2)}) collective-permute-start(bf16[3,192,512]{2,1,0:T(8,128)(2,1)S(1)} %shard_map.107.refs_0_), channel_id=1, source_target_pairs={{8,0},{13,5},{2,10},{7,15},{24,16},{29,21},{18,26},{23,31}} | collective-permute-start | bytes 1769480 | tf_op jit(solution)/shard_map/ppermute | solution.py:95
  56.0 25.3 %collective-permute-start.25 = (bf16[3,192,512]{2,1,0:T(8,128)(2,1)S(1)}, bf16[3,192,512]{2,1,0:T(8,128)(2,1)S(1)}, u32[]{:S(2)}, u32[]{:S(2)}) collective-permute-start(bf16[3,192,512]{2,1,0:T(8,128)(2,1)S(1)} %get-tuple-element.84), channel_id=1, source_target_pairs={{0,4},{4,0},{8,12},{12,8},{1,5},{5,1},{9,13},{13,9},{2,6},{6,2},{1... | collective-permute-start | bytes 1769480 | tf_op jit(solution)/shard_map/ppermute | solution.py:89
  81.4 26.5 %collective-permute-start.26 = (bf16[3,192,512]{2,1,0:T(8,128)(2,1)S(1)}, bf16[3,192,512]{2,1,0:T(8,128)(2,1)S(1)}, u32[]{:S(2)}, u32[]{:S(2)}) collective-permute-start(bf16[3,192,512]{2,1,0:T(8,128)(2,1)S(1)} %shard_map.109.refs_0_), channel_id=1, source_target_pairs={{0,8},{4,12},{8,0},{12,4},{1,9},{5,13},{9,1},{13,5},{2,10},{6,14},... | collective-permute-start | bytes 1769480 | tf_op jit(solution)/shard_map/ppermute | solution.py:89
  85.6 15.1 %collective-permute-start.27 = (bf16[2,192,512]{2,1,0:T(8,128)(2,1)S(1)}, bf16[2,192,512]{2,1,0:T(8,128)(2,1)S(1)}, u32[]{:S(2)}, u32[]{:S(2)}) collective-permute-start(bf16[2,192,512]{2,1,0:T(8,128)(2,1)S(1)} %get-tuple-element.101.refs_0_), channel_id=1, source_target_pairs={{0,2},{5,7},{10,8},{15,13},{16,18},{21,23},{26,24},{31,29}} | collective-permute-start | bytes 1179656 | tf_op jit(solution)/shard_map/ppermute | solution.py:95
  89.7 10.9 %collective-permute-start.28 = (bf16[2,192,512]{2,1,0:T(8,128)(2,1)S(1)}, bf16[2,192,512]{2,1,0:T(8,128)(2,1)S(1)}, u32[]{:S(2)}, u32[]{:S(2)}) collective-permute-start(bf16[2,192,512]{2,1,0:T(8,128)(2,1)S(1)} %get-tuple-element.103.refs_1_.refs_2_), channel_id=1, source_target_pairs={{0,2},{5,7},{10,8},{15,13},{16,18},{21,23},{26,24},{31,29}} | collective-permute-start | bytes 1179656 | tf_op jit(solution)/shard_map/ppermute | solution.py:95
  91.0 12.4 %collective-permute-start.29 = (bf16[2,192,512]{2,1,0:T(8,128)(2,1)S(1)}, bf16[2,192,512]{2,1,0:T(8,128)(2,1)S(1)}, u32[]{:S(2)}, u32[]{:S(2)}) collective-permute-start(bf16[2,192,512]{2,1,0:T(8,128)(2,1)S(1)} %get-tuple-element.105.refs_2_.refs_4_), channel_id=1, source_target_pairs={{0,2},{5,7},{10,8},{15,13},{16,18},{21,23},{26,24},{31,29}} | collective-permute-start | bytes 1179656 | tf_op jit(solution)/shard_map/ppermute | solution.py:95
  111.8 15.6 %collective-permute-start.40 = (bf16[3,192,512]{2,1,0:T(8,128)(2,1)S(1)}, bf16[3,192,512]{2,1,0:T(8,128)(2,1)S(1)}, u32[]{:S(2)}, u32[]{:S(2)}) collective-permute-start(bf16[3,192,512]{2,1,0:T(8,128)(2,1)S(1)} %shard_map.112.refs_0_.refs_3_), channel_id=1, source_target_pairs={{0,4},{4,0},{8,12},{12,8},{1,5},{5,1},{9,13},{13,9},{2,6},{6,2},{1... | collective-permute-start | bytes 1769480 | tf_op jit(solution)/shard_map/ppermute | solution.py:89
  112.0 5.5 %collective-permute-start.35 = (f32[6,512]{1,0:T(8,128)S(1)}, f32[6,512]{1,0:T(8,128)S(1)}, u32[]{:S(2)}, u32[]{:S(2)}) collective-permute-start(f32[6,512]{1,0:T(8,128)S(1)} %shard_map.114.refs_4_), channel_id=1, source_target_pairs={{0,2},{1,3},{2,0},{3,1},{4,6},{5,7},{6,4},{7,5},{8,10},{9,11},{10,... | collective-permute-start | bytes 36872 | tf_op jit(solution)/shard_map/ppermute | solution.py:89
  117.5 7.5 %collective-permute-start.37 = (bf16[2,192,512]{2,1,0:T(8,128)(2,1)S(1)}, bf16[2,192,512]{2,1,0:T(8,128)(2,1)S(1)}, u32[]{:S(2)}, u32[]{:S(2)}) collective-permute-start(bf16[2,192,512]{2,1,0:T(8,128)(2,1)S(1)} %get-tuple-element.107.refs_0_), channel_id=1, source_target_pairs={{0,1},{2,3},{5,4},{7,6},{10,11},{8,9},{15,14},{13,12},{16,17},{18,... | collective-permute-start | bytes 1179656 | tf_op jit(solution)/shard_map/ppermute | solution.py:95
  (21 other events, 130.8 us)

commit v7 on v6

--- a/solution.py
+++ b/solution.py
@@ -152,7 +152,7 @@
     return pl.pallas_call(
         kernel,
         out_shape=[jax.ShapeDtypeStruct(shape, jnp.bfloat16) for shape in shapes],
-        in_specs=[scalar_spec] + [pl.BlockSpec(memory_space=pltpu.HBM)] * 2 + [vmem_spec] * len(pieces),
+        in_specs=[scalar_spec] + [pl.BlockSpec(memory_space=pltpu.HBM), pl.BlockSpec(memory_space=pl.ANY)] + [vmem_spec] * len(pieces),
         out_specs=[vmem_spec] * len(shapes),
         scratch_shapes=[
             pltpu.VMEM((layers, tok_rows, tile), jnp.bfloat16),
@@ -161,7 +161,7 @@
         ],
         compiler_params=pltpu.CompilerParams(vmem_limit_bytes=16 * 1024 * 1024),
         cost_estimate=light,
-    )(scalars, *[pltpu.with_memory_space_constraint(array, pltpu.HBM) for array in (tokens, basis)], *pieces)
+    )(scalars, pltpu.with_memory_space_constraint(tokens, pltpu.HBM), basis, *pieces)
 
 
 def add(*pairs):
@@ -183,24 +183,47 @@
     )(*[array for pair in pairs for array in pair])
 
 
-def add_by_layer(*pairs):
+def add_rows(pairs, cut=None):
     layers, height, cols = pairs[0][0].shape
-
-    def kernel(*refs):
-        in_refs, out_refs = refs[: 2 * len(pairs)], refs[2 * len(pairs) :]
-        for layer in range(layers):
-            for number in range(len(pairs)):
-                near, far = [ref[layer].astype(jnp.float32) for ref in in_refs[2 * number : 2 * number + 2]]
-                out_refs[layer][number] = (near + far).astype(out_refs[layer].dtype)
-
-    return pl.pallas_call(
-        kernel,
-        out_shape=[jax.ShapeDtypeStruct((len(pairs), height, cols), pairs[0][0].dtype)] * layers,
+    spans = [(0, cut), (cut, height)] if cut else [(n * height, (n + 1) * height) for n in range(len(pairs))]
+
+    def kernel(*refs):
+        out_refs = refs[2 * len(pairs) :]
+        for number, (start, stop) in enumerate(spans):
+            if cut:
+                total = refs[0][:, start:stop].astype(jnp.float32) + refs[1][:, start:stop].astype(jnp.float32)
+                out_refs[number][...] = total.astype(out_refs[number].dtype)
+            else:
+                total = refs[2 * number][...].astype(jnp.float32) + refs[2 * number + 1][...].astype(jnp.float32)
+                out_refs[0][:, start:stop] = total.astype(out_refs[0].dtype)
+
+    heights = [stop - start for start, stop in spans] if cut else [spans[-1][1]]
+    return pl.pallas_call(
+        kernel,
+        out_shape=[jax.ShapeDtypeStruct((layers, rows, cols), pairs[0][0].dtype) for rows in heights],
         in_specs=[vmem_spec] * (2 * len(pairs)),
+        out_specs=[vmem_spec] * len(heights),
+        compiler_params=pltpu.CompilerParams(vmem_limit_bytes=8 * 1024 * 1024),
+        cost_estimate=light,
+    )(*[array for pair in pairs for array in pair])
+
+
+def by_layer(near, far):
+    layers, height, cols = near.shape
+
+    def kernel(near_ref, far_ref, *out_refs):
+        for layer, out_ref in enumerate(out_refs):
+            out_ref[0] = near_ref[layer]
+            out_ref[1] = far_ref[layer]
+
+    return pl.pallas_call(
+        kernel,
+        out_shape=[jax.ShapeDtypeStruct((2, height, cols), near.dtype)] * layers,
+        in_specs=[vmem_spec] * 2,
         out_specs=[vmem_spec] * layers,
         compiler_params=pltpu.CompilerParams(vmem_limit_bytes=8 * 1024 * 1024),
         cost_estimate=light,
-    )(*[array for pair in pairs for array in pair])
+    )(near, far)
 
 
 def join(arrays):
@@ -274,46 +297,54 @@
     )(home, *flat)
 
 
-def squares_of(panels, by_layer):
-    layers = len(panels) if by_layer else panels[0].shape[0]
-    cols = panels[0].shape[2]
-
-    def kernel(*refs):
+def squares_of(aside, panel):
+    layers, _, cols = panel.shape
+
+    def kernel(aside_ref, panel_ref, out_ref):
         for layer in range(layers):
-            parts = [refs[layer][at] for at in range(panels[0].shape[0])] if by_layer else [refs[0][layer]]
-            wide = [part.astype(jnp.float32) for part in parts]
-            total = sum(part * part for part in wide)
-            refs[-1][layer : layer + 1] = jnp.sum(total, axis=0, keepdims=True)
+            wide = panel_ref[layer].astype(jnp.float32)
+            total = jnp.sum(wide * wide, axis=0, keepdims=True)
+            out_ref[layer : layer + 1] = jnp.where(aside_ref[0] == 0, total, 0.0)
 
     return pl.pallas_call(
         kernel,
         out_shape=jax.ShapeDtypeStruct((layers, cols), jnp.float32),
-        in_specs=[vmem_spec] * len(panels),
+        in_specs=[scalar_spec, vmem_spec],
         out_specs=vmem_spec,
         compiler_params=pltpu.CompilerParams(vmem_limit_bytes=8 * 1024 * 1024),
         cost_estimate=light,
-    )(*panels)
-
-
-def packet_of(home, act_halves, grads):
-    layers, cols = grads[0].shape
-    arrays = [*act_halves, *grads]
-
-    def kernel(home_ref, *refs):
-        refs[-1][:layers] = refs[0][...] + refs[1][...]
-        total = jnp.where(home_ref[0] == 0, refs[2][...], 0.0)
-        for ref in refs[3:-1]:
-            total += ref[...]
-        refs[-1][layers:] = total
+    )(aside, panel)
+
+
+def total_of(arrays):
+    def kernel(*refs):
+        refs[-1][...] = (refs[0][...] + refs[1][...]) + (refs[2][...] + refs[3][...])
+
+    return pl.pallas_call(
+        kernel,
+        out_shape=jax.ShapeDtypeStruct(arrays[0].shape, arrays[0].dtype),
+        in_specs=[vmem_spec] * len(arrays),
+        out_specs=vmem_spec,
+        compiler_params=pltpu.CompilerParams(vmem_limit_bytes=4 * 1024 * 1024),
+        cost_estimate=light,
+    )(*arrays)
+
+
+def packet_of(acts, grad):
+    layers, cols = grad.shape
+
+    def kernel(near_ref, far_ref, grad_ref, out_ref):
+        out_ref[:layers] = near_ref[...] + far_ref[...]
+        out_ref[layers:] = grad_ref[...]
 
     return pl.pallas_call(
         kernel,
         out_shape=jax.ShapeDtypeStruct((2 * layers, cols), jnp.float32),
-        in_specs=[scalar_spec] + [vmem_spec] * len(arrays),
-        out_specs=vmem_spec,
-        compiler_params=pltpu.CompilerParams(vmem_limit_bytes=8 * 1024 * 1024),
-        cost_estimate=light,
-    )(home, *arrays)
+        in_specs=[vmem_spec] * 3,
+        out_specs=vmem_spec,
+        compiler_params=pltpu.CompilerParams(vmem_limit_bytes=4 * 1024 * 1024),
+        cost_estimate=light,
+    )(*acts, grad)
 
 
 def gram_of(grads, act):
@@ -373,6 +404,7 @@
         for mask in range(n_own):
             at = pl.ds(pl.multiple_of((own ^ mask) * tile, tile), tile)
             act_full[:, at] = packet_refs[mask][:layers] / total
+            at = pl.ds(pl.multiple_of((n_own - (own ^ mask)) % n_own * tile, tile), tile)
             grad_full[:, at] = packet_refs[mask][layers:] / total
         new_act_ref[...] = state_refs[0][:slot_count]
         new_grad_ref[...] = state_refs[0][slot_count:]
@@ -438,53 +470,59 @@
     def step(arrays, *others):
         return lax.optimization_barrier((*arrays, *others))[: len(arrays)]
 
+    owners = range(n_own)
+    held = [-o % n_own for o in owners]
     cuts = cut_rows((out_grads, activations), tile, n_own, n_dp)
     cuts = [flip(cut, "dp", number % (n_dp - 1) + 1) for number, cut in enumerate(cuts)]
     got_grad, got_act = cuts[: n_dp - 1], cuts[n_dp - 1 :]
     pieces = got_grad[:-1] + [after(got_grad[-1], got_act[0])]
     pieces += [flip(piece, "owner", 2) for piece in pieces]
     pieces += [flip(piece, "owner", 1) for piece in pieces]
-    keep, send = project_rows(scalars, out_grads, pieces, basis_grad, n_own, n_dp)
-
-    owners = range(n_own)
-    to_home = [((o ^ 1, o), (o, o)) for o in owners]
-    swaps = [((a, o), (a ^ 1, o)) for a in range(n_dp) for o in owners if (a ^ o) & 2]
-    near = hop(after(send, *got_act), to_home + swaps)
-    far = hop(after(keep, *got_act), to_home)
+    stay = pltpu.with_memory_space_constraint(basis_grad, pltpu.HBM)
+    keep, send = project_rows(scalars, out_grads, pieces, stay, n_own, n_dp)
+
+    near = flip(after(send, *got_act), "dp", 1)
     pieces = [join(got_act)]
     pieces += [flip(pieces[0], "owner", 2)]
     pieces += [flip(piece, "owner", 1) for piece in pieces]
-    keep_act, send_act = project_rows(scalars, activations, pieces, basis_act, n_own, n_dp)
+    stay = pltpu.with_memory_space_constraint(basis_act, pltpu.HBM)
+    keep_act, send_act = project_rows(scalars, activations, pieces, stay, n_own, n_dp)
 
     state = after(jnp.concatenate([state_act, state_grad], axis=0), keep)
     states = [state] + [flip(state, "owner", mask) for mask in range(1, n_own)]
 
-    keep, send, near, far, keep_act, send_act, *states = step([keep, send, near, far, keep_act, send_act, *states])
-    part = add((keep, near))
-    rest = add((send, far))
-    near = hop(part, [((o ^ 2, o), (o, o)) for o in owners])
-    far = hop(part, [((o ^ 3, o), (o, o)) for o in owners])
+    keep, near, keep_act, send_act, *states = step([keep, near, keep_act, send_act, *states])
+    parts = add_rows([(keep, near)], keep.shape[1] // 2)
+    parts = [lax.ppermute(array, "owner", [*enumerate(held)]) for array in parts]
+    to_pair = [((a, o), (a ^ 2, o)) for a in range(n_dp) for o in owners if (a ^ held[o]) & 2]
+    crosses = [hop(array, to_pair) for array in parts]
     near_act = flip(send_act, "dp", 1)
 
-    part, rest, near, far, keep_act, near_act = step([part, rest, near, far, keep_act, near_act])
-    part_act = add((keep_act, near_act))
+    (near,) = add_rows([*zip(parts, crosses, strict=True)])
+    aside = ((dp ^ (-own % n_own)) // 2).astype(jnp.int32)[None]
+    squares = [squares_of(aside, near)]
+    squares += [flip(squares[0], "dp", mask) for mask in range(1, n_dp)]
+    square_grad = total_of(squares)
+    far = hop(after(near, square_grad), [((held[o] ^ 1, o), (held[o], o)) for o in owners])
+    full = by_layer(near, far)
+    chip = [hop(array, [((held[o], o), (held[o], o ^ 2)) for o in owners]) for array in full]
+
+    part_act = add((keep_act, after(near_act, square_grad)))
     cross_act = flip(part_act, "dp", 2)
-    full = add_by_layer((part, near), (rest, far))
-    chip = [hop(array, [((o, o), (o, o ^ 2)) for o in owners]) for array in full]
-    squares = [squares_of(full, True)]
-    squares += [hop(squares[0], [((o, o), (o ^ mask, o)) for o in owners]) for mask in range(1, n_dp)]
-
-    done = step([part_act, cross_act, *full, *chip, *squares])
-    (part_act, cross_act), full, chip, squares = done[:2], done[2:][:layers], done[2 + layers :][:layers], done[2 + 2 * layers :]
+
+    done = step([part_act, cross_act, *full, *chip])
+    (part_act, cross_act), full, chip = done[:2], done[2:][:layers], done[2 + layers :]
     full_act = add((part_act, cross_act))
-    halves = [squares_of([full_act], False)]
+    halves = [squares_of(aside * 0, full_act)]
     halves += [flip(halves[0], "dp", 1)]
-    home = jnp.where(own == dp, 0, jnp.where(own == dp ^ 2, 1, 2)).astype(jnp.int32)[None]
-    packet = packet_of(home, halves, squares)
+    packet = packet_of(halves, square_grad)
     back_act = flip(after(full_act, packet), "dp", 1)
     packets = [packet] + [flip(packet, "owner", mask) for mask in range(1, n_own)]
+    source = -dp % n_own
+    home = jnp.where(own == source, 0, jnp.where(own == source ^ 2, 1, 2)).astype(jnp.int32)[None]
     full = pick(after(home, *packets), [*zip(full, chip, strict=True)])
-    core = [hop(array, [((o, o ^ b), (o, o ^ b ^ 1)) for o in owners for b in (0, 2)]) for array in full]
+    to_core = [((held[o], o ^ b), (held[o], o ^ b ^ 1)) for o in owners for b in (0, 2)]
+    core = [hop(array, to_core) for array in full]
     factors, new_act, new_grad = eigenvalues(scalars, states, packets, n_dp)
     grads = pick(home // 2, [*zip(full, core, strict=True)])
     grams = gram_of(grads, full_act)

time: 130 us -> 127 us (0.977)
  starting transfers between devices: 50.6 us -> 46.1 us
  waiting for transfers between devices: 63.1 us -> 65 us
    ppermute x28 -> x32, waiting for transfers between devices: 22.8 us -> 37.7 us  [flip(): lax.ppermute(array, axis, [(i, i ^ mask) for i in range(lax.axis_size(axi...]
    ppermute x13 -> x9, waiting for transfers between devices: 40.3 us -> 27.3 us  [hop(): return lax.ppermute(array, ('dp', 'owner'), flat)]
    ppermute x13 -> x9, starting transfers between devices: 21.4 us -> 12.1 us  [hop(): return lax.ppermute(array, ('dp', 'owner'), flat)]
    ppermute x28 -> x32, starting transfers between devices: 29.2 us -> 32.7 us  [flip(): lax.ppermute(array, axis, [(i, i ^ mask) for i in range(lax.axis_size(axi...]
    ppermute x0 -> x2, starting transfers between devices: none -> 1.36 us  [line_plan(): lax.ppermute(array, 'owner', [*enumerate(held)])]
  transfers between devices with their start and end apart: 41 -> 43, of which waited for: 19 -> 15; matrix products, arithmetic and copies ran while one was open for 0% -> 0% of each run, Pallas kernels for 8% -> 9%
where the time goes in v7:
time: 127 us
  waiting for transfers between devices  65 us (51%)
  starting transfers between devices  46.1 us (36%)
  Pallas kernels  14.1 us (11%)
    ppermute x32, waiting for transfers between devices, flip(): lax.ppermute(array, axis, [(i, i ^ mask) for i in range(lax.axis_size(axi...  37.7 us
    ppermute x32, starting transfers between devices, flip(): lax.ppermute(array, axis, [(i, i ^ mask) for i in range(lax.axis_size(axi...  32.7 us
    ppermute x9, waiting for transfers between devices, hop(): return lax.ppermute(array, ('dp', 'owner'), flat)  27.3 us
    ppermute x9, starting transfers between devices, hop(): return lax.ppermute(array, ('dp', 'owner'), flat)  12.1 us
    pallas_call x2, Pallas kernels, project_rows(): pl.pallas_call(kernel, out_shape=[jax.ShapeDtypeStruct(shape, jnp.bfloat1...  7.46 us
  transfers between devices with their start and end apart: 43, of which 15 were waited for; matrix products, arithmetic and copies ran while one was open for 0% of the time, Pallas kernels for 9%

profile of v7, /device:TPU:0, one launch (start us, length us, event | category | flops | bytes accessed | tf_op | source)
XLA Modules:
  0.0 126.6 jit_solution(13060091162024951147)
XLA Ops:
  1.9 5.1 %collective-permute-start.2 = (bf16[3,32,512]{2,1,0:T(8,128)(2,1)S(1)}, bf16[3,32,512]{2,1,0:T(8,128)(2,1)S(1)}, u32[]{:S(2)}, u32[]{:S(2)}) collective-permute-start(bf16[3,32,512]{2,1,0:T(8,128)(2,1)S(1)} %get-tuple-element.58), channel_id=1, source_target_pairs={{0,12},{4,8},{8,4},{12,0},{1,13},{5,9},{9,5},{13,1},{2,14},{6,10},... | collective-permute-start | bytes 294920 | tf_op jit(solution)/shard_map/ppermute | solution.py:89
  7.0 2.0 %collective-permute-start = (bf16[3,32,512]{2,1,0:T(8,128)(2,1)S(1)}, bf16[3,32,512]{2,1,0:T(8,128)(2,1)S(1)}, u32[]{:S(2)}, u32[]{:S(2)}) collective-permute-start(bf16[3,32,512]{2,1,0:T(8,128)(2,1)S(1)} %get-tuple-element.56), channel_id=1, source_target_pairs={{0,4},{4,0},{8,12},{12,8},{1,5},{5,1},{9,13},{13,9},{2,6},{6,2},{1... | collective-permute-start | bytes 294920 | tf_op jit(solution)/shard_map/ppermute | solution.py:89
  9.0 2.9 %collective-permute-start.13 = (bf16[3,32,512]{2,1,0:T(8,128)(2,1)S(1)}, bf16[3,32,512]{2,1,0:T(8,128)(2,1)S(1)}, u32[]{:S(2)}, u32[]{:S(2)}) collective-permute-start(bf16[3,32,512]{2,1,0:T(8,128)(2,1)S(1)} %get-tuple-element.63), channel_id=1, source_target_pairs={{0,8},{4,12},{8,0},{12,4},{1,9},{5,13},{9,1},{13,5},{2,10},{6,14},... | collective-permute-start | bytes 294920 | tf_op jit(solution)/shard_map/ppermute | solution.py:89
  11.9 2.6 %collective-permute-start.14 = (bf16[3,32,512]{2,1,0:T(8,128)(2,1)S(1)}, bf16[3,32,512]{2,1,0:T(8,128)(2,1)S(1)}, u32[]{:S(2)}, u32[]{:S(2)}) collective-permute-start(bf16[3,32,512]{2,1,0:T(8,128)(2,1)S(1)} %get-tuple-element.64), channel_id=1, source_target_pairs={{0,12},{4,8},{8,4},{12,0},{1,13},{5,9},{9,5},{13,1},{2,14},{6,10},... | collective-permute-start | bytes 294920 | tf_op jit(solution)/shard_map/ppermute | solution.py:89
  16.6 1.6 %collective-permute-start.4 = (bf16[3,32,512]{2,1,0:T(8,128)(2,1)S(1)}, bf16[3,32,512]{2,1,0:T(8,128)(2,1)S(1)}, u32[]{:S(2)}, u32[]{:S(2)}) collective-permute-start(bf16[3,32,512]{2,1,0:T(8,128)(2,1)S(1)} %collective-permute-done.refs_0_), channel_id=1, source_target_pairs={{0,2},{1,3},{2,0},{3,1},{4,6},{5,7},{6,4},{7,5},{8,10},{9,11},{10,... | collective-permute-start | bytes 294920 | tf_op jit(solution)/shard_map/ppermute | solution.py:89
  18.2 3.6 %collective-permute-done.1.refs_1_ = bf16[3,32,512]{2,1,0:T(8,128)(2,1)S(1)} collective-permute-done((bf16[3,32,512]{2,1,0:T(8,128)(2,1)S(1)}, bf16[3,32,512]{2,1,0:T(8,128)(2,1)S(1)}, u32[]{:S(2)}, u32[]{:S(2)}) %collective-permute-start.1) | collective-permute-done | bytes 98336 | tf_op jit(solution)/shard_map/ppermute | solution.py:89
  28.0 1.5 %collective-permute-start.16 = (bf16[3,96,512]{2,1,0:T(8,128)(2,1)S(1)}, bf16[3,96,512]{2,1,0:T(8,128)(2,1)S(1)}, u32[]{:S(2)}, u32[]{:S(2)}) collective-permute-start(bf16[3,96,512]{2,1,0:T(8,128)(2,1)S(1)} %shard_map.105.refs_0_), channel_id=1, source_target_pairs={{0,2},{1,3},{2,0},{3,1},{4,6},{5,7},{6,4},{7,5},{8,10},{9,11},{10,... | collective-permute-start | bytes 884744 | tf_op jit(solution)/shard_map/ppermute | solution.py:89
  29.5 3.7 %shard_map.104 = (bf16[3,192,512]{2,1,0:T(8,128)(2,1)S(1)}, bf16[3,192,512]{2,1,0:T(8,128)(2,1)S(1)}) custom-call(s32[9]{0:T(128)S(1)} %pad_add_fusion.scalar_ref, bf16[3,128,2048]{2,1,0:T(8,128)(2,1)} %tokens_hbm.2, bf16[3,512,512]{2,1,0:T(8,128)(2,1)} %basis_hbm.2, bf16[3,32,512]{2,1,0:T(8,128)(2,1)S(1)} %collective-permute-done.refs_0_, ...), custom_call_target="tpu_custom_call" | custom-call | tf_op jit(solution)/shard_map/pallas_call | solution.py:152
  33.6 3.9 %collective-permute-done.16.refs_1_ = bf16[3,96,512]{2,1,0:T(8,128)(2,1)S(1)} collective-permute-done((bf16[3,96,512]{2,1,0:T(8,128)(2,1)S(1)}, bf16[3,96,512]{2,1,0:T(8,128)(2,1)S(1)}, u32[]{:S(2)}, u32[]{:S(2)}) %collective-permute-start.16) | collective-permute-done | bytes 294944 | tf_op jit(solution)/shard_map/ppermute | solution.py:89
  37.5 1.6 %collective-permute-start.21 = (f32[4,2048]{1,0:T(4,128)S(1)}, f32[4,2048]{1,0:T(4,128)S(1)}, u32[]{:S(2)}, u32[]{:S(2)}) collective-permute-start(f32[4,2048]{1,0:T(4,128)S(1)} %pad_maximum_fusion.refs_0_), channel_id=1, source_target_pairs={{0,3},{1,2},{2,1},{3,0},{4,7},{5,6},{6,5},{7,4},{8,11},{9,10},{10,... | collective-permute-start | bytes 98312 | tf_op jit(solution)/shard_map/ppermute | solution.py:89
  39.7 3.7 %shard_map.106 = (bf16[3,192,512]{2,1,0:T(8,128)(2,1)S(1)}, bf16[3,192,512]{2,1,0:T(8,128)(2,1)S(1)}) custom-call(s32[9]{0:T(128)S(1)} %pad_add_fusion.scalar_ref, bf16[3,128,2048]{2,1,0:T(8,128)(2,1)} %tokens_hbm.3, bf16[3,512,512]{2,1,0:T(8,128)(2,1)} %basis_hbm.3, bf16[3,96,512]{2,1,0:T(8,128)(2,1)S(1)} %shard_map.105.refs_0_, ...), custom_call_target="tpu_custom_call" | custom-call | tf_op jit(solution)/shard_map/pallas_call | solution.py:152
  43.5 5.2 %collective-permute-done.15.refs_1_ = bf16[3,192,512]{2,1,0:T(8,128)(2,1)S(1)} collective-permute-done((bf16[3,192,512]{2,1,0:T(8,128)(2,1)S(1)}, bf16[3,192,512]{2,1,0:T(8,128)(2,1)S(1)}, u32[]{:S(2)}, u32[]{:S(2)}) %collective-permute-start.15) | collective-permute-done | bytes 589856 | tf_op jit(solution)/shard_map/ppermute | solution.py:89
  53.3 12.7 %collective-permute-done.24.refs_1_ = bf16[3,96,512]{2,1,0:T(8,128)(2,1)S(1)} collective-permute-done((bf16[3,96,512]{2,1,0:T(8,128)(2,1)S(1)}, bf16[3,96,512]{2,1,0:T(8,128)(2,1)S(1)}, u32[]{:S(2)}, u32[]{:S(2)}) %collective-permute-start.24) | collective-permute-done | bytes 294944 | tf_op jit(solution)/shard_map/ppermute | solution.py:95
  65.9 3.2 %collective-permute-done.26.refs_3_ = bf16[3,96,512]{2,1,0:T(8,128)(2,1)S(1)} collective-permute-done((bf16[3,96,512]{2,1,0:T(8,128)(2,1)S(1)}, bf16[3,96,512]{2,1,0:T(8,128)(2,1)S(1)}, u32[]{:S(2)}, u32[]{:S(2)}) %collective-permute-start.26) | collective-permute-done | bytes 294944 | tf_op jit(solution)/shard_map/ppermute | solution.py:95
  69.5 4.3 %collective-permute-start.27 = (f32[3,512]{1,0:T(4,128)S(1)}, f32[3,512]{1,0:T(4,128)S(1)}, u32[]{:S(2)}, u32[]{:S(2)}) collective-permute-start(f32[3,512]{1,0:T(4,128)S(1)} %shard_map.109.refs_0_), channel_id=1, source_target_pairs={{0,4},{4,0},{8,12},{12,8},{1,5},{5,1},{9,13},{13,9},{2,6},{6,2},{1... | collective-permute-start | bytes 18440 | tf_op jit(solution)/shard_map/ppermute | solution.py:89
  77.1 11.5 %collective-permute-done.31.far_ref = bf16[3,192,512]{2,1,0:T(8,128)(2,1)S(1)} collective-permute-done((bf16[3,192,512]{2,1,0:T(8,128)(2,1)S(1)}, bf16[3,192,512]{2,1,0:T(8,128)(2,1)S(1)}, u32[]{:S(2)}, u32[]{:S(2)}) %collective-permute-start.31) | collective-permute-done | bytes 589856 | tf_op jit(solution)/shard_map/ppermute | solution.py:95
  92.6 12.9 %collective-permute-done.30.refs_1_ = bf16[3,192,512]{2,1,0:T(8,128)(2,1)S(1)} collective-permute-done((bf16[3,192,512]{2,1,0:T(8,128)(2,1)S(1)}, bf16[3,192,512]{2,1,0:T(8,128)(2,1)S(1)}, u32[]{:S(2)}, u32[]{:S(2)}) %collective-permute-start.30) | collective-permute-done | bytes 589856 | tf_op jit(solution)/shard_map/ppermute | solution.py:89
  105.8 3.6 %collective-permute-done.35.far_ref = f32[3,512]{1,0:T(4,128)S(1)} collective-permute-done((f32[3,512]{1,0:T(4,128)S(1)}, f32[3,512]{1,0:T(4,128)S(1)}, u32[]{:S(2)}, u32[]{:S(2)}) %collective-permute-start.35) | collective-permute-done | bytes 6176 | tf_op jit(solution)/shard_map/ppermute | solution.py:89
  109.4 3.5 %collective-permute-start.38 = (f32[6,512]{1,0:T(8,128)S(1)}, f32[6,512]{1,0:T(8,128)}, u32[]{:S(2)}, u32[]{:S(2)}) collective-permute-start(f32[6,512]{1,0:T(8,128)S(1)} %shard_map.115.refs_4_), channel_id=1, source_target_pairs={{0,3},{1,2},{2,1},{3,0},{4,7},{5,6},{6,5},{7,4},{8,11},{9,10},{10,... | collective-permute-start | bytes 36872 | tf_op jit(solution)/shard_map/ppermute | solution.py:89
  112.9 2.5 %collective-permute-start.37 = (f32[6,512]{1,0:T(8,128)S(1)}, f32[6,512]{1,0:T(8,128)}, u32[]{:S(2)}, u32[]{:S(2)}) collective-permute-start(f32[6,512]{1,0:T(8,128)S(1)} %shard_map.115.refs_4_), channel_id=1, source_target_pairs={{0,2},{1,3},{2,0},{3,1},{4,6},{5,7},{6,4},{7,5},{8,10},{9,11},{10,... | collective-permute-start | bytes 36872 | tf_op jit(solution)/shard_map/ppermute | solution.py:89
  115.5 1.9 %collective-permute-done.37.refs_6_ = f32[6,512]{1,0:T(8,128)} collective-permute-done((f32[6,512]{1,0:T(8,128)S(1)}, f32[6,512]{1,0:T(8,128)}, u32[]{:S(2)}, u32[]{:S(2)}) %collective-permute-start.37) | collective-permute-done | bytes 12320 | tf_op jit(solution)/shard_map/ppermute | solution.py:89
  117.5 1.7 %collective-permute-start.39 = (bf16[2,192,512]{2,1,0:T(8,128)(2,1)S(1)}, bf16[2,192,512]{2,1,0:T(8,128)(2,1)S(1)}, u32[]{:S(2)}, u32[]{:S(2)}) collective-permute-start(bf16[2,192,512]{2,1,0:T(8,128)(2,1)S(1)} %get-tuple-element.89.refs_0_), channel_id=1, source_target_pairs={{0,1},{2,3},{13,12},{15,14},{10,11},{8,9},{7,6},{5,4},{16,17},{18,... | collective-permute-start | bytes 1179656 | tf_op jit(solution)/shard_map/ppermute | solution.py:95
  121.9 2.2 %shard_map.119 = (f32[3,512,512]{2,1,0:T(8,128)S(1)}, f32[2,2048]{1,0:T(2,128)}, f32[2,2048]{1,0:T(2,128)}) custom-call(s32[9]{0:T(128)S(1)} %copy-done.9, f32[4,2048]{1,0:T(4,128)S(1)} %copy-done.1, f32[4,2048]{1,0:T(4,128)S(1)} %copy-done.7, f32[4,2048]{1,0:T(4,128)S(1)} %copy-done.5, f32[4,2048]{1,0:T(4,128)S(1)} %copy-done.3, ...), custom_call_target="tpu_custom_call" | custom-call | tf_op jit(solution)/shard_map/pallas_call | solution.py:447
  124.8 1.8 %shard_map.120 = bf16[3,512,512]{2,1,0:T(8,128)(2,1)} custom-call(bf16[2,192,512]{2,1,0:T(8,128)(2,1)S(1)} %get-tuple-element.101.refs_0_, bf16[2,192,512]{2,1,0:T(8,128)(2,1)S(1)} %get-tuple-element.102.refs_1_, bf16[2,192,512]{2,1,0:T(8,128)(2,1)S(1)} %get-tuple-element.103.refs_2_, bf16[3,192,512]{2,1,0:T(8,128)(2,1)S(1)} %collective-permute-done.42.refs_3_, ...), custom_call_target="tpu_custom_call" | custom-call | tf_op jit(solution)/shard_map/pallas_call | solution.py:380
  (110 shorter events, 26.3 us)
Async XLA Ops:
  1.9 10.1 %collective-permute-start.2 = (bf16[3,32,512]{2,1,0:T(8,128)(2,1)S(1)}, bf16[3,32,512]{2,1,0:T(8,128)(2,1)S(1)}, u32[]{:S(2)}, u32[]{:S(2)}) collective-permute-start(bf16[3,32,512]{2,1,0:T(8,128)(2,1)S(1)} %get-tuple-element.58), channel_id=1, source_target_pairs={{0,12},{4,8},{8,4},{12,0},{1,13},{5,9},{9,5},{13,1},{2,14},{6,10},... | collective-permute-start | bytes 294920 | tf_op jit(solution)/shard_map/ppermute | solution.py:89
  7.0 8.2 %collective-permute-start.3 = (bf16[3,32,512]{2,1,0:T(8,128)(2,1)S(1)}, bf16[3,32,512]{2,1,0:T(8,128)(2,1)S(1)}, u32[]{:S(2)}, u32[]{:S(2)}) collective-permute-start(bf16[3,32,512]{2,1,0:T(8,128)(2,1)S(1)} %get-tuple-element.59), channel_id=1, source_target_pairs={{0,4},{4,0},{8,12},{12,8},{1,5},{5,1},{9,13},{13,9},{2,6},{6,2},{1... | collective-permute-start | bytes 294920 | tf_op jit(solution)/shard_map/ppermute | solution.py:89
  7.0 9.6 %collective-permute-start = (bf16[3,32,512]{2,1,0:T(8,128)(2,1)S(1)}, bf16[3,32,512]{2,1,0:T(8,128)(2,1)S(1)}, u32[]{:S(2)}, u32[]{:S(2)}) collective-permute-start(bf16[3,32,512]{2,1,0:T(8,128)(2,1)S(1)} %get-tuple-element.56), channel_id=1, source_target_pairs={{0,4},{4,0},{8,12},{12,8},{1,5},{5,1},{9,13},{13,9},{2,6},{6,2},{1... | collective-permute-start | bytes 294920 | tf_op jit(solution)/shard_map/ppermute | solution.py:89
  9.0 12.8 %collective-permute-start.1 = (bf16[3,32,512]{2,1,0:T(8,128)(2,1)S(1)}, bf16[3,32,512]{2,1,0:T(8,128)(2,1)S(1)}, u32[]{:S(2)}, u32[]{:S(2)}) collective-permute-start(bf16[3,32,512]{2,1,0:T(8,128)(2,1)S(1)} %get-tuple-element.57), channel_id=1, source_target_pairs={{0,8},{4,12},{8,0},{12,4},{1,9},{5,13},{9,1},{13,5},{2,10},{6,14},... | collective-permute-start | bytes 294920 | tf_op jit(solution)/shard_map/ppermute | solution.py:89
  9.0 14.2 %collective-permute-start.13 = (bf16[3,32,512]{2,1,0:T(8,128)(2,1)S(1)}, bf16[3,32,512]{2,1,0:T(8,128)(2,1)S(1)}, u32[]{:S(2)}, u32[]{:S(2)}) collective-permute-start(bf16[3,32,512]{2,1,0:T(8,128)(2,1)S(1)} %get-tuple-element.63), channel_id=1, source_target_pairs={{0,8},{4,12},{8,0},{12,4},{1,9},{5,13},{9,1},{13,5},{2,10},{6,14},... | collective-permute-start | bytes 294920 | tf_op jit(solution)/shard_map/ppermute | solution.py:89
  11.9 12.7 %collective-permute-start.14 = (bf16[3,32,512]{2,1,0:T(8,128)(2,1)S(1)}, bf16[3,32,512]{2,1,0:T(8,128)(2,1)S(1)}, u32[]{:S(2)}, u32[]{:S(2)}) collective-permute-start(bf16[3,32,512]{2,1,0:T(8,128)(2,1)S(1)} %get-tuple-element.64), channel_id=1, source_target_pairs={{0,12},{4,8},{8,4},{12,0},{1,13},{5,9},{9,5},{13,1},{2,14},{6,10},... | collective-permute-start | bytes 294920 | tf_op jit(solution)/shard_map/ppermute | solution.py:89
  16.6 8.1 %collective-permute-start.7 = (bf16[3,32,512]{2,1,0:T(8,128)(2,1)S(1)}, bf16[3,32,512]{2,1,0:T(8,128)(2,1)S(1)}, u32[]{:S(2)}, u32[]{:S(2)}) collective-permute-start(bf16[3,32,512]{2,1,0:T(8,128)(2,1)S(1)} %collective-permute-done.refs_0_), channel_id=1, source_target_pairs={{0,1},{1,0},{2,3},{3,2},{4,5},{5,4},{6,7},{7,6},{8,9},{9,8},{10,11... | collective-permute-start | bytes 294920 | tf_op jit(solution)/shard_map/ppermute | solution.py:89
  16.6 8.6 %collective-permute-start.4 = (bf16[3,32,512]{2,1,0:T(8,128)(2,1)S(1)}, bf16[3,32,512]{2,1,0:T(8,128)(2,1)S(1)}, u32[]{:S(2)}, u32[]{:S(2)}) collective-permute-start(bf16[3,32,512]{2,1,0:T(8,128)(2,1)S(1)} %collective-permute-done.refs_0_), channel_id=1, source_target_pairs={{0,2},{1,3},{2,0},{3,1},{4,6},{5,7},{6,4},{7,5},{8,10},{9,11},{10,... | collective-permute-start | bytes 294920 | tf_op jit(solution)/shard_map/ppermute | solution.py:89
  28.0 9.5 %collective-permute-start.16 = (bf16[3,96,512]{2,1,0:T(8,128)(2,1)S(1)}, bf16[3,96,512]{2,1,0:T(8,128)(2,1)S(1)}, u32[]{:S(2)}, u32[]{:S(2)}) collective-permute-start(bf16[3,96,512]{2,1,0:T(8,128)(2,1)S(1)} %shard_map.105.refs_0_), channel_id=1, source_target_pairs={{0,2},{1,3},{2,0},{3,1},{4,6},{5,7},{6,4},{7,5},{8,10},{9,11},{10,... | collective-permute-start | bytes 884744 | tf_op jit(solution)/shard_map/ppermute | solution.py:89
  33.2 15.5 %collective-permute-start.15 = (bf16[3,192,512]{2,1,0:T(8,128)(2,1)S(1)}, bf16[3,192,512]{2,1,0:T(8,128)(2,1)S(1)}, u32[]{:S(2)}, u32[]{:S(2)}) collective-permute-start(bf16[3,192,512]{2,1,0:T(8,128)(2,1)S(1)} %get-tuple-element.65), channel_id=1, source_target_pairs={{0,4},{4,0},{8,12},{12,8},{1,5},{5,1},{9,13},{13,9},{2,6},{6,2},{1... | collective-permute-start | bytes 1769480 | tf_op jit(solution)/shard_map/ppermute | solution.py:89
  33.3 6.4 %collective-permute-start.17 = (bf16[3,96,512]{2,1,0:T(8,128)(2,1)S(1)}, bf16[3,96,512]{2,1,0:T(8,128)(2,1)S(1)}, u32[]{:S(2)}, u32[]{:S(2)}) collective-permute-start(bf16[3,96,512]{2,1,0:T(8,128)(2,1)S(1)} %shard_map.105.refs_0_), channel_id=1, source_target_pairs={{0,1},{1,0},{2,3},{3,2},{4,5},{5,4},{6,7},{7,6},{8,9},{9,8},{10,11... | collective-permute-start | bytes 884744 | tf_op jit(solution)/shard_map/ppermute | solution.py:89
  37.5 6.0 %collective-permute-start.21 = (f32[4,2048]{1,0:T(4,128)S(1)}, f32[4,2048]{1,0:T(4,128)S(1)}, u32[]{:S(2)}, u32[]{:S(2)}) collective-permute-start(f32[4,2048]{1,0:T(4,128)S(1)} %pad_maximum_fusion.refs_0_), channel_id=1, source_target_pairs={{0,3},{1,2},{2,1},{3,0},{4,7},{5,6},{6,5},{7,4},{8,11},{9,10},{10,... | collective-permute-start | bytes 98312 | tf_op jit(solution)/shard_map/ppermute | solution.py:89
  50.3 15.7 %collective-permute-start.24 = (bf16[3,96,512]{2,1,0:T(8,128)(2,1)S(1)}, bf16[3,96,512]{2,1,0:T(8,128)(2,1)S(1)}, u32[]{:S(2)}, u32[]{:S(2)}) collective-permute-start(bf16[3,96,512]{2,1,0:T(8,128)(2,1)S(1)} %collective-permute-done.23.refs_0_), channel_id=1, source_target_pairs={{1,9},{2,10},{5,13},{6,14},{8,0},{11,3},{12,4},{15,7},{17,25},{18,... | collective-permute-start | bytes 884744 | tf_op jit(solution)/shard_map/ppermute | solution.py:95
  51.6 17.5 %collective-permute-start.26 = (bf16[3,96,512]{2,1,0:T(8,128)(2,1)S(1)}, bf16[3,96,512]{2,1,0:T(8,128)(2,1)S(1)}, u32[]{:S(2)}, u32[]{:S(2)}) collective-permute-start(bf16[3,96,512]{2,1,0:T(8,128)(2,1)S(1)} %collective-permute-done.25.refs_2_), channel_id=1, source_target_pairs={{1,9},{2,10},{5,13},{6,14},{8,0},{11,3},{12,4},{15,7},{17,25},{18,... | collective-permute-start | bytes 884744 | tf_op jit(solution)/shard_map/ppermute | solution.py:95
  52.9 23.9 %collective-permute-start.22 = (bf16[3,192,512]{2,1,0:T(8,128)(2,1)S(1)}, bf16[3,192,512]{2,1,0:T(8,128)(2,1)S(1)}, u32[]{:S(2)}, u32[]{:S(2)}) collective-permute-start(bf16[3,192,512]{2,1,0:T(8,128)(2,1)S(1)} %get-tuple-element.70), channel_id=1, source_target_pairs={{0,4},{4,0},{8,12},{12,8},{1,5},{5,1},{9,13},{13,9},{2,6},{6,2},{1... | collective-permute-start | bytes 1769480 | tf_op jit(solution)/shard_map/ppermute | solution.py:89
  69.5 6.1 %collective-permute-start.27 = (f32[3,512]{1,0:T(4,128)S(1)}, f32[3,512]{1,0:T(4,128)S(1)}, u32[]{:S(2)}, u32[]{:S(2)}) collective-permute-start(f32[3,512]{1,0:T(4,128)S(1)} %shard_map.109.refs_0_), channel_id=1, source_target_pairs={{0,4},{4,0},{8,12},{12,8},{1,5},{5,1},{9,13},{13,9},{2,6},{6,2},{1... | collective-permute-start | bytes 18440 | tf_op jit(solution)/shard_map/ppermute | solution.py:89
  75.5 13.0 %collective-permute-start.31 = (bf16[3,192,512]{2,1,0:T(8,128)(2,1)S(1)}, bf16[3,192,512]{2,1,0:T(8,128)(2,1)S(1)}, u32[]{:S(2)}, u32[]{:S(2)}) collective-permute-start(bf16[3,192,512]{2,1,0:T(8,128)(2,1)S(1)} %shard_map.108.panel_ref.near_ref), channel_id=1, source_target_pairs={{4,0},{9,13},{14,10},{3,7},{20,16},{25,29},{30,26},{19,23}} | collective-permute-start | bytes 1769480 | tf_op jit(solution)/shard_map/ppermute | solution.py:95
  77.0 28.5 %collective-permute-start.30 = (bf16[3,192,512]{2,1,0:T(8,128)(2,1)S(1)}, bf16[3,192,512]{2,1,0:T(8,128)(2,1)S(1)}, u32[]{:S(2)}, u32[]{:S(2)}) collective-permute-start(bf16[3,192,512]{2,1,0:T(8,128)(2,1)S(1)} %shard_map.111.refs_0_), channel_id=1, source_target_pairs={{0,8},{4,12},{8,0},{12,4},{1,9},{5,13},{9,1},{13,5},{2,10},{6,14},... | collective-permute-start | bytes 1769480 | tf_op jit(solution)/shard_map/ppermute | solution.py:89
  88.6 16.9 %collective-permute-start.32 = (bf16[2,192,512]{2,1,0:T(8,128)(2,1)S(1)}, bf16[2,192,512]{2,1,0:T(8,128)(2,1)S(1)}, u32[]{:S(2)}, u32[]{:S(2)}) collective-permute-start(bf16[2,192,512]{2,1,0:T(8,128)(2,1)S(1)} %get-tuple-element.83.refs_0_), channel_id=1, source_target_pairs={{0,2},{13,15},{10,8},{7,5},{16,18},{29,31},{26,24},{23,21}} | collective-permute-start | bytes 1179656 | tf_op jit(solution)/shard_map/ppermute | solution.py:95
  90.0 15.5 %collective-permute-start.33 = (bf16[2,192,512]{2,1,0:T(8,128)(2,1)S(1)}, bf16[2,192,512]{2,1,0:T(8,128)(2,1)S(1)}, u32[]{:S(2)}, u32[]{:S(2)}) collective-permute-start(bf16[2,192,512]{2,1,0:T(8,128)(2,1)S(1)} %get-tuple-element.85.refs_2_), channel_id=1, source_target_pairs={{0,2},{13,15},{10,8},{7,5},{16,18},{29,31},{26,24},{23,21}} | collective-permute-start | bytes 1179656 | tf_op jit(solution)/shard_map/ppermute | solution.py:95
  91.3 14.2 %collective-permute-start.34 = (bf16[2,192,512]{2,1,0:T(8,128)(2,1)S(1)}, bf16[2,192,512]{2,1,0:T(8,128)(2,1)S(1)}, u32[]{:S(2)}, u32[]{:S(2)}) collective-permute-start(bf16[2,192,512]{2,1,0:T(8,128)(2,1)S(1)} %get-tuple-element.87.refs_4_), channel_id=1, source_target_pairs={{0,2},{13,15},{10,8},{7,5},{16,18},{29,31},{26,24},{23,21}} | collective-permute-start | bytes 1179656 | tf_op jit(solution)/shard_map/ppermute | solution.py:95
  109.4 15.4 %collective-permute-start.42 = (bf16[3,192,512]{2,1,0:T(8,128)(2,1)S(1)}, bf16[3,192,512]{2,1,0:T(8,128)(2,1)S(1)}, u32[]{:S(2)}, u32[]{:S(2)}) collective-permute-start(bf16[3,192,512]{2,1,0:T(8,128)(2,1)S(1)} %shard_map.113.panel_ref.refs_3_), channel_id=1, source_target_pairs={{0,4},{4,0},{8,12},{12,8},{1,5},{5,1},{9,13},{13,9},{2,6},{6,2},{1... | collective-permute-start | bytes 1769480 | tf_op jit(solution)/shard_map/ppermute | solution.py:89
  109.4 6.0 %collective-permute-start.38 = (f32[6,512]{1,0:T(8,128)S(1)}, f32[6,512]{1,0:T(8,128)}, u32[]{:S(2)}, u32[]{:S(2)}) collective-permute-start(f32[6,512]{1,0:T(8,128)S(1)} %shard_map.115.refs_4_), channel_id=1, source_target_pairs={{0,3},{1,2},{2,1},{3,0},{4,7},{5,6},{6,5},{7,4},{8,11},{9,10},{10,... | collective-permute-start | bytes 36872 | tf_op jit(solution)/shard_map/ppermute | solution.py:89
  117.5 6.5 %collective-permute-start.39 = (bf16[2,192,512]{2,1,0:T(8,128)(2,1)S(1)}, bf16[2,192,512]{2,1,0:T(8,128)(2,1)S(1)}, u32[]{:S(2)}, u32[]{:S(2)}) collective-permute-start(bf16[2,192,512]{2,1,0:T(8,128)(2,1)S(1)} %get-tuple-element.89.refs_0_), channel_id=1, source_target_pairs={{0,1},{2,3},{13,12},{15,14},{10,11},{8,9},{7,6},{5,4},{16,17},{18,... | collective-permute-start | bytes 1179656 | tf_op jit(solution)/shard_map/ppermute | solution.py:95
  (33 other events, 220.8 us)

commit v8 on v7

--- a/solution.py
+++ b/solution.py
@@ -183,47 +183,46 @@
     )(*[array for pair in pairs for array in pair])
 
 
-def add_rows(pairs, cut=None):
-    layers, height, cols = pairs[0][0].shape
-    spans = [(0, cut), (cut, height)] if cut else [(n * height, (n + 1) * height) for n in range(len(pairs))]
+def add_rows(near, far, cut):
+    layers, height, cols = near.shape
+    spans = [(0, cut), (cut, height)]
+
+    def kernel(near_ref, far_ref, *out_refs):
+        for out_ref, (start, stop) in zip(out_refs, spans, strict=True):
+            total = near_ref[:, start:stop].astype(jnp.float32) + far_ref[:, start:stop].astype(jnp.float32)
+            out_ref[...] = total.astype(out_ref.dtype)
+
+    return pl.pallas_call(
+        kernel,
+        out_shape=[jax.ShapeDtypeStruct((layers, stop - start, cols), near.dtype) for start, stop in spans],
+        in_specs=[vmem_spec] * 2,
+        out_specs=[vmem_spec] * len(spans),
+        compiler_params=pltpu.CompilerParams(vmem_limit_bytes=8 * 1024 * 1024),
+        cost_estimate=light,
+    )(near, far)
+
+
+def by_layer(nears, fars):
+    layers, _, cols = nears[0].shape
+    count = len(nears)
+    height = sum(array.shape[1] for array in nears)
 
     def kernel(*refs):
-        out_refs = refs[2 * len(pairs) :]
-        for number, (start, stop) in enumerate(spans):
-            if cut:
-                total = refs[0][:, start:stop].astype(jnp.float32) + refs[1][:, start:stop].astype(jnp.float32)
-                out_refs[number][...] = total.astype(out_refs[number].dtype)
-            else:
-                total = refs[2 * number][...].astype(jnp.float32) + refs[2 * number + 1][...].astype(jnp.float32)
-                out_refs[0][:, start:stop] = total.astype(out_refs[0].dtype)
-
-    heights = [stop - start for start, stop in spans] if cut else [spans[-1][1]]
-    return pl.pallas_call(
-        kernel,
-        out_shape=[jax.ShapeDtypeStruct((layers, rows, cols), pairs[0][0].dtype) for rows in heights],
-        in_specs=[vmem_spec] * (2 * len(pairs)),
-        out_specs=[vmem_spec] * len(heights),
-        compiler_params=pltpu.CompilerParams(vmem_limit_bytes=8 * 1024 * 1024),
-        cost_estimate=light,
-    )(*[array for pair in pairs for array in pair])
-
-
-def by_layer(near, far):
-    layers, height, cols = near.shape
-
-    def kernel(near_ref, far_ref, *out_refs):
-        for layer, out_ref in enumerate(out_refs):
-            out_ref[0] = near_ref[layer]
-            out_ref[1] = far_ref[layer]
-
-    return pl.pallas_call(
-        kernel,
-        out_shape=[jax.ShapeDtypeStruct((2, height, cols), near.dtype)] * layers,
-        in_specs=[vmem_spec] * 2,
+        for side in range(2):
+            start = 0
+            for ref in refs[side * count : (side + 1) * count]:
+                for layer, out_ref in enumerate(refs[2 * count :]):
+                    out_ref[side, start : start + ref.shape[1]] = ref[layer]
+                start += ref.shape[1]
+
+    return pl.pallas_call(
+        kernel,
+        out_shape=[jax.ShapeDtypeStruct((2, height, cols), nears[0].dtype)] * layers,
+        in_specs=[vmem_spec] * (2 * count),
         out_specs=[vmem_spec] * layers,
         compiler_params=pltpu.CompilerParams(vmem_limit_bytes=8 * 1024 * 1024),
         cost_estimate=light,
-    )(near, far)
+    )(*nears, *fars)
 
 
 def join(arrays):
@@ -297,54 +296,58 @@
     )(home, *flat)
 
 
-def squares_of(aside, panel):
-    layers, _, cols = panel.shape
-
-    def kernel(aside_ref, panel_ref, out_ref):
-        for layer in range(layers):
-            wide = panel_ref[layer].astype(jnp.float32)
-            total = jnp.sum(wide * wide, axis=0, keepdims=True)
-            out_ref[layer : layer + 1] = jnp.where(aside_ref[0] == 0, total, 0.0)
+def squares_of(aside, panels):
+    layers, _, cols = panels[0].shape
+
+    def kernel(aside_ref, *refs):
+        for layer in range(layers):
+            total = jnp.zeros((1, cols), jnp.float32)
+            for ref in refs[:-1]:
+                wide = ref[layer].astype(jnp.float32)
+                total += jnp.sum(wide * wide, axis=0, keepdims=True)
+            refs[-1][layer : layer + 1] = jnp.where(aside_ref[0] == 0, total, 0.0)
 
     return pl.pallas_call(
         kernel,
         out_shape=jax.ShapeDtypeStruct((layers, cols), jnp.float32),
-        in_specs=[scalar_spec, vmem_spec],
-        out_specs=vmem_spec,
-        compiler_params=pltpu.CompilerParams(vmem_limit_bytes=8 * 1024 * 1024),
-        cost_estimate=light,
-    )(aside, panel)
-
-
-def total_of(arrays):
-    def kernel(*refs):
-        refs[-1][...] = (refs[0][...] + refs[1][...]) + (refs[2][...] + refs[3][...])
-
-    return pl.pallas_call(
-        kernel,
-        out_shape=jax.ShapeDtypeStruct(arrays[0].shape, arrays[0].dtype),
-        in_specs=[vmem_spec] * len(arrays),
-        out_specs=vmem_spec,
-        compiler_params=pltpu.CompilerParams(vmem_limit_bytes=4 * 1024 * 1024),
-        cost_estimate=light,
-    )(*arrays)
-
-
-def packet_of(acts, grad):
-    layers, cols = grad.shape
-
-    def kernel(near_ref, far_ref, grad_ref, out_ref):
-        out_ref[:layers] = near_ref[...] + far_ref[...]
-        out_ref[layers:] = grad_ref[...]
+        in_specs=[scalar_spec] + [vmem_spec] * len(panels),
+        out_specs=vmem_spec,
+        compiler_params=pltpu.CompilerParams(vmem_limit_bytes=8 * 1024 * 1024),
+        cost_estimate=light,
+    )(aside, *panels)
+
+
+def halves_of(act, near, far):
+    layers, _, cols = act.shape
+
+    def kernel(act_ref, near_ref, far_ref, out_ref):
+        for layer in range(layers):
+            wide = act_ref[layer].astype(jnp.float32)
+            out_ref[layer : layer + 1] = jnp.sum(wide * wide, axis=0, keepdims=True)
+        out_ref[layers:] = near_ref[...] + far_ref[...]
 
     return pl.pallas_call(
         kernel,
         out_shape=jax.ShapeDtypeStruct((2 * layers, cols), jnp.float32),
         in_specs=[vmem_spec] * 3,
         out_specs=vmem_spec,
+        compiler_params=pltpu.CompilerParams(vmem_limit_bytes=8 * 1024 * 1024),
+        cost_estimate=light,
+    )(act, near, far)
+
+
+def total_of(near, far):
+    def kernel(near_ref, far_ref, out_ref):
+        out_ref[...] = near_ref[...] + far_ref[...]
+
+    return pl.pallas_call(
+        kernel,
+        out_shape=jax.ShapeDtypeStruct(near.shape, near.dtype),
+        in_specs=[vmem_spec] * 2,
+        out_specs=vmem_spec,
         compiler_params=pltpu.CompilerParams(vmem_limit_bytes=4 * 1024 * 1024),
         cost_estimate=light,
-    )(*acts, grad)
+    )(near, far)
 
 
 def gram_of(grads, act):
@@ -492,30 +495,28 @@
     states = [state] + [flip(state, "owner", mask) for mask in range(1, n_own)]
 
     keep, near, keep_act, send_act, *states = step([keep, near, keep_act, send_act, *states])
-    parts = add_rows([(keep, near)], keep.shape[1] // 2)
+    parts = add_rows(keep, near, keep.shape[1] // 2)
     parts = [lax.ppermute(array, "owner", [*enumerate(held)]) for array in parts]
     to_pair = [((a, o), (a ^ 2, o)) for a in range(n_dp) for o in owners if (a ^ held[o]) & 2]
     crosses = [hop(array, to_pair) for array in parts]
     near_act = flip(send_act, "dp", 1)
 
-    (near,) = add_rows([*zip(parts, crosses, strict=True)])
+    nears = [add(pair) for pair in zip(parts, crosses, strict=True)]
     aside = ((dp ^ (-own % n_own)) // 2).astype(jnp.int32)[None]
-    squares = [squares_of(aside, near)]
-    squares += [flip(squares[0], "dp", mask) for mask in range(1, n_dp)]
-    square_grad = total_of(squares)
-    far = hop(after(near, square_grad), [((held[o] ^ 1, o), (held[o], o)) for o in owners])
-    full = by_layer(near, far)
+    square_grad = squares_of(aside, nears)
+    square_far = flip(square_grad, "dp", 2)
+    fars = [hop(array, [((held[o] ^ 1, o), (held[o], o)) for o in owners]) for array in nears]
+    full = by_layer(nears, fars)
     chip = [hop(array, [((held[o], o), (held[o], o ^ 2)) for o in owners]) for array in full]
 
-    part_act = add((keep_act, after(near_act, square_grad)))
+    part_act = add((keep_act, near_act))
     cross_act = flip(part_act, "dp", 2)
 
-    done = step([part_act, cross_act, *full, *chip])
-    (part_act, cross_act), full, chip = done[:2], done[2:][:layers], done[2 + layers :]
+    done = step([part_act, cross_act, square_grad, square_far, *full, *chip])
+    (part_act, cross_act, square_grad, square_far), full, chip = done[:4], done[4:][:layers], done[4 + layers :]
     full_act = add((part_act, cross_act))
-    halves = [squares_of(aside * 0, full_act)]
-    halves += [flip(halves[0], "dp", 1)]
-    packet = packet_of(halves, square_grad)
+    half = halves_of(full_act, square_grad, square_far)
+    packet = total_of(half, flip(half, "dp", 1))
     back_act = flip(after(full_act, packet), "dp", 1)
     packets = [packet] + [flip(packet, "owner", mask) for mask in range(1, n_own)]
     source = -dp % n_own

time: 127 us -> 121 us (0.953)
  waiting for transfers between devices: 65 us -> 59.5 us
  starting transfers between devices: 46.1 us -> 44.3 us
    ppermute x9 -> x10, waiting for transfers between devices: 27.3 us -> 20.4 us  [hop(): return lax.ppermute(array, ('dp', 'owner'), flat)]
    ppermute x32 -> x30, starting transfers between devices: 32.7 us -> 28.3 us  [flip(): lax.ppermute(array, axis, [(i, i ^ mask) for i in range(lax.axis_size(axi...]
    ppermute x9 -> x10, starting transfers between devices: 12.1 us -> 14.6 us  [hop(): return lax.ppermute(array, ('dp', 'owner'), flat)]
    ppermute x32 -> x30, waiting for transfers between devices: 37.7 us -> 39 us  [flip(): lax.ppermute(array, axis, [(i, i ^ mask) for i in range(lax.axis_size(axi...]
  transfers between devices with their start and end apart: 43 -> 42, of which waited for: 15 -> 16; matrix products, arithmetic and copies ran while one was open for 0% -> 0% of each run, Pallas kernels for 9% -> 10%
where the time goes in v8:
time: 121 us; the launch traced here: 120 us
  waiting for transfers between devices  59.5 us (49%)
  starting transfers between devices  44.3 us (37%)
  Pallas kernels  15 us (12%)
    ppermute x30, waiting for transfers between devices, flip(): lax.ppermute(array, axis, [(i, i ^ mask) for i in range(lax.axis_size(axi...  39 us
    ppermute x30, starting transfers between devices, flip(): lax.ppermute(array, axis, [(i, i ^ mask) for i in range(lax.axis_size(axi...  28.3 us
    ppermute x10, waiting for transfers between devices, hop(): return lax.ppermute(array, ('dp', 'owner'), flat)  20.4 us
    ppermute x10, starting transfers between devices, hop(): return lax.ppermute(array, ('dp', 'owner'), flat)  14.6 us
    pallas_call x2, Pallas kernels, project_rows(): pl.pallas_call(kernel, out_shape=[jax.ShapeDtypeStruct(shape, jnp.bfloat1...  7.47 us
  transfers between devices with their start and end apart: 42, of which 16 were waited for; matrix products, arithmetic and copies ran while one was open for 0% of the time, Pallas kernels for 10%

profile of v8, /device:TPU:0, one launch (start us, length us, event | category | flops | bytes accessed | tf_op | source)
XLA Modules:
  0.0 119.9 jit_solution(7599192768917915452)
XLA Ops:
  1.9 5.1 %collective-permute-start.2 = (bf16[3,32,512]{2,1,0:T(8,128)(2,1)S(1)}, bf16[3,32,512]{2,1,0:T(8,128)(2,1)S(1)}, u32[]{:S(2)}, u32[]{:S(2)}) collective-permute-start(bf16[3,32,512]{2,1,0:T(8,128)(2,1)S(1)} %get-tuple-element.58), channel_id=1, source_target_pairs={{0,12},{4,8},{8,4},{12,0},{1,13},{5,9},{9,5},{13,1},{2,14},{6,10},... | collective-permute-start | bytes 294920 | tf_op jit(solution)/shard_map/ppermute | solution.py:89
  7.0 2.0 %collective-permute-start = (bf16[3,32,512]{2,1,0:T(8,128)(2,1)S(1)}, bf16[3,32,512]{2,1,0:T(8,128)(2,1)S(1)}, u32[]{:S(2)}, u32[]{:S(2)}) collective-permute-start(bf16[3,32,512]{2,1,0:T(8,128)(2,1)S(1)} %get-tuple-element.56), channel_id=1, source_target_pairs={{0,4},{4,0},{8,12},{12,8},{1,5},{5,1},{9,13},{13,9},{2,6},{6,2},{1... | collective-permute-start | bytes 294920 | tf_op jit(solution)/shard_map/ppermute | solution.py:89
  9.0 2.9 %collective-permute-start.13 = (bf16[3,32,512]{2,1,0:T(8,128)(2,1)S(1)}, bf16[3,32,512]{2,1,0:T(8,128)(2,1)S(1)}, u32[]{:S(2)}, u32[]{:S(2)}) collective-permute-start(bf16[3,32,512]{2,1,0:T(8,128)(2,1)S(1)} %get-tuple-element.63), channel_id=1, source_target_pairs={{0,8},{4,12},{8,0},{12,4},{1,9},{5,13},{9,1},{13,5},{2,10},{6,14},... | collective-permute-start | bytes 294920 | tf_op jit(solution)/shard_map/ppermute | solution.py:89
  11.9 2.6 %collective-permute-start.14 = (bf16[3,32,512]{2,1,0:T(8,128)(2,1)S(1)}, bf16[3,32,512]{2,1,0:T(8,128)(2,1)S(1)}, u32[]{:S(2)}, u32[]{:S(2)}) collective-permute-start(bf16[3,32,512]{2,1,0:T(8,128)(2,1)S(1)} %get-tuple-element.64), channel_id=1, source_target_pairs={{0,12},{4,8},{8,4},{12,0},{1,13},{5,9},{9,5},{13,1},{2,14},{6,10},... | collective-permute-start | bytes 294920 | tf_op jit(solution)/shard_map/ppermute | solution.py:89
  16.6 1.6 %collective-permute-start.4 = (bf16[3,32,512]{2,1,0:T(8,128)(2,1)S(1)}, bf16[3,32,512]{2,1,0:T(8,128)(2,1)S(1)}, u32[]{:S(2)}, u32[]{:S(2)}) collective-permute-start(bf16[3,32,512]{2,1,0:T(8,128)(2,1)S(1)} %collective-permute-done.refs_0_), channel_id=1, source_target_pairs={{0,2},{1,3},{2,0},{3,1},{4,6},{5,7},{6,4},{7,5},{8,10},{9,11},{10,... | collective-permute-start | bytes 294920 | tf_op jit(solution)/shard_map/ppermute | solution.py:89
  18.2 3.6 %collective-permute-done.1.refs_1_ = bf16[3,32,512]{2,1,0:T(8,128)(2,1)S(1)} collective-permute-done((bf16[3,32,512]{2,1,0:T(8,128)(2,1)S(1)}, bf16[3,32,512]{2,1,0:T(8,128)(2,1)S(1)}, u32[]{:S(2)}, u32[]{:S(2)}) %collective-permute-start.1) | collective-permute-done | bytes 98336 | tf_op jit(solution)/shard_map/ppermute | solution.py:89
  29.5 3.7 %shard_map.104 = (bf16[3,192,512]{2,1,0:T(8,128)(2,1)S(1)}, bf16[3,192,512]{2,1,0:T(8,128)(2,1)S(1)}) custom-call(s32[9]{0:T(128)S(1)} %pad_add_fusion.scalar_ref, bf16[3,128,2048]{2,1,0:T(8,128)(2,1)} %tokens_hbm.2, bf16[3,512,512]{2,1,0:T(8,128)(2,1)} %basis_hbm.2, bf16[3,32,512]{2,1,0:T(8,128)(2,1)S(1)} %collective-permute-done.refs_0_, ...), custom_call_target="tpu_custom_call" | custom-call | tf_op jit(solution)/shard_map/pallas_call | solution.py:152
  33.6 3.9 %collective-permute-done.16.refs_1_ = bf16[3,96,512]{2,1,0:T(8,128)(2,1)S(1)} collective-permute-done((bf16[3,96,512]{2,1,0:T(8,128)(2,1)S(1)}, bf16[3,96,512]{2,1,0:T(8,128)(2,1)S(1)}, u32[]{:S(2)}, u32[]{:S(2)}) %collective-permute-start.16) | collective-permute-done | bytes 294944 | tf_op jit(solution)/shard_map/ppermute | solution.py:89
  37.5 1.6 %collective-permute-start.21 = (f32[4,2048]{1,0:T(4,128)S(1)}, f32[4,2048]{1,0:T(4,128)S(1)}, u32[]{:S(2)}, u32[]{:S(2)}) collective-permute-start(f32[4,2048]{1,0:T(4,128)S(1)} %pad_maximum_fusion.refs_0_), channel_id=1, source_target_pairs={{0,3},{1,2},{2,1},{3,0},{4,7},{5,6},{6,5},{7,4},{8,11},{9,10},{10,... | collective-permute-start | bytes 98312 | tf_op jit(solution)/shard_map/ppermute | solution.py:89
  39.7 3.7 %shard_map.106 = (bf16[3,192,512]{2,1,0:T(8,128)(2,1)S(1)}, bf16[3,192,512]{2,1,0:T(8,128)(2,1)S(1)}) custom-call(s32[9]{0:T(128)S(1)} %pad_add_fusion.scalar_ref, bf16[3,128,2048]{2,1,0:T(8,128)(2,1)} %tokens_hbm.3, bf16[3,512,512]{2,1,0:T(8,128)(2,1)} %basis_hbm.3, bf16[3,96,512]{2,1,0:T(8,128)(2,1)S(1)} %shard_map.105.refs_0_, ...), custom_call_target="tpu_custom_call" | custom-call | tf_op jit(solution)/shard_map/pallas_call | solution.py:152
  43.5 5.3 %collective-permute-done.15.far_ref = bf16[3,192,512]{2,1,0:T(8,128)(2,1)S(1)} collective-permute-done((bf16[3,192,512]{2,1,0:T(8,128)(2,1)S(1)}, bf16[3,192,512]{2,1,0:T(8,128)(2,1)S(1)}, u32[]{:S(2)}, u32[]{:S(2)}) %collective-permute-start.15) | collective-permute-done | bytes 589856 | tf_op jit(solution)/shard_map/ppermute | solution.py:89
  53.2 7.0 %collective-permute-done.25.refs_1_ = bf16[3,96,512]{2,1,0:T(8,128)(2,1)S(1)} collective-permute-done((bf16[3,96,512]{2,1,0:T(8,128)(2,1)S(1)}, bf16[3,96,512]{2,1,0:T(8,128)(2,1)S(1)}, u32[]{:S(2)}, u32[]{:S(2)}) %collective-permute-start.25) | collective-permute-done | bytes 294944 | tf_op jit(solution)/shard_map/ppermute | solution.py:95
  61.6 1.8 %collective-permute-done.27.refs_1_ = bf16[3,96,512]{2,1,0:T(8,128)(2,1)S(1)} collective-permute-done((bf16[3,96,512]{2,1,0:T(8,128)(2,1)S(1)}, bf16[3,96,512]{2,1,0:T(8,128)(2,1)S(1)}, u32[]{:S(2)}, u32[]{:S(2)}) %collective-permute-start.27) | collective-permute-done | bytes 294944 | tf_op jit(solution)/shard_map/ppermute | solution.py:95
  64.8 5.7 %collective-permute-done.22.refs_1_ = bf16[3,192,512]{2,1,0:T(8,128)(2,1)S(1)} collective-permute-done((bf16[3,192,512]{2,1,0:T(8,128)(2,1)S(1)}, bf16[3,192,512]{2,1,0:T(8,128)(2,1)S(1)}, u32[]{:S(2)}, u32[]{:S(2)}) %collective-permute-start.22) | collective-permute-done | bytes 589856 | tf_op jit(solution)/shard_map/ppermute | solution.py:89
  70.6 8.5 %collective-permute-done.29.refs_2_ = bf16[3,96,512]{2,1,0:T(8,128)(2,1)S(1)} collective-permute-done((bf16[3,96,512]{2,1,0:T(8,128)(2,1)S(1)}, bf16[3,96,512]{2,1,0:T(8,128)(2,1)S(1)}, u32[]{:S(2)}, u32[]{:S(2)}) %collective-permute-start.29) | collective-permute-done | bytes 294944 | tf_op jit(solution)/shard_map/ppermute | solution.py:95
  79.1 3.2 %collective-permute-done.30.refs_3_ = bf16[3,96,512]{2,1,0:T(8,128)(2,1)S(1)} collective-permute-done((bf16[3,96,512]{2,1,0:T(8,128)(2,1)S(1)}, bf16[3,96,512]{2,1,0:T(8,128)(2,1)S(1)}, u32[]{:S(2)}, u32[]{:S(2)}) %collective-permute-start.30) | collective-permute-done | bytes 294944 | tf_op jit(solution)/shard_map/ppermute | solution.py:95
  83.7 2.0 %collective-permute-start.32 = (bf16[2,192,512]{2,1,0:T(8,128)(2,1)S(1)}, bf16[2,192,512]{2,1,0:T(8,128)(2,1)}, u32[]{:S(2)}, u32[]{:S(2)}) collective-permute-start(bf16[2,192,512]{2,1,0:T(8,128)(2,1)S(1)} %get-tuple-element.85.refs_2_), channel_id=1, source_target_pairs={{0,2},{13,15},{10,8},{7,5},{16,18},{29,31},{26,24},{23,21}} | collective-permute-start | bytes 1179656 | tf_op jit(solution)/shard_map/ppermute | solution.py:95
  85.7 2.0 %collective-permute-start.33 = (bf16[2,192,512]{2,1,0:T(8,128)(2,1)S(1)}, bf16[2,192,512]{2,1,0:T(8,128)(2,1)}, u32[]{:S(2)}, u32[]{:S(2)}) collective-permute-start(bf16[2,192,512]{2,1,0:T(8,128)(2,1)S(1)} %get-tuple-element.87.refs_4_), channel_id=1, source_target_pairs={{0,2},{13,15},{10,8},{7,5},{16,18},{29,31},{26,24},{23,21}} | collective-permute-start | bytes 1179656 | tf_op jit(solution)/shard_map/ppermute | solution.py:95
  87.9 9.8 %collective-permute-done.28.far_ref = f32[3,512]{1,0:T(4,128)S(1)} collective-permute-done((f32[3,512]{1,0:T(4,128)S(1)}, f32[3,512]{1,0:T(4,128)S(1)}, u32[]{:S(2)}, u32[]{:S(2)}) %collective-permute-start.28) | collective-permute-done | bytes 6176 | tf_op jit(solution)/shard_map/ppermute | solution.py:89
  99.0 2.7 %collective-permute-done.34.far_ref = f32[6,512]{1,0:T(8,128)S(1)} collective-permute-done((f32[6,512]{1,0:T(8,128)S(1)}, f32[6,512]{1,0:T(8,128)S(1)}, u32[]{:S(2)}, u32[]{:S(2)}) %collective-permute-start.34) | collective-permute-done | bytes 12320 | tf_op jit(solution)/shard_map/ppermute | solution.py:89
  102.7 3.7 %collective-permute-start.37 = (f32[6,512]{1,0:T(8,128)S(1)}, f32[6,512]{1,0:T(8,128)S(1)}, u32[]{:S(2)}, u32[]{:S(2)}) collective-permute-start(f32[6,512]{1,0:T(8,128)S(1)} %shard_map.115.refs_4_), channel_id=1, source_target_pairs={{0,3},{1,2},{2,1},{3,0},{4,7},{5,6},{6,5},{7,4},{8,11},{9,10},{10,... | collective-permute-start | bytes 36872 | tf_op jit(solution)/shard_map/ppermute | solution.py:89
  107.9 2.3 %collective-permute-done.36.refs_6_ = f32[6,512]{1,0:T(8,128)S(1)} collective-permute-done((f32[6,512]{1,0:T(8,128)S(1)}, f32[6,512]{1,0:T(8,128)S(1)}, u32[]{:S(2)}, u32[]{:S(2)}) %collective-permute-start.36) | collective-permute-done | bytes 12320 | tf_op jit(solution)/shard_map/ppermute | solution.py:89
  115.5 1.9 %shard_map.119 = (f32[3,512,512]{2,1,0:T(8,128)S(1)}, f32[2,2048]{1,0:T(2,128)}, f32[2,2048]{1,0:T(2,128)}) custom-call(s32[9]{0:T(128)S(1)} %pad_add_fusion.scalar_ref, f32[4,2048]{1,0:T(4,128)S(1)} %pad_maximum_fusion.refs_0_, f32[4,2048]{1,0:T(4,128)S(1)} %collective-permute-done.19.refs_1_, f32[4,2048]{1,0:T(4,128)S(1)} %collective-permute-done.20.refs_2_, ...), custom_call_target="tpu_custom_call" | custom-call | tf_op jit(solution)/shard_map/pallas_call | solution.py:450
  118.1 1.8 %shard_map.120 = bf16[3,512,512]{2,1,0:T(8,128)(2,1)} custom-call(bf16[2,192,512]{2,1,0:T(8,128)(2,1)S(1)} %get-tuple-element.101.refs_0_, bf16[2,192,512]{2,1,0:T(8,128)(2,1)S(1)} %get-tuple-element.102.refs_1_, bf16[2,192,512]{2,1,0:T(8,128)(2,1)S(1)} %get-tuple-element.103.refs_2_, bf16[3,192,512]{2,1,0:T(8,128)(2,1)S(1)} %collective-permute-done.41.refs_3_, ...), custom_call_target="tpu_custom_call" | custom-call | tf_op jit(solution)/shard_map/pallas_call | solution.py:383
  (88 shorter events, 30.4 us)
Async XLA Ops:
  1.9 10.1 %collective-permute-start.2 = (bf16[3,32,512]{2,1,0:T(8,128)(2,1)S(1)}, bf16[3,32,512]{2,1,0:T(8,128)(2,1)S(1)}, u32[]{:S(2)}, u32[]{:S(2)}) collective-permute-start(bf16[3,32,512]{2,1,0:T(8,128)(2,1)S(1)} %get-tuple-element.58), channel_id=1, source_target_pairs={{0,12},{4,8},{8,4},{12,0},{1,13},{5,9},{9,5},{13,1},{2,14},{6,10},... | collective-permute-start | bytes 294920 | tf_op jit(solution)/shard_map/ppermute | solution.py:89
  7.0 8.2 %collective-permute-start.3 = (bf16[3,32,512]{2,1,0:T(8,128)(2,1)S(1)}, bf16[3,32,512]{2,1,0:T(8,128)(2,1)S(1)}, u32[]{:S(2)}, u32[]{:S(2)}) collective-permute-start(bf16[3,32,512]{2,1,0:T(8,128)(2,1)S(1)} %get-tuple-element.59), channel_id=1, source_target_pairs={{0,4},{4,0},{8,12},{12,8},{1,5},{5,1},{9,13},{13,9},{2,6},{6,2},{1... | collective-permute-start | bytes 294920 | tf_op jit(solution)/shard_map/ppermute | solution.py:89
  7.0 9.6 %collective-permute-start = (bf16[3,32,512]{2,1,0:T(8,128)(2,1)S(1)}, bf16[3,32,512]{2,1,0:T(8,128)(2,1)S(1)}, u32[]{:S(2)}, u32[]{:S(2)}) collective-permute-start(bf16[3,32,512]{2,1,0:T(8,128)(2,1)S(1)} %get-tuple-element.56), channel_id=1, source_target_pairs={{0,4},{4,0},{8,12},{12,8},{1,5},{5,1},{9,13},{13,9},{2,6},{6,2},{1... | collective-permute-start | bytes 294920 | tf_op jit(solution)/shard_map/ppermute | solution.py:89
  9.0 12.8 %collective-permute-start.1 = (bf16[3,32,512]{2,1,0:T(8,128)(2,1)S(1)}, bf16[3,32,512]{2,1,0:T(8,128)(2,1)S(1)}, u32[]{:S(2)}, u32[]{:S(2)}) collective-permute-start(bf16[3,32,512]{2,1,0:T(8,128)(2,1)S(1)} %get-tuple-element.57), channel_id=1, source_target_pairs={{0,8},{4,12},{8,0},{12,4},{1,9},{5,13},{9,1},{13,5},{2,10},{6,14},... | collective-permute-start | bytes 294920 | tf_op jit(solution)/shard_map/ppermute | solution.py:89
  9.0 14.2 %collective-permute-start.13 = (bf16[3,32,512]{2,1,0:T(8,128)(2,1)S(1)}, bf16[3,32,512]{2,1,0:T(8,128)(2,1)S(1)}, u32[]{:S(2)}, u32[]{:S(2)}) collective-permute-start(bf16[3,32,512]{2,1,0:T(8,128)(2,1)S(1)} %get-tuple-element.63), channel_id=1, source_target_pairs={{0,8},{4,12},{8,0},{12,4},{1,9},{5,13},{9,1},{13,5},{2,10},{6,14},... | collective-permute-start | bytes 294920 | tf_op jit(solution)/shard_map/ppermute | solution.py:89
  11.9 12.7 %collective-permute-start.14 = (bf16[3,32,512]{2,1,0:T(8,128)(2,1)S(1)}, bf16[3,32,512]{2,1,0:T(8,128)(2,1)S(1)}, u32[]{:S(2)}, u32[]{:S(2)}) collective-permute-start(bf16[3,32,512]{2,1,0:T(8,128)(2,1)S(1)} %get-tuple-element.64), channel_id=1, source_target_pairs={{0,12},{4,8},{8,4},{12,0},{1,13},{5,9},{9,5},{13,1},{2,14},{6,10},... | collective-permute-start | bytes 294920 | tf_op jit(solution)/shard_map/ppermute | solution.py:89
  16.6 8.1 %collective-permute-start.7 = (bf16[3,32,512]{2,1,0:T(8,128)(2,1)S(1)}, bf16[3,32,512]{2,1,0:T(8,128)(2,1)S(1)}, u32[]{:S(2)}, u32[]{:S(2)}) collective-permute-start(bf16[3,32,512]{2,1,0:T(8,128)(2,1)S(1)} %collective-permute-done.refs_0_), channel_id=1, source_target_pairs={{0,1},{1,0},{2,3},{3,2},{4,5},{5,4},{6,7},{7,6},{8,9},{9,8},{10,11... | collective-permute-start | bytes 294920 | tf_op jit(solution)/shard_map/ppermute | solution.py:89
  16.6 8.6 %collective-permute-start.4 = (bf16[3,32,512]{2,1,0:T(8,128)(2,1)S(1)}, bf16[3,32,512]{2,1,0:T(8,128)(2,1)S(1)}, u32[]{:S(2)}, u32[]{:S(2)}) collective-permute-start(bf16[3,32,512]{2,1,0:T(8,128)(2,1)S(1)} %collective-permute-done.refs_0_), channel_id=1, source_target_pairs={{0,2},{1,3},{2,0},{3,1},{4,6},{5,7},{6,4},{7,5},{8,10},{9,11},{10,... | collective-permute-start | bytes 294920 | tf_op jit(solution)/shard_map/ppermute | solution.py:89
  28.0 9.5 %collective-permute-start.16 = (bf16[3,96,512]{2,1,0:T(8,128)(2,1)S(1)}, bf16[3,96,512]{2,1,0:T(8,128)(2,1)S(1)}, u32[]{:S(2)}, u32[]{:S(2)}) collective-permute-start(bf16[3,96,512]{2,1,0:T(8,128)(2,1)S(1)} %shard_map.105.refs_0_), channel_id=1, source_target_pairs={{0,2},{1,3},{2,0},{3,1},{4,6},{5,7},{6,4},{7,5},{8,10},{9,11},{10,... | collective-permute-start | bytes 884744 | tf_op jit(solution)/shard_map/ppermute | solution.py:89
  33.2 15.5 %collective-permute-start.15 = (bf16[3,192,512]{2,1,0:T(8,128)(2,1)S(1)}, bf16[3,192,512]{2,1,0:T(8,128)(2,1)S(1)}, u32[]{:S(2)}, u32[]{:S(2)}) collective-permute-start(bf16[3,192,512]{2,1,0:T(8,128)(2,1)S(1)} %get-tuple-element.65), channel_id=1, source_target_pairs={{0,4},{4,0},{8,12},{12,8},{1,5},{5,1},{9,13},{13,9},{2,6},{6,2},{1... | collective-permute-start | bytes 1769480 | tf_op jit(solution)/shard_map/ppermute | solution.py:89
  33.3 6.4 %collective-permute-start.17 = (bf16[3,96,512]{2,1,0:T(8,128)(2,1)S(1)}, bf16[3,96,512]{2,1,0:T(8,128)(2,1)S(1)}, u32[]{:S(2)}, u32[]{:S(2)}) collective-permute-start(bf16[3,96,512]{2,1,0:T(8,128)(2,1)S(1)} %shard_map.105.refs_0_), channel_id=1, source_target_pairs={{0,1},{1,0},{2,3},{3,2},{4,5},{5,4},{6,7},{7,6},{8,9},{9,8},{10,11... | collective-permute-start | bytes 884744 | tf_op jit(solution)/shard_map/ppermute | solution.py:89
  37.5 6.0 %collective-permute-start.21 = (f32[4,2048]{1,0:T(4,128)S(1)}, f32[4,2048]{1,0:T(4,128)S(1)}, u32[]{:S(2)}, u32[]{:S(2)}) collective-permute-start(f32[4,2048]{1,0:T(4,128)S(1)} %pad_maximum_fusion.refs_0_), channel_id=1, source_target_pairs={{0,3},{1,2},{2,1},{3,0},{4,7},{5,6},{6,5},{7,4},{8,11},{9,10},{10,... | collective-permute-start | bytes 98312 | tf_op jit(solution)/shard_map/ppermute | solution.py:89
  50.3 20.2 %collective-permute-start.22 = (bf16[3,192,512]{2,1,0:T(8,128)(2,1)S(1)}, bf16[3,192,512]{2,1,0:T(8,128)(2,1)S(1)}, u32[]{:S(2)}, u32[]{:S(2)}) collective-permute-start(bf16[3,192,512]{2,1,0:T(8,128)(2,1)S(1)} %get-tuple-element.70), channel_id=1, source_target_pairs={{0,4},{4,0},{8,12},{12,8},{1,5},{5,1},{9,13},{13,9},{2,6},{6,2},{1... | collective-permute-start | bytes 1769480 | tf_op jit(solution)/shard_map/ppermute | solution.py:89
  50.6 9.6 %collective-permute-start.25 = (bf16[3,96,512]{2,1,0:T(8,128)(2,1)S(1)}, bf16[3,96,512]{2,1,0:T(8,128)(2,1)S(1)}, u32[]{:S(2)}, u32[]{:S(2)}) collective-permute-start(bf16[3,96,512]{2,1,0:T(8,128)(2,1)S(1)} %collective-permute-done.24.refs_0_), channel_id=1, source_target_pairs={{1,9},{2,10},{5,13},{6,14},{8,0},{11,3},{12,4},{15,7},{17,25},{18,... | collective-permute-start | bytes 884744 | tf_op jit(solution)/shard_map/ppermute | solution.py:95
  51.9 11.5 %collective-permute-start.27 = (bf16[3,96,512]{2,1,0:T(8,128)(2,1)S(1)}, bf16[3,96,512]{2,1,0:T(8,128)(2,1)S(1)}, u32[]{:S(2)}, u32[]{:S(2)}) collective-permute-start(bf16[3,96,512]{2,1,0:T(8,128)(2,1)S(1)} %collective-permute-done.26.refs_0_), channel_id=1, source_target_pairs={{1,9},{2,10},{5,13},{6,14},{8,0},{11,3},{12,4},{15,7},{17,25},{18,... | collective-permute-start | bytes 884744 | tf_op jit(solution)/shard_map/ppermute | solution.py:95
  60.3 18.8 %collective-permute-start.29 = (bf16[3,96,512]{2,1,0:T(8,128)(2,1)S(1)}, bf16[3,96,512]{2,1,0:T(8,128)(2,1)S(1)}, u32[]{:S(2)}, u32[]{:S(2)}) collective-permute-start(bf16[3,96,512]{2,1,0:T(8,128)(2,1)S(1)} %shard_map.109.refs_0_), channel_id=1, source_target_pairs={{4,0},{9,13},{14,10},{3,7},{20,16},{25,29},{30,26},{19,23}} | collective-permute-start | bytes 884744 | tf_op jit(solution)/shard_map/ppermute | solution.py:95
  63.5 18.8 %collective-permute-start.30 = (bf16[3,96,512]{2,1,0:T(8,128)(2,1)S(1)}, bf16[3,96,512]{2,1,0:T(8,128)(2,1)S(1)}, u32[]{:S(2)}, u32[]{:S(2)}) collective-permute-start(bf16[3,96,512]{2,1,0:T(8,128)(2,1)S(1)} %shard_map.110.refs_1_), channel_id=1, source_target_pairs={{4,0},{9,13},{14,10},{3,7},{20,16},{25,29},{30,26},{19,23}} | collective-permute-start | bytes 884744 | tf_op jit(solution)/shard_map/ppermute | solution.py:95
  70.6 27.2 %collective-permute-start.23 = (bf16[3,192,512]{2,1,0:T(8,128)(2,1)S(1)}, bf16[3,192,512]{2,1,0:T(8,128)(2,1)S(1)}, u32[]{:S(2)}, u32[]{:S(2)}) collective-permute-start(bf16[3,192,512]{2,1,0:T(8,128)(2,1)S(1)} %shard_map.107.refs_0_), channel_id=1, source_target_pairs={{0,8},{4,12},{8,0},{12,4},{1,9},{5,13},{9,1},{13,5},{2,10},{6,14},... | collective-permute-start | bytes 1769480 | tf_op jit(solution)/shard_map/ppermute | solution.py:89
  82.3 15.4 %collective-permute-start.31 = (bf16[2,192,512]{2,1,0:T(8,128)(2,1)S(1)}, bf16[2,192,512]{2,1,0:T(8,128)(2,1)S(1)}, u32[]{:S(2)}, u32[]{:S(2)}) collective-permute-start(bf16[2,192,512]{2,1,0:T(8,128)(2,1)S(1)} %get-tuple-element.83.refs_0_), channel_id=1, source_target_pairs={{0,2},{13,15},{10,8},{7,5},{16,18},{29,31},{26,24},{23,21}} | collective-permute-start | bytes 1179656 | tf_op jit(solution)/shard_map/ppermute | solution.py:95
  83.7 14.1 %collective-permute-start.32 = (bf16[2,192,512]{2,1,0:T(8,128)(2,1)S(1)}, bf16[2,192,512]{2,1,0:T(8,128)(2,1)}, u32[]{:S(2)}, u32[]{:S(2)}) collective-permute-start(bf16[2,192,512]{2,1,0:T(8,128)(2,1)S(1)} %get-tuple-element.85.refs_2_), channel_id=1, source_target_pairs={{0,2},{13,15},{10,8},{7,5},{16,18},{29,31},{26,24},{23,21}} | collective-permute-start | bytes 1179656 | tf_op jit(solution)/shard_map/ppermute | solution.py:95
  85.7 12.0 %collective-permute-start.33 = (bf16[2,192,512]{2,1,0:T(8,128)(2,1)S(1)}, bf16[2,192,512]{2,1,0:T(8,128)(2,1)}, u32[]{:S(2)}, u32[]{:S(2)}) collective-permute-start(bf16[2,192,512]{2,1,0:T(8,128)(2,1)S(1)} %get-tuple-element.87.refs_4_), channel_id=1, source_target_pairs={{0,2},{13,15},{10,8},{7,5},{16,18},{29,31},{26,24},{23,21}} | collective-permute-start | bytes 1179656 | tf_op jit(solution)/shard_map/ppermute | solution.py:95
  87.8 9.9 %collective-permute-start.28 = (f32[3,512]{1,0:T(4,128)S(1)}, f32[3,512]{1,0:T(4,128)S(1)}, u32[]{:S(2)}, u32[]{:S(2)}) collective-permute-start(f32[3,512]{1,0:T(4,128)S(1)} %shard_map.111.near_ref), channel_id=1, source_target_pairs={{0,8},{4,12},{8,0},{12,4},{1,9},{5,13},{9,1},{13,5},{2,10},{6,14},... | collective-permute-start | bytes 18440 | tf_op jit(solution)/shard_map/ppermute | solution.py:89
  101.7 16.4 %collective-permute-start.41 = (bf16[3,192,512]{2,1,0:T(8,128)(2,1)S(1)}, bf16[3,192,512]{2,1,0:T(8,128)(2,1)S(1)}, u32[]{:S(2)}, u32[]{:S(2)}) collective-permute-start(bf16[3,192,512]{2,1,0:T(8,128)(2,1)S(1)} %shard_map.113.act_ref.refs_3_), channel_id=1, source_target_pairs={{0,4},{4,0},{8,12},{12,8},{1,5},{5,1},{9,13},{13,9},{2,6},{6,2},{1... | collective-permute-start | bytes 1769480 | tf_op jit(solution)/shard_map/ppermute | solution.py:89
  111.4 6.0 %collective-permute-start.38 = (bf16[2,192,512]{2,1,0:T(8,128)(2,1)S(1)}, bf16[2,192,512]{2,1,0:T(8,128)(2,1)S(1)}, u32[]{:S(2)}, u32[]{:S(2)}) collective-permute-start(bf16[2,192,512]{2,1,0:T(8,128)(2,1)S(1)} %get-tuple-element.89.refs_0_), channel_id=1, source_target_pairs={{0,1},{2,3},{13,12},{15,14},{10,11},{8,9},{7,6},{5,4},{16,17},{18,... | collective-permute-start | bytes 1179656 | tf_op jit(solution)/shard_map/ppermute | solution.py:95
  (22 other events, 138.3 us)

commit v9 on v8

--- a/solution.py
+++ b/solution.py
@@ -485,22 +485,22 @@
     keep, send = project_rows(scalars, out_grads, pieces, stay, n_own, n_dp)
 
     near = flip(after(send, *got_act), "dp", 1)
-    pieces = [join(got_act)]
-    pieces += [flip(pieces[0], "owner", 2)]
+    pieces = [join(got_act[:-1]), got_act[-1]]
+    pieces += [flip(after(piece, keep), "owner", 2) for piece in pieces]
     pieces += [flip(piece, "owner", 1) for piece in pieces]
     stay = pltpu.with_memory_space_constraint(basis_act, pltpu.HBM)
     keep_act, send_act = project_rows(scalars, activations, pieces, stay, n_own, n_dp)
 
-    state = after(jnp.concatenate([state_act, state_grad], axis=0), keep)
+    state = jnp.concatenate([state_act, state_grad], axis=0)
+    keep, near, keep_act, send_act, state = step([keep, near, keep_act, send_act, state])
     states = [state] + [flip(state, "owner", mask) for mask in range(1, n_own)]
-
-    keep, near, keep_act, send_act, *states = step([keep, near, keep_act, send_act, *states])
     parts = add_rows(keep, near, keep.shape[1] // 2)
     parts = [lax.ppermute(array, "owner", [*enumerate(held)]) for array in parts]
     to_pair = [((a, o), (a ^ 2, o)) for a in range(n_dp) for o in owners if (a ^ held[o]) & 2]
     crosses = [hop(array, to_pair) for array in parts]
     near_act = flip(send_act, "dp", 1)
 
+    crosses[0] = after(crosses[0], *states)
     nears = [add(pair) for pair in zip(parts, crosses, strict=True)]
     aside = ((dp ^ (-own % n_own)) // 2).astype(jnp.int32)[None]
     square_grad = squares_of(aside, nears)

time: 121 us -> 119 us (0.983)
  the two profiles are of different devices: /device:TPU:0 before, /device:TPU:25 now
where the time goes in v9:
time: 119 us
  starting transfers between devices  53.3 us (45%)
  waiting for transfers between devices  49.5 us (42%)
  Pallas kernels  15 us (13%)
    ppermute x33, starting transfers between devices, flip(): lax.ppermute(array, axis, [(i, i ^ mask) for i in range(lax.axis_size(axi...  30.6 us
    ppermute x10, waiting for transfers between devices, hop(): return lax.ppermute(array, ('dp', 'owner'), flat)  27.9 us
    ppermute x10, starting transfers between devices, hop(): return lax.ppermute(array, ('dp', 'owner'), flat)  17.4 us
    ppermute x33, waiting for transfers between devices, flip(): lax.ppermute(array, axis, [(i, i ^ mask) for i in range(lax.axis_size(axi...  17.3 us
    pallas_call x2, Pallas kernels, project_rows(): pl.pallas_call(kernel, out_shape=[jax.ShapeDtypeStruct(shape, jnp.bfloat1...  7.45 us
    ppermute x2, starting transfers between devices, line_plan(): lax.ppermute(array, 'owner', [*enumerate(held)])  5.28 us
    ppermute x2, waiting for transfers between devices, line_plan(): lax.ppermute(array, 'owner', [*enumerate(held)])  4.17 us
  transfers between devices with their start and end apart: 45, of which 18 were waited for; matrix products, arithmetic and copies ran while one was open for 0% of the time, Pallas kernels for 10%

profile of v9, /device:TPU:25, one launch (start us, length us, event | category | flops | bytes accessed | tf_op | source)
XLA Modules:
  0.0 118.8 jit_solution(11563858167139472560)
XLA Ops:
  2.1 3.4 %collective-permute-start.2 = (bf16[3,32,512]{2,1,0:T(8,128)(2,1)S(1)}, bf16[3,32,512]{2,1,0:T(8,128)(2,1)S(1)}, u32[]{:S(2)}, u32[]{:S(2)}) collective-permute-start(bf16[3,32,512]{2,1,0:T(8,128)(2,1)S(1)} %get-tuple-element.57), channel_id=1, source_target_pairs={{0,12},{4,8},{8,4},{12,0},{1,13},{5,9},{9,5},{13,1},{2,14},{6,10},... | collective-permute-start | bytes 294920 | tf_op jit(solution)/shard_map/ppermute | solution.py:89
  5.5 2.7 %collective-permute-start.7 = (bf16[3,32,512]{2,1,0:T(8,128)(2,1)S(1)}, bf16[3,32,512]{2,1,0:T(8,128)(2,1)S(1)}, u32[]{:S(2)}, u32[]{:S(2)}) collective-permute-start(bf16[3,32,512]{2,1,0:T(8,128)(2,1)S(1)} %collective-permute-done.refs_0_), channel_id=1, source_target_pairs={{0,1},{1,0},{2,3},{3,2},{4,5},{5,4},{6,7},{7,6},{8,9},{9,8},{10,11... | collective-permute-start | bytes 294920 | tf_op jit(solution)/shard_map/ppermute | solution.py:89
  9.4 4.1 %collective-permute-start.8 = (bf16[3,32,512]{2,1,0:T(8,128)(2,1)S(1)}, bf16[3,32,512]{2,1,0:T(8,128)(2,1)S(1)}, u32[]{:S(2)}, u32[]{:S(2)}) collective-permute-start(bf16[3,32,512]{2,1,0:T(8,128)(2,1)S(1)} %collective-permute-done.1.refs_1_), channel_id=1, source_target_pairs={{0,1},{1,0},{2,3},{3,2},{4,5},{5,4},{6,7},{7,6},{8,9},{9,8},{10,11... | collective-permute-start | bytes 294920 | tf_op jit(solution)/shard_map/ppermute | solution.py:89
  16.5 2.2 %collective-permute-start.14 = (bf16[3,32,512]{2,1,0:T(8,128)(2,1)S(1)}, bf16[3,32,512]{2,1,0:T(8,128)(2,1)S(1)}, u32[]{:S(2)}, u32[]{:S(2)}) collective-permute-start(bf16[3,32,512]{2,1,0:T(8,128)(2,1)S(1)} %get-tuple-element.63), channel_id=1, source_target_pairs={{0,12},{4,8},{8,4},{12,0},{1,13},{5,9},{9,5},{13,1},{2,14},{6,10},... | collective-permute-start | bytes 294920 | tf_op jit(solution)/shard_map/ppermute | solution.py:89
  21.8 3.7 %shard_map.104 = (bf16[3,192,512]{2,1,0:T(8,128)(2,1)S(1)}, bf16[3,192,512]{2,1,0:T(8,128)(2,1)S(1)}) custom-call(s32[9]{0:T(128)S(1)} %pad_add_fusion.scalar_ref, bf16[3,128,2048]{2,1,0:T(8,128)(2,1)} %tokens_hbm.2, bf16[3,512,512]{2,1,0:T(8,128)(2,1)} %basis_hbm.2, bf16[3,32,512]{2,1,0:T(8,128)(2,1)S(1)} %collective-permute-done.refs_0_, ...), custom_call_target="tpu_custom_call" | custom-call | tf_op jit(solution)/shard_map/pallas_call | solution.py:152
  28.5 2.0 %collective-permute-start.18 = (bf16[3,64,512]{2,1,0:T(8,128)(2,1)S(1)}, bf16[3,64,512]{2,1,0:T(8,128)(2,1)S(1)}, u32[]{:S(2)}, u32[]{:S(2)}) collective-permute-start(bf16[3,64,512]{2,1,0:T(8,128)(2,1)S(1)} %shard_map.105.refs_0_), channel_id=1, source_target_pairs={{0,1},{1,0},{2,3},{3,2},{4,5},{5,4},{6,7},{7,6},{8,9},{9,8},{10,11... | collective-permute-start | bytes 589832 | tf_op jit(solution)/shard_map/ppermute | solution.py:89
  30.5 3.6 %collective-permute-done.17.refs_3_ = bf16[3,32,512]{2,1,0:T(8,128)(2,1)S(1)} collective-permute-done((bf16[3,32,512]{2,1,0:T(8,128)(2,1)S(1)}, bf16[3,32,512]{2,1,0:T(8,128)(2,1)S(1)}, u32[]{:S(2)}, u32[]{:S(2)}) %collective-permute-start.17) | collective-permute-done | bytes 98336 | tf_op jit(solution)/shard_map/ppermute | solution.py:89
  34.1 2.4 %collective-permute-start.21 = (bf16[3,32,512]{2,1,0:T(8,128)(2,1)S(1)}, bf16[3,32,512]{2,1,0:T(8,128)(2,1)S(1)}, u32[]{:S(2)}, u32[]{:S(2)}) collective-permute-start(bf16[3,32,512]{2,1,0:T(8,128)(2,1)S(1)} %collective-permute-done.17.refs_3_), channel_id=1, source_target_pairs={{0,1},{1,0},{2,3},{3,2},{4,5},{5,4},{6,7},{7,6},{8,9},{9,8},{10,11... | collective-permute-start | bytes 294920 | tf_op jit(solution)/shard_map/ppermute | solution.py:89
  37.9 3.7 %shard_map.106 = (bf16[3,192,512]{2,1,0:T(8,128)(2,1)S(1)}, bf16[3,192,512]{2,1,0:T(8,128)(2,1)S(1)}) custom-call(s32[9]{0:T(128)S(1)} %pad_add_fusion.scalar_ref, bf16[3,128,2048]{2,1,0:T(8,128)(2,1)} %tokens_hbm.3, bf16[3,512,512]{2,1,0:T(8,128)(2,1)} %basis_hbm.3, bf16[3,64,512]{2,1,0:T(8,128)(2,1)S(1)} %shard_map.105.refs_0_, ...), custom_call_target="tpu_custom_call" | custom-call | tf_op jit(solution)/shard_map/pallas_call | solution.py:152
  41.8 3.1 %collective-permute-start.24 = (bf16[3,96,512]{2,1,0:T(8,128)(2,1)S(1)}, bf16[3,96,512]{2,1,0:T(8,128)(2,1)S(1)}, u32[]{:S(2)}, u32[]{:S(2)}) collective-permute-start(bf16[3,96,512]{2,1,0:T(8,128)(2,1)S(1)} %get-tuple-element.73), channel_id=1, source_target_pairs={{0,0},{1,3},{2,2},{3,1},{4,4},{5,7},{6,6},{7,5},{8,8},{9,11},{10,1... | collective-permute-start | bytes 884744 | tf_op jit(solution)/shard_map/ppermute | solution.py:498
  44.9 2.2 %collective-permute-start.29 = (bf16[3,96,512]{2,1,0:T(8,128)(2,1)S(1)}, bf16[3,96,512]{2,1,0:T(8,128)(2,1)S(1)}, u32[]{:S(2)}, u32[]{:S(2)}) collective-permute-start(bf16[3,96,512]{2,1,0:T(8,128)(2,1)S(1)} %get-tuple-element.76), channel_id=1, source_target_pairs={{0,0},{1,3},{2,2},{3,1},{4,4},{5,7},{6,6},{7,5},{8,8},{9,11},{10,1... | collective-permute-start | bytes 884744 | tf_op jit(solution)/shard_map/ppermute | solution.py:498
  47.3 2.3 %collective-permute-done.24.refs_0_ = bf16[3,96,512]{2,1,0:T(8,128)(2,1)S(1)} collective-permute-done((bf16[3,96,512]{2,1,0:T(8,128)(2,1)S(1)}, bf16[3,96,512]{2,1,0:T(8,128)(2,1)S(1)}, u32[]{:S(2)}, u32[]{:S(2)}) %collective-permute-start.24) | collective-permute-done | bytes 294944 | tf_op jit(solution)/shard_map/ppermute | solution.py:498
  54.1 1.9 %collective-permute-start.27 = (f32[4,2048]{1,0:T(4,128)S(1)}, f32[4,2048]{1,0:T(4,128)S(1)}, u32[]{:S(2)}, u32[]{:S(2)}) collective-permute-start(f32[4,2048]{1,0:T(4,128)S(1)} %pad_maximum_fusion.refs_0_), channel_id=1, source_target_pairs={{0,2},{1,3},{2,0},{3,1},{4,6},{5,7},{6,4},{7,5},{8,10},{9,11},{10,... | collective-permute-start | bytes 98312 | tf_op jit(solution)/shard_map/ppermute | solution.py:89
  56.0 2.1 %collective-permute-done.28.refs_3_ = f32[4,2048]{1,0:T(4,128)S(1)} collective-permute-done((f32[4,2048]{1,0:T(4,128)S(1)}, f32[4,2048]{1,0:T(4,128)S(1)}, u32[]{:S(2)}, u32[]{:S(2)}) %collective-permute-start.28) | collective-permute-done | bytes 32800 | tf_op jit(solution)/shard_map/ppermute | solution.py:89
  60.6 14.1 %collective-permute-done.30.refs_1_ = bf16[3,96,512]{2,1,0:T(8,128)(2,1)S(1)} collective-permute-done((bf16[3,96,512]{2,1,0:T(8,128)(2,1)S(1)}, bf16[3,96,512]{2,1,0:T(8,128)(2,1)S(1)}, u32[]{:S(2)}, u32[]{:S(2)}) %collective-permute-start.30) | collective-permute-done | bytes 294944 | tf_op jit(solution)/shard_map/ppermute | solution.py:95
  76.4 8.3 %collective-permute-done.33.refs_3_ = bf16[3,96,512]{2,1,0:T(8,128)(2,1)S(1)} collective-permute-done((bf16[3,96,512]{2,1,0:T(8,128)(2,1)S(1)}, bf16[3,96,512]{2,1,0:T(8,128)(2,1)S(1)}, u32[]{:S(2)}, u32[]{:S(2)}) %collective-permute-start.33) | collective-permute-done | bytes 294944 | tf_op jit(solution)/shard_map/ppermute | solution.py:95
  86.1 2.1 %collective-permute-start.35 = (bf16[2,192,512]{2,1,0:T(8,128)(2,1)S(1)}, bf16[2,192,512]{2,1,0:T(8,128)(2,1)}, u32[]{:S(2)}, u32[]{:S(2)}) collective-permute-start(bf16[2,192,512]{2,1,0:T(8,128)(2,1)S(1)} %get-tuple-element.87.refs_2_), channel_id=1, source_target_pairs={{0,2},{13,15},{10,8},{7,5},{16,18},{29,31},{26,24},{23,21}} | collective-permute-start | bytes 1179656 | tf_op jit(solution)/shard_map/ppermute | solution.py:95
  88.2 2.0 %collective-permute-start.36 = (bf16[2,192,512]{2,1,0:T(8,128)(2,1)S(1)}, bf16[2,192,512]{2,1,0:T(8,128)(2,1)}, u32[]{:S(2)}, u32[]{:S(2)}) collective-permute-start(bf16[2,192,512]{2,1,0:T(8,128)(2,1)S(1)} %get-tuple-element.89.refs_4_), channel_id=1, source_target_pairs={{0,2},{13,15},{10,8},{7,5},{16,18},{29,31},{26,24},{23,21}} | collective-permute-start | bytes 1179656 | tf_op jit(solution)/shard_map/ppermute | solution.py:95
  90.4 3.4 %collective-permute-done.31.far_ref = f32[3,512]{1,0:T(4,128)S(1)} collective-permute-done((f32[3,512]{1,0:T(4,128)S(1)}, f32[3,512]{1,0:T(4,128)S(1)}, u32[]{:S(2)}, u32[]{:S(2)}) %collective-permute-start.31) | collective-permute-done | bytes 6176 | tf_op jit(solution)/shard_map/ppermute | solution.py:89
  95.0 4.2 %collective-permute-done.36.refs_5_ = bf16[2,192,512]{2,1,0:T(8,128)(2,1)} collective-permute-done((bf16[2,192,512]{2,1,0:T(8,128)(2,1)S(1)}, bf16[2,192,512]{2,1,0:T(8,128)(2,1)}, u32[]{:S(2)}, u32[]{:S(2)}) %collective-permute-start.36) | collective-permute-done | bytes 393248 | tf_op jit(solution)/shard_map/ppermute | solution.py:95
  99.5 3.1 %collective-permute-done.37.far_ref = f32[6,512]{1,0:T(8,128)S(1)} collective-permute-done((f32[6,512]{1,0:T(8,128)S(1)}, f32[6,512]{1,0:T(8,128)S(1)}, u32[]{:S(2)}, u32[]{:S(2)}) %collective-permute-start.37) | collective-permute-done | bytes 12320 | tf_op jit(solution)/shard_map/ppermute | solution.py:89
  102.7 1.9 %collective-permute-start.39 = (f32[6,512]{1,0:T(8,128)S(1)}, f32[6,512]{1,0:T(8,128)S(1)}, u32[]{:S(2)}, u32[]{:S(2)}) collective-permute-start(f32[6,512]{1,0:T(8,128)S(1)} %shard_map.115.refs_4_), channel_id=1, source_target_pairs={{0,2},{1,3},{2,0},{3,1},{4,6},{5,7},{6,4},{7,5},{8,10},{9,11},{10,... | collective-permute-start | bytes 36872 | tf_op jit(solution)/shard_map/ppermute | solution.py:89
  107.5 4.2 %collective-permute-start.41 = (bf16[2,192,512]{2,1,0:T(8,128)(2,1)S(1)}, bf16[2,192,512]{2,1,0:T(8,128)(2,1)S(1)}, u32[]{:S(2)}, u32[]{:S(2)}) collective-permute-start(bf16[2,192,512]{2,1,0:T(8,128)(2,1)S(1)} %get-tuple-element.91.refs_0_), channel_id=1, source_target_pairs={{0,1},{2,3},{13,12},{15,14},{10,11},{8,9},{7,6},{5,4},{16,17},{18,... | collective-permute-start | bytes 1179656 | tf_op jit(solution)/shard_map/ppermute | solution.py:95
  114.4 1.9 %shard_map.119 = (f32[3,512,512]{2,1,0:T(8,128)S(1)}, f32[2,2048]{1,0:T(2,128)}, f32[2,2048]{1,0:T(2,128)}) custom-call(s32[9]{0:T(128)S(1)} %pad_add_fusion.scalar_ref, f32[4,2048]{1,0:T(4,128)S(1)} %pad_maximum_fusion.refs_0_, f32[4,2048]{1,0:T(4,128)S(1)} %collective-permute-done.26.refs_1_, f32[4,2048]{1,0:T(4,128)S(1)} %collective-permute-done.27.refs_2_, ...), custom_call_target="tpu_custom_call" | custom-call | tf_op jit(solution)/shard_map/pallas_call | solution.py:450
  (94 shorter events, 33.2 us)
Async XLA Ops:
  2.1 7.3 %collective-permute-start.1 = (bf16[3,32,512]{2,1,0:T(8,128)(2,1)S(1)}, bf16[3,32,512]{2,1,0:T(8,128)(2,1)S(1)}, u32[]{:S(2)}, u32[]{:S(2)}) collective-permute-start(bf16[3,32,512]{2,1,0:T(8,128)(2,1)S(1)} %get-tuple-element.56), channel_id=1, source_target_pairs={{0,8},{4,12},{8,0},{12,4},{1,9},{5,13},{9,1},{13,5},{2,10},{6,14},... | collective-permute-start | bytes 294920 | tf_op jit(solution)/shard_map/ppermute | solution.py:89
  2.1 11.4 %collective-permute-start.2 = (bf16[3,32,512]{2,1,0:T(8,128)(2,1)S(1)}, bf16[3,32,512]{2,1,0:T(8,128)(2,1)S(1)}, u32[]{:S(2)}, u32[]{:S(2)}) collective-permute-start(bf16[3,32,512]{2,1,0:T(8,128)(2,1)S(1)} %get-tuple-element.57), channel_id=1, source_target_pairs={{0,12},{4,8},{8,4},{12,0},{1,13},{5,9},{9,5},{13,1},{2,14},{6,10},... | collective-permute-start | bytes 294920 | tf_op jit(solution)/shard_map/ppermute | solution.py:89
  5.5 8.0 %collective-permute-start.3 = (bf16[3,32,512]{2,1,0:T(8,128)(2,1)S(1)}, bf16[3,32,512]{2,1,0:T(8,128)(2,1)S(1)}, u32[]{:S(2)}, u32[]{:S(2)}) collective-permute-start(bf16[3,32,512]{2,1,0:T(8,128)(2,1)S(1)} %get-tuple-element.58), channel_id=1, source_target_pairs={{0,4},{4,0},{8,12},{12,8},{1,5},{5,1},{9,13},{13,9},{2,6},{6,2},{1... | collective-permute-start | bytes 294920 | tf_op jit(solution)/shard_map/ppermute | solution.py:89
  5.5 9.7 %collective-permute-start.7 = (bf16[3,32,512]{2,1,0:T(8,128)(2,1)S(1)}, bf16[3,32,512]{2,1,0:T(8,128)(2,1)S(1)}, u32[]{:S(2)}, u32[]{:S(2)}) collective-permute-start(bf16[3,32,512]{2,1,0:T(8,128)(2,1)S(1)} %collective-permute-done.refs_0_), channel_id=1, source_target_pairs={{0,1},{1,0},{2,3},{3,2},{4,5},{5,4},{6,7},{7,6},{8,9},{9,8},{10,11... | collective-permute-start | bytes 294920 | tf_op jit(solution)/shard_map/ppermute | solution.py:89
  8.2 7.2 %collective-permute-start.4 = (bf16[3,32,512]{2,1,0:T(8,128)(2,1)S(1)}, bf16[3,32,512]{2,1,0:T(8,128)(2,1)S(1)}, u32[]{:S(2)}, u32[]{:S(2)}) collective-permute-start(bf16[3,32,512]{2,1,0:T(8,128)(2,1)S(1)} %collective-permute-done.refs_0_), channel_id=1, source_target_pairs={{0,2},{1,3},{2,0},{3,1},{4,6},{5,7},{6,4},{7,5},{8,10},{9,11},{10,... | collective-permute-start | bytes 294920 | tf_op jit(solution)/shard_map/ppermute | solution.py:89
  9.4 7.0 %collective-permute-start.8 = (bf16[3,32,512]{2,1,0:T(8,128)(2,1)S(1)}, bf16[3,32,512]{2,1,0:T(8,128)(2,1)S(1)}, u32[]{:S(2)}, u32[]{:S(2)}) collective-permute-start(bf16[3,32,512]{2,1,0:T(8,128)(2,1)S(1)} %collective-permute-done.1.refs_1_), channel_id=1, source_target_pairs={{0,1},{1,0},{2,3},{3,2},{4,5},{5,4},{6,7},{7,6},{8,9},{9,8},{10,11... | collective-permute-start | bytes 294920 | tf_op jit(solution)/shard_map/ppermute | solution.py:89
  15.4 10.1 %collective-permute-start.13 = (bf16[3,32,512]{2,1,0:T(8,128)(2,1)S(1)}, bf16[3,32,512]{2,1,0:T(8,128)(2,1)S(1)}, u32[]{:S(2)}, u32[]{:S(2)}) collective-permute-start(bf16[3,32,512]{2,1,0:T(8,128)(2,1)S(1)} %get-tuple-element.62), channel_id=1, source_target_pairs={{0,8},{4,12},{8,0},{12,4},{1,9},{5,13},{9,1},{13,5},{2,10},{6,14},... | collective-permute-start | bytes 294920 | tf_op jit(solution)/shard_map/ppermute | solution.py:89
  16.5 9.0 %collective-permute-start.14 = (bf16[3,32,512]{2,1,0:T(8,128)(2,1)S(1)}, bf16[3,32,512]{2,1,0:T(8,128)(2,1)S(1)}, u32[]{:S(2)}, u32[]{:S(2)}) collective-permute-start(bf16[3,32,512]{2,1,0:T(8,128)(2,1)S(1)} %get-tuple-element.63), channel_id=1, source_target_pairs={{0,12},{4,8},{8,4},{12,0},{1,13},{5,9},{9,5},{13,1},{2,14},{6,10},... | collective-permute-start | bytes 294920 | tf_op jit(solution)/shard_map/ppermute | solution.py:89
  25.5 16.1 %collective-permute-start.15 = (bf16[3,192,512]{2,1,0:T(8,128)(2,1)S(1)}, bf16[3,192,512]{2,1,0:T(8,128)(2,1)S(1)}, u32[]{:S(2)}, u32[]{:S(2)}) collective-permute-start(bf16[3,192,512]{2,1,0:T(8,128)(2,1)S(1)} %get-tuple-element.64), channel_id=1, source_target_pairs={{0,4},{4,0},{8,12},{12,8},{1,5},{5,1},{9,13},{13,9},{2,6},{6,2},{1... | collective-permute-start | bytes 1769480 | tf_op jit(solution)/shard_map/ppermute | solution.py:89
  27.0 9.5 %collective-permute-start.16 = (bf16[3,64,512]{2,1,0:T(8,128)(2,1)S(1)}, bf16[3,64,512]{2,1,0:T(8,128)(2,1)S(1)}, u32[]{:S(2)}, u32[]{:S(2)}) collective-permute-start(bf16[3,64,512]{2,1,0:T(8,128)(2,1)S(1)} %shard_map.105.refs_0_), channel_id=1, source_target_pairs={{0,2},{1,3},{2,0},{3,1},{4,6},{5,7},{6,4},{7,5},{8,10},{9,11},{10,... | collective-permute-start | bytes 589832 | tf_op jit(solution)/shard_map/ppermute | solution.py:89
  28.5 8.0 %collective-permute-start.18 = (bf16[3,64,512]{2,1,0:T(8,128)(2,1)S(1)}, bf16[3,64,512]{2,1,0:T(8,128)(2,1)S(1)}, u32[]{:S(2)}, u32[]{:S(2)}) collective-permute-start(bf16[3,64,512]{2,1,0:T(8,128)(2,1)S(1)} %shard_map.105.refs_0_), channel_id=1, source_target_pairs={{0,1},{1,0},{2,3},{3,2},{4,5},{5,4},{6,7},{7,6},{8,9},{9,8},{10,11... | collective-permute-start | bytes 589832 | tf_op jit(solution)/shard_map/ppermute | solution.py:89
  41.8 7.8 %collective-permute-start.24 = (bf16[3,96,512]{2,1,0:T(8,128)(2,1)S(1)}, bf16[3,96,512]{2,1,0:T(8,128)(2,1)S(1)}, u32[]{:S(2)}, u32[]{:S(2)}) collective-permute-start(bf16[3,96,512]{2,1,0:T(8,128)(2,1)S(1)} %get-tuple-element.73), channel_id=1, source_target_pairs={{0,0},{1,3},{2,2},{3,1},{4,4},{5,7},{6,6},{7,5},{8,8},{9,11},{10,1... | collective-permute-start | bytes 884744 | tf_op jit(solution)/shard_map/ppermute | solution.py:498
  44.9 7.8 %collective-permute-start.29 = (bf16[3,96,512]{2,1,0:T(8,128)(2,1)S(1)}, bf16[3,96,512]{2,1,0:T(8,128)(2,1)S(1)}, u32[]{:S(2)}, u32[]{:S(2)}) collective-permute-start(bf16[3,96,512]{2,1,0:T(8,128)(2,1)S(1)} %get-tuple-element.76), channel_id=1, source_target_pairs={{0,0},{1,3},{2,2},{3,1},{4,4},{5,7},{6,6},{7,5},{8,8},{9,11},{10,1... | collective-permute-start | bytes 884744 | tf_op jit(solution)/shard_map/ppermute | solution.py:498
  47.1 29.1 %collective-permute-start.22 = (bf16[3,192,512]{2,1,0:T(8,128)(2,1)S(1)}, bf16[3,192,512]{2,1,0:T(8,128)(2,1)S(1)}, u32[]{:S(2)}, u32[]{:S(2)}) collective-permute-start(bf16[3,192,512]{2,1,0:T(8,128)(2,1)S(1)} %get-tuple-element.70), channel_id=1, source_target_pairs={{0,4},{4,0},{8,12},{12,8},{1,5},{5,1},{9,13},{13,9},{2,6},{6,2},{1... | collective-permute-start | bytes 1769480 | tf_op jit(solution)/shard_map/ppermute | solution.py:89
  49.6 9.7 %collective-permute-start.25 = (bf16[3,96,512]{2,1,0:T(8,128)(2,1)S(1)}, bf16[3,96,512]{2,1,0:T(8,128)(2,1)S(1)}, u32[]{:S(2)}, u32[]{:S(2)}) collective-permute-start(bf16[3,96,512]{2,1,0:T(8,128)(2,1)S(1)} %collective-permute-done.24.refs_0_), channel_id=1, source_target_pairs={{1,9},{2,10},{5,13},{6,14},{8,0},{11,3},{12,4},{15,7},{17,25},{18,... | collective-permute-start | bytes 884744 | tf_op jit(solution)/shard_map/ppermute | solution.py:95
  52.7 22.1 %collective-permute-start.30 = (bf16[3,96,512]{2,1,0:T(8,128)(2,1)S(1)}, bf16[3,96,512]{2,1,0:T(8,128)(2,1)S(1)}, u32[]{:S(2)}, u32[]{:S(2)}) collective-permute-start(bf16[3,96,512]{2,1,0:T(8,128)(2,1)S(1)} %collective-permute-done.29.refs_0_), channel_id=1, source_target_pairs={{1,9},{2,10},{5,13},{6,14},{8,0},{11,3},{12,4},{15,7},{17,25},{18,... | collective-permute-start | bytes 884744 | tf_op jit(solution)/shard_map/ppermute | solution.py:95
  59.3 17.1 %collective-permute-start.32 = (bf16[3,96,512]{2,1,0:T(8,128)(2,1)S(1)}, bf16[3,96,512]{2,1,0:T(8,128)(2,1)S(1)}, u32[]{:S(2)}, u32[]{:S(2)}) collective-permute-start(bf16[3,96,512]{2,1,0:T(8,128)(2,1)S(1)} %shard_map.109.refs_0_), channel_id=1, source_target_pairs={{4,0},{9,13},{14,10},{3,7},{20,16},{25,29},{30,26},{19,23}} | collective-permute-start | bytes 884744 | tf_op jit(solution)/shard_map/ppermute | solution.py:95
  74.9 9.9 %collective-permute-start.33 = (bf16[3,96,512]{2,1,0:T(8,128)(2,1)S(1)}, bf16[3,96,512]{2,1,0:T(8,128)(2,1)S(1)}, u32[]{:S(2)}, u32[]{:S(2)}) collective-permute-start(bf16[3,96,512]{2,1,0:T(8,128)(2,1)S(1)} %shard_map.110.refs_1_), channel_id=1, source_target_pairs={{4,0},{9,13},{14,10},{3,7},{20,16},{25,29},{30,26},{19,23}} | collective-permute-start | bytes 884744 | tf_op jit(solution)/shard_map/ppermute | solution.py:95
  76.3 17.5 %collective-permute-start.23 = (bf16[3,192,512]{2,1,0:T(8,128)(2,1)S(1)}, bf16[3,192,512]{2,1,0:T(8,128)(2,1)S(1)}, u32[]{:S(2)}, u32[]{:S(2)}) collective-permute-start(bf16[3,192,512]{2,1,0:T(8,128)(2,1)S(1)} %shard_map.107.refs_0_), channel_id=1, source_target_pairs={{0,8},{4,12},{8,0},{12,4},{1,9},{5,13},{9,1},{13,5},{2,10},{6,14},... | collective-permute-start | bytes 1769480 | tf_op jit(solution)/shard_map/ppermute | solution.py:89
  84.8 9.0 %collective-permute-start.34 = (bf16[2,192,512]{2,1,0:T(8,128)(2,1)S(1)}, bf16[2,192,512]{2,1,0:T(8,128)(2,1)S(1)}, u32[]{:S(2)}, u32[]{:S(2)}) collective-permute-start(bf16[2,192,512]{2,1,0:T(8,128)(2,1)S(1)} %get-tuple-element.85.refs_0_), channel_id=1, source_target_pairs={{0,2},{13,15},{10,8},{7,5},{16,18},{29,31},{26,24},{23,21}} | collective-permute-start | bytes 1179656 | tf_op jit(solution)/shard_map/ppermute | solution.py:95
  86.1 8.9 %collective-permute-start.35 = (bf16[2,192,512]{2,1,0:T(8,128)(2,1)S(1)}, bf16[2,192,512]{2,1,0:T(8,128)(2,1)}, u32[]{:S(2)}, u32[]{:S(2)}) collective-permute-start(bf16[2,192,512]{2,1,0:T(8,128)(2,1)S(1)} %get-tuple-element.87.refs_2_), channel_id=1, source_target_pairs={{0,2},{13,15},{10,8},{7,5},{16,18},{29,31},{26,24},{23,21}} | collective-permute-start | bytes 1179656 | tf_op jit(solution)/shard_map/ppermute | solution.py:95
  88.2 11.0 %collective-permute-start.36 = (bf16[2,192,512]{2,1,0:T(8,128)(2,1)S(1)}, bf16[2,192,512]{2,1,0:T(8,128)(2,1)}, u32[]{:S(2)}, u32[]{:S(2)}) collective-permute-start(bf16[2,192,512]{2,1,0:T(8,128)(2,1)S(1)} %get-tuple-element.89.refs_4_), channel_id=1, source_target_pairs={{0,2},{13,15},{10,8},{7,5},{16,18},{29,31},{26,24},{23,21}} | collective-permute-start | bytes 1179656 | tf_op jit(solution)/shard_map/ppermute | solution.py:95
  102.6 14.5 %collective-permute-start.44 = (bf16[3,192,512]{2,1,0:T(8,128)(2,1)S(1)}, bf16[3,192,512]{2,1,0:T(8,128)(2,1)S(1)}, u32[]{:S(2)}, u32[]{:S(2)}) collective-permute-start(bf16[3,192,512]{2,1,0:T(8,128)(2,1)S(1)} %shard_map.113.act_ref.refs_3_), channel_id=1, source_target_pairs={{0,4},{4,0},{8,12},{12,8},{1,5},{5,1},{9,13},{13,9},{2,6},{6,2},{1... | collective-permute-start | bytes 1769480 | tf_op jit(solution)/shard_map/ppermute | solution.py:89
  107.5 8.8 %collective-permute-start.41 = (bf16[2,192,512]{2,1,0:T(8,128)(2,1)S(1)}, bf16[2,192,512]{2,1,0:T(8,128)(2,1)S(1)}, u32[]{:S(2)}, u32[]{:S(2)}) collective-permute-start(bf16[2,192,512]{2,1,0:T(8,128)(2,1)S(1)} %get-tuple-element.91.refs_0_), channel_id=1, source_target_pairs={{0,1},{2,3},{13,12},{15,14},{10,11},{8,9},{7,6},{5,4},{16,17},{18,... | collective-permute-start | bytes 1179656 | tf_op jit(solution)/shard_map/ppermute | solution.py:95
  (25 other events, 144.9 us)

commit v10 on v9

--- a/solution.py
+++ b/solution.py
@@ -95,31 +95,45 @@
     return lax.ppermute(array, ("dp", "owner"), flat)
 
 
+def load(arrays, cut, *gates):
+    tile = arrays[-1].shape[1]
+    shapes = [(*array.shape[:2], tile) if number < cut else array.shape for number, array in enumerate(arrays)]
+
+    def kernel(*refs):
+        in_refs, out_refs, sems = refs[: len(arrays)], refs[len(arrays) + len(gates) : -1], refs[-1]
+        cols = pl.ds(pl.multiple_of(lax.axis_index("dp") * tile, tile), tile)
+        copies = []
+        for number, (in_ref, out_ref) in enumerate(zip(in_refs, out_refs, strict=True)):
+            source = in_ref.at[:, :, cols] if number < cut else in_ref
+            copies.append(pltpu.make_async_copy(source, out_ref, sems.at[number]))
+            copies[-1].start()
+        for copy in copies:
+            copy.wait()
+
+    return pl.pallas_call(
+        kernel,
+        out_shape=[
+            jax.ShapeDtypeStruct(shape, array.dtype) for shape, array in zip(shapes, arrays, strict=True)
+        ],
+        in_specs=[pl.BlockSpec(memory_space=pltpu.HBM)] * len(arrays) + [pl.BlockSpec(memory_space=pl.ANY)] * len(gates),
+        out_specs=[vmem_spec] * len(arrays),
+        scratch_shapes=[pltpu.SemaphoreType.DMA((len(arrays),))],
+        compiler_params=pltpu.CompilerParams(vmem_limit_bytes=8 * 1024 * 1024),
+        cost_estimate=light,
+    )(*[pltpu.with_memory_space_constraint(array, pltpu.HBM) for array in arrays], *gates)
+
+
 def project_rows(scalars, tokens, pieces, basis, n_own, n_dp):
-    layers, tok_rows, _ = tokens.shape
-    tile, cols = basis.shape[1:]
+    layers, tok_rows, tile = tokens.shape
+    cols = basis.shape[2]
     part_rows = tok_rows // n_own
     packed = 3 * n_dp * tok_rows // 4
     half = packed // 2
     shapes = [(layers, half, cols)] * 2
 
-    def kernel(scalar_ref, tokens_hbm, basis_hbm, *refs):
-        piece_refs, refs = refs[: len(pieces)], refs[len(pieces) :]
-        out_refs, (tokens_ref, basis_ref, sems) = refs[: len(shapes)], refs[len(shapes) :]
+    def kernel(scalar_ref, tokens_ref, basis_ref, *refs):
+        piece_refs, out_refs = refs[: len(pieces)], refs[len(pieces) :]
         dp, own = scalar_ref[0], scalar_ref[1]
-        at = pl.ds(pl.multiple_of(dp * tile, tile), tile)
-        copies = []
-        for layer in range(layers):
-            copies.append(
-                [
-                    pltpu.make_async_copy(
-                        tokens_hbm.at[layer, :, at], tokens_ref.at[layer], sems.at[2 * layer]
-                    ),
-                    pltpu.make_async_copy(basis_hbm.at[layer], basis_ref.at[layer], sems.at[2 * layer + 1]),
-                ]
-            )
-            for copy in copies[-1]:
-                copy.start()
         col = lax.broadcasted_iota(jnp.int32, (1, n_dp * tok_rows), 1)
         turn = (col - tok_rows) // part_rows
         peer = turn // (n_dp - 1)
@@ -139,10 +153,8 @@
         row = row + jnp.where(dp % 2 == 0, 0, jnp.where(row < half, half, -half))
         select = (row == place).astype(jnp.bfloat16)
         for layer in range(layers):
-            copies[layer][0].wait()
             rows = jnp.concatenate([tokens_ref[layer]] + [p[layer] for p in piece_refs], axis=0)
             chosen = jnp.dot(select, rows, preferred_element_type=jnp.float32).astype(jnp.bfloat16)
-            copies[layer][1].wait()
             result = jnp.dot(chosen, basis_ref[layer], preferred_element_type=jnp.float32).astype(
                 jnp.bfloat16
             )
@@ -152,16 +164,11 @@
     return pl.pallas_call(
         kernel,
         out_shape=[jax.ShapeDtypeStruct(shape, jnp.bfloat16) for shape in shapes],
-        in_specs=[scalar_spec] + [pl.BlockSpec(memory_space=pltpu.HBM), pl.BlockSpec(memory_space=pl.ANY)] + [vmem_spec] * len(pieces),
+        in_specs=[scalar_spec] + [vmem_spec] * (2 + len(pieces)),
         out_specs=[vmem_spec] * len(shapes),
-        scratch_shapes=[
-            pltpu.VMEM((layers, tok_rows, tile), jnp.bfloat16),
-            pltpu.VMEM((layers, tile, cols), jnp.bfloat16),
-            pltpu.SemaphoreType.DMA((2 * layers,)),
-        ],
         compiler_params=pltpu.CompilerParams(vmem_limit_bytes=16 * 1024 * 1024),
         cost_estimate=light,
-    )(scalars, pltpu.with_memory_space_constraint(tokens, pltpu.HBM), basis, *pieces)
+    )(scalars, tokens, basis, *pieces)
 
 
 def add(*pairs):
@@ -478,18 +485,18 @@
     cuts = cut_rows((out_grads, activations), tile, n_own, n_dp)
     cuts = [flip(cut, "dp", number % (n_dp - 1) + 1) for number, cut in enumerate(cuts)]
     got_grad, got_act = cuts[: n_dp - 1], cuts[n_dp - 1 :]
-    pieces = got_grad[:-1] + [after(got_grad[-1], got_act[0])]
+    own_grad, stay_grad = load((out_grads, basis_grad), 1)
+    pieces = got_grad[:-1] + [after(got_grad[-1], got_act[0], own_grad)]
     pieces += [flip(piece, "owner", 2) for piece in pieces]
     pieces += [flip(piece, "owner", 1) for piece in pieces]
-    stay = pltpu.with_memory_space_constraint(basis_grad, pltpu.HBM)
-    keep, send = project_rows(scalars, out_grads, pieces, stay, n_own, n_dp)
+    keep, send = project_rows(scalars, own_grad, pieces, stay_grad, n_own, n_dp)
 
     near = flip(after(send, *got_act), "dp", 1)
     pieces = [join(got_act[:-1]), got_act[-1]]
     pieces += [flip(after(piece, keep), "owner", 2) for piece in pieces]
-    pieces += [flip(piece, "owner", 1) for piece in pieces]
-    stay = pltpu.with_memory_space_constraint(basis_act, pltpu.HBM)
-    keep_act, send_act = project_rows(scalars, activations, pieces, stay, n_own, n_dp)
+    own_act, stay_act = load((activations, basis_act), 1, keep)
+    pieces += [flip(after(piece, own_act), "owner", 1) for piece in pieces]
+    keep_act, send_act = project_rows(scalars, own_act, pieces, stay_act, n_own, n_dp)
 
     state = jnp.concatenate([state_act, state_grad], axis=0)
     keep, near, keep_act, send_act, state = step([keep, near, keep_act, send_act, state])

time: 119 us -> 118 us (level)
  the two profiles are of different devices: /device:TPU:25 before, /device:TPU:0 now
where the time goes in v10:
time: 118 us; the launch traced here: 117 us
  starting transfers between devices  53.7 us (46%)
  waiting for transfers between devices  47.1 us (40%)
  Pallas kernels  14.8 us (13%)
    ppermute x33, starting transfers between devices, flip(): lax.ppermute(array, axis, [(i, i ^ mask) for i in range(lax.axis_size(axi...  36.7 us
    ppermute x33, waiting for transfers between devices, flip(): lax.ppermute(array, axis, [(i, i ^ mask) for i in range(lax.axis_size(axi...  26 us
    ppermute x10, waiting for transfers between devices, hop(): return lax.ppermute(array, ('dp', 'owner'), flat)  21.2 us
    ppermute x10, starting transfers between devices, hop(): return lax.ppermute(array, ('dp', 'owner'), flat)  15.6 us
    pallas_call x2, Pallas kernels, project_rows(): pl.pallas_call(kernel, out_shape=[jax.ShapeDtypeStruct(shape, jnp.bfloat1...  4.17 us
    pallas_call x2, Pallas kernels, load(): pl.pallas_call(kernel, out_shape=[jax.ShapeDtypeStruct(shape, array.dtype...  3.12 us
  transfers between devices with their start and end apart: 45, of which 20 were waited for; matrix products, arithmetic and copies ran while one was open for 0% of the time, Pallas kernels for 10%

profile of v10, /device:TPU:0, one launch (start us, length us, event | category | flops | bytes accessed | tf_op | source)
XLA Modules:
  0.0 116.7 jit_solution(14029895728332934054)
XLA Ops:
  1.8 3.1 %collective-permute-start = (bf16[3,32,512]{2,1,0:T(8,128)(2,1)S(1)}, bf16[3,32,512]{2,1,0:T(8,128)(2,1)S(1)}, u32[]{:S(2)}, u32[]{:S(2)}) collective-permute-start(bf16[3,32,512]{2,1,0:T(8,128)(2,1)S(1)} %get-tuple-element.65), channel_id=1, source_target_pairs={{0,4},{4,0},{8,12},{12,8},{1,5},{5,1},{9,13},{13,9},{2,6},{6,2},{1... | collective-permute-start | bytes 294920 | tf_op jit(solution)/shard_map/ppermute | solution.py:89
  4.9 2.6 %collective-permute-start.1 = (bf16[3,32,512]{2,1,0:T(8,128)(2,1)S(1)}, bf16[3,32,512]{2,1,0:T(8,128)(2,1)S(1)}, u32[]{:S(2)}, u32[]{:S(2)}) collective-permute-start(bf16[3,32,512]{2,1,0:T(8,128)(2,1)S(1)} %get-tuple-element.66), channel_id=1, source_target_pairs={{0,8},{4,12},{8,0},{12,4},{1,9},{5,13},{9,1},{13,5},{2,10},{6,14},... | collective-permute-start | bytes 294920 | tf_op jit(solution)/shard_map/ppermute | solution.py:89
  11.6 3.8 %collective-permute-done.1.refs_1_ = bf16[3,32,512]{2,1,0:T(8,128)(2,1)S(1)} collective-permute-done((bf16[3,32,512]{2,1,0:T(8,128)(2,1)S(1)}, bf16[3,32,512]{2,1,0:T(8,128)(2,1)S(1)}, u32[]{:S(2)}, u32[]{:S(2)}) %collective-permute-start.1) | collective-permute-done | bytes 98336 | tf_op jit(solution)/shard_map/ppermute | solution.py:89
  17.6 2.4 %collective-permute-start.13 = (bf16[3,32,512]{2,1,0:T(8,128)(2,1)S(1)}, bf16[3,32,512]{2,1,0:T(8,128)(2,1)S(1)}, u32[]{:S(2)}, u32[]{:S(2)}) collective-permute-start(bf16[3,32,512]{2,1,0:T(8,128)(2,1)S(1)} %get-tuple-element.72), channel_id=1, source_target_pairs={{0,8},{4,12},{8,0},{12,4},{1,9},{5,13},{9,1},{13,5},{2,10},{6,14},... | collective-permute-start | bytes 294920 | tf_op jit(solution)/shard_map/ppermute | solution.py:89
  24.0 2.1 %shard_map.105 = (bf16[3,192,512]{2,1,0:T(8,128)(2,1)S(1)}, bf16[3,192,512]{2,1,0:T(8,128)(2,1)S(1)}) custom-call(s32[9]{0:T(128)S(1)} %pad_add_fusion.scalar_ref, bf16[3,128,512]{2,1,0:T(8,128)(2,1)S(1)} %get-tuple-element.63.tokens_ref, bf16[3,512,512]{2,1,0:T(8,128)(2,1)S(1)} %get-tuple-element.64.basis_ref, ...), custom_call_target="tpu_custom_call" | custom-call | tf_op jit(solution)/shard_map/pallas_call | solution.py:164
  26.1 2.3 %collective-permute-done.13.refs_1_ = bf16[3,32,512]{2,1,0:T(8,128)(2,1)S(1)} collective-permute-done((bf16[3,32,512]{2,1,0:T(8,128)(2,1)S(1)}, bf16[3,32,512]{2,1,0:T(8,128)(2,1)S(1)}, u32[]{:S(2)}, u32[]{:S(2)}) %collective-permute-start.13) | collective-permute-done | bytes 98336 | tf_op jit(solution)/shard_map/ppermute | solution.py:89
  28.4 1.8 %collective-permute-start.15 = (bf16[3,192,512]{2,1,0:T(8,128)(2,1)S(1)}, bf16[3,192,512]{2,1,0:T(8,128)(2,1)S(1)}, u32[]{:S(2)}, u32[]{:S(2)}) collective-permute-start(bf16[3,192,512]{2,1,0:T(8,128)(2,1)S(1)} %get-tuple-element.74), channel_id=1, source_target_pairs={{0,4},{4,0},{8,12},{12,8},{1,5},{5,1},{9,13},{13,9},{2,6},{6,2},{1... | collective-permute-start | bytes 1769480 | tf_op jit(solution)/shard_map/ppermute | solution.py:89
  34.5 3.7 %collective-permute-done.17.refs_3_ = bf16[3,32,512]{2,1,0:T(8,128)(2,1)S(1)} collective-permute-done((bf16[3,32,512]{2,1,0:T(8,128)(2,1)S(1)}, bf16[3,32,512]{2,1,0:T(8,128)(2,1)S(1)}, u32[]{:S(2)}, u32[]{:S(2)}) %collective-permute-start.17) | collective-permute-done | bytes 98336 | tf_op jit(solution)/shard_map/ppermute | solution.py:89
  39.7 2.1 %shard_map.108 = (bf16[3,192,512]{2,1,0:T(8,128)(2,1)S(1)}, bf16[3,192,512]{2,1,0:T(8,128)(2,1)S(1)}) custom-call(s32[9]{0:T(128)S(1)} %pad_add_fusion.scalar_ref, bf16[3,128,512]{2,1,0:T(8,128)(2,1)S(1)} %get-tuple-element.75.tokens_ref, bf16[3,512,512]{2,1,0:T(8,128)(2,1)S(1)} %get-tuple-element.76.basis_ref, bf16[3,64,512]{2,1,0:T(8,128)(2,1)S(1)} %shard_map.107.refs_0_, ...), custom_call_target="tpu_custom_call" | custom-call | tf_op jit(solution)/shard_map/pallas_call | solution.py:164
  44.4 1.8 %collective-permute-start.22 = (bf16[3,192,512]{2,1,0:T(8,128)(2,1)S(1)}, bf16[3,192,512]{2,1,0:T(8,128)(2,1)S(1)}, u32[]{:S(2)}, u32[]{:S(2)}) collective-permute-start(bf16[3,192,512]{2,1,0:T(8,128)(2,1)S(1)} %get-tuple-element.86), channel_id=1, source_target_pairs={{0,4},{4,0},{8,12},{12,8},{1,5},{5,1},{9,13},{13,9},{2,6},{6,2},{1... | collective-permute-start | bytes 1769480 | tf_op jit(solution)/shard_map/ppermute | solution.py:89
  48.8 6.9 %collective-permute-start.28 = (f32[4,2048]{1,0:T(4,128)S(1)}, f32[4,2048]{1,0:T(4,128)S(1)}, u32[]{:S(2)}, u32[]{:S(2)}) collective-permute-start(f32[4,2048]{1,0:T(4,128)S(1)} %pad_maximum_fusion.refs_0_), channel_id=1, source_target_pairs={{0,3},{1,2},{2,1},{3,0},{4,7},{5,6},{6,5},{7,4},{8,11},{9,10},{10,... | collective-permute-start | bytes 98312 | tf_op jit(solution)/shard_map/ppermute | solution.py:89
  55.7 3.0 %collective-permute-start.27 = (f32[4,2048]{1,0:T(4,128)S(1)}, f32[4,2048]{1,0:T(4,128)S(1)}, u32[]{:S(2)}, u32[]{:S(2)}) collective-permute-start(f32[4,2048]{1,0:T(4,128)S(1)} %pad_maximum_fusion.refs_0_), channel_id=1, source_target_pairs={{0,2},{1,3},{2,0},{3,1},{4,6},{5,7},{6,4},{7,5},{8,10},{9,11},{10,... | collective-permute-start | bytes 98312 | tf_op jit(solution)/shard_map/ppermute | solution.py:89
  58.7 2.0 %collective-permute-start.26 = (f32[4,2048]{1,0:T(4,128)S(1)}, f32[4,2048]{1,0:T(4,128)S(1)}, u32[]{:S(2)}, u32[]{:S(2)}) collective-permute-start(f32[4,2048]{1,0:T(4,128)S(1)} %pad_maximum_fusion.refs_0_), channel_id=1, source_target_pairs={{0,1},{1,0},{2,3},{3,2},{4,5},{5,4},{6,7},{7,6},{8,9},{9,8},{10,11... | collective-permute-start | bytes 98312 | tf_op jit(solution)/shard_map/ppermute | solution.py:89
  65.4 13.3 %collective-permute-done.32.refs_2_ = bf16[3,96,512]{2,1,0:T(8,128)(2,1)S(1)} collective-permute-done((bf16[3,96,512]{2,1,0:T(8,128)(2,1)S(1)}, bf16[3,96,512]{2,1,0:T(8,128)(2,1)S(1)}, u32[]{:S(2)}, u32[]{:S(2)}) %collective-permute-start.32) | collective-permute-done | bytes 294944 | tf_op jit(solution)/shard_map/ppermute | solution.py:95
  78.7 3.2 %collective-permute-done.33.refs_3_ = bf16[3,96,512]{2,1,0:T(8,128)(2,1)S(1)} collective-permute-done((bf16[3,96,512]{2,1,0:T(8,128)(2,1)S(1)}, bf16[3,96,512]{2,1,0:T(8,128)(2,1)S(1)}, u32[]{:S(2)}, u32[]{:S(2)}) %collective-permute-start.33) | collective-permute-done | bytes 294944 | tf_op jit(solution)/shard_map/ppermute | solution.py:95
  83.3 2.1 %collective-permute-start.35 = (bf16[2,192,512]{2,1,0:T(8,128)(2,1)S(1)}, bf16[2,192,512]{2,1,0:T(8,128)(2,1)}, u32[]{:S(2)}, u32[]{:S(2)}) collective-permute-start(bf16[2,192,512]{2,1,0:T(8,128)(2,1)S(1)} %get-tuple-element.103.refs_2_), channel_id=1, source_target_pairs={{0,2},{13,15},{10,8},{7,5},{16,18},{29,31},{26,24},{23,21}} | collective-permute-start | bytes 1179656 | tf_op jit(solution)/shard_map/ppermute | solution.py:95
  85.3 2.1 %collective-permute-start.36 = (bf16[2,192,512]{2,1,0:T(8,128)(2,1)S(1)}, bf16[2,192,512]{2,1,0:T(8,128)(2,1)}, u32[]{:S(2)}, u32[]{:S(2)}) collective-permute-start(bf16[2,192,512]{2,1,0:T(8,128)(2,1)S(1)} %get-tuple-element.105.refs_4_), channel_id=1, source_target_pairs={{0,2},{13,15},{10,8},{7,5},{16,18},{29,31},{26,24},{23,21}} | collective-permute-start | bytes 1179656 | tf_op jit(solution)/shard_map/ppermute | solution.py:95
  87.5 4.7 %collective-permute-done.31.far_ref = f32[3,512]{1,0:T(4,128)S(1)} collective-permute-done((f32[3,512]{1,0:T(4,128)S(1)}, f32[3,512]{1,0:T(4,128)S(1)}, u32[]{:S(2)}, u32[]{:S(2)}) %collective-permute-start.31) | collective-permute-done | bytes 6176 | tf_op jit(solution)/shard_map/ppermute | solution.py:89
  92.7 4.2 %collective-permute-done.36.refs_5_ = bf16[2,192,512]{2,1,0:T(8,128)(2,1)} collective-permute-done((bf16[2,192,512]{2,1,0:T(8,128)(2,1)S(1)}, bf16[2,192,512]{2,1,0:T(8,128)(2,1)}, u32[]{:S(2)}, u32[]{:S(2)}) %collective-permute-start.36) | collective-permute-done | bytes 393248 | tf_op jit(solution)/shard_map/ppermute | solution.py:95
  97.2 3.8 %collective-permute-done.37.far_ref = f32[6,512]{1,0:T(8,128)S(1)} collective-permute-done((f32[6,512]{1,0:T(8,128)S(1)}, f32[6,512]{1,0:T(8,128)S(1)}, u32[]{:S(2)}, u32[]{:S(2)}) %collective-permute-start.37) | collective-permute-done | bytes 12320 | tf_op jit(solution)/shard_map/ppermute | solution.py:89
  104.3 1.8 %collective-permute-done.39.refs_6_ = f32[6,512]{1,0:T(8,128)S(1)} collective-permute-done((f32[6,512]{1,0:T(8,128)S(1)}, f32[6,512]{1,0:T(8,128)S(1)}, u32[]{:S(2)}, u32[]{:S(2)}) %collective-permute-start.39) | collective-permute-done | bytes 12320 | tf_op jit(solution)/shard_map/ppermute | solution.py:89
  107.2 2.4 %collective-permute-start.41 = (bf16[2,192,512]{2,1,0:T(8,128)(2,1)S(1)}, bf16[2,192,512]{2,1,0:T(8,128)(2,1)S(1)}, u32[]{:S(2)}, u32[]{:S(2)}) collective-permute-start(bf16[2,192,512]{2,1,0:T(8,128)(2,1)S(1)} %get-tuple-element.107.refs_0_), channel_id=1, source_target_pairs={{0,1},{2,3},{13,12},{15,14},{10,11},{8,9},{7,6},{5,4},{16,17},{18,... | collective-permute-start | bytes 1179656 | tf_op jit(solution)/shard_map/ppermute | solution.py:95
  112.3 1.9 %shard_map.121 = (f32[3,512,512]{2,1,0:T(8,128)S(1)}, f32[2,2048]{1,0:T(2,128)}, f32[2,2048]{1,0:T(2,128)}) custom-call(s32[9]{0:T(128)S(1)} %pad_add_fusion.scalar_ref, f32[4,2048]{1,0:T(4,128)S(1)} %pad_maximum_fusion.refs_0_, f32[4,2048]{1,0:T(4,128)S(1)} %collective-permute-done.26.refs_1_, f32[4,2048]{1,0:T(4,128)S(1)} %collective-permute-done.27.refs_2_, ...), custom_call_target="tpu_custom_call" | custom-call | tf_op jit(solution)/shard_map/pallas_call | solution.py:457
  115.0 1.8 %shard_map.122 = bf16[3,512,512]{2,1,0:T(8,128)(2,1)} custom-call(bf16[2,192,512]{2,1,0:T(8,128)(2,1)S(1)} %get-tuple-element.115.refs_0_, bf16[2,192,512]{2,1,0:T(8,128)(2,1)S(1)} %get-tuple-element.116.refs_1_, bf16[2,192,512]{2,1,0:T(8,128)(2,1)S(1)} %get-tuple-element.117.refs_2_, bf16[3,192,512]{2,1,0:T(8,128)(2,1)S(1)} %collective-permute-done.44.refs_3_, ...), custom_call_target="tpu_custom_call" | custom-call | tf_op jit(solution)/shard_map/pallas_call | solution.py:390
  (96 shorter events, 37.2 us)
Async XLA Ops:
  1.8 6.6 %collective-permute-start = (bf16[3,32,512]{2,1,0:T(8,128)(2,1)S(1)}, bf16[3,32,512]{2,1,0:T(8,128)(2,1)S(1)}, u32[]{:S(2)}, u32[]{:S(2)}) collective-permute-start(bf16[3,32,512]{2,1,0:T(8,128)(2,1)S(1)} %get-tuple-element.65), channel_id=1, source_target_pairs={{0,4},{4,0},{8,12},{12,8},{1,5},{5,1},{9,13},{13,9},{2,6},{6,2},{1... | collective-permute-start | bytes 294920 | tf_op jit(solution)/shard_map/ppermute | solution.py:89
  4.9 10.4 %collective-permute-start.1 = (bf16[3,32,512]{2,1,0:T(8,128)(2,1)S(1)}, bf16[3,32,512]{2,1,0:T(8,128)(2,1)S(1)}, u32[]{:S(2)}, u32[]{:S(2)}) collective-permute-start(bf16[3,32,512]{2,1,0:T(8,128)(2,1)S(1)} %get-tuple-element.66), channel_id=1, source_target_pairs={{0,8},{4,12},{8,0},{12,4},{1,9},{5,13},{9,1},{13,5},{2,10},{6,14},... | collective-permute-start | bytes 294920 | tf_op jit(solution)/shard_map/ppermute | solution.py:89
  7.5 7.8 %collective-permute-start.2 = (bf16[3,32,512]{2,1,0:T(8,128)(2,1)S(1)}, bf16[3,32,512]{2,1,0:T(8,128)(2,1)S(1)}, u32[]{:S(2)}, u32[]{:S(2)}) collective-permute-start(bf16[3,32,512]{2,1,0:T(8,128)(2,1)S(1)} %get-tuple-element.67), channel_id=1, source_target_pairs={{0,12},{4,8},{8,4},{12,0},{1,13},{5,9},{9,5},{13,1},{2,14},{6,10},... | collective-permute-start | bytes 294920 | tf_op jit(solution)/shard_map/ppermute | solution.py:89
  7.5 7.8 %collective-permute-start.3 = (bf16[3,32,512]{2,1,0:T(8,128)(2,1)S(1)}, bf16[3,32,512]{2,1,0:T(8,128)(2,1)S(1)}, u32[]{:S(2)}, u32[]{:S(2)}) collective-permute-start(bf16[3,32,512]{2,1,0:T(8,128)(2,1)S(1)} %get-tuple-element.68), channel_id=1, source_target_pairs={{0,4},{4,0},{8,12},{12,8},{1,5},{5,1},{9,13},{13,9},{2,6},{6,2},{1... | collective-permute-start | bytes 294920 | tf_op jit(solution)/shard_map/ppermute | solution.py:89
  8.4 8.7 %collective-permute-start.7 = (bf16[3,32,512]{2,1,0:T(8,128)(2,1)S(1)}, bf16[3,32,512]{2,1,0:T(8,128)(2,1)S(1)}, u32[]{:S(2)}, u32[]{:S(2)}) collective-permute-start(bf16[3,32,512]{2,1,0:T(8,128)(2,1)S(1)} %collective-permute-done.refs_0_), channel_id=1, source_target_pairs={{0,1},{1,0},{2,3},{3,2},{4,5},{5,4},{6,7},{7,6},{8,9},{9,8},{10,11... | collective-permute-start | bytes 294920 | tf_op jit(solution)/shard_map/ppermute | solution.py:89
  10.0 7.6 %collective-permute-start.4 = (bf16[3,32,512]{2,1,0:T(8,128)(2,1)S(1)}, bf16[3,32,512]{2,1,0:T(8,128)(2,1)S(1)}, u32[]{:S(2)}, u32[]{:S(2)}) collective-permute-start(bf16[3,32,512]{2,1,0:T(8,128)(2,1)S(1)} %collective-permute-done.refs_0_), channel_id=1, source_target_pairs={{0,2},{1,3},{2,0},{3,1},{4,6},{5,7},{6,4},{7,5},{8,10},{9,11},{10,... | collective-permute-start | bytes 294920 | tf_op jit(solution)/shard_map/ppermute | solution.py:89
  15.4 6.0 %collective-permute-start.5 = (bf16[3,32,512]{2,1,0:T(8,128)(2,1)S(1)}, bf16[3,32,512]{2,1,0:T(8,128)(2,1)S(1)}, u32[]{:S(2)}, u32[]{:S(2)}) collective-permute-start(bf16[3,32,512]{2,1,0:T(8,128)(2,1)S(1)} %collective-permute-done.1.refs_1_), channel_id=1, source_target_pairs={{0,2},{1,3},{2,0},{3,1},{4,6},{5,7},{6,4},{7,5},{8,10},{9,11},{10,... | collective-permute-start | bytes 294920 | tf_op jit(solution)/shard_map/ppermute | solution.py:89
  17.6 10.8 %collective-permute-start.13 = (bf16[3,32,512]{2,1,0:T(8,128)(2,1)S(1)}, bf16[3,32,512]{2,1,0:T(8,128)(2,1)S(1)}, u32[]{:S(2)}, u32[]{:S(2)}) collective-permute-start(bf16[3,32,512]{2,1,0:T(8,128)(2,1)S(1)} %get-tuple-element.72), channel_id=1, source_target_pairs={{0,8},{4,12},{8,0},{12,4},{1,9},{5,13},{9,1},{13,5},{2,10},{6,14},... | collective-permute-start | bytes 294920 | tf_op jit(solution)/shard_map/ppermute | solution.py:89
  20.0 8.4 %collective-permute-start.14 = (bf16[3,32,512]{2,1,0:T(8,128)(2,1)S(1)}, bf16[3,32,512]{2,1,0:T(8,128)(2,1)S(1)}, u32[]{:S(2)}, u32[]{:S(2)}) collective-permute-start(bf16[3,32,512]{2,1,0:T(8,128)(2,1)S(1)} %get-tuple-element.73), channel_id=1, source_target_pairs={{0,12},{4,8},{8,4},{12,0},{1,13},{5,9},{9,5},{13,1},{2,14},{6,10},... | collective-permute-start | bytes 294920 | tf_op jit(solution)/shard_map/ppermute | solution.py:89
  28.4 14.5 %collective-permute-start.15 = (bf16[3,192,512]{2,1,0:T(8,128)(2,1)S(1)}, bf16[3,192,512]{2,1,0:T(8,128)(2,1)S(1)}, u32[]{:S(2)}, u32[]{:S(2)}) collective-permute-start(bf16[3,192,512]{2,1,0:T(8,128)(2,1)S(1)} %get-tuple-element.74), channel_id=1, source_target_pairs={{0,4},{4,0},{8,12},{12,8},{1,5},{5,1},{9,13},{13,9},{2,6},{6,2},{1... | collective-permute-start | bytes 1769480 | tf_op jit(solution)/shard_map/ppermute | solution.py:89
  30.2 7.9 %collective-permute-start.16 = (bf16[3,64,512]{2,1,0:T(8,128)(2,1)S(1)}, bf16[3,64,512]{2,1,0:T(8,128)(2,1)S(1)}, u32[]{:S(2)}, u32[]{:S(2)}) collective-permute-start(bf16[3,64,512]{2,1,0:T(8,128)(2,1)S(1)} %shard_map.107.refs_0_), channel_id=1, source_target_pairs={{0,2},{1,3},{2,0},{3,1},{4,6},{5,7},{6,4},{7,5},{8,10},{9,11},{10,... | collective-permute-start | bytes 589832 | tf_op jit(solution)/shard_map/ppermute | solution.py:89
  31.8 6.4 %collective-permute-start.17 = (bf16[3,32,512]{2,1,0:T(8,128)(2,1)S(1)}, bf16[3,32,512]{2,1,0:T(8,128)(2,1)S(1)}, u32[]{:S(2)}, u32[]{:S(2)}) collective-permute-start(bf16[3,32,512]{2,1,0:T(8,128)(2,1)S(1)} %collective-permute-done.14.refs_1_), channel_id=1, source_target_pairs={{0,2},{1,3},{2,0},{3,1},{4,6},{5,7},{6,4},{7,5},{8,10},{9,11},{10,... | collective-permute-start | bytes 294920 | tf_op jit(solution)/shard_map/ppermute | solution.py:89
  44.4 20.3 %collective-permute-start.22 = (bf16[3,192,512]{2,1,0:T(8,128)(2,1)S(1)}, bf16[3,192,512]{2,1,0:T(8,128)(2,1)S(1)}, u32[]{:S(2)}, u32[]{:S(2)}) collective-permute-start(bf16[3,192,512]{2,1,0:T(8,128)(2,1)S(1)} %get-tuple-element.86), channel_id=1, source_target_pairs={{0,4},{4,0},{8,12},{12,8},{1,5},{5,1},{9,13},{13,9},{2,6},{6,2},{1... | collective-permute-start | bytes 1769480 | tf_op jit(solution)/shard_map/ppermute | solution.py:89
  46.2 15.3 %collective-permute-start.25 = (bf16[3,96,512]{2,1,0:T(8,128)(2,1)S(1)}, bf16[3,96,512]{2,1,0:T(8,128)(2,1)S(1)}, u32[]{:S(2)}, u32[]{:S(2)}) collective-permute-start(bf16[3,96,512]{2,1,0:T(8,128)(2,1)S(1)} %collective-permute-done.24.refs_0_), channel_id=1, source_target_pairs={{1,9},{2,10},{5,13},{6,14},{8,0},{11,3},{12,4},{15,7},{17,25},{18,... | collective-permute-start | bytes 884744 | tf_op jit(solution)/shard_map/ppermute | solution.py:95
  47.5 15.4 %collective-permute-start.30 = (bf16[3,96,512]{2,1,0:T(8,128)(2,1)S(1)}, bf16[3,96,512]{2,1,0:T(8,128)(2,1)S(1)}, u32[]{:S(2)}, u32[]{:S(2)}) collective-permute-start(bf16[3,96,512]{2,1,0:T(8,128)(2,1)S(1)} %collective-permute-done.29.refs_0_), channel_id=1, source_target_pairs={{1,9},{2,10},{5,13},{6,14},{8,0},{11,3},{12,4},{15,7},{17,25},{18,... | collective-permute-start | bytes 884744 | tf_op jit(solution)/shard_map/ppermute | solution.py:95
  48.8 9.9 %collective-permute-start.28 = (f32[4,2048]{1,0:T(4,128)S(1)}, f32[4,2048]{1,0:T(4,128)S(1)}, u32[]{:S(2)}, u32[]{:S(2)}) collective-permute-start(f32[4,2048]{1,0:T(4,128)S(1)} %pad_maximum_fusion.refs_0_), channel_id=1, source_target_pairs={{0,3},{1,2},{2,1},{3,0},{4,7},{5,6},{6,5},{7,4},{8,11},{9,10},{10,... | collective-permute-start | bytes 98312 | tf_op jit(solution)/shard_map/ppermute | solution.py:89
  61.6 17.1 %collective-permute-start.32 = (bf16[3,96,512]{2,1,0:T(8,128)(2,1)S(1)}, bf16[3,96,512]{2,1,0:T(8,128)(2,1)S(1)}, u32[]{:S(2)}, u32[]{:S(2)}) collective-permute-start(bf16[3,96,512]{2,1,0:T(8,128)(2,1)S(1)} %shard_map.111.refs_0_), channel_id=1, source_target_pairs={{4,0},{9,13},{14,10},{3,7},{20,16},{25,29},{30,26},{19,23}} | collective-permute-start | bytes 884744 | tf_op jit(solution)/shard_map/ppermute | solution.py:95
  63.0 18.9 %collective-permute-start.33 = (bf16[3,96,512]{2,1,0:T(8,128)(2,1)S(1)}, bf16[3,96,512]{2,1,0:T(8,128)(2,1)S(1)}, u32[]{:S(2)}, u32[]{:S(2)}) collective-permute-start(bf16[3,96,512]{2,1,0:T(8,128)(2,1)S(1)} %shard_map.112.refs_1_), channel_id=1, source_target_pairs={{4,0},{9,13},{14,10},{3,7},{20,16},{25,29},{30,26},{19,23}} | collective-permute-start | bytes 884744 | tf_op jit(solution)/shard_map/ppermute | solution.py:95
  64.8 27.4 %collective-permute-start.23 = (bf16[3,192,512]{2,1,0:T(8,128)(2,1)S(1)}, bf16[3,192,512]{2,1,0:T(8,128)(2,1)S(1)}, u32[]{:S(2)}, u32[]{:S(2)}) collective-permute-start(bf16[3,192,512]{2,1,0:T(8,128)(2,1)S(1)} %shard_map.109.refs_0_), channel_id=1, source_target_pairs={{0,8},{4,12},{8,0},{12,4},{1,9},{5,13},{9,1},{13,5},{2,10},{6,14},... | collective-permute-start | bytes 1769480 | tf_op jit(solution)/shard_map/ppermute | solution.py:89
  81.9 10.3 %collective-permute-start.34 = (bf16[2,192,512]{2,1,0:T(8,128)(2,1)S(1)}, bf16[2,192,512]{2,1,0:T(8,128)(2,1)S(1)}, u32[]{:S(2)}, u32[]{:S(2)}) collective-permute-start(bf16[2,192,512]{2,1,0:T(8,128)(2,1)S(1)} %get-tuple-element.101.refs_0_), channel_id=1, source_target_pairs={{0,2},{13,15},{10,8},{7,5},{16,18},{29,31},{26,24},{23,21}} | collective-permute-start | bytes 1179656 | tf_op jit(solution)/shard_map/ppermute | solution.py:95
  83.3 9.5 %collective-permute-start.35 = (bf16[2,192,512]{2,1,0:T(8,128)(2,1)S(1)}, bf16[2,192,512]{2,1,0:T(8,128)(2,1)}, u32[]{:S(2)}, u32[]{:S(2)}) collective-permute-start(bf16[2,192,512]{2,1,0:T(8,128)(2,1)S(1)} %get-tuple-element.103.refs_2_), channel_id=1, source_target_pairs={{0,2},{13,15},{10,8},{7,5},{16,18},{29,31},{26,24},{23,21}} | collective-permute-start | bytes 1179656 | tf_op jit(solution)/shard_map/ppermute | solution.py:95
  85.3 11.6 %collective-permute-start.36 = (bf16[2,192,512]{2,1,0:T(8,128)(2,1)S(1)}, bf16[2,192,512]{2,1,0:T(8,128)(2,1)}, u32[]{:S(2)}, u32[]{:S(2)}) collective-permute-start(bf16[2,192,512]{2,1,0:T(8,128)(2,1)S(1)} %get-tuple-element.105.refs_4_), channel_id=1, source_target_pairs={{0,2},{13,15},{10,8},{7,5},{16,18},{29,31},{26,24},{23,21}} | collective-permute-start | bytes 1179656 | tf_op jit(solution)/shard_map/ppermute | solution.py:95
  101.0 13.9 %collective-permute-start.44 = (bf16[3,192,512]{2,1,0:T(8,128)(2,1)S(1)}, bf16[3,192,512]{2,1,0:T(8,128)(2,1)S(1)}, u32[]{:S(2)}, u32[]{:S(2)}) collective-permute-start(bf16[3,192,512]{2,1,0:T(8,128)(2,1)S(1)} %shard_map.115.act_ref.refs_3_), channel_id=1, source_target_pairs={{0,4},{4,0},{8,12},{12,8},{1,5},{5,1},{9,13},{13,9},{2,6},{6,2},{1... | collective-permute-start | bytes 1769480 | tf_op jit(solution)/shard_map/ppermute | solution.py:89
  107.2 7.0 %collective-permute-start.41 = (bf16[2,192,512]{2,1,0:T(8,128)(2,1)S(1)}, bf16[2,192,512]{2,1,0:T(8,128)(2,1)S(1)}, u32[]{:S(2)}, u32[]{:S(2)}) collective-permute-start(bf16[2,192,512]{2,1,0:T(8,128)(2,1)S(1)} %get-tuple-element.107.refs_0_), channel_id=1, source_target_pairs={{0,1},{2,3},{13,12},{15,14},{10,11},{8,9},{7,6},{5,4},{16,17},{18,... | collective-permute-start | bytes 1179656 | tf_op jit(solution)/shard_map/ppermute | solution.py:95
  (25 other events, 120.2 us)

commit v11 on v10

--- a/solution.py
+++ b/solution.py
@@ -324,23 +324,29 @@
     )(aside, *panels)
 
 
-def halves_of(act, near, far):
-    layers, _, cols = act.shape
-
-    def kernel(act_ref, near_ref, far_ref, out_ref):
+def settle(part, cross, near, far):
+    layers, _, cols = part.shape
+
+    def kernel(part_ref, cross_ref, near_ref, far_ref, act_ref, out_ref):
         for layer in range(layers):
-            wide = act_ref[layer].astype(jnp.float32)
+            total = part_ref[layer].astype(jnp.float32) + cross_ref[layer].astype(jnp.float32)
+            total = total.astype(act_ref.dtype)
+            act_ref[layer] = total
+            wide = total.astype(jnp.float32)
             out_ref[layer : layer + 1] = jnp.sum(wide * wide, axis=0, keepdims=True)
         out_ref[layers:] = near_ref[...] + far_ref[...]
 
     return pl.pallas_call(
         kernel,
-        out_shape=jax.ShapeDtypeStruct((2 * layers, cols), jnp.float32),
-        in_specs=[vmem_spec] * 3,
-        out_specs=vmem_spec,
-        compiler_params=pltpu.CompilerParams(vmem_limit_bytes=8 * 1024 * 1024),
-        cost_estimate=light,
-    )(act, near, far)
+        out_shape=[
+            jax.ShapeDtypeStruct(part.shape, part.dtype),
+            jax.ShapeDtypeStruct((2 * layers, cols), jnp.float32),
+        ],
+        in_specs=[vmem_spec] * 4,
+        out_specs=[vmem_spec] * 2,
+        compiler_params=pltpu.CompilerParams(vmem_limit_bytes=8 * 1024 * 1024),
+        cost_estimate=light,
+    )(part, cross, near, far)
 
 
 def total_of(near, far):
@@ -521,16 +527,16 @@
 
     done = step([part_act, cross_act, square_grad, square_far, *full, *chip])
     (part_act, cross_act, square_grad, square_far), full, chip = done[:4], done[4:][:layers], done[4 + layers :]
-    full_act = add((part_act, cross_act))
-    half = halves_of(full_act, square_grad, square_far)
-    packet = total_of(half, flip(half, "dp", 1))
-    back_act = flip(after(full_act, packet), "dp", 1)
-    packets = [packet] + [flip(packet, "owner", mask) for mask in range(1, n_own)]
+    full_act, half = settle(part_act, cross_act, square_grad, square_far)
+    other = flip(half, "dp", 1)
     source = -dp % n_own
     home = jnp.where(own == source, 0, jnp.where(own == source ^ 2, 1, 2)).astype(jnp.int32)[None]
-    full = pick(after(home, *packets), [*zip(full, chip, strict=True)])
+    full = pick(after(home, half), [*zip(full, chip, strict=True)])
+    back_act = flip(after(full_act, other, *full), "dp", 1)
+    packet = total_of(half, other)
+    packets = [packet] + [flip(packet, "owner", mask) for mask in range(1, n_own)]
     to_core = [((held[o], o ^ b), (held[o], o ^ b ^ 1)) for o in owners for b in (0, 2)]
-    core = [hop(array, to_core) for array in full]
+    core = [hop(after(array, *packets), to_core) for array in full]
     factors, new_act, new_grad = eigenvalues(scalars, states, packets, n_dp)
     grads = pick(home // 2, [*zip(full, core, strict=True)])
     grams = gram_of(grads, full_act)

time: 118 us -> 118 us (level)
  no operation moved by 1% of the time
where the time goes in v11:
time: 118 us; the launch traced here: 116 us
  starting transfers between devices  53.7 us (46%)
  waiting for transfers between devices  46 us (39%)
  Pallas kernels  14.9 us (13%)
    ppermute x33, starting transfers between devices, flip(): lax.ppermute(array, axis, [(i, i ^ mask) for i in range(lax.axis_size(axi...  36.7 us
    ppermute x33, waiting for transfers between devices, flip(): lax.ppermute(array, axis, [(i, i ^ mask) for i in range(lax.axis_size(axi...  24.8 us
    ppermute x10, waiting for transfers between devices, hop(): return lax.ppermute(array, ('dp', 'owner'), flat)  21.2 us
    ppermute x10, starting transfers between devices, hop(): return lax.ppermute(array, ('dp', 'owner'), flat)  15.6 us
    pallas_call x2, Pallas kernels, project_rows(): pl.pallas_call(kernel, out_shape=[jax.ShapeDtypeStruct(shape, jnp.bfloat1...  4.17 us
    pallas_call x2, Pallas kernels, load(): pl.pallas_call(kernel, out_shape=[jax.ShapeDtypeStruct(shape, array.dtype...  3.12 us
  transfers between devices with their start and end apart: 45, of which 20 were waited for; matrix products, arithmetic and copies ran while one was open for 0% of the time, Pallas kernels for 10%

profile of v11, /device:TPU:0, one launch (start us, length us, event | category | flops | bytes accessed | tf_op | source)
XLA Modules:
  0.0 115.7 jit_solution(12413758312412065688)
XLA Ops:
  1.8 3.1 %collective-permute-start = (bf16[3,32,512]{2,1,0:T(8,128)(2,1)S(1)}, bf16[3,32,512]{2,1,0:T(8,128)(2,1)S(1)}, u32[]{:S(2)}, u32[]{:S(2)}) collective-permute-start(bf16[3,32,512]{2,1,0:T(8,128)(2,1)S(1)} %get-tuple-element.70), channel_id=1, source_target_pairs={{0,4},{4,0},{8,12},{12,8},{1,5},{5,1},{9,13},{13,9},{2,6},{6,2},{1... | collective-permute-start | bytes 294920 | tf_op jit(solution)/shard_map/ppermute | solution.py:89
  4.9 2.6 %collective-permute-start.1 = (bf16[3,32,512]{2,1,0:T(8,128)(2,1)S(1)}, bf16[3,32,512]{2,1,0:T(8,128)(2,1)S(1)}, u32[]{:S(2)}, u32[]{:S(2)}) collective-permute-start(bf16[3,32,512]{2,1,0:T(8,128)(2,1)S(1)} %get-tuple-element.71), channel_id=1, source_target_pairs={{0,8},{4,12},{8,0},{12,4},{1,9},{5,13},{9,1},{13,5},{2,10},{6,14},... | collective-permute-start | bytes 294920 | tf_op jit(solution)/shard_map/ppermute | solution.py:89
  11.6 3.8 %collective-permute-done.1.refs_1_ = bf16[3,32,512]{2,1,0:T(8,128)(2,1)S(1)} collective-permute-done((bf16[3,32,512]{2,1,0:T(8,128)(2,1)S(1)}, bf16[3,32,512]{2,1,0:T(8,128)(2,1)S(1)}, u32[]{:S(2)}, u32[]{:S(2)}) %collective-permute-start.1) | collective-permute-done | bytes 98336 | tf_op jit(solution)/shard_map/ppermute | solution.py:89
  17.6 2.4 %collective-permute-start.13 = (bf16[3,32,512]{2,1,0:T(8,128)(2,1)S(1)}, bf16[3,32,512]{2,1,0:T(8,128)(2,1)S(1)}, u32[]{:S(2)}, u32[]{:S(2)}) collective-permute-start(bf16[3,32,512]{2,1,0:T(8,128)(2,1)S(1)} %get-tuple-element.77), channel_id=1, source_target_pairs={{0,8},{4,12},{8,0},{12,4},{1,9},{5,13},{9,1},{13,5},{2,10},{6,14},... | collective-permute-start | bytes 294920 | tf_op jit(solution)/shard_map/ppermute | solution.py:89
  24.0 2.1 %shard_map.105 = (bf16[3,192,512]{2,1,0:T(8,128)(2,1)S(1)}, bf16[3,192,512]{2,1,0:T(8,128)(2,1)S(1)}) custom-call(s32[9]{0:T(128)S(1)} %pad_add_fusion.scalar_ref, bf16[3,128,512]{2,1,0:T(8,128)(2,1)S(1)} %get-tuple-element.68.tokens_ref, bf16[3,512,512]{2,1,0:T(8,128)(2,1)S(1)} %get-tuple-element.69.basis_ref, ...), custom_call_target="tpu_custom_call" | custom-call | tf_op jit(solution)/shard_map/pallas_call | solution.py:164
  26.1 2.3 %collective-permute-done.13.refs_1_ = bf16[3,32,512]{2,1,0:T(8,128)(2,1)S(1)} collective-permute-done((bf16[3,32,512]{2,1,0:T(8,128)(2,1)S(1)}, bf16[3,32,512]{2,1,0:T(8,128)(2,1)S(1)}, u32[]{:S(2)}, u32[]{:S(2)}) %collective-permute-start.13) | collective-permute-done | bytes 98336 | tf_op jit(solution)/shard_map/ppermute | solution.py:89
  28.4 1.8 %collective-permute-start.15 = (bf16[3,192,512]{2,1,0:T(8,128)(2,1)S(1)}, bf16[3,192,512]{2,1,0:T(8,128)(2,1)S(1)}, u32[]{:S(2)}, u32[]{:S(2)}) collective-permute-start(bf16[3,192,512]{2,1,0:T(8,128)(2,1)S(1)} %get-tuple-element.79), channel_id=1, source_target_pairs={{0,4},{4,0},{8,12},{12,8},{1,5},{5,1},{9,13},{13,9},{2,6},{6,2},{1... | collective-permute-start | bytes 1769480 | tf_op jit(solution)/shard_map/ppermute | solution.py:89
  34.5 3.7 %collective-permute-done.17.refs_3_ = bf16[3,32,512]{2,1,0:T(8,128)(2,1)S(1)} collective-permute-done((bf16[3,32,512]{2,1,0:T(8,128)(2,1)S(1)}, bf16[3,32,512]{2,1,0:T(8,128)(2,1)S(1)}, u32[]{:S(2)}, u32[]{:S(2)}) %collective-permute-start.17) | collective-permute-done | bytes 98336 | tf_op jit(solution)/shard_map/ppermute | solution.py:89
  39.7 2.1 %shard_map.108 = (bf16[3,192,512]{2,1,0:T(8,128)(2,1)S(1)}, bf16[3,192,512]{2,1,0:T(8,128)(2,1)S(1)}) custom-call(s32[9]{0:T(128)S(1)} %pad_add_fusion.scalar_ref, bf16[3,128,512]{2,1,0:T(8,128)(2,1)S(1)} %get-tuple-element.80.tokens_ref, bf16[3,512,512]{2,1,0:T(8,128)(2,1)S(1)} %get-tuple-element.81.basis_ref, bf16[3,64,512]{2,1,0:T(8,128)(2,1)S(1)} %shard_map.107.refs_0_, ...), custom_call_target="tpu_custom_call" | custom-call | tf_op jit(solution)/shard_map/pallas_call | solution.py:164
  44.4 1.8 %collective-permute-start.22 = (bf16[3,192,512]{2,1,0:T(8,128)(2,1)S(1)}, bf16[3,192,512]{2,1,0:T(8,128)(2,1)S(1)}, u32[]{:S(2)}, u32[]{:S(2)}) collective-permute-start(bf16[3,192,512]{2,1,0:T(8,128)(2,1)S(1)} %get-tuple-element.91), channel_id=1, source_target_pairs={{0,4},{4,0},{8,12},{12,8},{1,5},{5,1},{9,13},{13,9},{2,6},{6,2},{1... | collective-permute-start | bytes 1769480 | tf_op jit(solution)/shard_map/ppermute | solution.py:89
  48.8 6.9 %collective-permute-start.28 = (f32[4,2048]{1,0:T(4,128)S(1)}, f32[4,2048]{1,0:T(4,128)S(1)}, u32[]{:S(2)}, u32[]{:S(2)}) collective-permute-start(f32[4,2048]{1,0:T(4,128)S(1)} %pad_maximum_fusion.refs_0_), channel_id=1, source_target_pairs={{0,3},{1,2},{2,1},{3,0},{4,7},{5,6},{6,5},{7,4},{8,11},{9,10},{10,... | collective-permute-start | bytes 98312 | tf_op jit(solution)/shard_map/ppermute | solution.py:89
  55.7 3.0 %collective-permute-start.27 = (f32[4,2048]{1,0:T(4,128)S(1)}, f32[4,2048]{1,0:T(4,128)S(1)}, u32[]{:S(2)}, u32[]{:S(2)}) collective-permute-start(f32[4,2048]{1,0:T(4,128)S(1)} %pad_maximum_fusion.refs_0_), channel_id=1, source_target_pairs={{0,2},{1,3},{2,0},{3,1},{4,6},{5,7},{6,4},{7,5},{8,10},{9,11},{10,... | collective-permute-start | bytes 98312 | tf_op jit(solution)/shard_map/ppermute | solution.py:89
  58.7 2.0 %collective-permute-start.26 = (f32[4,2048]{1,0:T(4,128)S(1)}, f32[4,2048]{1,0:T(4,128)S(1)}, u32[]{:S(2)}, u32[]{:S(2)}) collective-permute-start(f32[4,2048]{1,0:T(4,128)S(1)} %pad_maximum_fusion.refs_0_), channel_id=1, source_target_pairs={{0,1},{1,0},{2,3},{3,2},{4,5},{5,4},{6,7},{7,6},{8,9},{9,8},{10,11... | collective-permute-start | bytes 98312 | tf_op jit(solution)/shard_map/ppermute | solution.py:89
  65.4 13.3 %collective-permute-done.32.refs_2_ = bf16[3,96,512]{2,1,0:T(8,128)(2,1)S(1)} collective-permute-done((bf16[3,96,512]{2,1,0:T(8,128)(2,1)S(1)}, bf16[3,96,512]{2,1,0:T(8,128)(2,1)S(1)}, u32[]{:S(2)}, u32[]{:S(2)}) %collective-permute-start.32) | collective-permute-done | bytes 294944 | tf_op jit(solution)/shard_map/ppermute | solution.py:95
  78.7 3.2 %collective-permute-done.33.refs_3_ = bf16[3,96,512]{2,1,0:T(8,128)(2,1)S(1)} collective-permute-done((bf16[3,96,512]{2,1,0:T(8,128)(2,1)S(1)}, bf16[3,96,512]{2,1,0:T(8,128)(2,1)S(1)}, u32[]{:S(2)}, u32[]{:S(2)}) %collective-permute-start.33) | collective-permute-done | bytes 294944 | tf_op jit(solution)/shard_map/ppermute | solution.py:95
  83.3 2.1 %collective-permute-start.35 = (bf16[2,192,512]{2,1,0:T(8,128)(2,1)S(1)}, bf16[2,192,512]{2,1,0:T(8,128)(2,1)}, u32[]{:S(2)}, u32[]{:S(2)}) collective-permute-start(bf16[2,192,512]{2,1,0:T(8,128)(2,1)S(1)} %get-tuple-element.109.refs_2_), channel_id=1, source_target_pairs={{0,2},{13,15},{10,8},{7,5},{16,18},{29,31},{26,24},{23,21}} | collective-permute-start | bytes 1179656 | tf_op jit(solution)/shard_map/ppermute | solution.py:95
  85.3 2.1 %collective-permute-start.36 = (bf16[2,192,512]{2,1,0:T(8,128)(2,1)S(1)}, bf16[2,192,512]{2,1,0:T(8,128)(2,1)}, u32[]{:S(2)}, u32[]{:S(2)}) collective-permute-start(bf16[2,192,512]{2,1,0:T(8,128)(2,1)S(1)} %get-tuple-element.111.refs_4_), channel_id=1, source_target_pairs={{0,2},{13,15},{10,8},{7,5},{16,18},{29,31},{26,24},{23,21}} | collective-permute-start | bytes 1179656 | tf_op jit(solution)/shard_map/ppermute | solution.py:95
  87.5 4.7 %collective-permute-done.31.far_ref = f32[3,512]{1,0:T(4,128)S(1)} collective-permute-done((f32[3,512]{1,0:T(4,128)S(1)}, f32[3,512]{1,0:T(4,128)S(1)}, u32[]{:S(2)}, u32[]{:S(2)}) %collective-permute-start.31) | collective-permute-done | bytes 6176 | tf_op jit(solution)/shard_map/ppermute | solution.py:89
  92.7 4.2 %collective-permute-done.36.refs_5_ = bf16[2,192,512]{2,1,0:T(8,128)(2,1)} collective-permute-done((bf16[2,192,512]{2,1,0:T(8,128)(2,1)S(1)}, bf16[2,192,512]{2,1,0:T(8,128)(2,1)}, u32[]{:S(2)}, u32[]{:S(2)}) %collective-permute-start.36) | collective-permute-done | bytes 393248 | tf_op jit(solution)/shard_map/ppermute | solution.py:95
  98.5 2.6 %collective-permute-done.37.far_ref = f32[6,512]{1,0:T(8,128)S(1)} collective-permute-done((f32[6,512]{1,0:T(8,128)S(1)}, f32[6,512]{1,0:T(8,128)S(1)}, u32[]{:S(2)}, u32[]{:S(2)}) %collective-permute-start.37) | collective-permute-done | bytes 12320 | tf_op jit(solution)/shard_map/ppermute | solution.py:89
  104.4 1.8 %collective-permute-done.39.refs_6_ = f32[6,512]{1,0:T(8,128)S(1)} collective-permute-done((f32[6,512]{1,0:T(8,128)S(1)}, f32[6,512]{1,0:T(8,128)S(1)}, u32[]{:S(2)}, u32[]{:S(2)}) %collective-permute-start.39) | collective-permute-done | bytes 12320 | tf_op jit(solution)/shard_map/ppermute | solution.py:89
  106.2 2.4 %collective-permute-start.41 = (bf16[2,192,512]{2,1,0:T(8,128)(2,1)S(1)}, bf16[2,192,512]{2,1,0:T(8,128)(2,1)S(1)}, u32[]{:S(2)}, u32[]{:S(2)}) collective-permute-start(bf16[2,192,512]{2,1,0:T(8,128)(2,1)S(1)} %get-tuple-element.114.refs_0_), channel_id=1, source_target_pairs={{0,1},{2,3},{13,12},{15,14},{10,11},{8,9},{7,6},{5,4},{16,17},{18,... | collective-permute-start | bytes 1179656 | tf_op jit(solution)/shard_map/ppermute | solution.py:95
  111.3 1.9 %shard_map.120 = (f32[3,512,512]{2,1,0:T(8,128)S(1)}, f32[2,2048]{1,0:T(2,128)}, f32[2,2048]{1,0:T(2,128)}) custom-call(s32[9]{0:T(128)S(1)} %pad_add_fusion.scalar_ref, f32[4,2048]{1,0:T(4,128)S(1)} %pad_maximum_fusion.refs_0_, f32[4,2048]{1,0:T(4,128)S(1)} %collective-permute-done.26.refs_1_, f32[4,2048]{1,0:T(4,128)S(1)} %collective-permute-done.27.refs_2_, ...), custom_call_target="tpu_custom_call" | custom-call | tf_op jit(solution)/shard_map/pallas_call | solution.py:463
  114.0 1.8 %shard_map.121 = bf16[3,512,512]{2,1,0:T(8,128)(2,1)} custom-call(bf16[2,192,512]{2,1,0:T(8,128)(2,1)S(1)} %get-tuple-element.125.refs_0_, bf16[2,192,512]{2,1,0:T(8,128)(2,1)S(1)} %get-tuple-element.126.refs_1_, bf16[2,192,512]{2,1,0:T(8,128)(2,1)S(1)} %get-tuple-element.127.refs_2_, bf16[3,192,512]{2,1,0:T(8,128)(2,1)S(1)} %collective-permute-done.44.refs_3_, ...), custom_call_target="tpu_custom_call" | custom-call | tf_op jit(solution)/shard_map/pallas_call | solution.py:396
  (95 shorter events, 37.3 us)
Async XLA Ops:
  1.8 6.6 %collective-permute-start = (bf16[3,32,512]{2,1,0:T(8,128)(2,1)S(1)}, bf16[3,32,512]{2,1,0:T(8,128)(2,1)S(1)}, u32[]{:S(2)}, u32[]{:S(2)}) collective-permute-start(bf16[3,32,512]{2,1,0:T(8,128)(2,1)S(1)} %get-tuple-element.70), channel_id=1, source_target_pairs={{0,4},{4,0},{8,12},{12,8},{1,5},{5,1},{9,13},{13,9},{2,6},{6,2},{1... | collective-permute-start | bytes 294920 | tf_op jit(solution)/shard_map/ppermute | solution.py:89
  4.9 10.4 %collective-permute-start.1 = (bf16[3,32,512]{2,1,0:T(8,128)(2,1)S(1)}, bf16[3,32,512]{2,1,0:T(8,128)(2,1)S(1)}, u32[]{:S(2)}, u32[]{:S(2)}) collective-permute-start(bf16[3,32,512]{2,1,0:T(8,128)(2,1)S(1)} %get-tuple-element.71), channel_id=1, source_target_pairs={{0,8},{4,12},{8,0},{12,4},{1,9},{5,13},{9,1},{13,5},{2,10},{6,14},... | collective-permute-start | bytes 294920 | tf_op jit(solution)/shard_map/ppermute | solution.py:89
  7.5 7.8 %collective-permute-start.2 = (bf16[3,32,512]{2,1,0:T(8,128)(2,1)S(1)}, bf16[3,32,512]{2,1,0:T(8,128)(2,1)S(1)}, u32[]{:S(2)}, u32[]{:S(2)}) collective-permute-start(bf16[3,32,512]{2,1,0:T(8,128)(2,1)S(1)} %get-tuple-element.72), channel_id=1, source_target_pairs={{0,12},{4,8},{8,4},{12,0},{1,13},{5,9},{9,5},{13,1},{2,14},{6,10},... | collective-permute-start | bytes 294920 | tf_op jit(solution)/shard_map/ppermute | solution.py:89
  7.5 7.8 %collective-permute-start.3 = (bf16[3,32,512]{2,1,0:T(8,128)(2,1)S(1)}, bf16[3,32,512]{2,1,0:T(8,128)(2,1)S(1)}, u32[]{:S(2)}, u32[]{:S(2)}) collective-permute-start(bf16[3,32,512]{2,1,0:T(8,128)(2,1)S(1)} %get-tuple-element.73), channel_id=1, source_target_pairs={{0,4},{4,0},{8,12},{12,8},{1,5},{5,1},{9,13},{13,9},{2,6},{6,2},{1... | collective-permute-start | bytes 294920 | tf_op jit(solution)/shard_map/ppermute | solution.py:89
  8.4 8.7 %collective-permute-start.7 = (bf16[3,32,512]{2,1,0:T(8,128)(2,1)S(1)}, bf16[3,32,512]{2,1,0:T(8,128)(2,1)S(1)}, u32[]{:S(2)}, u32[]{:S(2)}) collective-permute-start(bf16[3,32,512]{2,1,0:T(8,128)(2,1)S(1)} %collective-permute-done.refs_0_), channel_id=1, source_target_pairs={{0,1},{1,0},{2,3},{3,2},{4,5},{5,4},{6,7},{7,6},{8,9},{9,8},{10,11... | collective-permute-start | bytes 294920 | tf_op jit(solution)/shard_map/ppermute | solution.py:89
  10.0 7.6 %collective-permute-start.4 = (bf16[3,32,512]{2,1,0:T(8,128)(2,1)S(1)}, bf16[3,32,512]{2,1,0:T(8,128)(2,1)S(1)}, u32[]{:S(2)}, u32[]{:S(2)}) collective-permute-start(bf16[3,32,512]{2,1,0:T(8,128)(2,1)S(1)} %collective-permute-done.refs_0_), channel_id=1, source_target_pairs={{0,2},{1,3},{2,0},{3,1},{4,6},{5,7},{6,4},{7,5},{8,10},{9,11},{10,... | collective-permute-start | bytes 294920 | tf_op jit(solution)/shard_map/ppermute | solution.py:89
  15.4 6.0 %collective-permute-start.5 = (bf16[3,32,512]{2,1,0:T(8,128)(2,1)S(1)}, bf16[3,32,512]{2,1,0:T(8,128)(2,1)S(1)}, u32[]{:S(2)}, u32[]{:S(2)}) collective-permute-start(bf16[3,32,512]{2,1,0:T(8,128)(2,1)S(1)} %collective-permute-done.1.refs_1_), channel_id=1, source_target_pairs={{0,2},{1,3},{2,0},{3,1},{4,6},{5,7},{6,4},{7,5},{8,10},{9,11},{10,... | collective-permute-start | bytes 294920 | tf_op jit(solution)/shard_map/ppermute | solution.py:89
  17.6 10.8 %collective-permute-start.13 = (bf16[3,32,512]{2,1,0:T(8,128)(2,1)S(1)}, bf16[3,32,512]{2,1,0:T(8,128)(2,1)S(1)}, u32[]{:S(2)}, u32[]{:S(2)}) collective-permute-start(bf16[3,32,512]{2,1,0:T(8,128)(2,1)S(1)} %get-tuple-element.77), channel_id=1, source_target_pairs={{0,8},{4,12},{8,0},{12,4},{1,9},{5,13},{9,1},{13,5},{2,10},{6,14},... | collective-permute-start | bytes 294920 | tf_op jit(solution)/shard_map/ppermute | solution.py:89
  20.0 8.4 %collective-permute-start.14 = (bf16[3,32,512]{2,1,0:T(8,128)(2,1)S(1)}, bf16[3,32,512]{2,1,0:T(8,128)(2,1)S(1)}, u32[]{:S(2)}, u32[]{:S(2)}) collective-permute-start(bf16[3,32,512]{2,1,0:T(8,128)(2,1)S(1)} %get-tuple-element.78), channel_id=1, source_target_pairs={{0,12},{4,8},{8,4},{12,0},{1,13},{5,9},{9,5},{13,1},{2,14},{6,10},... | collective-permute-start | bytes 294920 | tf_op jit(solution)/shard_map/ppermute | solution.py:89
  28.4 14.5 %collective-permute-start.15 = (bf16[3,192,512]{2,1,0:T(8,128)(2,1)S(1)}, bf16[3,192,512]{2,1,0:T(8,128)(2,1)S(1)}, u32[]{:S(2)}, u32[]{:S(2)}) collective-permute-start(bf16[3,192,512]{2,1,0:T(8,128)(2,1)S(1)} %get-tuple-element.79), channel_id=1, source_target_pairs={{0,4},{4,0},{8,12},{12,8},{1,5},{5,1},{9,13},{13,9},{2,6},{6,2},{1... | collective-permute-start | bytes 1769480 | tf_op jit(solution)/shard_map/ppermute | solution.py:89
  30.2 7.9 %collective-permute-start.16 = (bf16[3,64,512]{2,1,0:T(8,128)(2,1)S(1)}, bf16[3,64,512]{2,1,0:T(8,128)(2,1)S(1)}, u32[]{:S(2)}, u32[]{:S(2)}) collective-permute-start(bf16[3,64,512]{2,1,0:T(8,128)(2,1)S(1)} %shard_map.107.refs_0_), channel_id=1, source_target_pairs={{0,2},{1,3},{2,0},{3,1},{4,6},{5,7},{6,4},{7,5},{8,10},{9,11},{10,... | collective-permute-start | bytes 589832 | tf_op jit(solution)/shard_map/ppermute | solution.py:89
  31.8 6.4 %collective-permute-start.17 = (bf16[3,32,512]{2,1,0:T(8,128)(2,1)S(1)}, bf16[3,32,512]{2,1,0:T(8,128)(2,1)S(1)}, u32[]{:S(2)}, u32[]{:S(2)}) collective-permute-start(bf16[3,32,512]{2,1,0:T(8,128)(2,1)S(1)} %collective-permute-done.14.refs_1_), channel_id=1, source_target_pairs={{0,2},{1,3},{2,0},{3,1},{4,6},{5,7},{6,4},{7,5},{8,10},{9,11},{10,... | collective-permute-start | bytes 294920 | tf_op jit(solution)/shard_map/ppermute | solution.py:89
  44.4 20.3 %collective-permute-start.22 = (bf16[3,192,512]{2,1,0:T(8,128)(2,1)S(1)}, bf16[3,192,512]{2,1,0:T(8,128)(2,1)S(1)}, u32[]{:S(2)}, u32[]{:S(2)}) collective-permute-start(bf16[3,192,512]{2,1,0:T(8,128)(2,1)S(1)} %get-tuple-element.91), channel_id=1, source_target_pairs={{0,4},{4,0},{8,12},{12,8},{1,5},{5,1},{9,13},{13,9},{2,6},{6,2},{1... | collective-permute-start | bytes 1769480 | tf_op jit(solution)/shard_map/ppermute | solution.py:89
  46.2 15.3 %collective-permute-start.25 = (bf16[3,96,512]{2,1,0:T(8,128)(2,1)S(1)}, bf16[3,96,512]{2,1,0:T(8,128)(2,1)S(1)}, u32[]{:S(2)}, u32[]{:S(2)}) collective-permute-start(bf16[3,96,512]{2,1,0:T(8,128)(2,1)S(1)} %collective-permute-done.24.refs_0_), channel_id=1, source_target_pairs={{1,9},{2,10},{5,13},{6,14},{8,0},{11,3},{12,4},{15,7},{17,25},{18,... | collective-permute-start | bytes 884744 | tf_op jit(solution)/shard_map/ppermute | solution.py:95
  47.5 15.4 %collective-permute-start.30 = (bf16[3,96,512]{2,1,0:T(8,128)(2,1)S(1)}, bf16[3,96,512]{2,1,0:T(8,128)(2,1)S(1)}, u32[]{:S(2)}, u32[]{:S(2)}) collective-permute-start(bf16[3,96,512]{2,1,0:T(8,128)(2,1)S(1)} %collective-permute-done.29.refs_0_), channel_id=1, source_target_pairs={{1,9},{2,10},{5,13},{6,14},{8,0},{11,3},{12,4},{15,7},{17,25},{18,... | collective-permute-start | bytes 884744 | tf_op jit(solution)/shard_map/ppermute | solution.py:95
  48.8 9.9 %collective-permute-start.28 = (f32[4,2048]{1,0:T(4,128)S(1)}, f32[4,2048]{1,0:T(4,128)S(1)}, u32[]{:S(2)}, u32[]{:S(2)}) collective-permute-start(f32[4,2048]{1,0:T(4,128)S(1)} %pad_maximum_fusion.refs_0_), channel_id=1, source_target_pairs={{0,3},{1,2},{2,1},{3,0},{4,7},{5,6},{6,5},{7,4},{8,11},{9,10},{10,... | collective-permute-start | bytes 98312 | tf_op jit(solution)/shard_map/ppermute | solution.py:89
  61.6 17.1 %collective-permute-start.32 = (bf16[3,96,512]{2,1,0:T(8,128)(2,1)S(1)}, bf16[3,96,512]{2,1,0:T(8,128)(2,1)S(1)}, u32[]{:S(2)}, u32[]{:S(2)}) collective-permute-start(bf16[3,96,512]{2,1,0:T(8,128)(2,1)S(1)} %shard_map.111.refs_0_), channel_id=1, source_target_pairs={{4,0},{9,13},{14,10},{3,7},{20,16},{25,29},{30,26},{19,23}} | collective-permute-start | bytes 884744 | tf_op jit(solution)/shard_map/ppermute | solution.py:95
  63.0 18.9 %collective-permute-start.33 = (bf16[3,96,512]{2,1,0:T(8,128)(2,1)S(1)}, bf16[3,96,512]{2,1,0:T(8,128)(2,1)S(1)}, u32[]{:S(2)}, u32[]{:S(2)}) collective-permute-start(bf16[3,96,512]{2,1,0:T(8,128)(2,1)S(1)} %shard_map.112.refs_1_), channel_id=1, source_target_pairs={{4,0},{9,13},{14,10},{3,7},{20,16},{25,29},{30,26},{19,23}} | collective-permute-start | bytes 884744 | tf_op jit(solution)/shard_map/ppermute | solution.py:95
  64.8 27.4 %collective-permute-start.23 = (bf16[3,192,512]{2,1,0:T(8,128)(2,1)S(1)}, bf16[3,192,512]{2,1,0:T(8,128)(2,1)S(1)}, u32[]{:S(2)}, u32[]{:S(2)}) collective-permute-start(bf16[3,192,512]{2,1,0:T(8,128)(2,1)S(1)} %shard_map.109.part_ref), channel_id=1, source_target_pairs={{0,8},{4,12},{8,0},{12,4},{1,9},{5,13},{9,1},{13,5},{2,10},{6,14},... | collective-permute-start | bytes 1769480 | tf_op jit(solution)/shard_map/ppermute | solution.py:89
  81.9 10.3 %collective-permute-start.34 = (bf16[2,192,512]{2,1,0:T(8,128)(2,1)S(1)}, bf16[2,192,512]{2,1,0:T(8,128)(2,1)S(1)}, u32[]{:S(2)}, u32[]{:S(2)}) collective-permute-start(bf16[2,192,512]{2,1,0:T(8,128)(2,1)S(1)} %get-tuple-element.107.refs_0_), channel_id=1, source_target_pairs={{0,2},{13,15},{10,8},{7,5},{16,18},{29,31},{26,24},{23,21}} | collective-permute-start | bytes 1179656 | tf_op jit(solution)/shard_map/ppermute | solution.py:95
  83.3 9.5 %collective-permute-start.35 = (bf16[2,192,512]{2,1,0:T(8,128)(2,1)S(1)}, bf16[2,192,512]{2,1,0:T(8,128)(2,1)}, u32[]{:S(2)}, u32[]{:S(2)}) collective-permute-start(bf16[2,192,512]{2,1,0:T(8,128)(2,1)S(1)} %get-tuple-element.109.refs_2_), channel_id=1, source_target_pairs={{0,2},{13,15},{10,8},{7,5},{16,18},{29,31},{26,24},{23,21}} | collective-permute-start | bytes 1179656 | tf_op jit(solution)/shard_map/ppermute | solution.py:95
  85.3 11.6 %collective-permute-start.36 = (bf16[2,192,512]{2,1,0:T(8,128)(2,1)S(1)}, bf16[2,192,512]{2,1,0:T(8,128)(2,1)}, u32[]{:S(2)}, u32[]{:S(2)}) collective-permute-start(bf16[2,192,512]{2,1,0:T(8,128)(2,1)S(1)} %get-tuple-element.111.refs_4_), channel_id=1, source_target_pairs={{0,2},{13,15},{10,8},{7,5},{16,18},{29,31},{26,24},{23,21}} | collective-permute-start | bytes 1179656 | tf_op jit(solution)/shard_map/ppermute | solution.py:95
  101.1 12.8 %collective-permute-start.44 = (bf16[3,192,512]{2,1,0:T(8,128)(2,1)S(1)}, bf16[3,192,512]{2,1,0:T(8,128)(2,1)S(1)}, u32[]{:S(2)}, u32[]{:S(2)}) collective-permute-start(bf16[3,192,512]{2,1,0:T(8,128)(2,1)S(1)} %get-tuple-element.124.refs_3_), channel_id=1, source_target_pairs={{0,4},{4,0},{8,12},{12,8},{1,5},{5,1},{9,13},{13,9},{2,6},{6,2},{1... | collective-permute-start | bytes 1769480 | tf_op jit(solution)/shard_map/ppermute | solution.py:89
  106.2 7.0 %collective-permute-start.41 = (bf16[2,192,512]{2,1,0:T(8,128)(2,1)S(1)}, bf16[2,192,512]{2,1,0:T(8,128)(2,1)S(1)}, u32[]{:S(2)}, u32[]{:S(2)}) collective-permute-start(bf16[2,192,512]{2,1,0:T(8,128)(2,1)S(1)} %get-tuple-element.114.refs_0_), channel_id=1, source_target_pairs={{0,1},{2,3},{13,12},{15,14},{10,11},{8,9},{7,6},{5,4},{16,17},{18,... | collective-permute-start | bytes 1179656 | tf_op jit(solution)/shard_map/ppermute | solution.py:95
  (25 other events, 120.3 us)

commit v12 on v10

--- a/solution.py
+++ b/solution.py
@@ -382,16 +382,22 @@
     layers, tile, cols = grams.shape
 
     def kernel(*refs):
-        grad_refs, (act_ref, gram_ref, factor_ref, out_ref) = refs[:layers], refs[layers:]
+        grad_refs, (act_ref, gram_ref, factor_ref, out_hbm, out_ref, sems) = refs[:layers], refs[layers:]
+        copies = []
         for layer in range(layers):
             gram = gram_ref[layer] + product_of(grad_refs[layer][1], act_ref[layer])
             out_ref[layer] = (gram * factor_ref[layer]).astype(jnp.bfloat16)
+            copies.append(pltpu.make_async_copy(out_ref.at[layer], out_hbm.at[layer], sems.at[layer]))
+            copies[-1].start()
+        for copy in copies:
+            copy.wait()
 
     return pl.pallas_call(
         kernel,
         out_shape=jax.ShapeDtypeStruct((layers, tile, cols), jnp.bfloat16),
         in_specs=[vmem_spec] * (layers + 3),
-        out_specs=vmem_spec,
+        out_specs=pl.BlockSpec(memory_space=pl.ANY),
+        scratch_shapes=[pltpu.VMEM((layers, tile, cols), jnp.bfloat16), pltpu.SemaphoreType.DMA((layers,))],
         compiler_params=pltpu.CompilerParams(vmem_limit_bytes=24 * 1024 * 1024),
         cost_estimate=light,
     )(*grads, act, grams, factors)

time: 118 us -> 117 us (level)
  no operation moved by 1% of the time
where the time goes in v12:
time: 117 us; the launch traced here: 116 us
  starting transfers between devices  53.7 us (46%)
  waiting for transfers between devices  47.1 us (40%)
  Pallas kernels  14.6 us (12%)
    ppermute x33, starting transfers between devices, flip(): lax.ppermute(array, axis, [(i, i ^ mask) for i in range(lax.axis_size(axi...  36.7 us
    ppermute x33, waiting for transfers between devices, flip(): lax.ppermute(array, axis, [(i, i ^ mask) for i in range(lax.axis_size(axi...  26 us
    ppermute x10, waiting for transfers between devices, hop(): return lax.ppermute(array, ('dp', 'owner'), flat)  21.2 us
    ppermute x10, starting transfers between devices, hop(): return lax.ppermute(array, ('dp', 'owner'), flat)  15.6 us
    pallas_call x2, Pallas kernels, project_rows(): pl.pallas_call(kernel, out_shape=[jax.ShapeDtypeStruct(shape, jnp.bfloat1...  4.17 us
    pallas_call x2, Pallas kernels, load(): pl.pallas_call(kernel, out_shape=[jax.ShapeDtypeStruct(shape, array.dtype...  3.12 us
  transfers between devices with their start and end apart: 45, of which 20 were waited for; matrix products, arithmetic and copies ran while one was open for 0% of the time, Pallas kernels for 10%

profile of v12, /device:TPU:0, one launch (start us, length us, event | category | flops | bytes accessed | tf_op | source)
XLA Modules:
  0.0 116.5 jit_solution(11919915974743544754)
XLA Ops:
  1.8 3.1 %collective-permute-start = (bf16[3,32,512]{2,1,0:T(8,128)(2,1)S(1)}, bf16[3,32,512]{2,1,0:T(8,128)(2,1)S(1)}, u32[]{:S(2)}, u32[]{:S(2)}) collective-permute-start(bf16[3,32,512]{2,1,0:T(8,128)(2,1)S(1)} %get-tuple-element.65), channel_id=1, source_target_pairs={{0,4},{4,0},{8,12},{12,8},{1,5},{5,1},{9,13},{13,9},{2,6},{6,2},{1... | collective-permute-start | bytes 294920 | tf_op jit(solution)/shard_map/ppermute | solution.py:89
  4.9 2.6 %collective-permute-start.1 = (bf16[3,32,512]{2,1,0:T(8,128)(2,1)S(1)}, bf16[3,32,512]{2,1,0:T(8,128)(2,1)S(1)}, u32[]{:S(2)}, u32[]{:S(2)}) collective-permute-start(bf16[3,32,512]{2,1,0:T(8,128)(2,1)S(1)} %get-tuple-element.66), channel_id=1, source_target_pairs={{0,8},{4,12},{8,0},{12,4},{1,9},{5,13},{9,1},{13,5},{2,10},{6,14},... | collective-permute-start | bytes 294920 | tf_op jit(solution)/shard_map/ppermute | solution.py:89
  8.4 1.6 %shard_map.103 = (bf16[3,128,512]{2,1,0:T(8,128)(2,1)S(1)}, bf16[3,512,512]{2,1,0:T(8,128)(2,1)S(1)}) custom-call(bf16[3,128,2048]{2,1,0:T(8,128)(2,1)} %refs_0_.4, bf16[3,512,512]{2,1,0:T(8,128)(2,1)} %refs_1_.3), custom_call_target="tpu_custom_call" | custom-call | tf_op jit(solution)/shard_map/pallas_call | solution.py:113
  11.6 3.8 %collective-permute-done.1.refs_1_ = bf16[3,32,512]{2,1,0:T(8,128)(2,1)S(1)} collective-permute-done((bf16[3,32,512]{2,1,0:T(8,128)(2,1)S(1)}, bf16[3,32,512]{2,1,0:T(8,128)(2,1)S(1)}, u32[]{:S(2)}, u32[]{:S(2)}) %collective-permute-start.1) | collective-permute-done | bytes 98336 | tf_op jit(solution)/shard_map/ppermute | solution.py:89
  17.6 2.4 %collective-permute-start.13 = (bf16[3,32,512]{2,1,0:T(8,128)(2,1)S(1)}, bf16[3,32,512]{2,1,0:T(8,128)(2,1)S(1)}, u32[]{:S(2)}, u32[]{:S(2)}) collective-permute-start(bf16[3,32,512]{2,1,0:T(8,128)(2,1)S(1)} %get-tuple-element.72), channel_id=1, source_target_pairs={{0,8},{4,12},{8,0},{12,4},{1,9},{5,13},{9,1},{13,5},{2,10},{6,14},... | collective-permute-start | bytes 294920 | tf_op jit(solution)/shard_map/ppermute | solution.py:89
  24.0 2.1 %shard_map.105 = (bf16[3,192,512]{2,1,0:T(8,128)(2,1)S(1)}, bf16[3,192,512]{2,1,0:T(8,128)(2,1)S(1)}) custom-call(s32[9]{0:T(128)S(1)} %pad_add_fusion.scalar_ref, bf16[3,128,512]{2,1,0:T(8,128)(2,1)S(1)} %get-tuple-element.63.tokens_ref, bf16[3,512,512]{2,1,0:T(8,128)(2,1)S(1)} %get-tuple-element.64.basis_ref, ...), custom_call_target="tpu_custom_call" | custom-call | tf_op jit(solution)/shard_map/pallas_call | solution.py:164
  26.1 2.3 %collective-permute-done.13.refs_1_ = bf16[3,32,512]{2,1,0:T(8,128)(2,1)S(1)} collective-permute-done((bf16[3,32,512]{2,1,0:T(8,128)(2,1)S(1)}, bf16[3,32,512]{2,1,0:T(8,128)(2,1)S(1)}, u32[]{:S(2)}, u32[]{:S(2)}) %collective-permute-start.13) | collective-permute-done | bytes 98336 | tf_op jit(solution)/shard_map/ppermute | solution.py:89
  28.4 1.8 %collective-permute-start.15 = (bf16[3,192,512]{2,1,0:T(8,128)(2,1)S(1)}, bf16[3,192,512]{2,1,0:T(8,128)(2,1)S(1)}, u32[]{:S(2)}, u32[]{:S(2)}) collective-permute-start(bf16[3,192,512]{2,1,0:T(8,128)(2,1)S(1)} %get-tuple-element.74), channel_id=1, source_target_pairs={{0,4},{4,0},{8,12},{12,8},{1,5},{5,1},{9,13},{13,9},{2,6},{6,2},{1... | collective-permute-start | bytes 1769480 | tf_op jit(solution)/shard_map/ppermute | solution.py:89
  34.5 3.7 %collective-permute-done.17.refs_3_ = bf16[3,32,512]{2,1,0:T(8,128)(2,1)S(1)} collective-permute-done((bf16[3,32,512]{2,1,0:T(8,128)(2,1)S(1)}, bf16[3,32,512]{2,1,0:T(8,128)(2,1)S(1)}, u32[]{:S(2)}, u32[]{:S(2)}) %collective-permute-start.17) | collective-permute-done | bytes 98336 | tf_op jit(solution)/shard_map/ppermute | solution.py:89
  39.7 2.1 %shard_map.108 = (bf16[3,192,512]{2,1,0:T(8,128)(2,1)S(1)}, bf16[3,192,512]{2,1,0:T(8,128)(2,1)S(1)}) custom-call(s32[9]{0:T(128)S(1)} %pad_add_fusion.scalar_ref, bf16[3,128,512]{2,1,0:T(8,128)(2,1)S(1)} %get-tuple-element.75.tokens_ref, bf16[3,512,512]{2,1,0:T(8,128)(2,1)S(1)} %get-tuple-element.76.basis_ref, bf16[3,64,512]{2,1,0:T(8,128)(2,1)S(1)} %shard_map.107.refs_0_, ...), custom_call_target="tpu_custom_call" | custom-call | tf_op jit(solution)/shard_map/pallas_call | solution.py:164
  44.4 1.8 %collective-permute-start.22 = (bf16[3,192,512]{2,1,0:T(8,128)(2,1)S(1)}, bf16[3,192,512]{2,1,0:T(8,128)(2,1)S(1)}, u32[]{:S(2)}, u32[]{:S(2)}) collective-permute-start(bf16[3,192,512]{2,1,0:T(8,128)(2,1)S(1)} %get-tuple-element.86), channel_id=1, source_target_pairs={{0,4},{4,0},{8,12},{12,8},{1,5},{5,1},{9,13},{13,9},{2,6},{6,2},{1... | collective-permute-start | bytes 1769480 | tf_op jit(solution)/shard_map/ppermute | solution.py:89
  48.8 6.9 %collective-permute-start.28 = (f32[4,2048]{1,0:T(4,128)S(1)}, f32[4,2048]{1,0:T(4,128)S(1)}, u32[]{:S(2)}, u32[]{:S(2)}) collective-permute-start(f32[4,2048]{1,0:T(4,128)S(1)} %pad_maximum_fusion.refs_0_), channel_id=1, source_target_pairs={{0,3},{1,2},{2,1},{3,0},{4,7},{5,6},{6,5},{7,4},{8,11},{9,10},{10,... | collective-permute-start | bytes 98312 | tf_op jit(solution)/shard_map/ppermute | solution.py:89
  55.7 3.0 %collective-permute-start.27 = (f32[4,2048]{1,0:T(4,128)S(1)}, f32[4,2048]{1,0:T(4,128)S(1)}, u32[]{:S(2)}, u32[]{:S(2)}) collective-permute-start(f32[4,2048]{1,0:T(4,128)S(1)} %pad_maximum_fusion.refs_0_), channel_id=1, source_target_pairs={{0,2},{1,3},{2,0},{3,1},{4,6},{5,7},{6,4},{7,5},{8,10},{9,11},{10,... | collective-permute-start | bytes 98312 | tf_op jit(solution)/shard_map/ppermute | solution.py:89
  58.7 2.0 %collective-permute-start.26 = (f32[4,2048]{1,0:T(4,128)S(1)}, f32[4,2048]{1,0:T(4,128)S(1)}, u32[]{:S(2)}, u32[]{:S(2)}) collective-permute-start(f32[4,2048]{1,0:T(4,128)S(1)} %pad_maximum_fusion.refs_0_), channel_id=1, source_target_pairs={{0,1},{1,0},{2,3},{3,2},{4,5},{5,4},{6,7},{7,6},{8,9},{9,8},{10,11... | collective-permute-start | bytes 98312 | tf_op jit(solution)/shard_map/ppermute | solution.py:89
  65.4 13.3 %collective-permute-done.32.refs_2_ = bf16[3,96,512]{2,1,0:T(8,128)(2,1)S(1)} collective-permute-done((bf16[3,96,512]{2,1,0:T(8,128)(2,1)S(1)}, bf16[3,96,512]{2,1,0:T(8,128)(2,1)S(1)}, u32[]{:S(2)}, u32[]{:S(2)}) %collective-permute-start.32) | collective-permute-done | bytes 294944 | tf_op jit(solution)/shard_map/ppermute | solution.py:95
  78.7 3.2 %collective-permute-done.33.refs_3_ = bf16[3,96,512]{2,1,0:T(8,128)(2,1)S(1)} collective-permute-done((bf16[3,96,512]{2,1,0:T(8,128)(2,1)S(1)}, bf16[3,96,512]{2,1,0:T(8,128)(2,1)S(1)}, u32[]{:S(2)}, u32[]{:S(2)}) %collective-permute-start.33) | collective-permute-done | bytes 294944 | tf_op jit(solution)/shard_map/ppermute | solution.py:95
  83.3 2.1 %collective-permute-start.35 = (bf16[2,192,512]{2,1,0:T(8,128)(2,1)S(1)}, bf16[2,192,512]{2,1,0:T(8,128)(2,1)}, u32[]{:S(2)}, u32[]{:S(2)}) collective-permute-start(bf16[2,192,512]{2,1,0:T(8,128)(2,1)S(1)} %get-tuple-element.103.refs_2_), channel_id=1, source_target_pairs={{0,2},{13,15},{10,8},{7,5},{16,18},{29,31},{26,24},{23,21}} | collective-permute-start | bytes 1179656 | tf_op jit(solution)/shard_map/ppermute | solution.py:95
  85.3 2.1 %collective-permute-start.36 = (bf16[2,192,512]{2,1,0:T(8,128)(2,1)S(1)}, bf16[2,192,512]{2,1,0:T(8,128)(2,1)}, u32[]{:S(2)}, u32[]{:S(2)}) collective-permute-start(bf16[2,192,512]{2,1,0:T(8,128)(2,1)S(1)} %get-tuple-element.105.refs_4_), channel_id=1, source_target_pairs={{0,2},{13,15},{10,8},{7,5},{16,18},{29,31},{26,24},{23,21}} | collective-permute-start | bytes 1179656 | tf_op jit(solution)/shard_map/ppermute | solution.py:95
  87.5 4.7 %collective-permute-done.31.far_ref = f32[3,512]{1,0:T(4,128)S(1)} collective-permute-done((f32[3,512]{1,0:T(4,128)S(1)}, f32[3,512]{1,0:T(4,128)S(1)}, u32[]{:S(2)}, u32[]{:S(2)}) %collective-permute-start.31) | collective-permute-done | bytes 6176 | tf_op jit(solution)/shard_map/ppermute | solution.py:89
  92.7 4.2 %collective-permute-done.36.refs_5_ = bf16[2,192,512]{2,1,0:T(8,128)(2,1)} collective-permute-done((bf16[2,192,512]{2,1,0:T(8,128)(2,1)S(1)}, bf16[2,192,512]{2,1,0:T(8,128)(2,1)}, u32[]{:S(2)}, u32[]{:S(2)}) %collective-permute-start.36) | collective-permute-done | bytes 393248 | tf_op jit(solution)/shard_map/ppermute | solution.py:95
  97.2 3.8 %collective-permute-done.37.far_ref = f32[6,512]{1,0:T(8,128)S(1)} collective-permute-done((f32[6,512]{1,0:T(8,128)S(1)}, f32[6,512]{1,0:T(8,128)S(1)}, u32[]{:S(2)}, u32[]{:S(2)}) %collective-permute-start.37) | collective-permute-done | bytes 12320 | tf_op jit(solution)/shard_map/ppermute | solution.py:89
  104.3 1.8 %collective-permute-done.39.refs_6_ = f32[6,512]{1,0:T(8,128)S(1)} collective-permute-done((f32[6,512]{1,0:T(8,128)S(1)}, f32[6,512]{1,0:T(8,128)S(1)}, u32[]{:S(2)}, u32[]{:S(2)}) %collective-permute-start.39) | collective-permute-done | bytes 12320 | tf_op jit(solution)/shard_map/ppermute | solution.py:89
  107.2 2.4 %collective-permute-start.41 = (bf16[2,192,512]{2,1,0:T(8,128)(2,1)S(1)}, bf16[2,192,512]{2,1,0:T(8,128)(2,1)S(1)}, u32[]{:S(2)}, u32[]{:S(2)}) collective-permute-start(bf16[2,192,512]{2,1,0:T(8,128)(2,1)S(1)} %get-tuple-element.107.refs_0_), channel_id=1, source_target_pairs={{0,1},{2,3},{13,12},{15,14},{10,11},{8,9},{7,6},{5,4},{16,17},{18,... | collective-permute-start | bytes 1179656 | tf_op jit(solution)/shard_map/ppermute | solution.py:95
  112.3 1.9 %shard_map.121 = (f32[3,512,512]{2,1,0:T(8,128)S(1)}, f32[2,2048]{1,0:T(2,128)}, f32[2,2048]{1,0:T(2,128)}) custom-call(s32[9]{0:T(128)S(1)} %pad_add_fusion.scalar_ref, f32[4,2048]{1,0:T(4,128)S(1)} %pad_maximum_fusion.refs_0_, f32[4,2048]{1,0:T(4,128)S(1)} %collective-permute-done.26.refs_1_, f32[4,2048]{1,0:T(4,128)S(1)} %collective-permute-done.27.refs_2_, ...), custom_call_target="tpu_custom_call" | custom-call | tf_op jit(solution)/shard_map/pallas_call | solution.py:463
  (96 shorter events, 37.1 us)
Async XLA Ops:
  1.8 6.6 %collective-permute-start = (bf16[3,32,512]{2,1,0:T(8,128)(2,1)S(1)}, bf16[3,32,512]{2,1,0:T(8,128)(2,1)S(1)}, u32[]{:S(2)}, u32[]{:S(2)}) collective-permute-start(bf16[3,32,512]{2,1,0:T(8,128)(2,1)S(1)} %get-tuple-element.65), channel_id=1, source_target_pairs={{0,4},{4,0},{8,12},{12,8},{1,5},{5,1},{9,13},{13,9},{2,6},{6,2},{1... | collective-permute-start | bytes 294920 | tf_op jit(solution)/shard_map/ppermute | solution.py:89
  4.9 10.4 %collective-permute-start.1 = (bf16[3,32,512]{2,1,0:T(8,128)(2,1)S(1)}, bf16[3,32,512]{2,1,0:T(8,128)(2,1)S(1)}, u32[]{:S(2)}, u32[]{:S(2)}) collective-permute-start(bf16[3,32,512]{2,1,0:T(8,128)(2,1)S(1)} %get-tuple-element.66), channel_id=1, source_target_pairs={{0,8},{4,12},{8,0},{12,4},{1,9},{5,13},{9,1},{13,5},{2,10},{6,14},... | collective-permute-start | bytes 294920 | tf_op jit(solution)/shard_map/ppermute | solution.py:89
  7.5 7.8 %collective-permute-start.2 = (bf16[3,32,512]{2,1,0:T(8,128)(2,1)S(1)}, bf16[3,32,512]{2,1,0:T(8,128)(2,1)S(1)}, u32[]{:S(2)}, u32[]{:S(2)}) collective-permute-start(bf16[3,32,512]{2,1,0:T(8,128)(2,1)S(1)} %get-tuple-element.67), channel_id=1, source_target_pairs={{0,12},{4,8},{8,4},{12,0},{1,13},{5,9},{9,5},{13,1},{2,14},{6,10},... | collective-permute-start | bytes 294920 | tf_op jit(solution)/shard_map/ppermute | solution.py:89
  7.5 7.8 %collective-permute-start.3 = (bf16[3,32,512]{2,1,0:T(8,128)(2,1)S(1)}, bf16[3,32,512]{2,1,0:T(8,128)(2,1)S(1)}, u32[]{:S(2)}, u32[]{:S(2)}) collective-permute-start(bf16[3,32,512]{2,1,0:T(8,128)(2,1)S(1)} %get-tuple-element.68), channel_id=1, source_target_pairs={{0,4},{4,0},{8,12},{12,8},{1,5},{5,1},{9,13},{13,9},{2,6},{6,2},{1... | collective-permute-start | bytes 294920 | tf_op jit(solution)/shard_map/ppermute | solution.py:89
  8.4 8.7 %collective-permute-start.7 = (bf16[3,32,512]{2,1,0:T(8,128)(2,1)S(1)}, bf16[3,32,512]{2,1,0:T(8,128)(2,1)S(1)}, u32[]{:S(2)}, u32[]{:S(2)}) collective-permute-start(bf16[3,32,512]{2,1,0:T(8,128)(2,1)S(1)} %collective-permute-done.refs_0_), channel_id=1, source_target_pairs={{0,1},{1,0},{2,3},{3,2},{4,5},{5,4},{6,7},{7,6},{8,9},{9,8},{10,11... | collective-permute-start | bytes 294920 | tf_op jit(solution)/shard_map/ppermute | solution.py:89
  10.0 7.6 %collective-permute-start.4 = (bf16[3,32,512]{2,1,0:T(8,128)(2,1)S(1)}, bf16[3,32,512]{2,1,0:T(8,128)(2,1)S(1)}, u32[]{:S(2)}, u32[]{:S(2)}) collective-permute-start(bf16[3,32,512]{2,1,0:T(8,128)(2,1)S(1)} %collective-permute-done.refs_0_), channel_id=1, source_target_pairs={{0,2},{1,3},{2,0},{3,1},{4,6},{5,7},{6,4},{7,5},{8,10},{9,11},{10,... | collective-permute-start | bytes 294920 | tf_op jit(solution)/shard_map/ppermute | solution.py:89
  15.4 6.0 %collective-permute-start.5 = (bf16[3,32,512]{2,1,0:T(8,128)(2,1)S(1)}, bf16[3,32,512]{2,1,0:T(8,128)(2,1)S(1)}, u32[]{:S(2)}, u32[]{:S(2)}) collective-permute-start(bf16[3,32,512]{2,1,0:T(8,128)(2,1)S(1)} %collective-permute-done.1.refs_1_), channel_id=1, source_target_pairs={{0,2},{1,3},{2,0},{3,1},{4,6},{5,7},{6,4},{7,5},{8,10},{9,11},{10,... | collective-permute-start | bytes 294920 | tf_op jit(solution)/shard_map/ppermute | solution.py:89
  17.6 10.8 %collective-permute-start.13 = (bf16[3,32,512]{2,1,0:T(8,128)(2,1)S(1)}, bf16[3,32,512]{2,1,0:T(8,128)(2,1)S(1)}, u32[]{:S(2)}, u32[]{:S(2)}) collective-permute-start(bf16[3,32,512]{2,1,0:T(8,128)(2,1)S(1)} %get-tuple-element.72), channel_id=1, source_target_pairs={{0,8},{4,12},{8,0},{12,4},{1,9},{5,13},{9,1},{13,5},{2,10},{6,14},... | collective-permute-start | bytes 294920 | tf_op jit(solution)/shard_map/ppermute | solution.py:89
  20.0 8.4 %collective-permute-start.14 = (bf16[3,32,512]{2,1,0:T(8,128)(2,1)S(1)}, bf16[3,32,512]{2,1,0:T(8,128)(2,1)S(1)}, u32[]{:S(2)}, u32[]{:S(2)}) collective-permute-start(bf16[3,32,512]{2,1,0:T(8,128)(2,1)S(1)} %get-tuple-element.73), channel_id=1, source_target_pairs={{0,12},{4,8},{8,4},{12,0},{1,13},{5,9},{9,5},{13,1},{2,14},{6,10},... | collective-permute-start | bytes 294920 | tf_op jit(solution)/shard_map/ppermute | solution.py:89
  28.4 14.5 %collective-permute-start.15 = (bf16[3,192,512]{2,1,0:T(8,128)(2,1)S(1)}, bf16[3,192,512]{2,1,0:T(8,128)(2,1)S(1)}, u32[]{:S(2)}, u32[]{:S(2)}) collective-permute-start(bf16[3,192,512]{2,1,0:T(8,128)(2,1)S(1)} %get-tuple-element.74), channel_id=1, source_target_pairs={{0,4},{4,0},{8,12},{12,8},{1,5},{5,1},{9,13},{13,9},{2,6},{6,2},{1... | collective-permute-start | bytes 1769480 | tf_op jit(solution)/shard_map/ppermute | solution.py:89
  30.2 7.9 %collective-permute-start.16 = (bf16[3,64,512]{2,1,0:T(8,128)(2,1)S(1)}, bf16[3,64,512]{2,1,0:T(8,128)(2,1)S(1)}, u32[]{:S(2)}, u32[]{:S(2)}) collective-permute-start(bf16[3,64,512]{2,1,0:T(8,128)(2,1)S(1)} %shard_map.107.refs_0_), channel_id=1, source_target_pairs={{0,2},{1,3},{2,0},{3,1},{4,6},{5,7},{6,4},{7,5},{8,10},{9,11},{10,... | collective-permute-start | bytes 589832 | tf_op jit(solution)/shard_map/ppermute | solution.py:89
  31.8 6.4 %collective-permute-start.17 = (bf16[3,32,512]{2,1,0:T(8,128)(2,1)S(1)}, bf16[3,32,512]{2,1,0:T(8,128)(2,1)S(1)}, u32[]{:S(2)}, u32[]{:S(2)}) collective-permute-start(bf16[3,32,512]{2,1,0:T(8,128)(2,1)S(1)} %collective-permute-done.14.refs_1_), channel_id=1, source_target_pairs={{0,2},{1,3},{2,0},{3,1},{4,6},{5,7},{6,4},{7,5},{8,10},{9,11},{10,... | collective-permute-start | bytes 294920 | tf_op jit(solution)/shard_map/ppermute | solution.py:89
  44.4 20.3 %collective-permute-start.22 = (bf16[3,192,512]{2,1,0:T(8,128)(2,1)S(1)}, bf16[3,192,512]{2,1,0:T(8,128)(2,1)S(1)}, u32[]{:S(2)}, u32[]{:S(2)}) collective-permute-start(bf16[3,192,512]{2,1,0:T(8,128)(2,1)S(1)} %get-tuple-element.86), channel_id=1, source_target_pairs={{0,4},{4,0},{8,12},{12,8},{1,5},{5,1},{9,13},{13,9},{2,6},{6,2},{1... | collective-permute-start | bytes 1769480 | tf_op jit(solution)/shard_map/ppermute | solution.py:89
  46.2 15.3 %collective-permute-start.25 = (bf16[3,96,512]{2,1,0:T(8,128)(2,1)S(1)}, bf16[3,96,512]{2,1,0:T(8,128)(2,1)S(1)}, u32[]{:S(2)}, u32[]{:S(2)}) collective-permute-start(bf16[3,96,512]{2,1,0:T(8,128)(2,1)S(1)} %collective-permute-done.24.refs_0_), channel_id=1, source_target_pairs={{1,9},{2,10},{5,13},{6,14},{8,0},{11,3},{12,4},{15,7},{17,25},{18,... | collective-permute-start | bytes 884744 | tf_op jit(solution)/shard_map/ppermute | solution.py:95
  47.5 15.4 %collective-permute-start.30 = (bf16[3,96,512]{2,1,0:T(8,128)(2,1)S(1)}, bf16[3,96,512]{2,1,0:T(8,128)(2,1)S(1)}, u32[]{:S(2)}, u32[]{:S(2)}) collective-permute-start(bf16[3,96,512]{2,1,0:T(8,128)(2,1)S(1)} %collective-permute-done.29.refs_0_), channel_id=1, source_target_pairs={{1,9},{2,10},{5,13},{6,14},{8,0},{11,3},{12,4},{15,7},{17,25},{18,... | collective-permute-start | bytes 884744 | tf_op jit(solution)/shard_map/ppermute | solution.py:95
  48.8 9.9 %collective-permute-start.28 = (f32[4,2048]{1,0:T(4,128)S(1)}, f32[4,2048]{1,0:T(4,128)S(1)}, u32[]{:S(2)}, u32[]{:S(2)}) collective-permute-start(f32[4,2048]{1,0:T(4,128)S(1)} %pad_maximum_fusion.refs_0_), channel_id=1, source_target_pairs={{0,3},{1,2},{2,1},{3,0},{4,7},{5,6},{6,5},{7,4},{8,11},{9,10},{10,... | collective-permute-start | bytes 98312 | tf_op jit(solution)/shard_map/ppermute | solution.py:89
  61.6 17.1 %collective-permute-start.32 = (bf16[3,96,512]{2,1,0:T(8,128)(2,1)S(1)}, bf16[3,96,512]{2,1,0:T(8,128)(2,1)S(1)}, u32[]{:S(2)}, u32[]{:S(2)}) collective-permute-start(bf16[3,96,512]{2,1,0:T(8,128)(2,1)S(1)} %shard_map.111.refs_0_), channel_id=1, source_target_pairs={{4,0},{9,13},{14,10},{3,7},{20,16},{25,29},{30,26},{19,23}} | collective-permute-start | bytes 884744 | tf_op jit(solution)/shard_map/ppermute | solution.py:95
  63.0 18.9 %collective-permute-start.33 = (bf16[3,96,512]{2,1,0:T(8,128)(2,1)S(1)}, bf16[3,96,512]{2,1,0:T(8,128)(2,1)S(1)}, u32[]{:S(2)}, u32[]{:S(2)}) collective-permute-start(bf16[3,96,512]{2,1,0:T(8,128)(2,1)S(1)} %shard_map.112.refs_1_), channel_id=1, source_target_pairs={{4,0},{9,13},{14,10},{3,7},{20,16},{25,29},{30,26},{19,23}} | collective-permute-start | bytes 884744 | tf_op jit(solution)/shard_map/ppermute | solution.py:95
  64.8 27.4 %collective-permute-start.23 = (bf16[3,192,512]{2,1,0:T(8,128)(2,1)S(1)}, bf16[3,192,512]{2,1,0:T(8,128)(2,1)S(1)}, u32[]{:S(2)}, u32[]{:S(2)}) collective-permute-start(bf16[3,192,512]{2,1,0:T(8,128)(2,1)S(1)} %shard_map.109.refs_0_), channel_id=1, source_target_pairs={{0,8},{4,12},{8,0},{12,4},{1,9},{5,13},{9,1},{13,5},{2,10},{6,14},... | collective-permute-start | bytes 1769480 | tf_op jit(solution)/shard_map/ppermute | solution.py:89
  81.9 10.3 %collective-permute-start.34 = (bf16[2,192,512]{2,1,0:T(8,128)(2,1)S(1)}, bf16[2,192,512]{2,1,0:T(8,128)(2,1)S(1)}, u32[]{:S(2)}, u32[]{:S(2)}) collective-permute-start(bf16[2,192,512]{2,1,0:T(8,128)(2,1)S(1)} %get-tuple-element.101.refs_0_), channel_id=1, source_target_pairs={{0,2},{13,15},{10,8},{7,5},{16,18},{29,31},{26,24},{23,21}} | collective-permute-start | bytes 1179656 | tf_op jit(solution)/shard_map/ppermute | solution.py:95
  83.3 9.5 %collective-permute-start.35 = (bf16[2,192,512]{2,1,0:T(8,128)(2,1)S(1)}, bf16[2,192,512]{2,1,0:T(8,128)(2,1)}, u32[]{:S(2)}, u32[]{:S(2)}) collective-permute-start(bf16[2,192,512]{2,1,0:T(8,128)(2,1)S(1)} %get-tuple-element.103.refs_2_), channel_id=1, source_target_pairs={{0,2},{13,15},{10,8},{7,5},{16,18},{29,31},{26,24},{23,21}} | collective-permute-start | bytes 1179656 | tf_op jit(solution)/shard_map/ppermute | solution.py:95
  85.3 11.6 %collective-permute-start.36 = (bf16[2,192,512]{2,1,0:T(8,128)(2,1)S(1)}, bf16[2,192,512]{2,1,0:T(8,128)(2,1)}, u32[]{:S(2)}, u32[]{:S(2)}) collective-permute-start(bf16[2,192,512]{2,1,0:T(8,128)(2,1)S(1)} %get-tuple-element.105.refs_4_), channel_id=1, source_target_pairs={{0,2},{13,15},{10,8},{7,5},{16,18},{29,31},{26,24},{23,21}} | collective-permute-start | bytes 1179656 | tf_op jit(solution)/shard_map/ppermute | solution.py:95
  101.0 13.9 %collective-permute-start.44 = (bf16[3,192,512]{2,1,0:T(8,128)(2,1)S(1)}, bf16[3,192,512]{2,1,0:T(8,128)(2,1)S(1)}, u32[]{:S(2)}, u32[]{:S(2)}) collective-permute-start(bf16[3,192,512]{2,1,0:T(8,128)(2,1)S(1)} %shard_map.115.act_ref.refs_3_), channel_id=1, source_target_pairs={{0,4},{4,0},{8,12},{12,8},{1,5},{5,1},{9,13},{13,9},{2,6},{6,2},{1... | collective-permute-start | bytes 1769480 | tf_op jit(solution)/shard_map/ppermute | solution.py:89
  107.2 7.0 %collective-permute-start.41 = (bf16[2,192,512]{2,1,0:T(8,128)(2,1)S(1)}, bf16[2,192,512]{2,1,0:T(8,128)(2,1)S(1)}, u32[]{:S(2)}, u32[]{:S(2)}) collective-permute-start(bf16[2,192,512]{2,1,0:T(8,128)(2,1)S(1)} %get-tuple-element.107.refs_0_), channel_id=1, source_target_pairs={{0,1},{2,3},{13,12},{15,14},{10,11},{8,9},{7,6},{5,4},{16,17},{18,... | collective-permute-start | bytes 1179656 | tf_op jit(solution)/shard_map/ppermute | solution.py:95
  (25 other events, 120.2 us)

commit v13 on v12

--- a/solution.py
+++ b/solution.py
@@ -422,8 +422,8 @@
             act_full[:, at] = packet_refs[mask][:layers] / total
             at = pl.ds(pl.multiple_of((n_own - (own ^ mask)) % n_own * tile, tile), tile)
             grad_full[:, at] = packet_refs[mask][layers:] / total
-        new_act_ref[...] = state_refs[0][:slot_count]
-        new_grad_ref[...] = state_refs[0][slot_count:]
+        new_acts = [state_refs[0][slot : slot + 1] for slot in range(slot_count)]
+        new_grads = [state_refs[0][slot_count + slot : slot_count + slot + 1] for slot in range(slot_count)]
         for layer in range(layers):
             owner_now = owners[layer]
             rank = jnp.int32(0)
@@ -442,11 +442,9 @@
             act_full[layer : layer + 1] = eigen_act
             grad_full[layer : layer + 1] = eigen_grad
             for slot in range(slot_count):
-
-                @pl.when((owner_now == own) & (rank == slot))
-                def _(slot=slot, eigen_act=eigen_act, eigen_grad=eigen_grad):
-                    new_act_ref[slot : slot + 1] = eigen_act
-                    new_grad_ref[slot : slot + 1] = eigen_grad
+                here = (owner_now == own) & (rank == slot)
+                new_acts[slot] = jnp.where(here, eigen_act, new_acts[slot])
+                new_grads[slot] = jnp.where(here, eigen_grad, new_grads[slot])
 
             damping = damping_rate * (jnp.sum(eigen_grad) / width) * (jnp.sum(eigen_act) / width)
             rows = grad_full[layer : layer + 1, pl.ds(pl.multiple_of(dp * tile, tile), tile)]
@@ -454,6 +452,9 @@
             rows = jnp.transpose(jnp.broadcast_to(rows, (128, tile)))
             rows = jnp.concatenate([rows] * (tile // 128), axis=1)
             out_ref[layer] = 1.0 / (total * (rows * cols + damping))
+        for slot in range(slot_count):
+            new_act_ref[slot : slot + 1] = new_acts[slot]
+            new_grad_ref[slot : slot + 1] = new_grads[slot]
 
     out_shape = [
         jax.ShapeDtypeStruct((layers, tile, tile), jnp.float32),
@@ -507,7 +508,7 @@
     state = jnp.concatenate([state_act, state_grad], axis=0)
     keep, near, keep_act, send_act, state = step([keep, near, keep_act, send_act, state])
     states = [state] + [flip(state, "owner", mask) for mask in range(1, n_own)]
-    parts = add_rows(keep, near, keep.shape[1] // 2)
+    parts = add_rows(keep, near, keep.shape[1] * 7 // 12)
     parts = [lax.ppermute(array, "owner", [*enumerate(held)]) for array in parts]
     to_pair = [((a, o), (a ^ 2, o)) for a in range(n_dp) for o in owners if (a ^ held[o]) & 2]
     crosses = [hop(array, to_pair) for array in parts]

time: 117 us -> 117 us (level)
    ppermute x10, waiting for transfers between devices: 21.2 us -> 18.5 us  [hop(): return lax.ppermute(array, ('dp', 'owner'), flat)]
    ppermute x33, waiting for transfers between devices: 26 us -> 27.5 us  [flip(): lax.ppermute(array, axis, [(i, i ^ mask) for i in range(lax.axis_size(axi...]
  transfers between devices with their start and end apart: 45 -> 45, of which waited for: 20 -> 19; matrix products, arithmetic and copies ran while one was open for 0% -> 0% of each run, Pallas kernels for 10% -> 10%
where the time goes in v13:
time: 117 us; the launch traced here: 115 us
  starting transfers between devices  53.9 us (46%)
  waiting for transfers between devices  46 us (39%)
  Pallas kernels  14.4 us (12%)
    ppermute x33, starting transfers between devices, flip(): lax.ppermute(array, axis, [(i, i ^ mask) for i in range(lax.axis_size(axi...  36.6 us
    ppermute x33, waiting for transfers between devices, flip(): lax.ppermute(array, axis, [(i, i ^ mask) for i in range(lax.axis_size(axi...  27.5 us
    ppermute x10, waiting for transfers between devices, hop(): return lax.ppermute(array, ('dp', 'owner'), flat)  18.5 us
    ppermute x10, starting transfers between devices, hop(): return lax.ppermute(array, ('dp', 'owner'), flat)  15.9 us
    pallas_call x2, Pallas kernels, project_rows(): pl.pallas_call(kernel, out_shape=[jax.ShapeDtypeStruct(shape, jnp.bfloat1...  4.17 us
    pallas_call x2, Pallas kernels, load(): pl.pallas_call(kernel, out_shape=[jax.ShapeDtypeStruct(shape, array.dtype...  3.12 us
  transfers between devices with their start and end apart: 45, of which 19 were waited for; matrix products, arithmetic and copies ran while one was open for 0% of the time, Pallas kernels for 10%

profile of v13, /device:TPU:0, one launch (start us, length us, event | category | flops | bytes accessed | tf_op | source)
XLA Modules:
  0.0 115.4 jit_solution(9910067502652825337)
XLA Ops:
  1.8 3.1 %collective-permute-start = (bf16[3,32,512]{2,1,0:T(8,128)(2,1)S(1)}, bf16[3,32,512]{2,1,0:T(8,128)(2,1)S(1)}, u32[]{:S(2)}, u32[]{:S(2)}) collective-permute-start(bf16[3,32,512]{2,1,0:T(8,128)(2,1)S(1)} %get-tuple-element.65), channel_id=1, source_target_pairs={{0,4},{4,0},{8,12},{12,8},{1,5},{5,1},{9,13},{13,9},{2,6},{6,2},{1... | collective-permute-start | bytes 294920 | tf_op jit(solution)/shard_map/ppermute | solution.py:89
  4.9 2.6 %collective-permute-start.1 = (bf16[3,32,512]{2,1,0:T(8,128)(2,1)S(1)}, bf16[3,32,512]{2,1,0:T(8,128)(2,1)S(1)}, u32[]{:S(2)}, u32[]{:S(2)}) collective-permute-start(bf16[3,32,512]{2,1,0:T(8,128)(2,1)S(1)} %get-tuple-element.66), channel_id=1, source_target_pairs={{0,8},{4,12},{8,0},{12,4},{1,9},{5,13},{9,1},{13,5},{2,10},{6,14},... | collective-permute-start | bytes 294920 | tf_op jit(solution)/shard_map/ppermute | solution.py:89
  8.4 1.6 %shard_map.103 = (bf16[3,128,512]{2,1,0:T(8,128)(2,1)S(1)}, bf16[3,512,512]{2,1,0:T(8,128)(2,1)S(1)}) custom-call(bf16[3,128,2048]{2,1,0:T(8,128)(2,1)} %refs_0_.4, bf16[3,512,512]{2,1,0:T(8,128)(2,1)} %refs_1_.3), custom_call_target="tpu_custom_call" | custom-call | tf_op jit(solution)/shard_map/pallas_call | solution.py:113
  11.6 3.8 %collective-permute-done.1.refs_1_ = bf16[3,32,512]{2,1,0:T(8,128)(2,1)S(1)} collective-permute-done((bf16[3,32,512]{2,1,0:T(8,128)(2,1)S(1)}, bf16[3,32,512]{2,1,0:T(8,128)(2,1)S(1)}, u32[]{:S(2)}, u32[]{:S(2)}) %collective-permute-start.1) | collective-permute-done | bytes 98336 | tf_op jit(solution)/shard_map/ppermute | solution.py:89
  17.6 2.4 %collective-permute-start.13 = (bf16[3,32,512]{2,1,0:T(8,128)(2,1)S(1)}, bf16[3,32,512]{2,1,0:T(8,128)(2,1)S(1)}, u32[]{:S(2)}, u32[]{:S(2)}) collective-permute-start(bf16[3,32,512]{2,1,0:T(8,128)(2,1)S(1)} %get-tuple-element.72), channel_id=1, source_target_pairs={{0,8},{4,12},{8,0},{12,4},{1,9},{5,13},{9,1},{13,5},{2,10},{6,14},... | collective-permute-start | bytes 294920 | tf_op jit(solution)/shard_map/ppermute | solution.py:89
  24.0 2.1 %shard_map.105 = (bf16[3,192,512]{2,1,0:T(8,128)(2,1)S(1)}, bf16[3,192,512]{2,1,0:T(8,128)(2,1)S(1)}) custom-call(s32[9]{0:T(128)S(1)} %pad_add_fusion.scalar_ref, bf16[3,128,512]{2,1,0:T(8,128)(2,1)S(1)} %get-tuple-element.63.tokens_ref, bf16[3,512,512]{2,1,0:T(8,128)(2,1)S(1)} %get-tuple-element.64.basis_ref, ...), custom_call_target="tpu_custom_call" | custom-call | tf_op jit(solution)/shard_map/pallas_call | solution.py:164
  26.1 2.3 %collective-permute-done.13.refs_1_ = bf16[3,32,512]{2,1,0:T(8,128)(2,1)S(1)} collective-permute-done((bf16[3,32,512]{2,1,0:T(8,128)(2,1)S(1)}, bf16[3,32,512]{2,1,0:T(8,128)(2,1)S(1)}, u32[]{:S(2)}, u32[]{:S(2)}) %collective-permute-start.13) | collective-permute-done | bytes 98336 | tf_op jit(solution)/shard_map/ppermute | solution.py:89
  28.4 1.8 %collective-permute-start.15 = (bf16[3,192,512]{2,1,0:T(8,128)(2,1)S(1)}, bf16[3,192,512]{2,1,0:T(8,128)(2,1)S(1)}, u32[]{:S(2)}, u32[]{:S(2)}) collective-permute-start(bf16[3,192,512]{2,1,0:T(8,128)(2,1)S(1)} %get-tuple-element.74), channel_id=1, source_target_pairs={{0,4},{4,0},{8,12},{12,8},{1,5},{5,1},{9,13},{13,9},{2,6},{6,2},{1... | collective-permute-start | bytes 1769480 | tf_op jit(solution)/shard_map/ppermute | solution.py:89
  34.5 3.7 %collective-permute-done.17.refs_3_ = bf16[3,32,512]{2,1,0:T(8,128)(2,1)S(1)} collective-permute-done((bf16[3,32,512]{2,1,0:T(8,128)(2,1)S(1)}, bf16[3,32,512]{2,1,0:T(8,128)(2,1)S(1)}, u32[]{:S(2)}, u32[]{:S(2)}) %collective-permute-start.17) | collective-permute-done | bytes 98336 | tf_op jit(solution)/shard_map/ppermute | solution.py:89
  39.7 2.1 %shard_map.108 = (bf16[3,192,512]{2,1,0:T(8,128)(2,1)S(1)}, bf16[3,192,512]{2,1,0:T(8,128)(2,1)S(1)}) custom-call(s32[9]{0:T(128)S(1)} %pad_add_fusion.scalar_ref, bf16[3,128,512]{2,1,0:T(8,128)(2,1)S(1)} %get-tuple-element.75.tokens_ref, bf16[3,512,512]{2,1,0:T(8,128)(2,1)S(1)} %get-tuple-element.76.basis_ref, bf16[3,64,512]{2,1,0:T(8,128)(2,1)S(1)} %shard_map.107.refs_0_, ...), custom_call_target="tpu_custom_call" | custom-call | tf_op jit(solution)/shard_map/pallas_call | solution.py:164
  43.7 1.8 %collective-permute-start.22 = (bf16[3,192,512]{2,1,0:T(8,128)(2,1)S(1)}, bf16[3,192,512]{2,1,0:T(8,128)(2,1)S(1)}, u32[]{:S(2)}, u32[]{:S(2)}) collective-permute-start(bf16[3,192,512]{2,1,0:T(8,128)(2,1)S(1)} %get-tuple-element.86), channel_id=1, source_target_pairs={{0,4},{4,0},{8,12},{12,8},{1,5},{5,1},{9,13},{13,9},{2,6},{6,2},{1... | collective-permute-start | bytes 1769480 | tf_op jit(solution)/shard_map/ppermute | solution.py:89
  48.8 6.9 %collective-permute-start.28 = (f32[4,2048]{1,0:T(4,128)S(1)}, f32[4,2048]{1,0:T(4,128)S(1)}, u32[]{:S(2)}, u32[]{:S(2)}) collective-permute-start(f32[4,2048]{1,0:T(4,128)S(1)} %pad_maximum_fusion.refs_0_), channel_id=1, source_target_pairs={{0,3},{1,2},{2,1},{3,0},{4,7},{5,6},{6,5},{7,4},{8,11},{9,10},{10,... | collective-permute-start | bytes 98312 | tf_op jit(solution)/shard_map/ppermute | solution.py:89
  55.7 3.3 %collective-permute-start.27 = (f32[4,2048]{1,0:T(4,128)S(1)}, f32[4,2048]{1,0:T(4,128)S(1)}, u32[]{:S(2)}, u32[]{:S(2)}) collective-permute-start(f32[4,2048]{1,0:T(4,128)S(1)} %pad_maximum_fusion.refs_0_), channel_id=1, source_target_pairs={{0,2},{1,3},{2,0},{3,1},{4,6},{5,7},{6,4},{7,5},{8,10},{9,11},{10,... | collective-permute-start | bytes 98312 | tf_op jit(solution)/shard_map/ppermute | solution.py:89
  59.1 2.0 %collective-permute-start.26 = (f32[4,2048]{1,0:T(4,128)S(1)}, f32[4,2048]{1,0:T(4,128)S(1)}, u32[]{:S(2)}, u32[]{:S(2)}) collective-permute-start(f32[4,2048]{1,0:T(4,128)S(1)} %pad_maximum_fusion.refs_0_), channel_id=1, source_target_pairs={{0,1},{1,0},{2,3},{3,2},{4,5},{5,4},{6,7},{7,6},{8,9},{9,8},{10,11... | collective-permute-start | bytes 98312 | tf_op jit(solution)/shard_map/ppermute | solution.py:89
  65.8 14.4 %collective-permute-done.33.refs_3_ = bf16[3,80,512]{2,1,0:T(8,128)(2,1)S(1)} collective-permute-done((bf16[3,80,512]{2,1,0:T(8,128)(2,1)S(1)}, bf16[3,80,512]{2,1,0:T(8,128)(2,1)S(1)}, u32[]{:S(2)}, u32[]{:S(2)}) %collective-permute-start.33) | collective-permute-done | bytes 245792 | tf_op jit(solution)/shard_map/ppermute | solution.py:95
  81.6 2.1 %collective-permute-start.35 = (bf16[2,192,512]{2,1,0:T(8,128)(2,1)S(1)}, bf16[2,192,512]{2,1,0:T(8,128)(2,1)}, u32[]{:S(2)}, u32[]{:S(2)}) collective-permute-start(bf16[2,192,512]{2,1,0:T(8,128)(2,1)S(1)} %get-tuple-element.103.refs_2_), channel_id=1, source_target_pairs={{0,2},{13,15},{10,8},{7,5},{16,18},{29,31},{26,24},{23,21}} | collective-permute-start | bytes 1179656 | tf_op jit(solution)/shard_map/ppermute | solution.py:95
  83.7 2.1 %collective-permute-start.36 = (bf16[2,192,512]{2,1,0:T(8,128)(2,1)S(1)}, bf16[2,192,512]{2,1,0:T(8,128)(2,1)}, u32[]{:S(2)}, u32[]{:S(2)}) collective-permute-start(bf16[2,192,512]{2,1,0:T(8,128)(2,1)S(1)} %get-tuple-element.105.refs_4_), channel_id=1, source_target_pairs={{0,2},{13,15},{10,8},{7,5},{16,18},{29,31},{26,24},{23,21}} | collective-permute-start | bytes 1179656 | tf_op jit(solution)/shard_map/ppermute | solution.py:95
  85.9 5.4 %collective-permute-done.31.far_ref = f32[3,512]{1,0:T(4,128)S(1)} collective-permute-done((f32[3,512]{1,0:T(4,128)S(1)}, f32[3,512]{1,0:T(4,128)S(1)}, u32[]{:S(2)}, u32[]{:S(2)}) %collective-permute-start.31) | collective-permute-done | bytes 6176 | tf_op jit(solution)/shard_map/ppermute | solution.py:89
  91.3 4.0 %collective-permute-done.36.refs_5_ = bf16[2,192,512]{2,1,0:T(8,128)(2,1)} collective-permute-done((bf16[2,192,512]{2,1,0:T(8,128)(2,1)S(1)}, bf16[2,192,512]{2,1,0:T(8,128)(2,1)}, u32[]{:S(2)}, u32[]{:S(2)}) %collective-permute-start.36) | collective-permute-done | bytes 393248 | tf_op jit(solution)/shard_map/ppermute | solution.py:95
  95.6 3.7 %collective-permute-done.37.far_ref = f32[6,512]{1,0:T(8,128)S(1)} collective-permute-done((f32[6,512]{1,0:T(8,128)S(1)}, f32[6,512]{1,0:T(8,128)S(1)}, u32[]{:S(2)}, u32[]{:S(2)}) %collective-permute-start.37) | collective-permute-done | bytes 12320 | tf_op jit(solution)/shard_map/ppermute | solution.py:89
  100.4 1.6 %collective-permute-start.39 = (f32[6,512]{1,0:T(8,128)S(1)}, f32[6,512]{1,0:T(8,128)S(1)}, u32[]{:S(2)}, u32[]{:S(2)}) collective-permute-start(f32[6,512]{1,0:T(8,128)S(1)} %shard_map.117.refs_4_), channel_id=1, source_target_pairs={{0,2},{1,3},{2,0},{3,1},{4,6},{5,7},{6,4},{7,5},{8,10},{9,11},{10,... | collective-permute-start | bytes 36872 | tf_op jit(solution)/shard_map/ppermute | solution.py:89
  102.5 1.6 %collective-permute-done.39.refs_6_ = f32[6,512]{1,0:T(8,128)S(1)} collective-permute-done((f32[6,512]{1,0:T(8,128)S(1)}, f32[6,512]{1,0:T(8,128)S(1)}, u32[]{:S(2)}, u32[]{:S(2)}) %collective-permute-start.39) | collective-permute-done | bytes 12320 | tf_op jit(solution)/shard_map/ppermute | solution.py:89
  105.3 2.7 %collective-permute-start.41 = (bf16[2,192,512]{2,1,0:T(8,128)(2,1)S(1)}, bf16[2,192,512]{2,1,0:T(8,128)(2,1)S(1)}, u32[]{:S(2)}, u32[]{:S(2)}) collective-permute-start(bf16[2,192,512]{2,1,0:T(8,128)(2,1)S(1)} %get-tuple-element.107.refs_0_), channel_id=1, source_target_pairs={{0,1},{2,3},{13,12},{15,14},{10,11},{8,9},{7,6},{5,4},{16,17},{18,... | collective-permute-start | bytes 1179656 | tf_op jit(solution)/shard_map/ppermute | solution.py:95
  110.7 1.8 %shard_map.121 = (f32[3,512,512]{2,1,0:T(8,128)S(1)}, f32[2,2048]{1,0:T(2,128)}, f32[2,2048]{1,0:T(2,128)}) custom-call(s32[9]{0:T(128)S(1)} %pad_add_fusion.scalar_ref, f32[4,2048]{1,0:T(4,128)S(1)} %pad_maximum_fusion.refs_0_, f32[4,2048]{1,0:T(4,128)S(1)} %collective-permute-done.26.refs_1_, f32[4,2048]{1,0:T(4,128)S(1)} %collective-permute-done.27.refs_2_, ...), custom_call_target="tpu_custom_call" | custom-call | tf_op jit(solution)/shard_map/pallas_call | solution.py:464
  (96 shorter events, 35.6 us)
Async XLA Ops:
  1.8 6.6 %collective-permute-start = (bf16[3,32,512]{2,1,0:T(8,128)(2,1)S(1)}, bf16[3,32,512]{2,1,0:T(8,128)(2,1)S(1)}, u32[]{:S(2)}, u32[]{:S(2)}) collective-permute-start(bf16[3,32,512]{2,1,0:T(8,128)(2,1)S(1)} %get-tuple-element.65), channel_id=1, source_target_pairs={{0,4},{4,0},{8,12},{12,8},{1,5},{5,1},{9,13},{13,9},{2,6},{6,2},{1... | collective-permute-start | bytes 294920 | tf_op jit(solution)/shard_map/ppermute | solution.py:89
  4.9 10.4 %collective-permute-start.1 = (bf16[3,32,512]{2,1,0:T(8,128)(2,1)S(1)}, bf16[3,32,512]{2,1,0:T(8,128)(2,1)S(1)}, u32[]{:S(2)}, u32[]{:S(2)}) collective-permute-start(bf16[3,32,512]{2,1,0:T(8,128)(2,1)S(1)} %get-tuple-element.66), channel_id=1, source_target_pairs={{0,8},{4,12},{8,0},{12,4},{1,9},{5,13},{9,1},{13,5},{2,10},{6,14},... | collective-permute-start | bytes 294920 | tf_op jit(solution)/shard_map/ppermute | solution.py:89
  7.5 7.8 %collective-permute-start.2 = (bf16[3,32,512]{2,1,0:T(8,128)(2,1)S(1)}, bf16[3,32,512]{2,1,0:T(8,128)(2,1)S(1)}, u32[]{:S(2)}, u32[]{:S(2)}) collective-permute-start(bf16[3,32,512]{2,1,0:T(8,128)(2,1)S(1)} %get-tuple-element.67), channel_id=1, source_target_pairs={{0,12},{4,8},{8,4},{12,0},{1,13},{5,9},{9,5},{13,1},{2,14},{6,10},... | collective-permute-start | bytes 294920 | tf_op jit(solution)/shard_map/ppermute | solution.py:89
  7.5 7.8 %collective-permute-start.3 = (bf16[3,32,512]{2,1,0:T(8,128)(2,1)S(1)}, bf16[3,32,512]{2,1,0:T(8,128)(2,1)S(1)}, u32[]{:S(2)}, u32[]{:S(2)}) collective-permute-start(bf16[3,32,512]{2,1,0:T(8,128)(2,1)S(1)} %get-tuple-element.68), channel_id=1, source_target_pairs={{0,4},{4,0},{8,12},{12,8},{1,5},{5,1},{9,13},{13,9},{2,6},{6,2},{1... | collective-permute-start | bytes 294920 | tf_op jit(solution)/shard_map/ppermute | solution.py:89
  8.4 8.7 %collective-permute-start.7 = (bf16[3,32,512]{2,1,0:T(8,128)(2,1)S(1)}, bf16[3,32,512]{2,1,0:T(8,128)(2,1)S(1)}, u32[]{:S(2)}, u32[]{:S(2)}) collective-permute-start(bf16[3,32,512]{2,1,0:T(8,128)(2,1)S(1)} %collective-permute-done.refs_0_), channel_id=1, source_target_pairs={{0,1},{1,0},{2,3},{3,2},{4,5},{5,4},{6,7},{7,6},{8,9},{9,8},{10,11... | collective-permute-start | bytes 294920 | tf_op jit(solution)/shard_map/ppermute | solution.py:89
  10.0 7.6 %collective-permute-start.4 = (bf16[3,32,512]{2,1,0:T(8,128)(2,1)S(1)}, bf16[3,32,512]{2,1,0:T(8,128)(2,1)S(1)}, u32[]{:S(2)}, u32[]{:S(2)}) collective-permute-start(bf16[3,32,512]{2,1,0:T(8,128)(2,1)S(1)} %collective-permute-done.refs_0_), channel_id=1, source_target_pairs={{0,2},{1,3},{2,0},{3,1},{4,6},{5,7},{6,4},{7,5},{8,10},{9,11},{10,... | collective-permute-start | bytes 294920 | tf_op jit(solution)/shard_map/ppermute | solution.py:89
  15.4 6.0 %collective-permute-start.5 = (bf16[3,32,512]{2,1,0:T(8,128)(2,1)S(1)}, bf16[3,32,512]{2,1,0:T(8,128)(2,1)S(1)}, u32[]{:S(2)}, u32[]{:S(2)}) collective-permute-start(bf16[3,32,512]{2,1,0:T(8,128)(2,1)S(1)} %collective-permute-done.1.refs_1_), channel_id=1, source_target_pairs={{0,2},{1,3},{2,0},{3,1},{4,6},{5,7},{6,4},{7,5},{8,10},{9,11},{10,... | collective-permute-start | bytes 294920 | tf_op jit(solution)/shard_map/ppermute | solution.py:89
  17.6 10.8 %collective-permute-start.13 = (bf16[3,32,512]{2,1,0:T(8,128)(2,1)S(1)}, bf16[3,32,512]{2,1,0:T(8,128)(2,1)S(1)}, u32[]{:S(2)}, u32[]{:S(2)}) collective-permute-start(bf16[3,32,512]{2,1,0:T(8,128)(2,1)S(1)} %get-tuple-element.72), channel_id=1, source_target_pairs={{0,8},{4,12},{8,0},{12,4},{1,9},{5,13},{9,1},{13,5},{2,10},{6,14},... | collective-permute-start | bytes 294920 | tf_op jit(solution)/shard_map/ppermute | solution.py:89
  20.0 8.4 %collective-permute-start.14 = (bf16[3,32,512]{2,1,0:T(8,128)(2,1)S(1)}, bf16[3,32,512]{2,1,0:T(8,128)(2,1)S(1)}, u32[]{:S(2)}, u32[]{:S(2)}) collective-permute-start(bf16[3,32,512]{2,1,0:T(8,128)(2,1)S(1)} %get-tuple-element.73), channel_id=1, source_target_pairs={{0,12},{4,8},{8,4},{12,0},{1,13},{5,9},{9,5},{13,1},{2,14},{6,10},... | collective-permute-start | bytes 294920 | tf_op jit(solution)/shard_map/ppermute | solution.py:89
  28.4 14.5 %collective-permute-start.15 = (bf16[3,192,512]{2,1,0:T(8,128)(2,1)S(1)}, bf16[3,192,512]{2,1,0:T(8,128)(2,1)S(1)}, u32[]{:S(2)}, u32[]{:S(2)}) collective-permute-start(bf16[3,192,512]{2,1,0:T(8,128)(2,1)S(1)} %get-tuple-element.74), channel_id=1, source_target_pairs={{0,4},{4,0},{8,12},{12,8},{1,5},{5,1},{9,13},{13,9},{2,6},{6,2},{1... | collective-permute-start | bytes 1769480 | tf_op jit(solution)/shard_map/ppermute | solution.py:89
  30.2 7.9 %collective-permute-start.16 = (bf16[3,64,512]{2,1,0:T(8,128)(2,1)S(1)}, bf16[3,64,512]{2,1,0:T(8,128)(2,1)S(1)}, u32[]{:S(2)}, u32[]{:S(2)}) collective-permute-start(bf16[3,64,512]{2,1,0:T(8,128)(2,1)S(1)} %shard_map.107.refs_0_), channel_id=1, source_target_pairs={{0,2},{1,3},{2,0},{3,1},{4,6},{5,7},{6,4},{7,5},{8,10},{9,11},{10,... | collective-permute-start | bytes 589832 | tf_op jit(solution)/shard_map/ppermute | solution.py:89
  31.8 6.4 %collective-permute-start.17 = (bf16[3,32,512]{2,1,0:T(8,128)(2,1)S(1)}, bf16[3,32,512]{2,1,0:T(8,128)(2,1)S(1)}, u32[]{:S(2)}, u32[]{:S(2)}) collective-permute-start(bf16[3,32,512]{2,1,0:T(8,128)(2,1)S(1)} %collective-permute-done.14.refs_1_), channel_id=1, source_target_pairs={{0,2},{1,3},{2,0},{3,1},{4,6},{5,7},{6,4},{7,5},{8,10},{9,11},{10,... | collective-permute-start | bytes 294920 | tf_op jit(solution)/shard_map/ppermute | solution.py:89
  43.7 21.8 %collective-permute-start.22 = (bf16[3,192,512]{2,1,0:T(8,128)(2,1)S(1)}, bf16[3,192,512]{2,1,0:T(8,128)(2,1)S(1)}, u32[]{:S(2)}, u32[]{:S(2)}) collective-permute-start(bf16[3,192,512]{2,1,0:T(8,128)(2,1)S(1)} %get-tuple-element.86), channel_id=1, source_target_pairs={{0,4},{4,0},{8,12},{12,8},{1,5},{5,1},{9,13},{13,9},{2,6},{6,2},{1... | collective-permute-start | bytes 1769480 | tf_op jit(solution)/shard_map/ppermute | solution.py:89
  46.2 15.7 %collective-permute-start.25 = (bf16[3,112,512]{2,1,0:T(8,128)(2,1)S(1)}, bf16[3,112,512]{2,1,0:T(8,128)(2,1)S(1)}, u32[]{:S(2)}, u32[]{:S(2)}) collective-permute-start(bf16[3,112,512]{2,1,0:T(8,128)(2,1)S(1)} %collective-permute-done.24.refs_0_), channel_id=1, source_target_pairs={{1,9},{2,10},{5,13},{6,14},{8,0},{11,3},{12,4},{15,7},{17,25},{18,... | collective-permute-start | bytes 1032200 | tf_op jit(solution)/shard_map/ppermute | solution.py:95
  47.5 15.8 %collective-permute-start.30 = (bf16[3,80,512]{2,1,0:T(8,128)(2,1)S(1)}, bf16[3,80,512]{2,1,0:T(8,128)(2,1)S(1)}, u32[]{:S(2)}, u32[]{:S(2)}) collective-permute-start(bf16[3,80,512]{2,1,0:T(8,128)(2,1)S(1)} %collective-permute-done.29.refs_0_), channel_id=1, source_target_pairs={{1,9},{2,10},{5,13},{6,14},{8,0},{11,3},{12,4},{15,7},{17,25},{18,... | collective-permute-start | bytes 737288 | tf_op jit(solution)/shard_map/ppermute | solution.py:95
  48.8 10.2 %collective-permute-start.28 = (f32[4,2048]{1,0:T(4,128)S(1)}, f32[4,2048]{1,0:T(4,128)S(1)}, u32[]{:S(2)}, u32[]{:S(2)}) collective-permute-start(f32[4,2048]{1,0:T(4,128)S(1)} %pad_maximum_fusion.refs_0_), channel_id=1, source_target_pairs={{0,3},{1,2},{2,1},{3,0},{4,7},{5,6},{6,5},{7,4},{8,11},{9,10},{10,... | collective-permute-start | bytes 98312 | tf_op jit(solution)/shard_map/ppermute | solution.py:89
  62.0 18.2 %collective-permute-start.32 = (bf16[3,112,512]{2,1,0:T(8,128)(2,1)S(1)}, bf16[3,112,512]{2,1,0:T(8,128)(2,1)S(1)}, u32[]{:S(2)}, u32[]{:S(2)}) collective-permute-start(bf16[3,112,512]{2,1,0:T(8,128)(2,1)S(1)} %shard_map.111.refs_0_), channel_id=1, source_target_pairs={{4,0},{9,13},{14,10},{3,7},{20,16},{25,29},{30,26},{19,23}} | collective-permute-start | bytes 1032200 | tf_op jit(solution)/shard_map/ppermute | solution.py:95
  63.4 16.8 %collective-permute-start.33 = (bf16[3,80,512]{2,1,0:T(8,128)(2,1)S(1)}, bf16[3,80,512]{2,1,0:T(8,128)(2,1)S(1)}, u32[]{:S(2)}, u32[]{:S(2)}) collective-permute-start(bf16[3,80,512]{2,1,0:T(8,128)(2,1)S(1)} %shard_map.112.refs_1_), channel_id=1, source_target_pairs={{4,0},{9,13},{14,10},{3,7},{20,16},{25,29},{30,26},{19,23}} | collective-permute-start | bytes 737288 | tf_op jit(solution)/shard_map/ppermute | solution.py:95
  65.7 25.6 %collective-permute-start.23 = (bf16[3,192,512]{2,1,0:T(8,128)(2,1)S(1)}, bf16[3,192,512]{2,1,0:T(8,128)(2,1)S(1)}, u32[]{:S(2)}, u32[]{:S(2)}) collective-permute-start(bf16[3,192,512]{2,1,0:T(8,128)(2,1)S(1)} %shard_map.109.refs_0_), channel_id=1, source_target_pairs={{0,8},{4,12},{8,0},{12,4},{1,9},{5,13},{9,1},{13,5},{2,10},{6,14},... | collective-permute-start | bytes 1769480 | tf_op jit(solution)/shard_map/ppermute | solution.py:89
  80.3 11.0 %collective-permute-start.34 = (bf16[2,192,512]{2,1,0:T(8,128)(2,1)S(1)}, bf16[2,192,512]{2,1,0:T(8,128)(2,1)S(1)}, u32[]{:S(2)}, u32[]{:S(2)}) collective-permute-start(bf16[2,192,512]{2,1,0:T(8,128)(2,1)S(1)} %get-tuple-element.101.refs_0_), channel_id=1, source_target_pairs={{0,2},{13,15},{10,8},{7,5},{16,18},{29,31},{26,24},{23,21}} | collective-permute-start | bytes 1179656 | tf_op jit(solution)/shard_map/ppermute | solution.py:95
  81.6 9.7 %collective-permute-start.35 = (bf16[2,192,512]{2,1,0:T(8,128)(2,1)S(1)}, bf16[2,192,512]{2,1,0:T(8,128)(2,1)}, u32[]{:S(2)}, u32[]{:S(2)}) collective-permute-start(bf16[2,192,512]{2,1,0:T(8,128)(2,1)S(1)} %get-tuple-element.103.refs_2_), channel_id=1, source_target_pairs={{0,2},{13,15},{10,8},{7,5},{16,18},{29,31},{26,24},{23,21}} | collective-permute-start | bytes 1179656 | tf_op jit(solution)/shard_map/ppermute | solution.py:95
  83.7 11.6 %collective-permute-start.36 = (bf16[2,192,512]{2,1,0:T(8,128)(2,1)S(1)}, bf16[2,192,512]{2,1,0:T(8,128)(2,1)}, u32[]{:S(2)}, u32[]{:S(2)}) collective-permute-start(bf16[2,192,512]{2,1,0:T(8,128)(2,1)S(1)} %get-tuple-element.105.refs_4_), channel_id=1, source_target_pairs={{0,2},{13,15},{10,8},{7,5},{16,18},{29,31},{26,24},{23,21}} | collective-permute-start | bytes 1179656 | tf_op jit(solution)/shard_map/ppermute | solution.py:95
  99.3 14.5 %collective-permute-start.44 = (bf16[3,192,512]{2,1,0:T(8,128)(2,1)S(1)}, bf16[3,192,512]{2,1,0:T(8,128)(2,1)S(1)}, u32[]{:S(2)}, u32[]{:S(2)}) collective-permute-start(bf16[3,192,512]{2,1,0:T(8,128)(2,1)S(1)} %shard_map.115.act_ref.refs_3_), channel_id=1, source_target_pairs={{0,4},{4,0},{8,12},{12,8},{1,5},{5,1},{9,13},{13,9},{2,6},{6,2},{1... | collective-permute-start | bytes 1769480 | tf_op jit(solution)/shard_map/ppermute | solution.py:89
  105.3 7.1 %collective-permute-start.41 = (bf16[2,192,512]{2,1,0:T(8,128)(2,1)S(1)}, bf16[2,192,512]{2,1,0:T(8,128)(2,1)S(1)}, u32[]{:S(2)}, u32[]{:S(2)}) collective-permute-start(bf16[2,192,512]{2,1,0:T(8,128)(2,1)S(1)} %get-tuple-element.107.refs_0_), channel_id=1, source_target_pairs={{0,1},{2,3},{13,12},{15,14},{10,11},{8,9},{7,6},{5,4},{16,17},{18,... | collective-permute-start | bytes 1179656 | tf_op jit(solution)/shard_map/ppermute | solution.py:95
  (25 other events, 118.8 us)

commit v14 on v13

--- a/solution.py
+++ b/solution.py
@@ -324,23 +324,29 @@
     )(aside, *panels)
 
 
-def halves_of(act, near, far):
-    layers, _, cols = act.shape
-
-    def kernel(act_ref, near_ref, far_ref, out_ref):
+def settle(part, cross, near, far):
+    layers, _, cols = part.shape
+
+    def kernel(part_ref, cross_ref, near_ref, far_ref, act_ref, out_ref):
         for layer in range(layers):
-            wide = act_ref[layer].astype(jnp.float32)
+            total = part_ref[layer].astype(jnp.float32) + cross_ref[layer].astype(jnp.float32)
+            total = total.astype(act_ref.dtype)
+            act_ref[layer] = total
+            wide = total.astype(jnp.float32)
             out_ref[layer : layer + 1] = jnp.sum(wide * wide, axis=0, keepdims=True)
         out_ref[layers:] = near_ref[...] + far_ref[...]
 
     return pl.pallas_call(
         kernel,
-        out_shape=jax.ShapeDtypeStruct((2 * layers, cols), jnp.float32),
-        in_specs=[vmem_spec] * 3,
-        out_specs=vmem_spec,
-        compiler_params=pltpu.CompilerParams(vmem_limit_bytes=8 * 1024 * 1024),
-        cost_estimate=light,
-    )(act, near, far)
+        out_shape=[
+            jax.ShapeDtypeStruct(part.shape, part.dtype),
+            jax.ShapeDtypeStruct((2 * layers, cols), jnp.float32),
+        ],
+        in_specs=[vmem_spec] * 4,
+        out_specs=[vmem_spec] * 2,
+        compiler_params=pltpu.CompilerParams(vmem_limit_bytes=8 * 1024 * 1024),
+        cost_estimate=light,
+    )(part, cross, near, far)
 
 
 def total_of(near, far):
@@ -528,10 +534,10 @@
 
     done = step([part_act, cross_act, square_grad, square_far, *full, *chip])
     (part_act, cross_act, square_grad, square_far), full, chip = done[:4], done[4:][:layers], done[4 + layers :]
-    full_act = add((part_act, cross_act))
-    half = halves_of(full_act, square_grad, square_far)
-    packet = total_of(half, flip(half, "dp", 1))
-    back_act = flip(after(full_act, packet), "dp", 1)
+    full_act, half = settle(part_act, cross_act, square_grad, square_far)
+    other = flip(half, "dp", 1)
+    back_act = flip(after(full_act, other), "dp", 1)
+    packet = total_of(half, other)
     packets = [packet] + [flip(packet, "owner", mask) for mask in range(1, n_own)]
     source = -dp % n_own
     home = jnp.where(own == source, 0, jnp.where(own == source ^ 2, 1, 2)).astype(jnp.int32)[None]

time: 117 us -> 117 us (level)
  no operation moved by 1% of the time
where the time goes in v14:
time: 117 us; the launch traced here: 115 us
  starting transfers between devices  54.6 us (47%)
  waiting for transfers between devices  45.2 us (39%)
  Pallas kernels  14.6 us (12%)
    ppermute x33, starting transfers between devices, flip(): lax.ppermute(array, axis, [(i, i ^ mask) for i in range(lax.axis_size(axi...  36.6 us
    ppermute x33, waiting for transfers between devices, flip(): lax.ppermute(array, axis, [(i, i ^ mask) for i in range(lax.axis_size(axi...  26.7 us
    ppermute x10, waiting for transfers between devices, hop(): return lax.ppermute(array, ('dp', 'owner'), flat)  18.5 us
    ppermute x10, starting transfers between devices, hop(): return lax.ppermute(array, ('dp', 'owner'), flat)  16.6 us
    pallas_call x2, Pallas kernels, project_rows(): pl.pallas_call(kernel, out_shape=[jax.ShapeDtypeStruct(shape, jnp.bfloat1...  4.17 us
    pallas_call x2, Pallas kernels, load(): pl.pallas_call(kernel, out_shape=[jax.ShapeDtypeStruct(shape, array.dtype...  3.12 us
  transfers between devices with their start and end apart: 45, of which 19 were waited for; matrix products, arithmetic and copies ran while one was open for 0% of the time, Pallas kernels for 10%

profile of v14, /device:TPU:0, one launch (start us, length us, event | category | flops | bytes accessed | tf_op | source)
XLA Modules:
  0.0 115.4 jit_solution(11004129886062466763)
XLA Ops:
  1.8 3.1 %collective-permute-start = (bf16[3,32,512]{2,1,0:T(8,128)(2,1)S(1)}, bf16[3,32,512]{2,1,0:T(8,128)(2,1)S(1)}, u32[]{:S(2)}, u32[]{:S(2)}) collective-permute-start(bf16[3,32,512]{2,1,0:T(8,128)(2,1)S(1)} %get-tuple-element.67), channel_id=1, source_target_pairs={{0,4},{4,0},{8,12},{12,8},{1,5},{5,1},{9,13},{13,9},{2,6},{6,2},{1... | collective-permute-start | bytes 294920 | tf_op jit(solution)/shard_map/ppermute | solution.py:89
  4.9 2.6 %collective-permute-start.1 = (bf16[3,32,512]{2,1,0:T(8,128)(2,1)S(1)}, bf16[3,32,512]{2,1,0:T(8,128)(2,1)S(1)}, u32[]{:S(2)}, u32[]{:S(2)}) collective-permute-start(bf16[3,32,512]{2,1,0:T(8,128)(2,1)S(1)} %get-tuple-element.68), channel_id=1, source_target_pairs={{0,8},{4,12},{8,0},{12,4},{1,9},{5,13},{9,1},{13,5},{2,10},{6,14},... | collective-permute-start | bytes 294920 | tf_op jit(solution)/shard_map/ppermute | solution.py:89
  11.6 3.8 %collective-permute-done.1.refs_1_ = bf16[3,32,512]{2,1,0:T(8,128)(2,1)S(1)} collective-permute-done((bf16[3,32,512]{2,1,0:T(8,128)(2,1)S(1)}, bf16[3,32,512]{2,1,0:T(8,128)(2,1)S(1)}, u32[]{:S(2)}, u32[]{:S(2)}) %collective-permute-start.1) | collective-permute-done | bytes 98336 | tf_op jit(solution)/shard_map/ppermute | solution.py:89
  17.6 2.4 %collective-permute-start.13 = (bf16[3,32,512]{2,1,0:T(8,128)(2,1)S(1)}, bf16[3,32,512]{2,1,0:T(8,128)(2,1)S(1)}, u32[]{:S(2)}, u32[]{:S(2)}) collective-permute-start(bf16[3,32,512]{2,1,0:T(8,128)(2,1)S(1)} %get-tuple-element.74), channel_id=1, source_target_pairs={{0,8},{4,12},{8,0},{12,4},{1,9},{5,13},{9,1},{13,5},{2,10},{6,14},... | collective-permute-start | bytes 294920 | tf_op jit(solution)/shard_map/ppermute | solution.py:89
  24.0 2.1 %shard_map.105 = (bf16[3,192,512]{2,1,0:T(8,128)(2,1)S(1)}, bf16[3,192,512]{2,1,0:T(8,128)(2,1)S(1)}) custom-call(s32[9]{0:T(128)S(1)} %pad_add_fusion.scalar_ref, bf16[3,128,512]{2,1,0:T(8,128)(2,1)S(1)} %get-tuple-element.65.tokens_ref, bf16[3,512,512]{2,1,0:T(8,128)(2,1)S(1)} %get-tuple-element.66.basis_ref, ...), custom_call_target="tpu_custom_call" | custom-call | tf_op jit(solution)/shard_map/pallas_call | solution.py:164
  26.1 2.3 %collective-permute-done.13.refs_1_ = bf16[3,32,512]{2,1,0:T(8,128)(2,1)S(1)} collective-permute-done((bf16[3,32,512]{2,1,0:T(8,128)(2,1)S(1)}, bf16[3,32,512]{2,1,0:T(8,128)(2,1)S(1)}, u32[]{:S(2)}, u32[]{:S(2)}) %collective-permute-start.13) | collective-permute-done | bytes 98336 | tf_op jit(solution)/shard_map/ppermute | solution.py:89
  28.4 1.8 %collective-permute-start.15 = (bf16[3,192,512]{2,1,0:T(8,128)(2,1)S(1)}, bf16[3,192,512]{2,1,0:T(8,128)(2,1)S(1)}, u32[]{:S(2)}, u32[]{:S(2)}) collective-permute-start(bf16[3,192,512]{2,1,0:T(8,128)(2,1)S(1)} %get-tuple-element.76), channel_id=1, source_target_pairs={{0,4},{4,0},{8,12},{12,8},{1,5},{5,1},{9,13},{13,9},{2,6},{6,2},{1... | collective-permute-start | bytes 1769480 | tf_op jit(solution)/shard_map/ppermute | solution.py:89
  34.5 3.7 %collective-permute-done.17.refs_3_ = bf16[3,32,512]{2,1,0:T(8,128)(2,1)S(1)} collective-permute-done((bf16[3,32,512]{2,1,0:T(8,128)(2,1)S(1)}, bf16[3,32,512]{2,1,0:T(8,128)(2,1)S(1)}, u32[]{:S(2)}, u32[]{:S(2)}) %collective-permute-start.17) | collective-permute-done | bytes 98336 | tf_op jit(solution)/shard_map/ppermute | solution.py:89
  39.7 2.1 %shard_map.108 = (bf16[3,192,512]{2,1,0:T(8,128)(2,1)S(1)}, bf16[3,192,512]{2,1,0:T(8,128)(2,1)S(1)}) custom-call(s32[9]{0:T(128)S(1)} %pad_add_fusion.scalar_ref, bf16[3,128,512]{2,1,0:T(8,128)(2,1)S(1)} %get-tuple-element.77.tokens_ref, bf16[3,512,512]{2,1,0:T(8,128)(2,1)S(1)} %get-tuple-element.78.basis_ref, bf16[3,64,512]{2,1,0:T(8,128)(2,1)S(1)} %shard_map.107.refs_0_, ...), custom_call_target="tpu_custom_call" | custom-call | tf_op jit(solution)/shard_map/pallas_call | solution.py:164
  43.7 1.8 %collective-permute-start.22 = (bf16[3,192,512]{2,1,0:T(8,128)(2,1)S(1)}, bf16[3,192,512]{2,1,0:T(8,128)(2,1)S(1)}, u32[]{:S(2)}, u32[]{:S(2)}) collective-permute-start(bf16[3,192,512]{2,1,0:T(8,128)(2,1)S(1)} %get-tuple-element.88), channel_id=1, source_target_pairs={{0,4},{4,0},{8,12},{12,8},{1,5},{5,1},{9,13},{13,9},{2,6},{6,2},{1... | collective-permute-start | bytes 1769480 | tf_op jit(solution)/shard_map/ppermute | solution.py:89
  48.8 6.9 %collective-permute-start.28 = (f32[4,2048]{1,0:T(4,128)S(1)}, f32[4,2048]{1,0:T(4,128)S(1)}, u32[]{:S(2)}, u32[]{:S(2)}) collective-permute-start(f32[4,2048]{1,0:T(4,128)S(1)} %pad_maximum_fusion.refs_0_), channel_id=1, source_target_pairs={{0,3},{1,2},{2,1},{3,0},{4,7},{5,6},{6,5},{7,4},{8,11},{9,10},{10,... | collective-permute-start | bytes 98312 | tf_op jit(solution)/shard_map/ppermute | solution.py:89
  55.7 3.3 %collective-permute-start.27 = (f32[4,2048]{1,0:T(4,128)S(1)}, f32[4,2048]{1,0:T(4,128)S(1)}, u32[]{:S(2)}, u32[]{:S(2)}) collective-permute-start(f32[4,2048]{1,0:T(4,128)S(1)} %pad_maximum_fusion.refs_0_), channel_id=1, source_target_pairs={{0,2},{1,3},{2,0},{3,1},{4,6},{5,7},{6,4},{7,5},{8,10},{9,11},{10,... | collective-permute-start | bytes 98312 | tf_op jit(solution)/shard_map/ppermute | solution.py:89
  59.1 2.0 %collective-permute-start.26 = (f32[4,2048]{1,0:T(4,128)S(1)}, f32[4,2048]{1,0:T(4,128)S(1)}, u32[]{:S(2)}, u32[]{:S(2)}) collective-permute-start(f32[4,2048]{1,0:T(4,128)S(1)} %pad_maximum_fusion.refs_0_), channel_id=1, source_target_pairs={{0,1},{1,0},{2,3},{3,2},{4,5},{5,4},{6,7},{7,6},{8,9},{9,8},{10,11... | collective-permute-start | bytes 98312 | tf_op jit(solution)/shard_map/ppermute | solution.py:89
  65.8 14.4 %collective-permute-done.33.refs_3_ = bf16[3,80,512]{2,1,0:T(8,128)(2,1)S(1)} collective-permute-done((bf16[3,80,512]{2,1,0:T(8,128)(2,1)S(1)}, bf16[3,80,512]{2,1,0:T(8,128)(2,1)S(1)}, u32[]{:S(2)}, u32[]{:S(2)}) %collective-permute-start.33) | collective-permute-done | bytes 245792 | tf_op jit(solution)/shard_map/ppermute | solution.py:95
  80.3 2.1 %collective-permute-start.34 = (bf16[2,192,512]{2,1,0:T(8,128)(2,1)S(1)}, bf16[2,192,512]{2,1,0:T(8,128)(2,1)}, u32[]{:S(2)}, u32[]{:S(2)}) collective-permute-start(bf16[2,192,512]{2,1,0:T(8,128)(2,1)S(1)} %get-tuple-element.104.refs_0_), channel_id=1, source_target_pairs={{0,2},{13,15},{10,8},{7,5},{16,18},{29,31},{26,24},{23,21}} | collective-permute-start | bytes 1179656 | tf_op jit(solution)/shard_map/ppermute | solution.py:95
  82.4 2.1 %collective-permute-start.35 = (bf16[2,192,512]{2,1,0:T(8,128)(2,1)S(1)}, bf16[2,192,512]{2,1,0:T(8,128)(2,1)}, u32[]{:S(2)}, u32[]{:S(2)}) collective-permute-start(bf16[2,192,512]{2,1,0:T(8,128)(2,1)S(1)} %get-tuple-element.106.refs_2_), channel_id=1, source_target_pairs={{0,2},{13,15},{10,8},{7,5},{16,18},{29,31},{26,24},{23,21}} | collective-permute-start | bytes 1179656 | tf_op jit(solution)/shard_map/ppermute | solution.py:95
  84.4 2.0 %collective-permute-start.36 = (bf16[2,192,512]{2,1,0:T(8,128)(2,1)S(1)}, bf16[2,192,512]{2,1,0:T(8,128)(2,1)}, u32[]{:S(2)}, u32[]{:S(2)}) collective-permute-start(bf16[2,192,512]{2,1,0:T(8,128)(2,1)S(1)} %get-tuple-element.108.refs_4_), channel_id=1, source_target_pairs={{0,2},{13,15},{10,8},{7,5},{16,18},{29,31},{26,24},{23,21}} | collective-permute-start | bytes 1179656 | tf_op jit(solution)/shard_map/ppermute | solution.py:95
  86.6 4.7 %collective-permute-done.31.far_ref = f32[3,512]{1,0:T(4,128)S(1)} collective-permute-done((f32[3,512]{1,0:T(4,128)S(1)}, f32[3,512]{1,0:T(4,128)S(1)}, u32[]{:S(2)}, u32[]{:S(2)}) %collective-permute-start.31) | collective-permute-done | bytes 6176 | tf_op jit(solution)/shard_map/ppermute | solution.py:89
  91.3 4.0 %collective-permute-done.36.refs_5_ = bf16[2,192,512]{2,1,0:T(8,128)(2,1)} collective-permute-done((bf16[2,192,512]{2,1,0:T(8,128)(2,1)S(1)}, bf16[2,192,512]{2,1,0:T(8,128)(2,1)}, u32[]{:S(2)}, u32[]{:S(2)}) %collective-permute-start.36) | collective-permute-done | bytes 393248 | tf_op jit(solution)/shard_map/ppermute | solution.py:95
  95.7 3.7 %collective-permute-done.37.far_ref = f32[6,512]{1,0:T(8,128)S(1)} collective-permute-done((f32[6,512]{1,0:T(8,128)S(1)}, f32[6,512]{1,0:T(8,128)S(1)}, u32[]{:S(2)}, u32[]{:S(2)}) %collective-permute-start.37) | collective-permute-done | bytes 12320 | tf_op jit(solution)/shard_map/ppermute | solution.py:89
  100.5 1.6 %collective-permute-start.39 = (f32[6,512]{1,0:T(8,128)S(1)}, f32[6,512]{1,0:T(8,128)S(1)}, u32[]{:S(2)}, u32[]{:S(2)}) collective-permute-start(f32[6,512]{1,0:T(8,128)S(1)} %shard_map.116.refs_4_), channel_id=1, source_target_pairs={{0,2},{1,3},{2,0},{3,1},{4,6},{5,7},{6,4},{7,5},{8,10},{9,11},{10,... | collective-permute-start | bytes 36872 | tf_op jit(solution)/shard_map/ppermute | solution.py:89
  102.6 1.6 %collective-permute-done.39.refs_6_ = f32[6,512]{1,0:T(8,128)S(1)} collective-permute-done((f32[6,512]{1,0:T(8,128)S(1)}, f32[6,512]{1,0:T(8,128)S(1)}, u32[]{:S(2)}, u32[]{:S(2)}) %collective-permute-start.39) | collective-permute-done | bytes 12320 | tf_op jit(solution)/shard_map/ppermute | solution.py:89
  105.6 2.7 %collective-permute-start.41 = (bf16[2,192,512]{2,1,0:T(8,128)(2,1)S(1)}, bf16[2,192,512]{2,1,0:T(8,128)(2,1)S(1)}, u32[]{:S(2)}, u32[]{:S(2)}) collective-permute-start(bf16[2,192,512]{2,1,0:T(8,128)(2,1)S(1)} %get-tuple-element.110.refs_0_), channel_id=1, source_target_pairs={{0,1},{2,3},{13,12},{15,14},{10,11},{8,9},{7,6},{5,4},{16,17},{18,... | collective-permute-start | bytes 1179656 | tf_op jit(solution)/shard_map/ppermute | solution.py:95
  110.9 1.8 %shard_map.120 = (f32[3,512,512]{2,1,0:T(8,128)S(1)}, f32[2,2048]{1,0:T(2,128)}, f32[2,2048]{1,0:T(2,128)}) custom-call(s32[9]{0:T(128)S(1)} %pad_add_fusion.scalar_ref, f32[4,2048]{1,0:T(4,128)S(1)} %pad_maximum_fusion.refs_0_, f32[4,2048]{1,0:T(4,128)S(1)} %collective-permute-done.26.refs_1_, f32[4,2048]{1,0:T(4,128)S(1)} %collective-permute-done.27.refs_2_, ...), custom_call_target="tpu_custom_call" | custom-call | tf_op jit(solution)/shard_map/pallas_call | solution.py:470
  (95 shorter events, 36.0 us)
Async XLA Ops:
  1.8 6.6 %collective-permute-start = (bf16[3,32,512]{2,1,0:T(8,128)(2,1)S(1)}, bf16[3,32,512]{2,1,0:T(8,128)(2,1)S(1)}, u32[]{:S(2)}, u32[]{:S(2)}) collective-permute-start(bf16[3,32,512]{2,1,0:T(8,128)(2,1)S(1)} %get-tuple-element.67), channel_id=1, source_target_pairs={{0,4},{4,0},{8,12},{12,8},{1,5},{5,1},{9,13},{13,9},{2,6},{6,2},{1... | collective-permute-start | bytes 294920 | tf_op jit(solution)/shard_map/ppermute | solution.py:89
  4.9 10.4 %collective-permute-start.1 = (bf16[3,32,512]{2,1,0:T(8,128)(2,1)S(1)}, bf16[3,32,512]{2,1,0:T(8,128)(2,1)S(1)}, u32[]{:S(2)}, u32[]{:S(2)}) collective-permute-start(bf16[3,32,512]{2,1,0:T(8,128)(2,1)S(1)} %get-tuple-element.68), channel_id=1, source_target_pairs={{0,8},{4,12},{8,0},{12,4},{1,9},{5,13},{9,1},{13,5},{2,10},{6,14},... | collective-permute-start | bytes 294920 | tf_op jit(solution)/shard_map/ppermute | solution.py:89
  7.5 7.8 %collective-permute-start.2 = (bf16[3,32,512]{2,1,0:T(8,128)(2,1)S(1)}, bf16[3,32,512]{2,1,0:T(8,128)(2,1)S(1)}, u32[]{:S(2)}, u32[]{:S(2)}) collective-permute-start(bf16[3,32,512]{2,1,0:T(8,128)(2,1)S(1)} %get-tuple-element.69), channel_id=1, source_target_pairs={{0,12},{4,8},{8,4},{12,0},{1,13},{5,9},{9,5},{13,1},{2,14},{6,10},... | collective-permute-start | bytes 294920 | tf_op jit(solution)/shard_map/ppermute | solution.py:89
  7.5 7.8 %collective-permute-start.3 = (bf16[3,32,512]{2,1,0:T(8,128)(2,1)S(1)}, bf16[3,32,512]{2,1,0:T(8,128)(2,1)S(1)}, u32[]{:S(2)}, u32[]{:S(2)}) collective-permute-start(bf16[3,32,512]{2,1,0:T(8,128)(2,1)S(1)} %get-tuple-element.70), channel_id=1, source_target_pairs={{0,4},{4,0},{8,12},{12,8},{1,5},{5,1},{9,13},{13,9},{2,6},{6,2},{1... | collective-permute-start | bytes 294920 | tf_op jit(solution)/shard_map/ppermute | solution.py:89
  8.4 8.7 %collective-permute-start.7 = (bf16[3,32,512]{2,1,0:T(8,128)(2,1)S(1)}, bf16[3,32,512]{2,1,0:T(8,128)(2,1)S(1)}, u32[]{:S(2)}, u32[]{:S(2)}) collective-permute-start(bf16[3,32,512]{2,1,0:T(8,128)(2,1)S(1)} %collective-permute-done.refs_0_), channel_id=1, source_target_pairs={{0,1},{1,0},{2,3},{3,2},{4,5},{5,4},{6,7},{7,6},{8,9},{9,8},{10,11... | collective-permute-start | bytes 294920 | tf_op jit(solution)/shard_map/ppermute | solution.py:89
  10.0 7.6 %collective-permute-start.4 = (bf16[3,32,512]{2,1,0:T(8,128)(2,1)S(1)}, bf16[3,32,512]{2,1,0:T(8,128)(2,1)S(1)}, u32[]{:S(2)}, u32[]{:S(2)}) collective-permute-start(bf16[3,32,512]{2,1,0:T(8,128)(2,1)S(1)} %collective-permute-done.refs_0_), channel_id=1, source_target_pairs={{0,2},{1,3},{2,0},{3,1},{4,6},{5,7},{6,4},{7,5},{8,10},{9,11},{10,... | collective-permute-start | bytes 294920 | tf_op jit(solution)/shard_map/ppermute | solution.py:89
  15.4 6.0 %collective-permute-start.5 = (bf16[3,32,512]{2,1,0:T(8,128)(2,1)S(1)}, bf16[3,32,512]{2,1,0:T(8,128)(2,1)S(1)}, u32[]{:S(2)}, u32[]{:S(2)}) collective-permute-start(bf16[3,32,512]{2,1,0:T(8,128)(2,1)S(1)} %collective-permute-done.1.refs_1_), channel_id=1, source_target_pairs={{0,2},{1,3},{2,0},{3,1},{4,6},{5,7},{6,4},{7,5},{8,10},{9,11},{10,... | collective-permute-start | bytes 294920 | tf_op jit(solution)/shard_map/ppermute | solution.py:89
  17.6 10.8 %collective-permute-start.13 = (bf16[3,32,512]{2,1,0:T(8,128)(2,1)S(1)}, bf16[3,32,512]{2,1,0:T(8,128)(2,1)S(1)}, u32[]{:S(2)}, u32[]{:S(2)}) collective-permute-start(bf16[3,32,512]{2,1,0:T(8,128)(2,1)S(1)} %get-tuple-element.74), channel_id=1, source_target_pairs={{0,8},{4,12},{8,0},{12,4},{1,9},{5,13},{9,1},{13,5},{2,10},{6,14},... | collective-permute-start | bytes 294920 | tf_op jit(solution)/shard_map/ppermute | solution.py:89
  20.0 8.4 %collective-permute-start.14 = (bf16[3,32,512]{2,1,0:T(8,128)(2,1)S(1)}, bf16[3,32,512]{2,1,0:T(8,128)(2,1)S(1)}, u32[]{:S(2)}, u32[]{:S(2)}) collective-permute-start(bf16[3,32,512]{2,1,0:T(8,128)(2,1)S(1)} %get-tuple-element.75), channel_id=1, source_target_pairs={{0,12},{4,8},{8,4},{12,0},{1,13},{5,9},{9,5},{13,1},{2,14},{6,10},... | collective-permute-start | bytes 294920 | tf_op jit(solution)/shard_map/ppermute | solution.py:89
  28.4 14.5 %collective-permute-start.15 = (bf16[3,192,512]{2,1,0:T(8,128)(2,1)S(1)}, bf16[3,192,512]{2,1,0:T(8,128)(2,1)S(1)}, u32[]{:S(2)}, u32[]{:S(2)}) collective-permute-start(bf16[3,192,512]{2,1,0:T(8,128)(2,1)S(1)} %get-tuple-element.76), channel_id=1, source_target_pairs={{0,4},{4,0},{8,12},{12,8},{1,5},{5,1},{9,13},{13,9},{2,6},{6,2},{1... | collective-permute-start | bytes 1769480 | tf_op jit(solution)/shard_map/ppermute | solution.py:89
  30.2 7.9 %collective-permute-start.16 = (bf16[3,64,512]{2,1,0:T(8,128)(2,1)S(1)}, bf16[3,64,512]{2,1,0:T(8,128)(2,1)S(1)}, u32[]{:S(2)}, u32[]{:S(2)}) collective-permute-start(bf16[3,64,512]{2,1,0:T(8,128)(2,1)S(1)} %shard_map.107.refs_0_), channel_id=1, source_target_pairs={{0,2},{1,3},{2,0},{3,1},{4,6},{5,7},{6,4},{7,5},{8,10},{9,11},{10,... | collective-permute-start | bytes 589832 | tf_op jit(solution)/shard_map/ppermute | solution.py:89
  31.8 6.4 %collective-permute-start.17 = (bf16[3,32,512]{2,1,0:T(8,128)(2,1)S(1)}, bf16[3,32,512]{2,1,0:T(8,128)(2,1)S(1)}, u32[]{:S(2)}, u32[]{:S(2)}) collective-permute-start(bf16[3,32,512]{2,1,0:T(8,128)(2,1)S(1)} %collective-permute-done.14.refs_1_), channel_id=1, source_target_pairs={{0,2},{1,3},{2,0},{3,1},{4,6},{5,7},{6,4},{7,5},{8,10},{9,11},{10,... | collective-permute-start | bytes 294920 | tf_op jit(solution)/shard_map/ppermute | solution.py:89
  43.7 21.8 %collective-permute-start.22 = (bf16[3,192,512]{2,1,0:T(8,128)(2,1)S(1)}, bf16[3,192,512]{2,1,0:T(8,128)(2,1)S(1)}, u32[]{:S(2)}, u32[]{:S(2)}) collective-permute-start(bf16[3,192,512]{2,1,0:T(8,128)(2,1)S(1)} %get-tuple-element.88), channel_id=1, source_target_pairs={{0,4},{4,0},{8,12},{12,8},{1,5},{5,1},{9,13},{13,9},{2,6},{6,2},{1... | collective-permute-start | bytes 1769480 | tf_op jit(solution)/shard_map/ppermute | solution.py:89
  46.2 15.7 %collective-permute-start.25 = (bf16[3,112,512]{2,1,0:T(8,128)(2,1)S(1)}, bf16[3,112,512]{2,1,0:T(8,128)(2,1)S(1)}, u32[]{:S(2)}, u32[]{:S(2)}) collective-permute-start(bf16[3,112,512]{2,1,0:T(8,128)(2,1)S(1)} %collective-permute-done.24.refs_0_), channel_id=1, source_target_pairs={{1,9},{2,10},{5,13},{6,14},{8,0},{11,3},{12,4},{15,7},{17,25},{18,... | collective-permute-start | bytes 1032200 | tf_op jit(solution)/shard_map/ppermute | solution.py:95
  47.5 15.8 %collective-permute-start.30 = (bf16[3,80,512]{2,1,0:T(8,128)(2,1)S(1)}, bf16[3,80,512]{2,1,0:T(8,128)(2,1)S(1)}, u32[]{:S(2)}, u32[]{:S(2)}) collective-permute-start(bf16[3,80,512]{2,1,0:T(8,128)(2,1)S(1)} %collective-permute-done.29.refs_0_), channel_id=1, source_target_pairs={{1,9},{2,10},{5,13},{6,14},{8,0},{11,3},{12,4},{15,7},{17,25},{18,... | collective-permute-start | bytes 737288 | tf_op jit(solution)/shard_map/ppermute | solution.py:95
  48.8 10.2 %collective-permute-start.28 = (f32[4,2048]{1,0:T(4,128)S(1)}, f32[4,2048]{1,0:T(4,128)S(1)}, u32[]{:S(2)}, u32[]{:S(2)}) collective-permute-start(f32[4,2048]{1,0:T(4,128)S(1)} %pad_maximum_fusion.refs_0_), channel_id=1, source_target_pairs={{0,3},{1,2},{2,1},{3,0},{4,7},{5,6},{6,5},{7,4},{8,11},{9,10},{10,... | collective-permute-start | bytes 98312 | tf_op jit(solution)/shard_map/ppermute | solution.py:89
  62.0 18.2 %collective-permute-start.32 = (bf16[3,112,512]{2,1,0:T(8,128)(2,1)S(1)}, bf16[3,112,512]{2,1,0:T(8,128)(2,1)S(1)}, u32[]{:S(2)}, u32[]{:S(2)}) collective-permute-start(bf16[3,112,512]{2,1,0:T(8,128)(2,1)S(1)} %shard_map.111.refs_0_), channel_id=1, source_target_pairs={{4,0},{9,13},{14,10},{3,7},{20,16},{25,29},{30,26},{19,23}} | collective-permute-start | bytes 1032200 | tf_op jit(solution)/shard_map/ppermute | solution.py:95
  63.4 16.8 %collective-permute-start.33 = (bf16[3,80,512]{2,1,0:T(8,128)(2,1)S(1)}, bf16[3,80,512]{2,1,0:T(8,128)(2,1)S(1)}, u32[]{:S(2)}, u32[]{:S(2)}) collective-permute-start(bf16[3,80,512]{2,1,0:T(8,128)(2,1)S(1)} %shard_map.112.refs_1_), channel_id=1, source_target_pairs={{4,0},{9,13},{14,10},{3,7},{20,16},{25,29},{30,26},{19,23}} | collective-permute-start | bytes 737288 | tf_op jit(solution)/shard_map/ppermute | solution.py:95
  65.7 25.6 %collective-permute-start.23 = (bf16[3,192,512]{2,1,0:T(8,128)(2,1)S(1)}, bf16[3,192,512]{2,1,0:T(8,128)(2,1)S(1)}, u32[]{:S(2)}, u32[]{:S(2)}) collective-permute-start(bf16[3,192,512]{2,1,0:T(8,128)(2,1)S(1)} %shard_map.109.part_ref), channel_id=1, source_target_pairs={{0,8},{4,12},{8,0},{12,4},{1,9},{5,13},{9,1},{13,5},{2,10},{6,14},... | collective-permute-start | bytes 1769480 | tf_op jit(solution)/shard_map/ppermute | solution.py:89
  80.3 11.0 %collective-permute-start.34 = (bf16[2,192,512]{2,1,0:T(8,128)(2,1)S(1)}, bf16[2,192,512]{2,1,0:T(8,128)(2,1)}, u32[]{:S(2)}, u32[]{:S(2)}) collective-permute-start(bf16[2,192,512]{2,1,0:T(8,128)(2,1)S(1)} %get-tuple-element.104.refs_0_), channel_id=1, source_target_pairs={{0,2},{13,15},{10,8},{7,5},{16,18},{29,31},{26,24},{23,21}} | collective-permute-start | bytes 1179656 | tf_op jit(solution)/shard_map/ppermute | solution.py:95
  82.4 8.9 %collective-permute-start.35 = (bf16[2,192,512]{2,1,0:T(8,128)(2,1)S(1)}, bf16[2,192,512]{2,1,0:T(8,128)(2,1)}, u32[]{:S(2)}, u32[]{:S(2)}) collective-permute-start(bf16[2,192,512]{2,1,0:T(8,128)(2,1)S(1)} %get-tuple-element.106.refs_2_), channel_id=1, source_target_pairs={{0,2},{13,15},{10,8},{7,5},{16,18},{29,31},{26,24},{23,21}} | collective-permute-start | bytes 1179656 | tf_op jit(solution)/shard_map/ppermute | solution.py:95
  84.4 10.9 %collective-permute-start.36 = (bf16[2,192,512]{2,1,0:T(8,128)(2,1)S(1)}, bf16[2,192,512]{2,1,0:T(8,128)(2,1)}, u32[]{:S(2)}, u32[]{:S(2)}) collective-permute-start(bf16[2,192,512]{2,1,0:T(8,128)(2,1)S(1)} %get-tuple-element.108.refs_4_), channel_id=1, source_target_pairs={{0,2},{13,15},{10,8},{7,5},{16,18},{29,31},{26,24},{23,21}} | collective-permute-start | bytes 1179656 | tf_op jit(solution)/shard_map/ppermute | solution.py:95
  99.4 14.5 %collective-permute-start.44 = (bf16[3,192,512]{2,1,0:T(8,128)(2,1)S(1)}, bf16[3,192,512]{2,1,0:T(8,128)(2,1)S(1)}, u32[]{:S(2)}, u32[]{:S(2)}) collective-permute-start(bf16[3,192,512]{2,1,0:T(8,128)(2,1)S(1)} %get-tuple-element.118.refs_3_), channel_id=1, source_target_pairs={{0,4},{4,0},{8,12},{12,8},{1,5},{5,1},{9,13},{13,9},{2,6},{6,2},{1... | collective-permute-start | bytes 1769480 | tf_op jit(solution)/shard_map/ppermute | solution.py:89
  105.6 7.1 %collective-permute-start.41 = (bf16[2,192,512]{2,1,0:T(8,128)(2,1)S(1)}, bf16[2,192,512]{2,1,0:T(8,128)(2,1)S(1)}, u32[]{:S(2)}, u32[]{:S(2)}) collective-permute-start(bf16[2,192,512]{2,1,0:T(8,128)(2,1)S(1)} %get-tuple-element.110.refs_0_), channel_id=1, source_target_pairs={{0,1},{2,3},{13,12},{15,14},{10,11},{8,9},{7,6},{5,4},{16,17},{18,... | collective-permute-start | bytes 1179656 | tf_op jit(solution)/shard_map/ppermute | solution.py:95
  (25 other events, 118.1 us)
